TPU v7x, 128 devices: a whole 4x4x4 slice. The times are simulated.
128 devices in a mesh: gx: 16 (over z, x), gy: 8 (over y, core).
Axes of the slice: x: 4, y: 4, z: 4, core: 2. Of those that a mesh axis runs over, the one named last changes fastest.
Arguments:
- ion_charge: float32 [512, 512, 128], P('gx', 'gy'), may hold values from -6 to 6
- density: float32 [512, 512, 128], P('gx', 'gy'), may hold values from 0.05 to 2
- charge_blocks: float32 [65536, 128], P(('gx', 'gy')), may hold values from -6 to 6
- panel_brick: int32 [16384], P(('gx', 'gy')), may hold values from 0 to 127, as said below
- row_counts: int32 [16384], P(('gx', 'gy')), may hold values from 1 to 4, as said below
- block_offset: int32 [65536], P(('gx', 'gy')), may hold values from 0 to 262136, as said below
- aperture_panel: int32 [2048], P(('gx', 'gy')), may hold values from 0 to 127
Outputs:
- potential: float32 [512, 512, 128], P('gx', 'gy')
- aperture_potential: float32 [2048], P(('gx', 'gy'))
Inputs may be any that keep to these rules, and one draw needn't show every extreme that they name: `panel_brick`: on every owner the 128 panels lie in the 128 bricks one each (a permutation for each owner). `row_counts`: on every owner some panel has exactly 4 live rows. `block_offset`: x below 32, y below 64, z at most 120.
All inputs are finite; a program needn't handle non-finite values.
Results may differ from a plain program's by a relative error of at most 0.00013.
Values sent between devices are 32-bit elements; how exact they have to be, the bound alone decides.
No kernel may reach another device: no remote copies, remote signals or barrier semaphores. Data moves between devices by JAX's collectives and lax.ppermute only.
A program may use at most 128 MiB of HBM per device.

v0:
```python
import math

import jax
import jax.numpy as jnp
from jax import lax
from jax.sharding import PartitionSpec as P

BX = 32
BY = 64
NZ = 128
NEWTON = 3
SWEEPS = 8
CAP = 4
BLX = 4
BLY = 4
BLZ = 8
BLK = 128


HIGH = lax.Precision.HIGHEST


def shifted(array, axis, by):
    length = lax.axis_size(axis)
    pairs = [(i, i + by) for i in range(length) if 0 <= i + by < length]
    return lax.ppermute(array, axis, pairs)


def extended_2(array, sides, width):
    for axis, dim in sides:
        size, length = (lax.axis_size(axis), array.shape[dim])
        up = [(i, (i + 1) % size) for i in range(size - 1)]
        down = [(j, i) for i, j in up]
        last = lax.slice_in_dim(array, length - width, length, axis=dim)
        first = lax.slice_in_dim(array, 0, width, axis=dim)
        before = lax.ppermute(last, axis, up)
        after = lax.ppermute(first, axis, down)
        array = jnp.concatenate([before, array, after], axis=dim)
    return array


def relax(padded, rhs, diagonal):
    inner = padded[1:-1, 1:-1]
    deep = jnp.pad(inner, ((0, 0), (0, 0), (1, 1)))
    total = padded[2:, 1:-1] + padded[:-2, 1:-1] + padded[1:-1, 2:] + padded[1:-1, :-2]
    total = total + deep[:, :, 2:] + deep[:, :, :-2]
    return (rhs + total) / diagonal


def selectors(offsets, wide_x, wide_y):
    corner_z = offsets % NZ
    remains = offsets // NZ
    corner_y = remains % BY
    corner_x = remains // BY
    pick_z = (
        jnp.arange(NZ, dtype=jnp.int32)[None, None, :]
        == corner_z[:, None, None] + jnp.arange(BLZ, dtype=jnp.int32)[None, :, None]
    ).astype(jnp.float32)
    pick_y = (
        jnp.arange(wide_y, dtype=jnp.int32)[None, None, :]
        == corner_y[:, None, None] + jnp.arange(BLY, dtype=jnp.int32)[None, :, None]
    ).astype(jnp.float32)
    pick_x = (
        jnp.arange(wide_x, dtype=jnp.int32)[None, None, :]
        == corner_x[:, None, None] + jnp.arange(BLX, dtype=jnp.int32)[None, :, None]
    ).astype(jnp.float32)
    return (pick_x, pick_y, pick_z)


def on_device(
    ion_charge, density, charge_blocks, panel_brick, row_counts, block_offset, aperture_panel
):
    panel_total = panel_brick.shape[0]
    peers = lax.axis_size("gx") * lax.axis_size("gy")
    slot_index = jnp.arange(CAP, dtype=jnp.int32)
    live_rows = (slot_index[None, :] < row_counts[:, None]).astype(jnp.float32)
    charges = charge_blocks.reshape(panel_total, CAP, BLK) * live_rows[:, :, None]
    placing = panel_brick[None, :] == jnp.arange(peers, dtype=jnp.int32)[:, None]
    placing_float = placing.astype(jnp.float32)
    send_rows = jnp.einsum("bp,pkc->bkc", placing_float, charges, precision=HIGH)
    send_offset = jnp.sum(
        placing.astype(jnp.int32)[:, :, None] * block_offset.reshape(panel_total, CAP)[None, :, :],
        axis=1,
    )
    got_rows, got_offset = (
        lax.all_to_all(send_rows, ("gx", "gy"), split_axis=0, concat_axis=0, tiled=True),
        lax.all_to_all(send_offset, ("gx", "gy"), split_axis=0, concat_axis=0, tiled=True),
    )
    row_total = peers * CAP
    got_rows = got_rows.reshape(row_total, BLK)
    got_offset = got_offset.reshape(row_total)
    wide_x = BX + BLX - 1
    wide_y = BY + BLY - 1
    block_rows = math.gcd(row_total, 64)
    turns = row_total // block_rows
    rows_blocked = got_rows.reshape(turns, block_rows, BLX, BLY, BLZ)
    offsets_blocked = got_offset.reshape(turns, block_rows)

    def deposit_block(extended, items):
        rows_here, offsets_here = items
        pick_x, pick_y, pick_z = selectors(offsets_here, wide_x, wide_y)
        along_z = jnp.einsum("rijl,rlz->rijz", rows_here, pick_z, precision=HIGH)
        along_y = jnp.einsum("rijz,rjy->riyz", along_z, pick_y, precision=HIGH)
        placed = jnp.einsum("rix,riyz->xyz", pick_x, along_y, precision=HIGH)
        return (extended + placed, None)

    extended, unused = lax.scan(
        deposit_block, jnp.zeros((wide_x, wide_y, NZ), jnp.float32), (rows_blocked, offsets_blocked)
    )
    lower_part = shifted(extended[BX:], "gx", 1)
    extended = extended.at[: BLX - 1].add(lower_part)
    side_part = shifted(extended[:BX, BY:], "gy", 1)
    extended = extended.at[:BX, : BLY - 1].add(side_part)
    source = ion_charge + extended[:BX, :BY]
    potential = jnp.zeros_like(ion_charge)
    for newton_step in range(NEWTON):
        coef = density * jnp.exp(potential)
        rhs = source + coef * (potential - 1.0)
        diagonal = 6.0 + coef
        for sweep_step in range(SWEEPS):
            padded = extended_2(potential, (("gx", 0), ("gy", 1)), 1)
            potential = relax(padded, rhs, diagonal)
    upper_x = shifted(potential[: BLX - 1], "gx", -1)
    grown = jnp.concatenate([potential, upper_x], axis=0)
    upper_y = shifted(grown[:, : BLY - 1], "gy", -1)
    grown = jnp.concatenate([grown, upper_y], axis=1)

    def read_block(carry, items):
        rows_here, offsets_here = items
        pick_x, pick_y, pick_z = selectors(offsets_here, wide_x, wide_y)
        along_x = jnp.einsum("rix,xyz->riyz", pick_x, grown, precision=HIGH)
        along_y = jnp.einsum("rjy,riyz->rijz", pick_y, along_x, precision=HIGH)
        values = jnp.einsum("rlz,rijz->rijl", pick_z, along_y, precision=HIGH)
        return (carry, jnp.sum(rows_here * values, axis=(1, 2, 3)))

    unused_carry, row_values = lax.scan(
        read_block, jnp.zeros((), jnp.float32), (rows_blocked, offsets_blocked)
    )
    row_potential = row_values.reshape(peers, CAP)
    returned = lax.all_to_all(row_potential, ("gx", "gy"), split_axis=0, concat_axis=0, tiled=True)
    panel_rows = jnp.einsum("bp,bk->pk", placing_float, returned, precision=HIGH)
    panel_potential = panel_rows.sum(axis=1) / row_counts.astype(jnp.float32)
    chooser = (aperture_panel[:, None] == jnp.arange(panel_total, dtype=jnp.int32)[None, :]).astype(
        jnp.float32
    )
    aperture_potential = jnp.sum(chooser * panel_potential[None, :], axis=1)
    return (potential, aperture_potential)


def solution(mesh):
    in_specs = (
        P("gx", "gy", None),
        P("gx", "gy", None),
        P(("gx", "gy"), None),
        P(("gx", "gy")),
        P(("gx", "gy")),
        P(("gx", "gy")),
        P(("gx", "gy")),
    )
    out_specs = (P("gx", "gy", None), P(("gx", "gy")))
    return jax.shard_map(
        on_device, mesh=mesh, in_specs=in_specs, out_specs=out_specs, check_vma=False
    )
```

profile of v0, /device:TPU:1, one launch (start us, length us, event | category | flops | bytes accessed | tf_op | source)
XLA Modules:
  0.0 808.0 jit_solution(781303517913804798)
XLA Ops:
  3.1 11.5 %all-to-all-start = ((s32[128,1,4]{2,1,0:T(1,128)}), s32[128,1,4]{2,1,0:T(1,128)S(1)}, u32[]{:S(2)}, u32[]{:S(2)}) async-start(s32[128,1,4]{2,1,0:T(1,128)} %copy.32), calls=%async_computation | async-start | bytes 131072 | tf_op jit(solution)/shard_map/all_to_all | solution.py:87
  17.5 6.7 all-to-all-done
  30.1 9.5 %all-to-all-done.1 = f32[128,4,128]{2,1,0:T(4,128)S(1)} async-done(((f32[128,4,128]{2,1,0:T(4,128)}), f32[128,4,128]{2,1,0:T(4,128)S(1)}, u32[]{:S(2)}, u32[]{:S(2)}) %all-to-all-start.1) | async-done | bytes 262176 | tf_op jit(solution)/shard_map/all_to_all | solution.py:86
  39.7 6.4 reshape_reshape.7
  46.1 165.7 %while.30 = (s32[]{:T(128)}, f32[35,67,128]{2,0,1:T(8,128)S(1)}, s32[8,64]{1,0:T(8,128)S(1)}, f32[8,64,4,4,8]{4,3,2,1,0:T(4,128)}, s32[]{:T(128)}, /*index=5*/s32[]{:T(128)}) while((s32[]{:T(128)}, f32[35,67,128]{2,0,1:T(8,128)S(1)}, s32[8,64]{1,0:T(8,128)S(1)}, f32[8,64,4,4,8]{4,3,2,1,0:T(4,128)}, s32[]{:T(128)}, ...), condition=%wide.region_2.3_spmd.clone, body=%wide.region_1.2_spmd.clone.sunk | while | flops 1040752256 | bytes 21549396 | solution.py:107
  48.1 7.0 convolution_bitcast_fusion.2
  55.1 11.9 %select_add_fusion.2 = f32[35,67,128]{2,0,1:T(8,128)S(1)} fusion(f32[35,67,128]{2,0,1:T(8,128)S(1)} %get-tuple-element.456, f32[64,4,67,128]{3,2,1,0:T(8,128)} %convolution_bitcast_fusion.2, pred[]{:T(512)S(6)} %compare.112, s32[64,4]{0,1:T(4,128)S(1)} %iota_add_fusion.17), kind=kOutput, calls=%fused_computation.35.clone.1 | convolution fusion | flops 922700800 | bytes 11184129 | tf_op jit(solution)/shard_map/while/body/eval_jaxpr/rix,riyz->xyz/dot_general | solution.py:104
  68.8 7.0 convolution_bitcast_fusion.2
  75.8 11.9 %select_add_fusion.2 = f32[35,67,128]{2,0,1:T(8,128)S(1)} fusion(f32[35,67,128]{2,0,1:T(8,128)S(1)} %get-tuple-element.456, f32[64,4,67,128]{3,2,1,0:T(8,128)} %convolution_bitcast_fusion.2, pred[]{:T(512)S(6)} %compare.112, s32[64,4]{0,1:T(4,128)S(1)} %iota_add_fusion.17), kind=kOutput, calls=%fused_computation.35.clone.1 | convolution fusion | flops 922700800 | bytes 11184129 | tf_op jit(solution)/shard_map/while/body/eval_jaxpr/rix,riyz->xyz/dot_general | solution.py:104
  89.5 7.0 convolution_bitcast_fusion.2
  96.5 11.9 %select_add_fusion.2 = f32[35,67,128]{2,0,1:T(8,128)S(1)} fusion(f32[35,67,128]{2,0,1:T(8,128)S(1)} %get-tuple-element.456, f32[64,4,67,128]{3,2,1,0:T(8,128)} %convolution_bitcast_fusion.2, pred[]{:T(512)S(6)} %compare.112, s32[64,4]{0,1:T(4,128)S(1)} %iota_add_fusion.17), kind=kOutput, calls=%fused_computation.35.clone.1 | convolution fusion | flops 922700800 | bytes 11184129 | tf_op jit(solution)/shard_map/while/body/eval_jaxpr/rix,riyz->xyz/dot_general | solution.py:104
  110.2 7.0 convolution_bitcast_fusion.2
  117.2 11.9 %select_add_fusion.2 = f32[35,67,128]{2,0,1:T(8,128)S(1)} fusion(f32[35,67,128]{2,0,1:T(8,128)S(1)} %get-tuple-element.456, f32[64,4,67,128]{3,2,1,0:T(8,128)} %convolution_bitcast_fusion.2, pred[]{:T(512)S(6)} %compare.112, s32[64,4]{0,1:T(4,128)S(1)} %iota_add_fusion.17), kind=kOutput, calls=%fused_computation.35.clone.1 | convolution fusion | flops 922700800 | bytes 11184129 | tf_op jit(solution)/shard_map/while/body/eval_jaxpr/rix,riyz->xyz/dot_general | solution.py:104
  130.8 7.0 convolution_bitcast_fusion.2
  137.9 11.9 %select_add_fusion.2 = f32[35,67,128]{2,0,1:T(8,128)S(1)} fusion(f32[35,67,128]{2,0,1:T(8,128)S(1)} %get-tuple-element.456, f32[64,4,67,128]{3,2,1,0:T(8,128)} %convolution_bitcast_fusion.2, pred[]{:T(512)S(6)} %compare.112, s32[64,4]{0,1:T(4,128)S(1)} %iota_add_fusion.17), kind=kOutput, calls=%fused_computation.35.clone.1 | convolution fusion | flops 922700800 | bytes 11184129 | tf_op jit(solution)/shard_map/while/body/eval_jaxpr/rix,riyz->xyz/dot_general | solution.py:104
  151.5 7.0 convolution_bitcast_fusion.2
  158.6 11.9 %select_add_fusion.2 = f32[35,67,128]{2,0,1:T(8,128)S(1)} fusion(f32[35,67,128]{2,0,1:T(8,128)S(1)} %get-tuple-element.456, f32[64,4,67,128]{3,2,1,0:T(8,128)} %convolution_bitcast_fusion.2, pred[]{:T(512)S(6)} %compare.112, s32[64,4]{0,1:T(4,128)S(1)} %iota_add_fusion.17), kind=kOutput, calls=%fused_computation.35.clone.1 | convolution fusion | flops 922700800 | bytes 11184129 | tf_op jit(solution)/shard_map/while/body/eval_jaxpr/rix,riyz->xyz/dot_general | solution.py:104
  172.2 7.0 convolution_bitcast_fusion.2
  179.3 11.9 %select_add_fusion.2 = f32[35,67,128]{2,0,1:T(8,128)S(1)} fusion(f32[35,67,128]{2,0,1:T(8,128)S(1)} %get-tuple-element.456, f32[64,4,67,128]{3,2,1,0:T(8,128)} %convolution_bitcast_fusion.2, pred[]{:T(512)S(6)} %compare.112, s32[64,4]{0,1:T(4,128)S(1)} %iota_add_fusion.17), kind=kOutput, calls=%fused_computation.35.clone.1 | convolution fusion | flops 922700800 | bytes 11184129 | tf_op jit(solution)/shard_map/while/body/eval_jaxpr/rix,riyz->xyz/dot_general | solution.py:104
  192.9 7.0 convolution_bitcast_fusion.2
  200.0 11.9 %select_add_fusion.2 = f32[35,67,128]{2,0,1:T(8,128)S(1)} fusion(f32[35,67,128]{2,0,1:T(8,128)S(1)} %get-tuple-element.456, f32[64,4,67,128]{3,2,1,0:T(8,128)} %convolution_bitcast_fusion.2, pred[]{:T(512)S(6)} %compare.112, s32[64,4]{0,1:T(4,128)S(1)} %iota_add_fusion.17), kind=kOutput, calls=%fused_computation.35.clone.1 | convolution fusion | flops 922700800 | bytes 11184129 | tf_op jit(solution)/shard_map/while/body/eval_jaxpr/rix,riyz->xyz/dot_general | solution.py:104
  279.8 5.5 collective-permute-start.19
  296.3 6.7 collective-permute-start.23
  306.0 5.1 collective-permute-start.25
  314.1 6.7 collective-permute-start.27
  323.7 5.1 collective-permute-start.29
  331.8 6.7 collective-permute-start.31
  341.5 5.1 collective-permute-start.33
  349.6 6.7 collective-permute-start.35
  359.2 5.1 collective-permute-start.37
  367.3 6.7 collective-permute-start.39
  377.0 5.1 collective-permute-start.41
  384.9 6.7 collective-permute-start.43
  394.6 5.1 collective-permute-start.45
  402.5 6.7 collective-permute-start.47
  412.2 5.2 collective-permute-start.49
  420.1 6.7 collective-permute-start.51
  429.8 5.1 collective-permute-start.53
  437.7 6.7 collective-permute-start.55
  455.3 6.7 collective-permute-start.59
  465.0 5.1 collective-permute-start.61
  472.9 6.7 collective-permute-start.63
  482.6 5.1 collective-permute-start.65
  490.5 6.7 collective-permute-start.67
  500.2 5.1 collective-permute-start.69
  508.3 6.7 collective-permute-start.71
  525.9 6.7 collective-permute-start.75
  543.5 6.7 collective-permute-start.79
  561.1 6.7 collective-permute-start.83
  578.8 6.7 collective-permute-start.87
  596.4 6.7 collective-permute-start.91
  614.0 6.7 collective-permute-start.95
  631.6 6.8 collective-permute-done.98
  640.3 5.1 collective-permute-done.99
  645.9 135.4 %while.29 = (s32[]{:T(128)}, f32[8,64]{1,0:T(8,128)S(1)}, f32[8,64,4,4,8]{4,3,2,1,0:T(4,128)}, s32[8,64]{1,0:T(8,128)S(1)}, f32[35,67,128]{2,0,1:T(8,128)S(1)}, /*index=5*/s32[]{:T(128)}, s32[]{:T(128)}) while((s32[]{:T(128)}, f32[8,64]{1,0:T(8,128)S(1)}, f32[8,64,4,4,8]{4,3,2,1,0:T(4,128)}, s32[8,64]{1,0:T(8,128)S(1)}, ...), condition=%wide.region_5.6_spmd, body=%wide.region_3.5_spmd.sunk | while | flops 1040168448 | bytes 19857756 | solution.py:136
  649.9 10.8 %fusion.267 = f32[64,4,4,128]{3,2,1,0:T(4,128)S(1)} fusion(f32[64,4,67,128]{3,0,2,1:T(8,128)S(1)} %fusion.266, s32[64,4]{1,0:T(8,128)S(1)} %iota_add_fusion.13), kind=kOutput, calls=%fused_computation.4.clone.1 | convolution fusion | flops 105399040 | bytes 9307136 | tf_op jit(solution)/shard_map/while/body/eval_jaxpr/rjy,riyz->rijz/dot_general | solution.py:132
  666.8 10.8 %fusion.267 = f32[64,4,4,128]{3,2,1,0:T(4,128)S(1)} fusion(f32[64,4,67,128]{3,0,2,1:T(8,128)S(1)} %fusion.266, s32[64,4]{1,0:T(8,128)S(1)} %iota_add_fusion.13), kind=kOutput, calls=%fused_computation.4.clone.1 | convolution fusion | flops 105399040 | bytes 9307136 | tf_op jit(solution)/shard_map/while/body/eval_jaxpr/rjy,riyz->rijz/dot_general | solution.py:132
  683.7 10.8 %fusion.267 = f32[64,4,4,128]{3,2,1,0:T(4,128)S(1)} fusion(f32[64,4,67,128]{3,0,2,1:T(8,128)S(1)} %fusion.266, s32[64,4]{1,0:T(8,128)S(1)} %iota_add_fusion.13), kind=kOutput, calls=%fused_computation.4.clone.1 | convolution fusion | flops 105399040 | bytes 9307136 | tf_op jit(solution)/shard_map/while/body/eval_jaxpr/rjy,riyz->rijz/dot_general | solution.py:132
  700.6 10.8 %fusion.267 = f32[64,4,4,128]{3,2,1,0:T(4,128)S(1)} fusion(f32[64,4,67,128]{3,0,2,1:T(8,128)S(1)} %fusion.266, s32[64,4]{1,0:T(8,128)S(1)} %iota_add_fusion.13), kind=kOutput, calls=%fused_computation.4.clone.1 | convolution fusion | flops 105399040 | bytes 9307136 | tf_op jit(solution)/shard_map/while/body/eval_jaxpr/rjy,riyz->rijz/dot_general | solution.py:132
  717.5 10.8 %fusion.267 = f32[64,4,4,128]{3,2,1,0:T(4,128)S(1)} fusion(f32[64,4,67,128]{3,0,2,1:T(8,128)S(1)} %fusion.266, s32[64,4]{1,0:T(8,128)S(1)} %iota_add_fusion.13), kind=kOutput, calls=%fused_computation.4.clone.1 | convolution fusion | flops 105399040 | bytes 9307136 | tf_op jit(solution)/shard_map/while/body/eval_jaxpr/rjy,riyz->rijz/dot_general | solution.py:132
  734.4 10.8 %fusion.267 = f32[64,4,4,128]{3,2,1,0:T(4,128)S(1)} fusion(f32[64,4,67,128]{3,0,2,1:T(8,128)S(1)} %fusion.266, s32[64,4]{1,0:T(8,128)S(1)} %iota_add_fusion.13), kind=kOutput, calls=%fused_computation.4.clone.1 | convolution fusion | flops 105399040 | bytes 9307136 | tf_op jit(solution)/shard_map/while/body/eval_jaxpr/rjy,riyz->rijz/dot_general | solution.py:132
  751.3 10.8 %fusion.267 = f32[64,4,4,128]{3,2,1,0:T(4,128)S(1)} fusion(f32[64,4,67,128]{3,0,2,1:T(8,128)S(1)} %fusion.266, s32[64,4]{1,0:T(8,128)S(1)} %iota_add_fusion.13), kind=kOutput, calls=%fused_computation.4.clone.1 | convolution fusion | flops 105399040 | bytes 9307136 | tf_op jit(solution)/shard_map/while/body/eval_jaxpr/rjy,riyz->rijz/dot_general | solution.py:132
  768.2 10.8 %fusion.267 = f32[64,4,4,128]{3,2,1,0:T(4,128)S(1)} fusion(f32[64,4,67,128]{3,0,2,1:T(8,128)S(1)} %fusion.266, s32[64,4]{1,0:T(8,128)S(1)} %iota_add_fusion.13), kind=kOutput, calls=%fused_computation.4.clone.1 | convolution fusion | flops 105399040 | bytes 9307136 | tf_op jit(solution)/shard_map/while/body/eval_jaxpr/rjy,riyz->rijz/dot_general | solution.py:132
  781.4 25.5 %all_to_all.26 = f32[128,1,4]{2,1,0:T(1,128)S(1)} all-to-all(f32[128,1,4]{2,1,0:T(1,128)S(1)} %bitcast.113), channel_id=1, replica_groups=mesh['gx'=16,'gy'=8] {'gx','gy'}, dimensions={0} | all-to-all | bytes 4096 | tf_op jit(solution)/shard_map/all_to_all | solution.py:140
  (402 shorter events, 307.0 us)
Async XLA Ops:
  3.1 21.1 %all-to-all-start = ((s32[128,1,4]{2,1,0:T(1,128)}), s32[128,1,4]{2,1,0:T(1,128)S(1)}, u32[]{:S(2)}, u32[]{:S(2)}) async-start(s32[128,1,4]{2,1,0:T(1,128)} %copy.32), calls=%async_computation | async-start | bytes 131072 | tf_op jit(solution)/shard_map/all_to_all | solution.py:87
  24.2 15.5 %all-to-all-start.1 = ((f32[128,4,128]{2,1,0:T(4,128)}), f32[128,4,128]{2,1,0:T(4,128)S(1)}, u32[]{:S(2)}, u32[]{:S(2)}) async-start(f32[128,4,128]{2,1,0:T(4,128)} %copy.34), calls=%async_computation.1 | async-start | bytes 524288 | tf_op jit(solution)/shard_map/all_to_all | solution.py:86
  212.1 7.6 collective-permute-start
  214.5 8.9 %collective-permute-start.2 = (f32[1,64,128]{2,1,0:T(8,128)S(1)}, f32[1,64,128]{2,1,0:T(8,128)S(1)}, u32[]{:S(2)}, u32[]{:S(2)}) collective-permute-start(f32[1,64,128]{2,1,0:T(8,128)S(1)} %broadcast.695), channel_id=1, source_target_pairs={{8,0},{16,8},{24,16},{32,24},{40,32},{48,40},{56,48},{64,56},{72,6... | collective-permute-start | bytes 98312 | tf_op jit(solution)/shard_map/ppermute | solution.py:37
  215.8 7.6 collective-permute-start.3
  219.8 9.3 %collective-permute-start.1 = (f32[32,3,128]{2,1,0:T(4,128)S(1)}, f32[32,3,128]{2,1,0:T(4,128)S(1)}, u32[]{:S(2)}, u32[]{:S(2)}) collective-permute-start(f32[32,3,128]{2,1,0:T(4,128)S(1)} %slice.1125), channel_id=1, source_target_pairs={{0,1},{1,2},{2,3},{3,4},{4,5},{5,6},{6,7},{8,9},{9,10},{10,11},{11... | collective-permute-start | bytes 147464 | tf_op jit(solution)/shard_map/ppermute | solution.py:26
  223.5 7.7 collective-permute-start.4
  254.2 7.0 collective-permute-start.12
  269.8 7.0 collective-permute-start.16
  286.3 7.0 collective-permute-start.20
  295.0 8.0 collective-permute-start.22
  296.3 7.7 collective-permute-start.23
  304.1 7.0 collective-permute-start.24
  312.8 8.0 collective-permute-start.26
  314.1 7.7 collective-permute-start.27
  321.8 7.0 collective-permute-start.28
  330.5 8.0 collective-permute-start.30
  331.8 7.7 collective-permute-start.31
  339.6 7.0 collective-permute-start.32
  348.3 8.0 collective-permute-start.34
  349.6 7.7 collective-permute-start.35
  357.3 7.0 collective-permute-start.36
  366.0 8.0 collective-permute-start.38
  367.3 7.7 collective-permute-start.39
  375.0 7.0 collective-permute-start.40
  383.6 8.0 collective-permute-start.42
  384.9 7.7 collective-permute-start.43
  392.6 7.0 collective-permute-start.44
  401.2 8.0 collective-permute-start.46
  402.5 7.7 collective-permute-start.47
  410.2 7.2 collective-permute-start.48
  418.8 8.0 collective-permute-start.50
  420.1 7.7 collective-permute-start.51
  427.8 7.0 collective-permute-start.52
  436.4 8.0 collective-permute-start.54
  437.7 7.7 collective-permute-start.55
  445.4 7.0 collective-permute-start.56
  454.0 8.0 collective-permute-start.58
  455.3 7.7 collective-permute-start.59
  463.0 7.0 collective-permute-start.60
  471.6 8.0 collective-permute-start.62
  472.9 7.7 collective-permute-start.63
  480.6 7.0 collective-permute-start.64
  489.2 8.0 collective-permute-start.66
  490.5 7.7 collective-permute-start.67
  498.3 7.0 collective-permute-start.68
  507.0 8.0 collective-permute-start.70
  508.3 7.7 collective-permute-start.71
  516.0 7.0 collective-permute-start.72
  524.6 8.0 collective-permute-start.74
  525.9 7.7 collective-permute-start.75
  542.2 8.0 collective-permute-start.78
  543.5 7.7 collective-permute-start.79
  559.8 8.0 collective-permute-start.82
  561.1 7.7 collective-permute-start.83
  568.8 7.0 collective-permute-start.84
  577.5 8.0 collective-permute-start.86
  578.8 7.7 collective-permute-start.87
  595.1 8.0 collective-permute-start.90
  596.4 7.7 collective-permute-start.91
  612.7 8.0 collective-permute-start.94
  614.0 7.7 collective-permute-start.95
  630.3 8.1 collective-permute-start.98
  638.4 7.1 collective-permute-start.99
  (45 other events, 774.9 us)
where the time goes:
time: 815 us; the launch traced here: 808 us
  starting transfers between devices  371 us (46%)
  matrix products  298 us (37%)
  waiting for transfers between devices  70.5 us (9%)
  other arithmetic  26.5 us (3%)
  blocking collectives  25.5 us (3%)
  local copies, waits for them, and re-layouts  12.8 us (2%)
    ppermute x48, starting transfers between devices, extended_2(): before = lax.ppermute(last, axis, up)  269 us
    dot_general x8, matrix products, deposit_block(): placed = jnp.einsum('rix,riyz->xyz', pick_x, along_y, precision=HIGH)  94.9 us
    dot_general x8, matrix products, read_block(): along_y = jnp.einsum('rjy,riyz->rijz', pick_y, along_x, precision=HIGH)  86.5 us
    ppermute x48, starting transfers between devices, extended_2(): after = lax.ppermute(first, axis, down)  77.1 us
    dot_general x8, matrix products, deposit_block(): along_y = jnp.einsum('rijz,rjy->riyz', along_z, pick_y, precision=HIGH)  56.1 us
    ppermute x48, waiting for transfers between devices, extended_2(): before = lax.ppermute(last, axis, up)  42.2 us
    dot_general x8, matrix products, read_block(): along_x = jnp.einsum('rix,xyz->riyz', pick_x, grown, precision=HIGH)  29 us
    all_to_all x1, blocking collectives, on_device(): lax.all_to_all(row_potential, ('gx', 'gy'), split_axis=0, concat_axis=0,...  25.5 us
  transfers between devices with their start and end apart: 102, of which 50 were waited for; matrix products, arithmetic and copies ran while one was open for 1% of the time, Pallas kernels for 0%

commit v1 on v0

v1 whole, which is shorter than its diff:
```python
import jax
import jax.numpy as jnp
from jax import lax
from jax.experimental import pallas as pl
from jax.experimental.pallas import tpu as pltpu
from jax.sharding import PartitionSpec as P

BX = 32
BY = 64
NZ = 128
NEWTON = 3
SWEEPS = 8
CAP = 4
BLX = 4
BLY = 4
BLZ = 8
N_GX = 16
N_GY = 8
PAN_DEV = 128
APER_DEV = 16
LOW = 8
HIGH = 11
WX = LOW + BX + HIGH
TILES = 11
WY = 8 * TILES
DEPX = BX + BLX - 1
DEPY = 72
UNROLL = 8

VMEM = pl.BlockSpec(memory_space=pltpu.VMEM)
SMEM = pl.BlockSpec(memory_space=pltpu.SMEM)
F32 = jnp.float32


def call(body, outs, ins, scratch=(), mib=24):
    return pl.pallas_call(
        body,
        out_shape=[jax.ShapeDtypeStruct(s, F32) for s in outs],
        in_specs=list(ins),
        out_specs=[VMEM] * len(outs),
        scratch_shapes=list(scratch),
        compiler_params=pltpu.CompilerParams(vmem_limit_bytes=mib << 20),
    )


def iota(shape, dim):
    return lax.broadcasted_iota(jnp.int32, shape, dim)


def pack_kernel(brick, counts, offsets, aper, rows, send, need):
    def clear(p, c):
        need[p] = 0
        return c

    lax.fori_loop(0, PAN_DEV, clear, 0)
    for a in range(APER_DEV):
        need[aper[a]] = 1
    sub = iota((8, 128), 0)
    group = (iota((8, 128), 1) >> 3) & 3
    j = sub & 3
    masks = {e: (group == j - e) for e in range(-3, 4)}
    lane1 = iota((1, 128), 1)

    def body(q, c):
        p = q * 2
        live = sub < jnp.where(sub < 4, counts[p], counts[p + 1] + 4)
        v = jnp.where(live, rows[pl.ds(pl.multiple_of(q * 8, 8), 8), :], 0.0)
        out = v
        for e in (-3, -2, -1, 1, 2, 3):
            moved = pltpu.roll(pltpu.roll(v, e % 8, 0), (-8 * e) % 128, 1)
            out = jnp.where(masks[e], moved, out)
        for h in range(2):
            b = brick[p + h]
            send[b, 0:4, :] = out[4 * h : 4 * h + 4]
            meta = jnp.zeros((1, 128), jnp.int32)
            for k in range(CAP):
                meta = jnp.where(lane1 == k, offsets[(p + h) * CAP + k], meta)
            meta = jnp.where(lane1 == CAP, need[p + h], meta)
            send[b, 4:5, :] = meta.astype(F32)
        return c

    lax.fori_loop(0, PAN_DEV // 2, body, 0, unroll=2)


def corner(meta, p, k):
    offset = meta[p, k].astype(jnp.int32)
    return offset >> 13, (offset >> 7) & 63, offset & 127


def block_rows(v, z, k, i, lane):
    moved = pltpu.roll(v, (z - 32 * i - 8 * k + 128) & 127, 1)
    return jnp.where((lane >= z) & (lane < z + BLZ), moved, 0.0)


def deposit_kernel(got, ion, out, low, high, meta, sem):
    copy = pltpu.make_async_copy(got.at[:, 4, :], meta, sem)
    copy.start()
    out[0:BX, 0:BY, :] = ion[...]
    out[0:BX, BY:DEPY, :] = jnp.zeros((BX, DEPY - BY, NZ), F32)
    out[BX:DEPX] = jnp.zeros((DEPX - BX, DEPY, NZ), F32)
    lane = iota((BLY, 128), 1)
    copy.wait()

    def body(p, c):
        v = got[p, 0:4, :]
        for k in range(CAP):
            x, y, z = corner(meta, p, k)
            for i in range(BLX):
                out[x + i, pl.ds(y, BLY), :] += block_rows(v, z, k, i, lane)
        return c

    lax.fori_loop(0, PAN_DEV, body, 0, unroll=4)
    low[...] = out[0:HIGH]
    high[...] = out[BX - LOW : DEPX]


def widen_kernel(own, below, above, out, low, high):
    inside = jnp.where(lax.axis_index("gx") > 0, 1.0, 0.0)
    spill = DEPX - BX
    out[0:LOW] = below[0:LOW]
    out[LOW : LOW + BX] = own[0:BX]
    out[LOW : LOW + spill] += below[LOW : LOW + spill] * inside
    out[LOW + BX : WX] = above[...]
    out[LOW + BX : LOW + BX + spill] += own[BX:DEPX]
    low[...] = out[:, 0:16]
    high[...] = out[:, BY - LOW : DEPY]


def bounds():
    gx, gy = lax.axis_index("gx"), lax.axis_index("gy")
    x_lo = jnp.where(gx == 0, LOW, 0)
    x_hi = jnp.where(gx == N_GX - 1, LOW + BX, WX)
    y_lo = jnp.where(gy == 0, LOW, 0)
    y_hi = jnp.where(gy == N_GY - 1, LOW + BY, WY)
    sub = iota((8, 128), 0)
    inside = []
    for t in range(TILES):
        y = sub * TILES + t
        inside.append((y >= y_lo) & (y < y_hi))
    return x_lo, x_hi, inside


def sweep(src, dst, rhs, inv, lo, hi):
    lane = iota((8, 128), 1)
    first, last = lane == 0, lane == NZ - 1

    def layer(x):
        return [src[x, t] for t in range(TILES)]

    def rows(x0, count):
        layers = [layer(x0 - 1 + u) for u in range(count + 2)]
        for u in range(count):
            prev, cur, nxt = layers[u : u + 3]
            before = [pltpu.roll(cur[-1], 1, 0)] + cur[:-1]
            after = cur[1:] + [pltpu.roll(cur[0], 7, 0)]
            for t in range(TILES):
                left = jnp.where(first, 0.0, pltpu.roll(cur[t], 1, 1))
                right = jnp.where(last, 0.0, pltpu.roll(cur[t], NZ - 1, 1))
                total = (prev[t] + nxt[t]) + (before[t] + after[t]) + (left + right)
                dst[x0 + u, t] = (rhs[x0 + u, t] + total) * inv[x0 + u, t]

    turns = (hi - lo) // UNROLL

    def body(i, c):
        rows(lo + i * UNROLL, UNROLL)
        return c

    lax.fori_loop(0, turns, body, 0)
    if (hi - lo) % UNROLL:
        rows(lo + turns * UNROLL, (hi - lo) % UNROLL)


def finish(pot, nat, out, low, high):
    def body(x, c):
        for t in range(TILES):
            nat[x, pl.ds(t, 8, stride=TILES), :] = pot[x + LOW, t]
        return c

    lax.fori_loop(0, DEPX, body, 0, unroll=5)
    out[...] = nat[0:BX, LOW : LOW + BY]
    if high is not None:
        low[...] = nat[0:HIGH, LOW : LOW + BY]
        high[...] = nat[BX - LOW : BX, LOW : LOW + BY]
    else:
        low[...] = nat[0:DEPX, LOW : LOW + DEPY]


def first_kernel(
    own, below, above, density, out, low, high, source, dens, nat, b0, b1, rhs, inv
):
    x_lo, x_hi, inside = bounds()
    spread = jnp.where(lax.axis_index("gy") > 0, 1.0, 0.0)
    nat[:, 0:LOW] = below[:, 0:LOW]
    nat[:, LOW : LOW + DEPY] = own[...]
    nat[:, LOW : LOW + 8] += below[:, 8:16] * spread
    nat[:, LOW + DEPY : WY] = above[:, 8:16]
    nat[:, LOW + BY : LOW + DEPY] += above[:, 0:8]

    def prep(x, c):
        f = jnp.where((x >= x_lo) & (x < x_hi), 1.0, 0.0)
        for t in range(TILES):
            s = nat[x, pl.ds(t, 8, stride=TILES), :]
            d = density[x, pl.ds(t, 8, stride=TILES), :]
            source[x, t] = s
            dens[x, t] = d
            scale = jnp.where(inside[t], f / (6.0 + d), 0.0)
            inv[x, t] = scale
            rhs[x, t] = s - d
            b1[x, t] = (s - d) * scale
        return c

    lax.fori_loop(0, WX, prep, 0, unroll=3)
    bufs = (b0, b1)
    for k in range(2, SWEEPS + 1):
        sweep(bufs[(k - 1) % 2], bufs[k % 2], rhs, inv, k, WX - k)
    finish(b0, nat, out, low, high)


def next_kernel(
    own, x_below, x_above, y_below, y_above, source, dens, out, low, high, nat, b0, b1, rhs, inv
):
    x_lo, x_hi, inside = bounds()
    nat[:, 0:LOW] = y_below[...]
    nat[0:LOW, LOW : LOW + BY] = x_below[...]
    nat[LOW : LOW + BX, LOW : LOW + BY] = own[...]
    nat[LOW + BX : WX, LOW : LOW + BY] = x_above[...]
    nat[:, LOW + BY : WY] = y_above[...]

    def prep(x, c):
        f = jnp.where((x >= x_lo) & (x < x_hi), 1.0, 0.0)
        for t in range(TILES):
            p = jnp.where(inside[t], nat[x, pl.ds(t, 8, stride=TILES), :] * f, 0.0)
            coef = dens[x, t] * jnp.exp(p)
            b0[x, t] = p
            rhs[x, t] = source[x, t] + coef * (p - 1.0)
            inv[x, t] = jnp.where(inside[t], f / (6.0 + coef), 0.0)
        return c

    lax.fori_loop(0, WX, prep, 0, unroll=3)
    bufs = (b0, b1)
    for k in range(1, SWEEPS + 1):
        sweep(bufs[(k - 1) % 2], bufs[k % 2], rhs, inv, k, WX - k)
    finish(b0, nat, out, low, high)


def last_kernel(*refs):
    next_kernel(*refs[:9], None, *refs[9:])


def read_kernel(got, field, out, meta, sem):
    copy = pltpu.make_async_copy(got.at[:, 4, :], meta, sem)
    copy.start()
    out[...] = jnp.zeros((PAN_DEV, 1, 128), F32)
    lane = iota((BLY, 128), 1)
    copy.wait()

    def body(p, c):
        @pl.when(meta[p, CAP].astype(jnp.int32) > 0)
        def _():
            v = got[p, 0:4, :]
            total = jnp.zeros((BLY, 128), F32)
            for k in range(CAP):
                x, y, z = corner(meta, p, k)
                for i in range(BLX):
                    total += block_rows(v, z, k, i, lane) * field[x + i, pl.ds(y, BLY), :]
            out[p] = jnp.sum(total, axis=0, keepdims=True)

        return c

    lax.fori_loop(0, PAN_DEV, body, 0)


def pick_kernel(brick, counts, aper, got, out, rows):
    sub = iota((APER_DEV, 1), 0)
    live = jnp.ones((APER_DEV, 1), F32)
    for a in range(APER_DEV):
        p = aper[a]
        rows[a : a + 1, :] = got[brick[p]]
        live = jnp.where(sub == a, counts[p].astype(F32), live)
    out[...] = jnp.sum(rows[...], axis=1, keepdims=True) / live


def ring(array, axis, by):
    size = lax.axis_size(axis)
    return lax.ppermute(array, axis, [(i, (i + by) % size) for i in range(size)])


def on_device(
    ion_charge, density, charge_blocks, panel_brick, row_counts, block_offset, aperture_panel
):
    everyone = ("gx", "gy")
    (send,) = call(
        pack_kernel,
        [(PAN_DEV, 8, 128)],
        [SMEM] * 4 + [VMEM],
        [pltpu.SMEM((PAN_DEV,), jnp.int32)],
    )(panel_brick, row_counts, block_offset, aperture_panel, charge_blocks)
    got = lax.all_to_all(send, everyone, split_axis=0, concat_axis=0, tiled=True)

    d_below = ring(density[BX - LOW :], "gx", 1)
    d_above = ring(density[:HIGH], "gx", -1)
    d_wide = jnp.concatenate([d_below, density, d_above], axis=0)
    d_left = ring(d_wide[:, BY - LOW :], "gy", 1)
    d_right = ring(d_wide[:, :16], "gy", -1)
    d_wide = jnp.concatenate([d_left, d_wide, d_right], axis=1)

    meta = [pltpu.SMEM((PAN_DEV, 128), F32), pltpu.SemaphoreType.DMA]
    own, low, high = call(
        deposit_kernel,
        [(DEPX, DEPY, NZ), (HIGH, DEPY, NZ), (HIGH, DEPY, NZ)],
        [VMEM] * 2,
        meta,
    )(got, ion_charge)
    below, above = ring(high, "gx", 1), ring(low, "gx", -1)
    wide, low, high = call(
        widen_kernel, [(WX, DEPY, NZ), (WX, 16, NZ), (WX, 16, NZ)], [VMEM] * 3
    )(own, below, above)
    below, above = ring(high, "gy", 1), ring(low, "gy", -1)

    tiles = (WX, TILES, 8, NZ)
    work = [pltpu.VMEM((WX, WY, NZ), F32)] + [pltpu.VMEM(tiles, F32)] * 4
    brick = [(BX, BY, NZ), (HIGH, BY, NZ), (LOW, BY, NZ)]
    pot, low, high, source, dens = call(
        first_kernel, brick + [tiles, tiles], [VMEM] * 4, work, 40
    )(wide, below, above, d_wide)
    for step in range(1, NEWTON):
        below, above = ring(high, "gx", 1), ring(low, "gx", -1)
        edge = jnp.concatenate(
            [below[:, BY - LOW :], pot[:, BY - LOW :], above[:, BY - LOW :]], axis=0
        )
        left = ring(edge, "gy", 1)
        edge = jnp.concatenate([below[:, :16], pot[:, :16], above[:, :16]], axis=0)
        right = ring(edge, "gy", -1)
        operands = (pot, below, above, left, right, source, dens)
        if step < NEWTON - 1:
            pot, low, high = call(next_kernel, brick, [VMEM] * 7, work, 40)(*operands)
        else:
            pot, grown = call(
                last_kernel, [brick[0], (DEPX, DEPY, NZ)], [VMEM] * 7, work, 40
            )(*operands)
    (sums,) = call(read_kernel, [(PAN_DEV, 1, 128)], [VMEM] * 2, meta)(got, grown)
    back = lax.all_to_all(sums, everyone, split_axis=0, concat_axis=0, tiled=True)
    (picked,) = call(
        pick_kernel,
        [(APER_DEV, 1)],
        [SMEM] * 3 + [VMEM],
        [pltpu.VMEM((APER_DEV, 128), F32)],
    )(panel_brick, row_counts, aperture_panel, back)
    return pot, picked.reshape(APER_DEV)


def solution(mesh):
    everyone = P(("gx", "gy"))
    grid = P("gx", "gy", None)
    return jax.shard_map(
        on_device,
        mesh=mesh,
        in_specs=(grid, grid, P(("gx", "gy"), None)) + (everyone,) * 4,
        out_specs=(grid, everyone),
        check_vma=False,
    )
```

time: 815 us -> 174 us (0.21)
  starting transfers between devices: 371 us -> 41.5 us
  matrix products: 298 us -> 0 us
  Pallas kernels: 0 us -> 55.4 us
  other arithmetic: 26.5 us -> 0.89 us
  waiting for transfers between devices: 70.5 us -> 51 us
  blocking collectives: 25.5 us -> 16.6 us
    ppermute x100 -> x16, starting transfers between devices: 355 us -> 30 us  [ring(): lax.ppermute(array, axis, [(i, (i + by) % size) for i in range(size)])]
    dot_general x50 -> x0, matrix products: 298 us -> none  [the longest x8 94.9 us: deposit_block(): placed = jnp.einsum('rix,riyz->xyz', pick_x, along_y, precision=HIGH)]
    pallas_call x0 -> x8, Pallas kernels: none -> 55.4 us  [the longest x1 13.9 us: on_device(): call(last_kernel, [brick[0], (DEPX, DEPY, NZ)], [VMEM] * 7, work, 40)]
    div x25 -> x0, other arithmetic: 19.7 us -> none  [the longest x24 19.7 us: relax(): return (rhs + total) / diagonal]
    all_to_all x2 -> x1, waiting for transfers between devices: 16.2 us -> 0.01 us  [on_device(): lax.all_to_all(send, everyone, split_axis=0, concat_axis=0, tiled=True)]
    all_to_all x1, blocking collectives: 25.5 us -> 16.6 us  [on_device(): lax.all_to_all(sums, everyone, split_axis=0, concat_axis=0, tiled=True)]
    ppermute x100 -> x16, waiting for transfers between devices: 54.2 us -> 51 us  [ring(): lax.ppermute(array, axis, [(i, (i + by) % size) for i in range(size)])]
  transfers between devices with their start and end apart: 102 -> 17, of which waited for: 50 -> 10; matrix products, arithmetic and copies ran while one was open for 1% -> 2% of each run, Pallas kernels for 0% -> 4%
where the time goes in v1:
time: 174 us
  Pallas kernels  55.4 us (32%)
  waiting for transfers between devices  51 us (29%)
  starting transfers between devices  41.5 us (24%)
  blocking collectives  16.6 us (10%)
  local copies, waits for them, and re-layouts  7.61 us (4%)
    ppermute x16, waiting for transfers between devices, ring(): lax.ppermute(array, axis, [(i, (i + by) % size) for i in range(size)])  51 us
    ppermute x16, starting transfers between devices, ring(): lax.ppermute(array, axis, [(i, (i + by) % size) for i in range(size)])  30 us
    all_to_all x1, blocking collectives, on_device(): lax.all_to_all(sums, everyone, split_axis=0, concat_axis=0, tiled=True)  16.6 us
    pallas_call x1, Pallas kernels, on_device(): call(last_kernel, [brick[0], (DEPX, DEPY, NZ)], [VMEM] * 7, work, 40)  13.9 us
    pallas_call x1, Pallas kernels, on_device(): pot, low, high = call(next_kernel, brick, [VMEM] * 7, work, 40)(*operands)  13 us
    all_to_all x1, starting transfers between devices, on_device(): lax.all_to_all(send, everyone, split_axis=0, concat_axis=0, tiled=True)  11.5 us
    pallas_call x1, Pallas kernels, on_device(): call(first_kernel, brick + [tiles, tiles], [VMEM] * 4, work, 40)  11 us
    pallas_call x1, Pallas kernels, on_device(): call(deposit_kernel, [(DEPX, DEPY, NZ), (HIGH, DEPY, NZ), (HIGH, DEPY, NZ...  6.84 us
  transfers between devices with their start and end apart: 17, of which 10 were waited for; matrix products, arithmetic and copies ran while one was open for 2% of the time, Pallas kernels for 4%

profile of v1, /device:TPU:1, one launch (start us, length us, event | category | flops | bytes accessed | tf_op | source)
XLA Modules:
  0.0 173.9 jit_solution(14463868264171753132)
XLA Ops:
  0.6 0.0 copy-start.1
  0.6 0.9 copy-done.1
  1.6 0.0 copy-start.2
  1.6 0.7 copy-done.2
  2.3 0.0 copy-start.3
  2.3 0.7 copy-done.3
  2.9 0.0 copy-start.5
  2.9 0.7 copy-done.5
  3.6 0.7 copy-done.7
  4.2 4.9 %shard_map.86 = f32[128,8,128]{2,1,0:T(8,128)} custom-call(s32[128]{0:T(128)S(1)} %copy-done.3, s32[128]{0:T(128)S(1)} %copy-done.5, s32[512]{0:T(512)S(1)} %copy-done.2, s32[16]{0:T(128)S(1)} %copy-done.7, f32[512,128]{1,0:T(8,128)S(1)} %copy-done.1), custom_call_target="tpu_custom_call" | custom-call | tf_op jit(solution)/shard_map/pallas_call | solution.py:292
  9.2 11.5 %all-to-all-start = ((f32[128,8,128]{2,1,0:T(8,128)}), f32[128,8,128]{2,1,0:T(8,128)S(1)}, u32[]{:S(2)}, u32[]{:S(2)}) async-start(f32[128,8,128]{2,1,0:T(8,128)} %shard_map.86), calls=%async_computation | async-start | bytes 1048576 | tf_op jit(solution)/shard_map/all_to_all | solution.py:298
  20.7 1.0 slice.48
  21.6 1.5 collective-permute-start.4
  23.1 1.7 %slice.49 = f32[11,64,128]{2,1,0:T(8,128)} slice(f32[32,64,128]{2,1,0:T(8,128)} %param.8), slice={[0:11], [0:64], [0:128]} | slice | bytes 720896 | tf_op jit(solution)/shard_map/slice | solution.py:301
  24.8 4.0 %collective-permute-start.5 = (f32[11,64,128]{2,1,0:T(8,128)}, f32[11,64,128]{2,1,0:T(8,128)}, u32[]{:S(2)}, u32[]{:S(2)}) collective-permute-start(f32[11,64,128]{2,1,0:T(8,128)} %slice.49), channel_id=1, source_target_pairs={{0,120},{8,0},{16,8},{24,16},{32,24},{40,32},{48,40},{56,48},{64,5... | collective-permute-start | bytes 1081352 | tf_op jit(solution)/shard_map/ppermute | solution.py:285
  28.9 9.4 %collective-permute-done.4 = f32[8,64,128]{2,1,0:T(8,128)S(1)} collective-permute-done((f32[8,64,128]{2,1,0:T(8,128)S(1)}, f32[8,64,128]{2,1,0:T(8,128)S(1)}, u32[]{:S(2)}, u32[]{:S(2)}) %collective-permute-start.4) | collective-permute-done | bytes 262176 | tf_op jit(solution)/shard_map/ppermute | solution.py:285
  38.3 0.0 all-to-all-done.got
  38.3 0.0 copy-done
  38.3 0.0 copy-start.9
  38.3 6.8 %shard_map.87 = (f32[35,72,128]{2,1,0:T(8,128)S(1)}, f32[11,72,128]{2,1,0:T(8,128)S(1)}, f32[11,72,128]{2,1,0:T(8,128)S(1)}) custom-call(f32[128,8,128]{2,1,0:T(8,128)S(1)} %all-to-all-done.got, f32[32,64,128]{2,1,0:T(8,128)S(1)} %copy-done), custom_call_target="tpu_custom_call" | custom-call | tf_op jit(solution)/shard_map/pallas_call | solution.py:308
  45.2 0.1 collective-permute-start
  45.3 4.8 %collective-permute-start.1 = (f32[11,72,128]{2,1,0:T(8,128)S(1)}, f32[11,72,128]{2,1,0:T(8,128)S(1)}, u32[]{:S(2)}, u32[]{:S(2)}) collective-permute-start(f32[11,72,128]{2,1,0:T(8,128)S(1)} %get-tuple-element.20), channel_id=1, source_target_pairs={{0,120},{8,0},{16,8},{24,16},{32,24},{40,32},{48,40},{56,48},{64,5... | collective-permute-start | bytes 1216520 | tf_op jit(solution)/shard_map/ppermute | solution.py:285
  50.0 0.0 copy-done.9
  50.0 0.1 constant_dynamic-update-slice_fusion.1
  50.1 0.0 collective-permute-done.5
  50.1 1.0 constant_dynamic-update-slice_fusion
  51.2 1.4 collective-permute-start.7
  52.6 6.1 %collective-permute-done.below = f32[11,72,128]{2,1,0:T(8,128)S(1)} collective-permute-done((f32[11,72,128]{2,1,0:T(8,128)S(1)}, f32[11,72,128]{2,1,0:T(8,128)S(1)}, u32[]{:S(2)}, u32[]{:S(2)}) %collective-permute-start) | collective-permute-done | bytes 405536 | tf_op jit(solution)/shard_map/ppermute | solution.py:285
  58.7 0.0 collective-permute-done.1.above
  58.7 0.2 shard_map.88
  58.8 2.3 %collective-permute-start.2 = (f32[51,16,128]{2,1,0:T(8,128)S(1)}, f32[51,16,128]{2,1,0:T(8,128)S(1)}, u32[]{:S(2)}, u32[]{:S(2)}) collective-permute-start(f32[51,16,128]{2,1,0:T(8,128)S(1)} %get-tuple-element.22), channel_id=1, source_target_pairs={{0,1},{1,2},{2,3},{3,4},{4,5},{5,6},{6,7},{7,0},{8,9},{9,10},{10,1... | collective-permute-start | bytes 1253384 | tf_op jit(solution)/shard_map/ppermute | solution.py:285
  61.2 0.0 collective-permute-start.3
  61.2 1.8 %collective-permute-start.6 = (f32[51,8,128]{2,1,0:T(8,128)S(1)}, f32[51,8,128]{2,1,0:T(8,128)S(1)}, u32[]{:S(2)}, u32[]{:S(2)}) collective-permute-start(f32[51,8,128]{2,1,0:T(8,128)S(1)} %slice.64), channel_id=1, source_target_pairs={{0,1},{1,2},{2,3},{3,4},{4,5},{5,6},{6,7},{7,0},{8,9},{9,10},{10,1... | collective-permute-start | bytes 626696 | tf_op jit(solution)/shard_map/ppermute | solution.py:285
  63.0 5.4 %collective-permute-done.6 = f32[51,8,128]{2,1,0:T(8,128)S(1)} collective-permute-done((f32[51,8,128]{2,1,0:T(8,128)S(1)}, f32[51,8,128]{2,1,0:T(8,128)S(1)}, u32[]{:S(2)}, u32[]{:S(2)}) %collective-permute-start.6) | collective-permute-done | bytes 208928 | tf_op jit(solution)/shard_map/ppermute | solution.py:285
  68.4 0.0 collective-permute-done.7
  68.4 0.2 pad_maximum_fusion.density
  68.6 0.0 collective-permute-done.2.below
  68.6 0.3 collective-permute-done.3.above
  68.9 11.0 %shard_map.89 = (f32[32,64,128]{2,1,0:T(8,128)S(1)}, f32[11,64,128]{2,1,0:T(8,128)S(1)}, f32[8,64,128]{2,1,0:T(8,128)S(1)}, f32[51,11,8,128]{3,2,1,0:T(8,128)S(1)}, f32[51,11,8,128]{3,2,1,0:T(8,128)S(1)}) custom-call(f32[51,72,128]{2,1,0:T(8,128)S(1)} %get-tuple-element.21.own, f32[51,16,128]{2,1,0:T(8,128)S(1)} %collective-permute-done.2.below, ...), custom_call_target="tpu_custom_call" | custom-call | tf_op jit(solution)/shard_map/pallas_call | solution.py:323
  79.9 4.9 %collective-permute-start.9 = (f32[11,64,128]{2,1,0:T(8,128)S(1)}, f32[11,64,128]{2,1,0:T(8,128)S(1)}, u32[]{:S(2)}, u32[]{:S(2)}) collective-permute-start(f32[11,64,128]{2,1,0:T(8,128)S(1)} %get-tuple-element.26), channel_id=1, source_target_pairs={{0,120},{8,0},{16,8},{24,16},{32,24},{40,32},{48,40},{56,48},{64,5... | collective-permute-start | bytes 1081352 | tf_op jit(solution)/shard_map/ppermute | solution.py:285
  84.8 0.0 collective-permute-start.8
  84.8 8.5 %collective-permute-done.8.x_below = f32[8,64,128]{2,1,0:T(8,128)S(1)} collective-permute-done((f32[8,64,128]{2,1,0:T(8,128)S(1)}, f32[8,64,128]{2,1,0:T(8,128)S(1)}, u32[]{:S(2)}, u32[]{:S(2)}) %collective-permute-start.8) | collective-permute-done | bytes 262176 | tf_op jit(solution)/shard_map/ppermute | solution.py:285
  93.3 0.0 collective-permute-done.9.x_above
  93.4 4.2 %collective-permute-start.11 = (f32[51,16,128]{2,1,0:T(8,128)S(1)}, f32[51,16,128]{2,1,0:T(8,128)S(1)}, u32[]{:S(2)}, u32[]{:S(2)}) collective-permute-start(f32[51,16,128]{2,1,0:T(8,128)S(1)} %pad_maximum_fusion.1), channel_id=1, source_target_pairs={{0,7},{1,0},{2,1},{3,2},{4,3},{5,4},{6,5},{7,6},{8,15},{9,8},{10,9... | collective-permute-start | bytes 1253384 | tf_op jit(solution)/shard_map/ppermute | solution.py:285
  97.6 0.3 collective-permute-start.10
  97.9 2.7 %collective-permute-done.10.y_below = f32[51,8,128]{2,1,0:T(8,128)S(1)} collective-permute-done((f32[51,8,128]{2,1,0:T(8,128)S(1)}, f32[51,8,128]{2,1,0:T(8,128)S(1)}, u32[]{:S(2)}, u32[]{:S(2)}) %collective-permute-start.10) | collective-permute-done | bytes 208928 | tf_op jit(solution)/shard_map/ppermute | solution.py:285
  100.7 3.2 %collective-permute-done.11.y_above = f32[51,16,128]{2,1,0:T(8,128)S(1)} collective-permute-done((f32[51,16,128]{2,1,0:T(8,128)S(1)}, f32[51,16,128]{2,1,0:T(8,128)S(1)}, u32[]{:S(2)}, u32[]{:S(2)}) %collective-permute-start.11) | collective-permute-done | bytes 417824 | tf_op jit(solution)/shard_map/ppermute | solution.py:285
  103.8 13.0 %shard_map.90 = (f32[32,64,128]{2,1,0:T(8,128)S(1)}, f32[11,64,128]{2,1,0:T(8,128)S(1)}, f32[8,64,128]{2,1,0:T(8,128)S(1)}) custom-call(f32[32,64,128]{2,1,0:T(8,128)S(1)} %get-tuple-element.24.own, f32[8,64,128]{2,1,0:T(8,128)S(1)} %collective-permute-done.8.x_below, f32[11,64,128]{2,1,0:T(8,128)S(1)} %collective-permute-done.9.x_above, ...), custom_call_target="tpu_custom_call" | custom-call | tf_op jit(solution)/shard_map/pallas_call | solution.py:336
  116.8 2.1 %collective-permute-start.13 = (f32[11,64,128]{2,1,0:T(8,128)S(1)}, f32[11,64,128]{2,1,0:T(8,128)S(1)}, u32[]{:S(2)}, u32[]{:S(2)}) collective-permute-start(f32[11,64,128]{2,1,0:T(8,128)S(1)} %get-tuple-element.31), channel_id=1, source_target_pairs={{0,120},{8,0},{16,8},{24,16},{32,24},{40,32},{48,40},{56,48},{64,5... | collective-permute-start | bytes 1081352 | tf_op jit(solution)/shard_map/ppermute | solution.py:285
  119.0 0.0 collective-permute-start.12
  119.0 9.4 %collective-permute-done.12.refs_1_ = f32[8,64,128]{2,1,0:T(8,128)S(1)} collective-permute-done((f32[8,64,128]{2,1,0:T(8,128)S(1)}, f32[8,64,128]{2,1,0:T(8,128)S(1)}, u32[]{:S(2)}, u32[]{:S(2)}) %collective-permute-start.12) | collective-permute-done | bytes 262176 | tf_op jit(solution)/shard_map/ppermute | solution.py:285
  128.4 0.0 collective-permute-done.13.refs_2_
  128.4 2.6 %collective-permute-start.15 = (f32[51,16,128]{2,1,0:T(8,128)S(1)}, f32[51,16,128]{2,1,0:T(8,128)S(1)}, u32[]{:S(2)}, u32[]{:S(2)}) collective-permute-start(f32[51,16,128]{2,1,0:T(8,128)S(1)} %pad_maximum_fusion.2), channel_id=1, source_target_pairs={{0,7},{1,0},{2,1},{3,2},{4,3},{5,4},{6,5},{7,6},{8,15},{9,8},{10,9... | collective-permute-start | bytes 1253384 | tf_op jit(solution)/shard_map/ppermute | solution.py:285
  131.2 0.0 collective-permute-start.14
  131.2 2.8 %collective-permute-done.14.refs_3_ = f32[51,8,128]{2,1,0:T(8,128)S(1)} collective-permute-done((f32[51,8,128]{2,1,0:T(8,128)S(1)}, f32[51,8,128]{2,1,0:T(8,128)S(1)}, u32[]{:S(2)}, u32[]{:S(2)}) %collective-permute-start.14) | collective-permute-done | bytes 208928 | tf_op jit(solution)/shard_map/ppermute | solution.py:285
  134.0 3.1 %collective-permute-done.15.refs_4_ = f32[51,16,128]{2,1,0:T(8,128)S(1)} collective-permute-done((f32[51,16,128]{2,1,0:T(8,128)S(1)}, f32[51,16,128]{2,1,0:T(8,128)S(1)}, u32[]{:S(2)}, u32[]{:S(2)}) %collective-permute-start.15) | collective-permute-done | bytes 417824 | tf_op jit(solution)/shard_map/ppermute | solution.py:285
  137.1 13.9 %shard_map.91 = (f32[32,64,128]{2,1,0:T(8,128)}, f32[35,72,128]{2,1,0:T(8,128)S(1)}) custom-call(f32[32,64,128]{2,1,0:T(8,128)S(1)} %get-tuple-element.29.refs_0_, f32[8,64,128]{2,1,0:T(8,128)S(1)} %collective-permute-done.12.refs_1_, f32[11,64,128]{2,1,0:T(8,128)S(1)} %collective-permute-done.13.refs_2_, f32[51,8,128]{2,1,0:T(8,128)S(1)} %collective-permute-done.14.refs_3_, ...), custom_call_target="tpu_custom_call" | custom-call | tf_op jit(solution)/shard_map/pallas_call | solution.py:338
  151.0 4.9 %shard_map.92 = f32[128,1,128]{2,1,0:T(1,128)S(1)} custom-call(f32[128,8,128]{2,1,0:T(8,128)S(1)} %all-to-all-done.got, f32[35,72,128]{2,1,0:T(8,128)S(1)} %get-tuple-element.33.field), custom_call_target="tpu_custom_call" | custom-call | tf_op jit(solution)/shard_map/pallas_call | solution.py:341
  156.0 16.6 %all_to_all.10.got = f32[128,1,128]{2,1,0:T(1,128)S(1)} all-to-all(f32[128,1,128]{2,1,0:T(1,128)S(1)} %shard_map.92), channel_id=1, replica_groups=mesh['gx'=16,'gy'=8] {'gx','gy'}, dimensions={0} | all-to-all | bytes 131072 | tf_op jit(solution)/shard_map/all_to_all | solution.py:342
  172.6 0.0 copy-done.4
  172.6 0.0 copy-done.6
  172.6 0.0 copy-done.8
  172.6 0.7 shard_map.93
  173.2 0.6 reduce
  (24 shorter events, 0.3 us)
Async XLA Ops:
  0.6 1.0 copy-start.1
  1.6 0.7 copy-start.2
  2.3 0.7 copy-start.3
  2.9 0.7 copy-start.5
  3.6 0.7 copy-start.7
  4.2 34.1 %copy-start = (f32[32,64,128]{2,1,0:T(8,128)S(1)}, f32[32,64,128]{2,1,0:T(8,128)}, u32[]{:S(2)}) copy-start(f32[32,64,128]{2,1,0:T(8,128)} %ion.1) | copy-start | bytes 3145732
  9.2 29.1 %all-to-all-start = ((f32[128,8,128]{2,1,0:T(8,128)}), f32[128,8,128]{2,1,0:T(8,128)S(1)}, u32[]{:S(2)}, u32[]{:S(2)}) async-start(f32[128,8,128]{2,1,0:T(8,128)} %shard_map.86), calls=%async_computation | async-start | bytes 1048576 | tf_op jit(solution)/shard_map/all_to_all | solution.py:298
  21.6 16.6 %collective-permute-start.4 = (f32[8,64,128]{2,1,0:T(8,128)S(1)}, f32[8,64,128]{2,1,0:T(8,128)S(1)}, u32[]{:S(2)}, u32[]{:S(2)}) collective-permute-start(f32[8,64,128]{2,1,0:T(8,128)S(1)} %slice.48), channel_id=1, source_target_pairs={{0,8},{8,16},{16,24},{24,32},{32,40},{40,48},{48,56},{56,64},{64,7... | collective-permute-start | bytes 786440 | tf_op jit(solution)/shard_map/ppermute | solution.py:285
  24.8 25.3 %collective-permute-start.5 = (f32[11,64,128]{2,1,0:T(8,128)}, f32[11,64,128]{2,1,0:T(8,128)}, u32[]{:S(2)}, u32[]{:S(2)}) collective-permute-start(f32[11,64,128]{2,1,0:T(8,128)} %slice.49), channel_id=1, source_target_pairs={{0,120},{8,0},{16,8},{24,16},{32,24},{40,32},{48,40},{56,48},{64,5... | collective-permute-start | bytes 1081352 | tf_op jit(solution)/shard_map/ppermute | solution.py:285
  38.3 11.7 %copy-start.9 = (f32[32,64,128]{2,1,0:T(8,128)S(1)}, f32[32,64,128]{2,1,0:T(8,128)}, u32[]{:S(2)}) copy-start(f32[32,64,128]{2,1,0:T(8,128)} %param.8) | copy-start | bytes 3145732
  45.2 13.5 %collective-permute-start = (f32[11,72,128]{2,1,0:T(8,128)S(1)}, f32[11,72,128]{2,1,0:T(8,128)S(1)}, u32[]{:S(2)}, u32[]{:S(2)}) collective-permute-start(f32[11,72,128]{2,1,0:T(8,128)S(1)} %get-tuple-element.19), channel_id=1, source_target_pairs={{0,8},{8,16},{16,24},{24,32},{32,40},{40,48},{48,56},{56,64},{64,7... | collective-permute-start | bytes 1216520 | tf_op jit(solution)/shard_map/ppermute | solution.py:285
  45.3 13.4 %collective-permute-start.1 = (f32[11,72,128]{2,1,0:T(8,128)S(1)}, f32[11,72,128]{2,1,0:T(8,128)S(1)}, u32[]{:S(2)}, u32[]{:S(2)}) collective-permute-start(f32[11,72,128]{2,1,0:T(8,128)S(1)} %get-tuple-element.20), channel_id=1, source_target_pairs={{0,120},{8,0},{16,8},{24,16},{32,24},{40,32},{48,40},{56,48},{64,5... | collective-permute-start | bytes 1216520 | tf_op jit(solution)/shard_map/ppermute | solution.py:285
  51.2 17.2 %collective-permute-start.7 = (f32[51,16,128]{2,1,0:T(8,128)S(1)}, f32[51,16,128]{2,1,0:T(8,128)S(1)}, u32[]{:S(2)}, u32[]{:S(2)}) collective-permute-start(f32[51,16,128]{2,1,0:T(8,128)S(1)} %slice.65), channel_id=1, source_target_pairs={{0,7},{1,0},{2,1},{3,2},{4,3},{5,4},{6,5},{7,6},{8,15},{9,8},{10,9... | collective-permute-start | bytes 1253384 | tf_op jit(solution)/shard_map/ppermute | solution.py:285
  58.8 9.7 %collective-permute-start.2 = (f32[51,16,128]{2,1,0:T(8,128)S(1)}, f32[51,16,128]{2,1,0:T(8,128)S(1)}, u32[]{:S(2)}, u32[]{:S(2)}) collective-permute-start(f32[51,16,128]{2,1,0:T(8,128)S(1)} %get-tuple-element.22), channel_id=1, source_target_pairs={{0,1},{1,2},{2,3},{3,4},{4,5},{5,6},{6,7},{7,0},{8,9},{9,10},{10,1... | collective-permute-start | bytes 1253384 | tf_op jit(solution)/shard_map/ppermute | solution.py:285
  61.2 7.8 %collective-permute-start.3 = (f32[51,16,128]{2,1,0:T(8,128)S(1)}, f32[51,16,128]{2,1,0:T(8,128)S(1)}, u32[]{:S(2)}, u32[]{:S(2)}) collective-permute-start(f32[51,16,128]{2,1,0:T(8,128)S(1)} %get-tuple-element.23), channel_id=1, source_target_pairs={{0,7},{1,0},{2,1},{3,2},{4,3},{5,4},{6,5},{7,6},{8,15},{9,8},{10,9... | collective-permute-start | bytes 1253384 | tf_op jit(solution)/shard_map/ppermute | solution.py:285
  61.2 7.2 %collective-permute-start.6 = (f32[51,8,128]{2,1,0:T(8,128)S(1)}, f32[51,8,128]{2,1,0:T(8,128)S(1)}, u32[]{:S(2)}, u32[]{:S(2)}) collective-permute-start(f32[51,8,128]{2,1,0:T(8,128)S(1)} %slice.64), channel_id=1, source_target_pairs={{0,1},{1,2},{2,3},{3,4},{4,5},{5,6},{6,7},{7,0},{8,9},{9,10},{10,1... | collective-permute-start | bytes 626696 | tf_op jit(solution)/shard_map/ppermute | solution.py:285
  79.9 13.4 %collective-permute-start.9 = (f32[11,64,128]{2,1,0:T(8,128)S(1)}, f32[11,64,128]{2,1,0:T(8,128)S(1)}, u32[]{:S(2)}, u32[]{:S(2)}) collective-permute-start(f32[11,64,128]{2,1,0:T(8,128)S(1)} %get-tuple-element.26), channel_id=1, source_target_pairs={{0,120},{8,0},{16,8},{24,16},{32,24},{40,32},{48,40},{56,48},{64,5... | collective-permute-start | bytes 1081352 | tf_op jit(solution)/shard_map/ppermute | solution.py:285
  84.8 8.5 %collective-permute-start.8 = (f32[8,64,128]{2,1,0:T(8,128)S(1)}, f32[8,64,128]{2,1,0:T(8,128)S(1)}, u32[]{:S(2)}, u32[]{:S(2)}) collective-permute-start(f32[8,64,128]{2,1,0:T(8,128)S(1)} %get-tuple-element.25), channel_id=1, source_target_pairs={{0,8},{8,16},{16,24},{24,32},{32,40},{40,48},{48,56},{56,64},{64,7... | collective-permute-start | bytes 786440 | tf_op jit(solution)/shard_map/ppermute | solution.py:285
  93.4 10.5 %collective-permute-start.11 = (f32[51,16,128]{2,1,0:T(8,128)S(1)}, f32[51,16,128]{2,1,0:T(8,128)S(1)}, u32[]{:S(2)}, u32[]{:S(2)}) collective-permute-start(f32[51,16,128]{2,1,0:T(8,128)S(1)} %pad_maximum_fusion.1), channel_id=1, source_target_pairs={{0,7},{1,0},{2,1},{3,2},{4,3},{5,4},{6,5},{7,6},{8,15},{9,8},{10,9... | collective-permute-start | bytes 1253384 | tf_op jit(solution)/shard_map/ppermute | solution.py:285
  97.6 3.0 %collective-permute-start.10 = (f32[51,8,128]{2,1,0:T(8,128)S(1)}, f32[51,8,128]{2,1,0:T(8,128)S(1)}, u32[]{:S(2)}, u32[]{:S(2)}) collective-permute-start(f32[51,8,128]{2,1,0:T(8,128)S(1)} %pad_maximum_fusion.3), channel_id=1, source_target_pairs={{0,1},{1,2},{2,3},{3,4},{4,5},{5,6},{6,7},{7,0},{8,9},{9,10},{10,1... | collective-permute-start | bytes 626696 | tf_op jit(solution)/shard_map/ppermute | solution.py:285
  116.8 11.6 %collective-permute-start.13 = (f32[11,64,128]{2,1,0:T(8,128)S(1)}, f32[11,64,128]{2,1,0:T(8,128)S(1)}, u32[]{:S(2)}, u32[]{:S(2)}) collective-permute-start(f32[11,64,128]{2,1,0:T(8,128)S(1)} %get-tuple-element.31), channel_id=1, source_target_pairs={{0,120},{8,0},{16,8},{24,16},{32,24},{40,32},{48,40},{56,48},{64,5... | collective-permute-start | bytes 1081352 | tf_op jit(solution)/shard_map/ppermute | solution.py:285
  119.0 9.4 %collective-permute-start.12 = (f32[8,64,128]{2,1,0:T(8,128)S(1)}, f32[8,64,128]{2,1,0:T(8,128)S(1)}, u32[]{:S(2)}, u32[]{:S(2)}) collective-permute-start(f32[8,64,128]{2,1,0:T(8,128)S(1)} %get-tuple-element.30), channel_id=1, source_target_pairs={{0,8},{8,16},{16,24},{24,32},{32,40},{40,48},{48,56},{56,64},{64,7... | collective-permute-start | bytes 786440 | tf_op jit(solution)/shard_map/ppermute | solution.py:285
  128.4 8.7 %collective-permute-start.15 = (f32[51,16,128]{2,1,0:T(8,128)S(1)}, f32[51,16,128]{2,1,0:T(8,128)S(1)}, u32[]{:S(2)}, u32[]{:S(2)}) collective-permute-start(f32[51,16,128]{2,1,0:T(8,128)S(1)} %pad_maximum_fusion.2), channel_id=1, source_target_pairs={{0,7},{1,0},{2,1},{3,2},{4,3},{5,4},{6,5},{7,6},{8,15},{9,8},{10,9... | collective-permute-start | bytes 1253384 | tf_op jit(solution)/shard_map/ppermute | solution.py:285
  131.2 2.9 %collective-permute-start.14 = (f32[51,8,128]{2,1,0:T(8,128)S(1)}, f32[51,8,128]{2,1,0:T(8,128)S(1)}, u32[]{:S(2)}, u32[]{:S(2)}) collective-permute-start(f32[51,8,128]{2,1,0:T(8,128)S(1)} %pad_maximum_fusion.4), channel_id=1, source_target_pairs={{0,1},{1,2},{2,3},{3,4},{4,5},{5,6},{6,7},{7,0},{8,9},{9,10},{10,1... | collective-permute-start | bytes 626696 | tf_op jit(solution)/shard_map/ppermute | solution.py:285
  151.0 21.5 %copy-start.4 = (s32[128]{0:T(128)S(1)}, s32[128]{0:T(128)}, u32[]{:S(2)}) copy-start(s32[128]{0:T(128)} %brick.3) | copy-start | bytes 1540
  151.0 21.5 %copy-start.6 = (s32[128]{0:T(128)S(1)}, s32[128]{0:T(128)}, u32[]{:S(2)}) copy-start(s32[128]{0:T(128)} %counts.3) | copy-start | bytes 1540
  151.0 21.5 %copy-start.8 = (s32[16]{0:T(128)S(1)}, s32[16]{0:T(128)}, u32[]{:S(2)}) copy-start(s32[16]{0:T(128)} %aper.3) | copy-start | bytes 196

commit v2 on v1

v2 whole, which is shorter than its diff:
```python
import functools

import jax
import jax.numpy as jnp
from jax import lax
from jax.experimental import pallas as pl
from jax.experimental.pallas import tpu as pltpu
from jax.sharding import PartitionSpec as P

BX = 32
BY = 64
NZ = 128
NEWTON = 3
SWEEPS = 8
CAP = 4
BLX = 4
BLY = 4
BLZ = 8
N_GX = 16
N_GY = 8
PAN_DEV = 128
APER_DEV = 16
LOW = 8
HIGH = 11
WX = LOW + BX + HIGH
TILES = 11
WY = 8 * TILES
DEPX = BX + BLX - 1
DEPY = 72
UNROLL = 8

VMEM = pl.BlockSpec(memory_space=pltpu.VMEM)
SMEM = pl.BlockSpec(memory_space=pltpu.SMEM)
F32 = jnp.float32


def call(body, outs, ins, scratch=(), mib=24, flops=None):
    cost = None
    if flops is not None:
        cost = pl.CostEstimate(flops=flops, bytes_accessed=1 << 20, transcendentals=0)
    return pl.pallas_call(
        body,
        out_shape=[jax.ShapeDtypeStruct(s, F32) for s in outs],
        in_specs=list(ins),
        out_specs=[VMEM] * len(outs),
        scratch_shapes=list(scratch),
        cost_estimate=cost,
        compiler_params=pltpu.CompilerParams(vmem_limit_bytes=mib << 20),
    )


def iota(shape, dim):
    return lax.broadcasted_iota(jnp.int32, shape, dim)


def pack_kernel(*refs):
    arrays, send, local, need, sems = refs[:5], refs[5], refs[6:11], refs[11], refs[12]
    copies = [pltpu.make_async_copy(a, b, sems.at[i]) for i, (a, b) in enumerate(zip(arrays, local))]
    for copy in copies:
        copy.start()
    brick, counts, offsets, aper, rows = local

    def clear(p, c):
        need[p] = 0
        return c

    lax.fori_loop(0, PAN_DEV, clear, 0, unroll=8)
    for copy in copies:
        copy.wait()
    for a in range(APER_DEV):
        need[aper[a]] = 1
    sub = iota((8, 128), 0)
    group = (iota((8, 128), 1) >> 3) & 3
    j = sub & 3
    masks = {e: (group == j - e) for e in range(-3, 4)}
    lane1 = iota((1, 128), 1)

    def body(q, c):
        p = q * 2
        live = sub < jnp.where(sub < 4, counts[p], counts[p + 1] + 4)
        v = jnp.where(live, rows[pl.ds(pl.multiple_of(q * 8, 8), 8), :], 0.0)
        out = v
        for e in (-3, -2, -1, 1, 2, 3):
            moved = pltpu.roll(pltpu.roll(v, e % 8, 0), (-8 * e) % 128, 1)
            out = jnp.where(masks[e], moved, out)
        for h in range(2):
            b = brick[p + h]
            send[b, 0:4, :] = out[4 * h : 4 * h + 4]
            meta = jnp.zeros((1, 128), jnp.int32)
            for k in range(CAP):
                meta = jnp.where(lane1 == k, offsets[(p + h) * CAP + k], meta)
            meta = jnp.where(lane1 == CAP, need[p + h], meta)
            send[b, 4:5, :] = meta.astype(F32)
        return c

    lax.fori_loop(0, PAN_DEV // 2, body, 0, unroll=2)


def corner(meta, p, k):
    offset = meta[p, k].astype(jnp.int32)
    return offset >> 13, (offset >> 7) & 63, offset & 127


def block_rows(v, z, k, i, lane):
    moved = pltpu.roll(v, (z - 32 * i - 8 * k + 128) & 127, 1)
    return jnp.where((lane >= z) & (lane < z + BLZ), moved, 0.0)


def deposit_kernel(got, ion, out, x_low, x_high, y_low, y_high, meta, sem):
    copy = pltpu.make_async_copy(got.at[:, 4, :], meta, sem)
    copy.start()
    out[0:BX, 0:BY, :] = ion[...]
    out[0:BX, BY:DEPY, :] = jnp.zeros((BX, DEPY - BY, NZ), F32)
    out[BX:DEPX] = jnp.zeros((DEPX - BX, DEPY, NZ), F32)
    lane = iota((BLY, 128), 1)
    copy.wait()

    def body(p, c):
        v = got[p, 0:4, :]
        for k in range(CAP):
            x, y, z = corner(meta, p, k)
            for i in range(BLX):
                out[x + i, pl.ds(y, BLY), :] += block_rows(v, z, k, i, lane)
        return c

    lax.fori_loop(0, PAN_DEV, body, 0, unroll=4)
    x_low[...] = out[0:HIGH]
    x_high[...] = out[BX - LOW : DEPX]
    y_low[...] = out[:, 0:16]
    y_high[...] = out[:, BY - LOW : DEPY]


def inside_y():
    gy = lax.axis_index("gy")
    lo = jnp.where(gy == 0, LOW, 0)
    hi = jnp.where(gy == N_GY - 1, LOW + BY, WY)
    sub = iota((8, 128), 0)
    ys = [sub * TILES + t for t in range(TILES)]
    return [(y >= lo) & (y < hi) for y in ys]


def lay(nat, at, count, own, below, above):
    nat[at : at + count, 0:LOW] = below
    nat[at : at + count, LOW : LOW + BY] = own
    nat[at : at + count, LOW + BY : WY] = above


def lay_charge(nat, at, count, own, below, above):
    spread = jnp.where(lax.axis_index("gy") > 0, 1.0, 0.0)
    nat[at : at + count, 0:LOW] = below[:, 0:LOW]
    nat[at : at + count, LOW : LOW + DEPY] = own
    nat[at : at + count, LOW : LOW + 8] += below[:, LOW : LOW + 8] * spread
    nat[at : at + count, LOW + BY : LOW + DEPY] += above[:, 0:8]
    nat[at : at + count, LOW + DEPY : WY] = above[:, 8:16]


def strided(nat, x, t):
    return nat[x, pl.ds(t, 8, stride=TILES), :]


def relax(layers, write):
    lane = iota((8, 128), 1)
    first, last = lane == 0, lane == NZ - 1
    for u in range(len(layers) - 2):
        prev, cur, nxt = layers[u : u + 3]
        before = [pltpu.roll(cur[-1], 1, 0)] + cur[:-1]
        after = cur[1:] + [pltpu.roll(cur[0], 7, 0)]
        for t in range(TILES):
            left = jnp.where(first, 0.0, pltpu.roll(cur[t], 1, 1))
            right = jnp.where(last, 0.0, pltpu.roll(cur[t], NZ - 1, 1))
            total = (prev[t] + nxt[t]) + (before[t] + after[t]) + (left + right)
            write(u, t, total)


def layer(buf, x):
    return [buf[x, t] for t in range(TILES)]


def sweep(src, dst, rhs, inv, lo, hi):
    def rows(x0, count):
        def write(u, t, total):
            dst[x0 + u, t] = (rhs[x0 + u, t] + total) * inv[x0 + u, t]

        relax([layer(src, x0 - 1 + u) for u in range(count + 2)], write)

    turns = (hi - lo) // UNROLL

    def body(i, c):
        rows(lo + i * UNROLL, UNROLL)
        return c

    lax.fori_loop(0, turns, body, 0)
    if (hi - lo) % UNROLL:
        rows(lo + turns * UNROLL, (hi - lo) % UNROLL)


def inner(b0, b1, rhs, inv, k0, a, h):
    bufs = (b0, b1)
    for k in range(k0, SWEEPS + 1):
        sweep(bufs[(k - 1) % 2], bufs[k % 2], rhs, inv, a + k, h - k)


def inner_first(charge, y_below, y_above, density, d_below, d_above, *refs):
    b0, b1, rhs, inv, source, dens, nat = refs
    inside = inside_y()
    lay(nat, 0, BX, density[...], d_below[...], d_above[...])

    def take(x, c):
        for t in range(TILES):
            dens[x, t] = strided(nat, x, t)
        return c

    lax.fori_loop(0, BX, take, 0, unroll=4)
    lay_charge(nat, 0, DEPX, charge[...], y_below, y_above)

    def prep(x, c):
        for t in range(TILES):
            s = strided(nat, x, t)
            d = dens[x, t]
            source[x, t] = s
            scale = jnp.where(inside[t], 1.0 / (6.0 + d), 0.0)
            inv[x, t] = scale
            rhs[x, t] = s - d
            b1[x, t] = (s - d) * scale
        return c

    lax.fori_loop(0, BX, prep, 0, unroll=4)
    for x in range(BX, DEPX):
        for t in range(TILES):
            source[x, t] = strided(nat, x, t)
    inner(b0, b1, rhs, inv, 2, BLX - 2, BX + 1)


def inner_next(own, y_below, y_above, source, s_low, dens, b0, b1, rhs, inv, nat):
    inside = inside_y()
    lay(nat, 0, BX, own[...], y_below[...], y_above[...])

    def prep_from(src, shift):
        def prep(x, c):
            for t in range(TILES):
                p = jnp.where(inside[t], strided(nat, x, t), 0.0)
                coef = dens[x, t] * jnp.exp(p)
                b0[x, t] = p
                rhs[x, t] = src[x + shift, t] + coef * (p - 1.0)
                inv[x, t] = jnp.where(inside[t], 1.0 / (6.0 + coef), 0.0)
            return c

        return prep

    for x in range(BLX - 1):
        prep_from(s_low, LOW)(x, 0)
    lax.fori_loop(BLX - 1, BX, prep_from(source, 0), 0)
    inner(b0, b1, rhs, inv, 1, 0, BX)


def flanks(b0, b1, lows, highs, rhs, inv, k0, a, h):
    (l0, l1, l_rhs, l_inv), (h0, h1, h_rhs, h_inv) = lows, highs
    n_low, n_high = LOW + a, BX + HIGH - h
    for i in range(LOW + a):
        if i + LOW >= len_low_halo(a):
            l_rhs[i + LOW], l_inv[i + LOW] = rhs[i], inv[i]
    for i in range(h - LOW, BX):
        h_rhs[i - (h - LOW)], h_inv[i - (h - LOW)] = rhs[i], inv[i]

    def one(k, near, l_src, l_dst, h_src, h_dst):
        def low_write(u, t, total):
            l_dst[k + u, t] = (l_rhs[k + u, t] + total) * l_inv[k + u, t]

        def high_write(u, t, total):
            r = LOW - k + u
            h_dst[r, t] = (h_rhs[r, t] + total) * h_inv[r, t]

        low = [layer(l_src, k - 1 + j) for j in range(n_low)]
        relax(low + [layer(near, a + k - 1), layer(near, a + k)], low_write)
        high = [layer(h_src, LOW + 1 - k + j) for j in range(n_high)]
        relax([layer(near, h - k - 1), layer(near, h - k)] + high, high_write)

    if k0 == 2:
        one(2, b1, l1, l0, h1, h0)

    def body(j, c):
        one(2 * j + 1, b0, l0, l1, h0, h1)
        one(2 * j + 2, b1, l1, l0, h1, h0)
        return c

    lax.fori_loop(k0 - 1, SWEEPS // 2, body, 0)


def len_low_halo(a):
    return LOW + (BLX - 1 if a else 0)


def finish(b0, l0, h0, nat, a, h):
    def take(src, shift):
        def body(x, c):
            for t in range(TILES):
                nat[x, pl.ds(t, 8, stride=TILES), :] = src[x + shift, t]
            return c

        return body

    lax.fori_loop(0, a + LOW, take(l0, LOW), 0, unroll=4)
    lax.fori_loop(a + LOW, h - LOW, take(b0, 0), 0, unroll=4)
    lax.fori_loop(h - LOW, DEPX, take(h0, LOW - h), 0, unroll=4)


def hand_on(nat, out, x_low, x_high, y_low, y_high):
    out[...] = nat[0:BX, LOW : LOW + BY]
    x_low[...] = nat[0:HIGH, LOW : LOW + BY]
    x_high[...] = nat[BX - LOW : BX, LOW : LOW + BY]
    y_low[...] = nat[0:BX, LOW : LOW + 16]
    y_high[...] = nat[0:BX, BY : LOW + BY]


def edges():
    gx = lax.axis_index("gx")
    return jnp.where(gx > 0, 1.0, 0.0), jnp.where(gx < N_GX - 1, 1.0, 0.0)


def flank_first(*refs):
    b0, b1, rhs, inv, source, dens, x_below, x_above, c_below, c_above = refs[:10]
    dx_below, dx_above, dc_below, dc_above = refs[10:14]
    outs, (s_low, s_high, d_low, d_high), nat, spare = refs[14:19], refs[19:23], refs[23], refs[24:]
    l0, l1, l_rhs, l_inv, h0, h1, h_rhs, h_inv = spare
    a, h = BLX - 2, BX + 1
    inside, (f_low, f_high) = inside_y(), edges()
    lay_charge(nat, 0, HIGH, x_below[...], c_below[:, 0:16], c_below[:, 16:32])
    lay_charge(nat, HIGH, HIGH, x_above[...], c_above[:, 0:16], c_above[:, 16:32])
    for r in range(HIGH):
        for t in range(TILES):
            s = strided(nat, r, t)
            if r >= LOW:
                s = source[r - LOW, t] + s * f_low
            s_low[r, t] = s
            s = strided(nat, HIGH + r, t)
            if r < DEPX - BX:
                s = s + source[BX + r, t]
            s_high[r, t] = s
    lay(nat, 0, LOW, dx_below[...], dc_below[:, 0:LOW], dc_below[:, LOW:24])
    lay(nat, LOW, HIGH, dx_above[...], dc_above[:, 0:LOW], dc_above[:, LOW:24])
    for r in range(LOW):
        for t in range(TILES):
            d_low[r, t] = strided(nat, r, t)
    for r in range(HIGH):
        for t in range(TILES):
            d_high[r, t] = strided(nat, LOW + r, t)
    for r in range(HIGH):
        for t in range(TILES):
            if r < LOW:
                d = d_low[r, t]
                scale = jnp.where(inside[t], f_low / (6.0 + d), 0.0)
            else:
                scale = inv[r - LOW, t]
                d = dens[r - LOW, t]
            value = s_low[r, t] - d
            l_rhs[r, t], l_inv[r, t], l1[r, t] = value, scale, value * scale
            d = d_high[r, t]
            scale = jnp.where(inside[t], f_high / (6.0 + d), 0.0)
            value = s_high[r, t] - d
            q = r + LOW - 1
            h_rhs[q, t], h_inv[q, t], h1[q, t] = value, scale, value * scale
    flanks(b0, b1, (l0, l1, l_rhs, l_inv), (h0, h1, h_rhs, h_inv), rhs, inv, 2, a, h)
    finish(b0, l0, h0, nat, a, h)
    hand_on(nat, *outs)


def flank_next(last, *refs):
    b0, b1, rhs, inv, x_below, x_above, c_below, c_above = refs[:8]
    s_low, s_high, d_low, d_high = refs[8:12]
    outs, rest = (refs[12:14], refs[14:]) if last else (refs[12:17], refs[17:])
    nat, l0, l1, l_rhs, l_inv, h0, h1, h_rhs, h_inv = rest
    a, h = 0, BX
    inside, (f_low, f_high) = inside_y(), edges()
    lay(nat, 0, LOW, x_below[...], c_below[:, 0:LOW], c_below[:, LOW:24])
    lay(nat, LOW, HIGH, x_above[...], c_above[:, 0:LOW], c_above[:, LOW:24])

    def prep(count, shift, at, f, d_ref, s_ref, p_out, rhs_out, inv_out):
        def body(r, c):
            for t in range(TILES):
                p = jnp.where(inside[t], strided(nat, r + shift, t) * f, 0.0)
                coef = d_ref[r, t] * jnp.exp(p)
                p_out[r + at, t] = p
                rhs_out[r + at, t] = s_ref[r, t] + coef * (p - 1.0)
                inv_out[r + at, t] = jnp.where(inside[t], f / (6.0 + coef), 0.0)
            return c

        lax.fori_loop(0, count, body, 0)

    prep(LOW, 0, 0, f_low, d_low, s_low, l0, l_rhs, l_inv)
    prep(HIGH, LOW, LOW, f_high, d_high, s_high, h0, h_rhs, h_inv)
    flanks(b0, b1, (l0, l1, l_rhs, l_inv), (h0, h1, h_rhs, h_inv), rhs, inv, 1, a, h)
    finish(b0, l0, h0, nat, a, h)
    if last:
        outs[0][...] = nat[0:BX, LOW : LOW + BY]
        outs[1][...] = nat[0:DEPX, LOW : LOW + DEPY]
    else:
        hand_on(nat, *outs)


def corner_kernel(below, above, low, high):
    n = below.shape[1]
    low[:, 0:n] = below[0:HIGH]
    low[:, n:] = above[0:HIGH]
    high[:, 0:n] = below[BX - LOW :]
    high[:, n:] = above[BX - LOW :]


def beside(x_low, x_high, y_low, y_high):
    y_below, y_above = ring(y_high, "gy", 1), ring(y_low, "gy", -1)
    x_below, x_above = ring(x_high, "gx", 1), ring(x_low, "gx", -1)
    rows, n = y_high.shape[0], y_high.shape[1] + y_low.shape[1]
    c_low, c_high = call(
        corner_kernel, [(HIGH, n, NZ), (rows - BX + LOW, n, NZ)], [VMEM] * 2
    )(y_below, y_above)
    c_below, c_above = ring(c_high, "gx", 1), ring(c_low, "gx", -1)
    return (y_below, y_above), (x_below, x_above, c_below, c_above)


def read_kernel(got, field, out, meta, sem):
    copy = pltpu.make_async_copy(got.at[:, 4, :], meta, sem)
    copy.start()
    out[...] = jnp.zeros((PAN_DEV, 1, 128), F32)
    lane = iota((BLY, 128), 1)
    copy.wait()

    def body(p, c):
        @pl.when(meta[p, CAP].astype(jnp.int32) > 0)
        def _():
            v = got[p, 0:4, :]
            total = jnp.zeros((BLY, 128), F32)
            for k in range(CAP):
                x, y, z = corner(meta, p, k)
                for i in range(BLX):
                    total += block_rows(v, z, k, i, lane) * field[x + i, pl.ds(y, BLY), :]
            out[p] = jnp.sum(total, axis=0, keepdims=True)

        return c

    lax.fori_loop(0, PAN_DEV, body, 0)


def pick_kernel(brick, counts, aper, got, out, rows):
    sub = iota((APER_DEV, 1), 0)
    live = jnp.ones((APER_DEV, 1), F32)
    for a in range(APER_DEV):
        p = aper[a]
        rows[a : a + 1, :] = got[brick[p]]
        live = jnp.where(sub == a, counts[p].astype(F32), live)
    out[...] = jnp.sum(rows[...], axis=1, keepdims=True) / live


def ring(array, axis, by):
    size = lax.axis_size(axis)
    return lax.ppermute(array, axis, [(i, (i + by) % size) for i in range(size)])


def on_device(
    ion_charge, density, charge_blocks, panel_brick, row_counts, block_offset, aperture_panel
):
    everyone = ("gx", "gy")
    ints = [pltpu.SMEM((n,), jnp.int32) for n in (PAN_DEV, PAN_DEV, PAN_DEV * CAP, APER_DEV)]
    (send,) = call(
        pack_kernel,
        [(PAN_DEV, 8, 128)],
        [pl.BlockSpec(memory_space=pl.ANY)] * 5,
        ints
        + [
            pltpu.VMEM((PAN_DEV * CAP, 128), F32),
            pltpu.SMEM((PAN_DEV,), jnp.int32),
            pltpu.SemaphoreType.DMA((5,)),
        ],
    )(panel_brick, row_counts, block_offset, aperture_panel, charge_blocks)
    got = lax.all_to_all(send, everyone, split_axis=0, concat_axis=0, tiled=True)
    dy, dx = beside(density[:HIGH], density[BX - LOW :], density[:, :16], density[:, BY - LOW :])

    meta = [pltpu.SMEM((PAN_DEV, 128), F32), pltpu.SemaphoreType.DMA]
    charge, *slabs = call(
        deposit_kernel,
        [(DEPX, DEPY, NZ)] + [(HIGH, DEPY, NZ)] * 2 + [(DEPX, 16, NZ)] * 2,
        [VMEM] * 2,
        meta,
    )(got, ion_charge)

    def tiles(n):
        return (n, TILES, 8, NZ)

    def nat(n):
        return [pltpu.VMEM((n, WY, NZ), F32)]

    spare = [pltpu.VMEM(tiles(LOW + LOW + BLX), F32)] * 8
    brick = [(BX, BY, NZ), (HIGH, BY, NZ), (LOW, BY, NZ), (BX, 16, NZ), (BX, LOW, NZ)]
    inner_out = [tiles(BX)] * 4
    work = 20_000_000_000

    cy, cx = beside(*slabs)
    *state, source, dens = call(
        inner_first, inner_out + [tiles(DEPX), tiles(BX)], [VMEM] * 6, nat(DEPX), 32, work
    )(charge, *cy, density, *dy)
    out = call(
        flank_first,
        brick + [tiles(HIGH), tiles(HIGH), tiles(LOW), tiles(HIGH)],
        [VMEM] * 14,
        nat(DEPX) + spare,
        32,
    )(*state, source, dens, *cx, *dx)
    pot, slabs, halo = out[0], out[1:5], out[5:]
    for step in range(1, NEWTON):
        py, px = beside(*slabs)
        state = call(inner_next, inner_out, [VMEM] * 6, nat(BX), 32, work)(
            pot, *py, source, halo[0], dens
        )
        last = step == NEWTON - 1
        outs = [brick[0], (DEPX, DEPY, NZ)] if last else brick
        out = call(functools.partial(flank_next, last), outs, [VMEM] * 12, nat(DEPX) + spare, 32)(
            *state, *px, *halo
        )
        pot, slabs = out[0], out[1:]
    (grown,) = slabs
    (sums,) = call(read_kernel, [(PAN_DEV, 1, 128)], [VMEM] * 2, meta)(got, grown)
    back = lax.all_to_all(sums, everyone, split_axis=0, concat_axis=0, tiled=True)
    (picked,) = call(
        pick_kernel,
        [(APER_DEV, 1)],
        [SMEM] * 3 + [VMEM],
        [pltpu.VMEM((APER_DEV, 128), F32)],
    )(panel_brick, row_counts, aperture_panel, back)
    return pot, picked.reshape(APER_DEV)


def solution(mesh):
    everyone = P(("gx", "gy"))
    grid = P("gx", "gy", None)
    return jax.shard_map(
        on_device,
        mesh=mesh,
        in_specs=(grid, grid, P(("gx", "gy"), None)) + (everyone,) * 4,
        out_specs=(grid, everyone),
        check_vma=False,
    )
```

time: 174 us -> 145 us (0.83)
  waiting for transfers between devices: 51 us -> 13 us
  starting transfers between devices: 41.5 us -> 56 us
  Pallas kernels: 55.4 us -> 51.8 us
  local copies, waits for them, and re-layouts: 7.61 us -> 5.21 us
    ppermute x16 -> x24, waiting for transfers between devices: 51 us -> 7.97 us  [ring(): lax.ppermute(array, axis, [(i, (i + by) % size) for i in range(size)])]
    ppermute x16 -> x24, starting transfers between devices: 30 us -> 44.5 us  [ring(): lax.ppermute(array, axis, [(i, (i + by) % size) for i in range(size)])]
    all_to_all x1, waiting for transfers between devices: 0.01 us -> 5.06 us  [on_device(): lax.all_to_all(send, everyone, split_axis=0, concat_axis=0, tiled=True)]
    pallas_call x6 -> x12, Pallas kernels: 49.8 us -> 45.7 us  [the longest x2 14.1 us: on_device(): call(inner_next, inner_out, [VMEM] * 6, nat(BX), 32, work)]
    unnamed x22 -> x20, local copies, waits for them, and re-layouts: 3.7 us -> 3.7 us
  transfers between devices with their start and end apart: 17 -> 25, of which waited for: 10 -> 5; matrix products, arithmetic and copies ran while one was open for 2% -> 1% of each run, Pallas kernels for 4% -> 18%
where the time goes in v2:
time: 145 us; the launch traced here: 144 us
  starting transfers between devices  56 us (39%)
  Pallas kernels  51.8 us (36%)
  blocking collectives  16.8 us (12%)
  waiting for transfers between devices  13 us (9%)
  local copies, waits for them, and re-layouts  5.21 us (4%)
    ppermute x24, starting transfers between devices, ring(): lax.ppermute(array, axis, [(i, (i + by) % size) for i in range(size)])  44.5 us
    all_to_all x1, blocking collectives, on_device(): lax.all_to_all(sums, everyone, split_axis=0, concat_axis=0, tiled=True)  16.8 us
    pallas_call x2, Pallas kernels, on_device(): call(inner_next, inner_out, [VMEM] * 6, nat(BX), 32, work)  14.1 us
    all_to_all x1, starting transfers between devices, on_device(): lax.all_to_all(send, everyone, split_axis=0, concat_axis=0, tiled=True)  11.5 us
    pallas_call x2, Pallas kernels, on_device(): call(functools.partial(flank_next, last), outs, [VMEM] * 12, nat(DEPX) +...  10.7 us
    ppermute x24, waiting for transfers between devices, ring(): lax.ppermute(array, axis, [(i, (i + by) % size) for i in range(size)])  7.97 us
    pallas_call x1, Pallas kernels, on_device(): call(deposit_kernel, [(DEPX, DEPY, NZ)] + [(HIGH, DEPY, NZ)] * 2 + [(DEPX...  6.87 us
    pallas_call x1, Pallas kernels, on_device(): call(inner_first, inner_out + [tiles(DEPX), tiles(BX)], [VMEM] * 6, nat(D...  5.52 us
  transfers between devices with their start and end apart: 25, of which 5 were waited for; matrix products, arithmetic and copies ran while one was open for 1% of the time, Pallas kernels for 18%

profile of v2, /device:TPU:1, one launch (start us, length us, event | category | flops | bytes accessed | tf_op | source)
XLA Modules:
  0.0 144.3 jit_solution(1767695231329523809)
XLA Ops:
  0.7 1.0 copy-done.2
  1.7 0.7 copy-done.3
  2.4 0.7 copy-done.4
  3.0 0.7 copy-done.6
  3.7 0.7 copy-done.8
  4.3 4.2 %shard_map.86 = f32[128,8,128]{2,1,0:T(8,128)} custom-call(s32[128]{0:T(128)S(1)} %copy-done.4, s32[128]{0:T(128)S(1)} %copy-done.6, s32[512]{0:T(512)S(1)} %copy-done.3, s32[16]{0:T(128)S(1)} %copy-done.8, f32[512,128]{1,0:T(8,128)S(1)} %copy-done.2), custom_call_target="tpu_custom_call" | custom-call | tf_op jit(solution)/shard_map/pallas_call | solution.py:462
  8.5 0.0 copy-start
  8.5 11.5 %all-to-all-start = ((f32[128,8,128]{2,1,0:T(8,128)}), f32[128,8,128]{2,1,0:T(8,128)S(1)}, u32[]{:S(2)}, u32[]{:S(2)}) async-start(f32[128,8,128]{2,1,0:T(8,128)} %shard_map.86), calls=%async_computation | async-start | bytes 1048576 | tf_op jit(solution)/shard_map/all_to_all | solution.py:473
  20.1 1.6 %collective-permute-start.2 = (f32[32,8,128]{2,1,0:T(8,128)S(1)}, f32[32,8,128]{2,1,0:T(8,128)S(1)}, u32[]{:S(2)}, u32[]{:S(2)}) collective-permute-start(f32[32,8,128]{2,1,0:T(8,128)S(1)} %slice.12), channel_id=1, source_target_pairs={{0,1},{1,2},{2,3},{3,4},{4,5},{5,6},{6,7},{7,0},{8,9},{9,10},{10,1... | collective-permute-start | bytes 393224 | tf_op jit(solution)/shard_map/ppermute | solution.py:454
  21.7 0.7 slice.13
  22.4 0.0 collective-permute-start.3
  22.4 0.8 slice.15
  23.2 5.3 %collective-permute-start.9 = (f32[11,64,128]{2,1,0:T(8,128)}, f32[11,64,128]{2,1,0:T(8,128)S(1)}, u32[]{:S(2)}, u32[]{:S(2)}) collective-permute-start(f32[11,64,128]{2,1,0:T(8,128)} %slice.15), channel_id=1, source_target_pairs={{0,120},{8,0},{16,8},{24,16},{32,24},{40,32},{48,40},{56,48},{64,5... | collective-permute-start | bytes 1081352 | tf_op jit(solution)/shard_map/ppermute | solution.py:454
  28.5 5.1 %all-to-all-done.got = f32[128,8,128]{2,1,0:T(8,128)S(1)} async-done(((f32[128,8,128]{2,1,0:T(8,128)}), f32[128,8,128]{2,1,0:T(8,128)S(1)}, u32[]{:S(2)}, u32[]{:S(2)}) %all-to-all-start) | async-done | bytes 524320 | tf_op jit(solution)/shard_map/all_to_all | solution.py:473
  33.5 6.9 %shard_map.87 = (f32[35,72,128]{2,1,0:T(8,128)S(1)}, f32[11,72,128]{2,1,0:T(8,128)S(1)}, f32[11,72,128]{2,1,0:T(8,128)S(1)}, f32[35,16,128]{2,1,0:T(8,128)S(1)}, f32[35,16,128]{2,1,0:T(8,128)S(1)}) custom-call(f32[128,8,128]{2,1,0:T(8,128)S(1)} %all-to-all-done.got, f32[32,64,128]{2,1,0:T(8,128)S(1)} %copy-done), custom_call_target="tpu_custom_call" | custom-call | tf_op jit(solution)/shard_map/pallas_call | solution.py:477
  40.4 1.1 collective-permute-start
  41.5 0.0 collective-permute-start.1
  41.6 0.0 collective-permute-done.2.d_below.below
  41.6 0.9 collective-permute-start.8
  42.4 0.0 collective-permute-done.3.d_above.above
  42.5 0.1 collective-permute-start.10
  42.6 2.6 %collective-permute-done.y_below.below = f32[35,16,128]{2,1,0:T(8,128)S(1)} collective-permute-done((f32[35,16,128]{2,1,0:T(8,128)S(1)}, f32[35,16,128]{2,1,0:T(8,128)S(1)}, u32[]{:S(2)}, u32[]{:S(2)}) %collective-permute-start) | collective-permute-done | bytes 286752 | tf_op jit(solution)/shard_map/ppermute | solution.py:454
  45.1 2.2 %collective-permute-start.11 = (f32[11,24,128]{2,1,0:T(8,128)S(1)}, f32[11,24,128]{2,1,0:T(8,128)S(1)}, u32[]{:S(2)}, u32[]{:S(2)}) collective-permute-start(f32[11,24,128]{2,1,0:T(8,128)S(1)} %get-tuple-element.59), channel_id=1, source_target_pairs={{0,120},{8,0},{16,8},{24,16},{32,24},{40,32},{48,40},{56,48},{64,5... | collective-permute-start | bytes 405512 | tf_op jit(solution)/shard_map/ppermute | solution.py:454
  47.3 0.6 collective-permute-done.1.y_above.above
  47.9 0.0 collective-permute-start.4
  47.9 2.3 %collective-permute-done.8.refs_10_ = f32[8,64,128]{2,1,0:T(8,128)S(1)} collective-permute-done((f32[8,64,128]{2,1,0:T(8,128)S(1)}, f32[8,64,128]{2,1,0:T(8,128)S(1)}, u32[]{:S(2)}, u32[]{:S(2)}) %collective-permute-start.8) | collective-permute-done | bytes 262176 | tf_op jit(solution)/shard_map/ppermute | solution.py:454
  50.2 2.6 %collective-permute-start.5 = (f32[11,72,128]{2,1,0:T(8,128)S(1)}, f32[11,72,128]{2,1,0:T(8,128)S(1)}, u32[]{:S(2)}, u32[]{:S(2)}) collective-permute-start(f32[11,72,128]{2,1,0:T(8,128)S(1)} %get-tuple-element.55), channel_id=1, source_target_pairs={{0,120},{8,0},{16,8},{24,16},{32,24},{40,32},{48,40},{56,48},{64,5... | collective-permute-start | bytes 1216520 | tf_op jit(solution)/shard_map/ppermute | solution.py:454
  52.8 0.0 collective-permute-done.10.refs_12_
  52.8 0.0 collective-permute-start.6
  52.8 0.0 collective-permute-done.9.refs_11_
  52.8 4.8 %collective-permute-start.7 = (f32[11,32,128]{2,1,0:T(8,128)S(1)}, f32[11,32,128]{2,1,0:T(8,128)S(1)}, u32[]{:S(2)}, u32[]{:S(2)}) collective-permute-start(f32[11,32,128]{2,1,0:T(8,128)S(1)} %get-tuple-element.57), channel_id=1, source_target_pairs={{0,120},{8,0},{16,8},{24,16},{32,24},{40,32},{48,40},{56,48},{64,5... | collective-permute-start | bytes 540680 | tf_op jit(solution)/shard_map/ppermute | solution.py:454
  57.6 5.5 %shard_map.88 = (f32[32,11,8,128]{3,2,1,0:T(8,128)S(1)}, f32[32,11,8,128]{3,2,1,0:T(8,128)S(1)}, f32[32,11,8,128]{3,2,1,0:T(8,128)S(1)}, f32[32,11,8,128]{3,2,1,...) custom-call(f32[35,72,128]{2,1,0:T(8,128)S(1)} %get-tuple-element.45.charge, ...), custom_call_target="tpu_custom_call" | custom-call | flops 20000000000 | bytes 1048576 | tf_op jit(solution)/shard_map/pallas_call | solution.py:496
  63.1 0.0 collective-permute-done.11.refs_13_
  63.1 0.0 collective-permute-done.4.refs_6_
  63.1 0.0 collective-permute-done.5.refs_7_
  63.1 2.5 %collective-permute-done.6.refs_8_ = f32[11,32,128]{2,1,0:T(8,128)S(1)} collective-permute-done((f32[11,32,128]{2,1,0:T(8,128)S(1)}, f32[11,32,128]{2,1,0:T(8,128)S(1)}, u32[]{:S(2)}, u32[]{:S(2)}) %collective-permute-start.6) | collective-permute-done | bytes 180256 | tf_op jit(solution)/shard_map/ppermute | solution.py:454
  65.7 0.0 collective-permute-done.7.refs_9_
  65.7 4.2 %shard_map.91 = (f32[32,64,128]{2,1,0:T(8,128)S(1)}, f32[11,64,128]{2,1,0:T(8,128)S(1)}, f32[8,64,128]{2,1,0:T(8,128)S(1)}, f32[32,16,128]{2,1,0:T(8,128)S(1)}, ...) custom-call(f32[32,11,8,128]{3,2,1,0:T(8,128)S(1)} %get-tuple-elemen, ...), custom_call_target="tpu_custom_call" | custom-call | tf_op jit(solution)/shard_map/pallas_call | solution.py:499
  69.9 2.7 %collective-permute-start.13 = (f32[32,16,128]{2,1,0:T(8,128)S(1)}, f32[32,16,128]{2,1,0:T(8,128)S(1)}, u32[]{:S(2)}, u32[]{:S(2)}) collective-permute-start(f32[32,16,128]{2,1,0:T(8,128)S(1)} %get-tuple-element.62), channel_id=1, source_target_pairs={{0,7},{1,0},{2,1},{3,2},{4,3},{5,4},{6,5},{7,6},{8,15},{9,8},{10,9... | collective-permute-start | bytes 786440 | tf_op jit(solution)/shard_map/ppermute | solution.py:454
  72.6 0.4 collective-permute-start.12
  73.0 0.0 collective-permute-start.14
  73.0 4.8 %collective-permute-start.15 = (f32[11,64,128]{2,1,0:T(8,128)S(1)}, f32[11,64,128]{2,1,0:T(8,128)S(1)}, u32[]{:S(2)}, u32[]{:S(2)}) collective-permute-start(f32[11,64,128]{2,1,0:T(8,128)S(1)} %get-tuple-element.69), channel_id=1, source_target_pairs={{0,120},{8,0},{16,8},{24,16},{32,24},{40,32},{48,40},{56,48},{64,5... | collective-permute-start | bytes 1081352 | tf_op jit(solution)/shard_map/ppermute | solution.py:454
  77.8 0.1 collective-permute-start.16
  77.9 4.8 %collective-permute-start.17 = (f32[11,24,128]{2,1,0:T(8,128)S(1)}, f32[11,24,128]{2,1,0:T(8,128)S(1)}, u32[]{:S(2)}, u32[]{:S(2)}) collective-permute-start(f32[11,24,128]{2,1,0:T(8,128)S(1)} %get-tuple-element.71), channel_id=1, source_target_pairs={{0,120},{8,0},{16,8},{24,16},{32,24},{40,32},{48,40},{56,48},{64,5... | collective-permute-start | bytes 405512 | tf_op jit(solution)/shard_map/ppermute | solution.py:454
  82.7 7.1 %shard_map.92 = (f32[32,11,8,128]{3,2,1,0:T(8,128)S(1)}, f32[32,11,8,128]{3,2,1,0:T(8,128)S(1)}, f32[32,11,8,128]{3,2,1,0:T(8,128)S(1)}, f32[32,11,8,128]{3,2,1,0:T(8,128)S(1)}) custom-call(f32[32,64,128]{2,1,0:T(8,128)S(1)} %get-tuple-element.60.own, f32[32,8,128]{2,1,0:T(8,128)S(1)} %collective-permute-done.12.y_below.below, ...), custom_call_target="tpu_custom_call" | custom-call | flops 20000000000 | bytes 1048576 | tf_op jit(solution)/shard_map/pallas_call | solution.py:509
  89.7 0.0 collective-permute-done.16.refs_6_
  89.8 0.0 collective-permute-done.17.refs_7_
  89.8 4.9 %shard_map.94 = (f32[32,64,128]{2,1,0:T(8,128)S(1)}, f32[11,64,128]{2,1,0:T(8,128)S(1)}, f32[8,64,128]{2,1,0:T(8,128)S(1)}, f32[32,16,128]{2,1,0:T(8,128)S(1)}, f32[32,8,128]{2,1,0:T(8,128)S(1)}) custom-call(f32[32,11,8,128]{3,2,1,0:T(8,128)S(1)} %get-tuple-element.64.refs_0_, f32[32,11,8,128]{3,2,1,0:T(8,128)S(1)} %get-tuple-element.65.refs_1_, ...), custom_call_target="tpu_custom_call" | custom-call | tf_op jit(solution)/shard_map/pallas_call | solution.py:514
  94.7 3.5 %collective-permute-start.19 = (f32[32,16,128]{2,1,0:T(8,128)S(1)}, f32[32,16,128]{2,1,0:T(8,128)S(1)}, u32[]{:S(2)}, u32[]{:S(2)}) collective-permute-start(f32[32,16,128]{2,1,0:T(8,128)S(1)} %get-tuple-element.77), channel_id=1, source_target_pairs={{0,7},{1,0},{2,1},{3,2},{4,3},{5,4},{6,5},{7,6},{8,15},{9,8},{10,9... | collective-permute-start | bytes 786440 | tf_op jit(solution)/shard_map/ppermute | solution.py:454
  98.2 0.0 collective-permute-start.18
  98.2 0.0 collective-permute-start.20
  98.2 4.8 %collective-permute-start.21 = (f32[11,64,128]{2,1,0:T(8,128)S(1)}, f32[11,64,128]{2,1,0:T(8,128)S(1)}, u32[]{:S(2)}, u32[]{:S(2)}) collective-permute-start(f32[11,64,128]{2,1,0:T(8,128)S(1)} %get-tuple-element.83), channel_id=1, source_target_pairs={{0,120},{8,0},{16,8},{24,16},{32,24},{40,32},{48,40},{56,48},{64,5... | collective-permute-start | bytes 1081352 | tf_op jit(solution)/shard_map/ppermute | solution.py:454
  103.0 0.0 collective-permute-done.18.y_below.below
  103.0 0.0 collective-permute-done.19.y_above.above
  103.0 0.1 collective-permute-start.22
  103.1 4.8 %collective-permute-start.23 = (f32[11,24,128]{2,1,0:T(8,128)S(1)}, f32[11,24,128]{2,1,0:T(8,128)S(1)}, u32[]{:S(2)}, u32[]{:S(2)}) collective-permute-start(f32[11,24,128]{2,1,0:T(8,128)S(1)} %get-tuple-element.85), channel_id=1, source_target_pairs={{0,120},{8,0},{16,8},{24,16},{32,24},{40,32},{48,40},{56,48},{64,5... | collective-permute-start | bytes 405512 | tf_op jit(solution)/shard_map/ppermute | solution.py:454
  107.8 7.1 %shard_map.95 = (f32[32,11,8,128]{3,2,1,0:T(8,128)S(1)}, f32[32,11,8,128]{3,2,1,0:T(8,128)S(1)}, f32[32,11,8,128]{3,2,1,0:T(8,128)S(1)}, f32[32,11,8,128]{3,2,1,0:T(8,128)S(1)}) custom-call(f32[32,64,128]{2,1,0:T(8,128)S(1)} %get-tuple-element.75.own, f32[32,8,128]{2,1,0:T(8,128)S(1)} %collective-permute-done.18.y_below.below, ...), custom_call_target="tpu_custom_call" | custom-call | flops 20000000000 | bytes 1048576 | tf_op jit(solution)/shard_map/pallas_call | solution.py:509
  114.9 0.0 collective-permute-done.22.refs_6_
  114.9 0.0 collective-permute-done.21.refs_5_
  115.0 5.8 %shard_map.97 = (f32[32,64,128]{2,1,0:T(8,128)}, f32[35,72,128]{2,1,0:T(8,128)S(1)}) custom-call(f32[32,11,8,128]{3,2,1,0:T(8,128)S(1)} %get-tuple-element.78.refs_0_, f32[32,11,8,128]{3,2,1,0:T(8,128)S(1)} %get-tuple-element.79.refs_1_, f32[32,11,8,128]{3,2,1,0:T(8,128)S(1)} %get-tuple-element.80.refs_2_, f32[32,11,8,128]{3,2,1,0:T(8,128)S(1)} %get-tuple-element.81.refs_3_, ...), custom_call_target="tpu_custom_call" | custom-call | tf_op jit(solution)/shard_map/pallas_call | solution.py:514
  120.8 5.4 %shard_map.98 = f32[128,1,128]{2,1,0:T(1,128)S(1)} custom-call(f32[128,8,128]{2,1,0:T(8,128)S(1)} %all-to-all-done.got, f32[35,72,128]{2,1,0:T(8,128)S(1)} %get-tuple-element.87.field), custom_call_target="tpu_custom_call" | custom-call | tf_op jit(solution)/shard_map/pallas_call | solution.py:519
  126.2 16.8 %all_to_all.10.got = f32[128,1,128]{2,1,0:T(1,128)S(1)} all-to-all(f32[128,1,128]{2,1,0:T(1,128)S(1)} %shard_map.98), channel_id=1, replica_groups=mesh['gx'=16,'gy'=8] {'gx','gy'}, dimensions={0} | all-to-all | bytes 131072 | tf_op jit(solution)/shard_map/all_to_all | solution.py:520
  143.0 0.7 shard_map.99
  143.6 0.6 reduce
  (26 shorter events, 0.2 us)
Async XLA Ops:
  0.6 19.4 %copy-start.1 = (f32[32,64,128]{2,1,0:T(8,128)S(1)}, f32[32,64,128]{2,1,0:T(8,128)}, u32[]{:S(2)}) copy-start(f32[32,64,128]{2,1,0:T(8,128)} %density.1) | copy-start | bytes 3145732
  0.6 1.0 copy-start.2
  1.7 0.7 copy-start.3
  2.4 0.7 copy-start.4
  3.0 0.7 copy-start.6
  3.7 0.7 copy-start.8
  8.5 25.0 %copy-start = (f32[32,64,128]{2,1,0:T(8,128)S(1)}, f32[32,64,128]{2,1,0:T(8,128)}, u32[]{:S(2)}) copy-start(f32[32,64,128]{2,1,0:T(8,128)} %ion.1) | copy-start | bytes 3145732
  8.5 25.0 %all-to-all-start = ((f32[128,8,128]{2,1,0:T(8,128)}), f32[128,8,128]{2,1,0:T(8,128)S(1)}, u32[]{:S(2)}, u32[]{:S(2)}) async-start(f32[128,8,128]{2,1,0:T(8,128)} %shard_map.86), calls=%async_computation | async-start | bytes 1048576 | tf_op jit(solution)/shard_map/all_to_all | solution.py:473
  20.1 21.5 %collective-permute-start.2 = (f32[32,8,128]{2,1,0:T(8,128)S(1)}, f32[32,8,128]{2,1,0:T(8,128)S(1)}, u32[]{:S(2)}, u32[]{:S(2)}) collective-permute-start(f32[32,8,128]{2,1,0:T(8,128)S(1)} %slice.12), channel_id=1, source_target_pairs={{0,1},{1,2},{2,3},{3,4},{4,5},{5,6},{6,7},{7,0},{8,9},{9,10},{10,1... | collective-permute-start | bytes 393224 | tf_op jit(solution)/shard_map/ppermute | solution.py:454
  22.4 20.0 %collective-permute-start.3 = (f32[32,16,128]{2,1,0:T(8,128)}, f32[32,16,128]{2,1,0:T(8,128)S(1)}, u32[]{:S(2)}, u32[]{:S(2)}) collective-permute-start(f32[32,16,128]{2,1,0:T(8,128)} %slice.13), channel_id=1, source_target_pairs={{0,7},{1,0},{2,1},{3,2},{4,3},{5,4},{6,5},{7,6},{8,15},{9,8},{10,9... | collective-permute-start | bytes 786440 | tf_op jit(solution)/shard_map/ppermute | solution.py:454
  23.2 29.6 %collective-permute-start.9 = (f32[11,64,128]{2,1,0:T(8,128)}, f32[11,64,128]{2,1,0:T(8,128)S(1)}, u32[]{:S(2)}, u32[]{:S(2)}) collective-permute-start(f32[11,64,128]{2,1,0:T(8,128)} %slice.15), channel_id=1, source_target_pairs={{0,120},{8,0},{16,8},{24,16},{32,24},{40,32},{48,40},{56,48},{64,5... | collective-permute-start | bytes 1081352 | tf_op jit(solution)/shard_map/ppermute | solution.py:454
  40.4 4.7 %collective-permute-start = (f32[35,16,128]{2,1,0:T(8,128)S(1)}, f32[35,16,128]{2,1,0:T(8,128)S(1)}, u32[]{:S(2)}, u32[]{:S(2)}) collective-permute-start(f32[35,16,128]{2,1,0:T(8,128)S(1)} %get-tuple-element.46), channel_id=1, source_target_pairs={{0,1},{1,2},{2,3},{3,4},{4,5},{5,6},{6,7},{7,0},{8,9},{9,10},{10,1... | collective-permute-start | bytes 860168 | tf_op jit(solution)/shard_map/ppermute | solution.py:454
  41.5 6.4 %collective-permute-start.1 = (f32[35,16,128]{2,1,0:T(8,128)S(1)}, f32[35,16,128]{2,1,0:T(8,128)S(1)}, u32[]{:S(2)}, u32[]{:S(2)}) collective-permute-start(f32[35,16,128]{2,1,0:T(8,128)S(1)} %get-tuple-element.47), channel_id=1, source_target_pairs={{0,7},{1,0},{2,1},{3,2},{4,3},{5,4},{6,5},{7,6},{8,15},{9,8},{10,9... | collective-permute-start | bytes 860168 | tf_op jit(solution)/shard_map/ppermute | solution.py:454
  41.6 8.6 %collective-permute-start.8 = (f32[8,64,128]{2,1,0:T(8,128)S(1)}, f32[8,64,128]{2,1,0:T(8,128)S(1)}, u32[]{:S(2)}, u32[]{:S(2)}) collective-permute-start(f32[8,64,128]{2,1,0:T(8,128)S(1)} %slice.14), channel_id=1, source_target_pairs={{0,8},{8,16},{16,24},{24,32},{32,40},{40,48},{48,56},{56,64},{64,7... | collective-permute-start | bytes 786440 | tf_op jit(solution)/shard_map/ppermute | solution.py:454
  42.5 10.3 %collective-permute-start.10 = (f32[8,24,128]{2,1,0:T(8,128)S(1)}, f32[8,24,128]{2,1,0:T(8,128)S(1)}, u32[]{:S(2)}, u32[]{:S(2)}) collective-permute-start(f32[8,24,128]{2,1,0:T(8,128)S(1)} %get-tuple-element.58), channel_id=1, source_target_pairs={{0,8},{8,16},{16,24},{24,32},{32,40},{40,48},{48,56},{56,64},{64,7... | collective-permute-start | bytes 294920 | tf_op jit(solution)/shard_map/ppermute | solution.py:454
  45.1 18.0 %collective-permute-start.11 = (f32[11,24,128]{2,1,0:T(8,128)S(1)}, f32[11,24,128]{2,1,0:T(8,128)S(1)}, u32[]{:S(2)}, u32[]{:S(2)}) collective-permute-start(f32[11,24,128]{2,1,0:T(8,128)S(1)} %get-tuple-element.59), channel_id=1, source_target_pairs={{0,120},{8,0},{16,8},{24,16},{32,24},{40,32},{48,40},{56,48},{64,5... | collective-permute-start | bytes 405512 | tf_op jit(solution)/shard_map/ppermute | solution.py:454
  47.9 15.2 %collective-permute-start.4 = (f32[11,72,128]{2,1,0:T(8,128)S(1)}, f32[11,72,128]{2,1,0:T(8,128)S(1)}, u32[]{:S(2)}, u32[]{:S(2)}) collective-permute-start(f32[11,72,128]{2,1,0:T(8,128)S(1)} %get-tuple-element.54), channel_id=1, source_target_pairs={{0,8},{8,16},{16,24},{24,32},{32,40},{40,48},{48,56},{56,64},{64,7... | collective-permute-start | bytes 1216520 | tf_op jit(solution)/shard_map/ppermute | solution.py:454
  50.2 12.9 %collective-permute-start.5 = (f32[11,72,128]{2,1,0:T(8,128)S(1)}, f32[11,72,128]{2,1,0:T(8,128)S(1)}, u32[]{:S(2)}, u32[]{:S(2)}) collective-permute-start(f32[11,72,128]{2,1,0:T(8,128)S(1)} %get-tuple-element.55), channel_id=1, source_target_pairs={{0,120},{8,0},{16,8},{24,16},{32,24},{40,32},{48,40},{56,48},{64,5... | collective-permute-start | bytes 1216520 | tf_op jit(solution)/shard_map/ppermute | solution.py:454
  52.8 12.9 %collective-permute-start.6 = (f32[11,32,128]{2,1,0:T(8,128)S(1)}, f32[11,32,128]{2,1,0:T(8,128)S(1)}, u32[]{:S(2)}, u32[]{:S(2)}) collective-permute-start(f32[11,32,128]{2,1,0:T(8,128)S(1)} %get-tuple-element.56), channel_id=1, source_target_pairs={{0,8},{8,16},{16,24},{24,32},{32,40},{40,48},{48,56},{56,64},{64,7... | collective-permute-start | bytes 540680 | tf_op jit(solution)/shard_map/ppermute | solution.py:454
  52.8 12.9 %collective-permute-start.7 = (f32[11,32,128]{2,1,0:T(8,128)S(1)}, f32[11,32,128]{2,1,0:T(8,128)S(1)}, u32[]{:S(2)}, u32[]{:S(2)}) collective-permute-start(f32[11,32,128]{2,1,0:T(8,128)S(1)} %get-tuple-element.57), channel_id=1, source_target_pairs={{0,120},{8,0},{16,8},{24,16},{32,24},{40,32},{48,40},{56,48},{64,5... | collective-permute-start | bytes 540680 | tf_op jit(solution)/shard_map/ppermute | solution.py:454
  69.9 7.8 %collective-permute-start.13 = (f32[32,16,128]{2,1,0:T(8,128)S(1)}, f32[32,16,128]{2,1,0:T(8,128)S(1)}, u32[]{:S(2)}, u32[]{:S(2)}) collective-permute-start(f32[32,16,128]{2,1,0:T(8,128)S(1)} %get-tuple-element.62), channel_id=1, source_target_pairs={{0,7},{1,0},{2,1},{3,2},{4,3},{5,4},{6,5},{7,6},{8,15},{9,8},{10,9... | collective-permute-start | bytes 786440 | tf_op jit(solution)/shard_map/ppermute | solution.py:454
  72.6 5.2 %collective-permute-start.12 = (f32[32,8,128]{2,1,0:T(8,128)S(1)}, f32[32,8,128]{2,1,0:T(8,128)S(1)}, u32[]{:S(2)}, u32[]{:S(2)}) collective-permute-start(f32[32,8,128]{2,1,0:T(8,128)S(1)} %get-tuple-element.61), channel_id=1, source_target_pairs={{0,1},{1,2},{2,3},{3,4},{4,5},{5,6},{6,7},{7,0},{8,9},{9,10},{10,1... | collective-permute-start | bytes 393224 | tf_op jit(solution)/shard_map/ppermute | solution.py:454
  73.0 16.8 %collective-permute-start.14 = (f32[8,64,128]{2,1,0:T(8,128)S(1)}, f32[8,64,128]{2,1,0:T(8,128)S(1)}, u32[]{:S(2)}, u32[]{:S(2)}) collective-permute-start(f32[8,64,128]{2,1,0:T(8,128)S(1)} %get-tuple-element.68), channel_id=1, source_target_pairs={{0,8},{8,16},{16,24},{24,32},{32,40},{40,48},{48,56},{56,64},{64,7... | collective-permute-start | bytes 786440 | tf_op jit(solution)/shard_map/ppermute | solution.py:454
  73.0 16.8 %collective-permute-start.15 = (f32[11,64,128]{2,1,0:T(8,128)S(1)}, f32[11,64,128]{2,1,0:T(8,128)S(1)}, u32[]{:S(2)}, u32[]{:S(2)}) collective-permute-start(f32[11,64,128]{2,1,0:T(8,128)S(1)} %get-tuple-element.69), channel_id=1, source_target_pairs={{0,120},{8,0},{16,8},{24,16},{32,24},{40,32},{48,40},{56,48},{64,5... | collective-permute-start | bytes 1081352 | tf_op jit(solution)/shard_map/ppermute | solution.py:454
  77.8 12.0 %collective-permute-start.16 = (f32[8,24,128]{2,1,0:T(8,128)S(1)}, f32[8,24,128]{2,1,0:T(8,128)S(1)}, u32[]{:S(2)}, u32[]{:S(2)}) collective-permute-start(f32[8,24,128]{2,1,0:T(8,128)S(1)} %get-tuple-element.70), channel_id=1, source_target_pairs={{0,8},{8,16},{16,24},{24,32},{32,40},{40,48},{48,56},{56,64},{64,7... | collective-permute-start | bytes 294920 | tf_op jit(solution)/shard_map/ppermute | solution.py:454
  77.9 11.9 %collective-permute-start.17 = (f32[11,24,128]{2,1,0:T(8,128)S(1)}, f32[11,24,128]{2,1,0:T(8,128)S(1)}, u32[]{:S(2)}, u32[]{:S(2)}) collective-permute-start(f32[11,24,128]{2,1,0:T(8,128)S(1)} %get-tuple-element.71), channel_id=1, source_target_pairs={{0,120},{8,0},{16,8},{24,16},{32,24},{40,32},{48,40},{56,48},{64,5... | collective-permute-start | bytes 405512 | tf_op jit(solution)/shard_map/ppermute | solution.py:454
  94.7 8.3 %collective-permute-start.19 = (f32[32,16,128]{2,1,0:T(8,128)S(1)}, f32[32,16,128]{2,1,0:T(8,128)S(1)}, u32[]{:S(2)}, u32[]{:S(2)}) collective-permute-start(f32[32,16,128]{2,1,0:T(8,128)S(1)} %get-tuple-element.77), channel_id=1, source_target_pairs={{0,7},{1,0},{2,1},{3,2},{4,3},{5,4},{6,5},{7,6},{8,15},{9,8},{10,9... | collective-permute-start | bytes 786440 | tf_op jit(solution)/shard_map/ppermute | solution.py:454
  98.2 4.8 %collective-permute-start.18 = (f32[32,8,128]{2,1,0:T(8,128)S(1)}, f32[32,8,128]{2,1,0:T(8,128)S(1)}, u32[]{:S(2)}, u32[]{:S(2)}) collective-permute-start(f32[32,8,128]{2,1,0:T(8,128)S(1)} %get-tuple-element.76), channel_id=1, source_target_pairs={{0,1},{1,2},{2,3},{3,4},{4,5},{5,6},{6,7},{7,0},{8,9},{9,10},{10,1... | collective-permute-start | bytes 393224 | tf_op jit(solution)/shard_map/ppermute | solution.py:454
  98.2 16.8 %collective-permute-start.20 = (f32[8,64,128]{2,1,0:T(8,128)S(1)}, f32[8,64,128]{2,1,0:T(8,128)S(1)}, u32[]{:S(2)}, u32[]{:S(2)}) collective-permute-start(f32[8,64,128]{2,1,0:T(8,128)S(1)} %get-tuple-element.82), channel_id=1, source_target_pairs={{0,8},{8,16},{16,24},{24,32},{32,40},{40,48},{48,56},{56,64},{64,7... | collective-permute-start | bytes 786440 | tf_op jit(solution)/shard_map/ppermute | solution.py:454
  98.2 16.8 %collective-permute-start.21 = (f32[11,64,128]{2,1,0:T(8,128)S(1)}, f32[11,64,128]{2,1,0:T(8,128)S(1)}, u32[]{:S(2)}, u32[]{:S(2)}) collective-permute-start(f32[11,64,128]{2,1,0:T(8,128)S(1)} %get-tuple-element.83), channel_id=1, source_target_pairs={{0,120},{8,0},{16,8},{24,16},{32,24},{40,32},{48,40},{56,48},{64,5... | collective-permute-start | bytes 1081352 | tf_op jit(solution)/shard_map/ppermute | solution.py:454
  103.0 11.9 %collective-permute-start.22 = (f32[8,24,128]{2,1,0:T(8,128)S(1)}, f32[8,24,128]{2,1,0:T(8,128)S(1)}, u32[]{:S(2)}, u32[]{:S(2)}) collective-permute-start(f32[8,24,128]{2,1,0:T(8,128)S(1)} %get-tuple-element.84), channel_id=1, source_target_pairs={{0,8},{8,16},{16,24},{24,32},{32,40},{40,48},{48,56},{56,64},{64,7... | collective-permute-start | bytes 294920 | tf_op jit(solution)/shard_map/ppermute | solution.py:454
  103.1 11.9 %collective-permute-start.23 = (f32[11,24,128]{2,1,0:T(8,128)S(1)}, f32[11,24,128]{2,1,0:T(8,128)S(1)}, u32[]{:S(2)}, u32[]{:S(2)}) collective-permute-start(f32[11,24,128]{2,1,0:T(8,128)S(1)} %get-tuple-element.85), channel_id=1, source_target_pairs={{0,120},{8,0},{16,8},{24,16},{32,24},{40,32},{48,40},{56,48},{64,5... | collective-permute-start | bytes 405512 | tf_op jit(solution)/shard_map/ppermute | solution.py:454
  120.8 22.2 %copy-start.5 = (s32[128]{0:T(128)S(1)}, s32[128]{0:T(128)}, u32[]{:S(2)}) copy-start(s32[128]{0:T(128)} %brick.1) | copy-start | bytes 1540
  120.8 22.2 %copy-start.7 = (s32[128]{0:T(128)S(1)}, s32[128]{0:T(128)}, u32[]{:S(2)}) copy-start(s32[128]{0:T(128)} %counts.1) | copy-start | bytes 1540
  120.8 22.2 %copy-start.9 = (s32[16]{0:T(128)S(1)}, s32[16]{0:T(128)}, u32[]{:S(2)}) copy-start(s32[16]{0:T(128)} %aper.1) | copy-start | bytes 196

commit v3 on v2

v3 whole, which is shorter than its diff:
```python
import functools

import jax
import jax.numpy as jnp
from jax import lax
from jax.experimental import pallas as pl
from jax.experimental.pallas import tpu as pltpu
from jax.sharding import PartitionSpec as P

BX = 32
BY = 64
NZ = 128
NEWTON = 3
SWEEPS = 8
CAP = 4
BLX = 4
BLY = 4
BLZ = 8
N_GX = 16
N_GY = 8
PAN_DEV = 128
APER_DEV = 16
LOW = 8
HIGH = 11
TILES = 11
WY = 8 * TILES
NEAR = (10, 8)
FAR = (TILES, HIGH)
DEPX = BX + BLX - 1
DEPY = 72

VMEM = pl.BlockSpec(memory_space=pltpu.VMEM)
SMEM = pl.BlockSpec(memory_space=pltpu.SMEM)
F32 = jnp.float32


def call(body, outs, ins, scratch=(), mib=24, flops=None):
    cost = None
    if flops is not None:
        cost = pl.CostEstimate(flops=flops, bytes_accessed=1 << 20, transcendentals=0)
    return pl.pallas_call(
        body,
        out_shape=[jax.ShapeDtypeStruct(s, F32) for s in outs],
        in_specs=list(ins),
        out_specs=[VMEM] * len(outs),
        scratch_shapes=list(scratch),
        cost_estimate=cost,
        compiler_params=pltpu.CompilerParams(vmem_limit_bytes=mib << 20),
    )


def iota(shape, dim):
    return lax.broadcasted_iota(jnp.int32, shape, dim)


def pack_kernel(*refs):
    arrays, send, local, need, sems = refs[:5], refs[5], refs[6:11], refs[11], refs[12]
    copies = [pltpu.make_async_copy(a, b, sems.at[i]) for i, (a, b) in enumerate(zip(arrays, local))]
    for copy in copies:
        copy.start()
    brick, counts, offsets, aper, rows = local

    def clear(p, c):
        need[p] = 0
        return c

    lax.fori_loop(0, PAN_DEV, clear, 0, unroll=8)
    for copy in copies:
        copy.wait()
    for a in range(APER_DEV):
        need[aper[a]] = 1
    sub = iota((8, 128), 0)
    group = (iota((8, 128), 1) >> 3) & 3
    j = sub & 3
    masks = {e: (group == j - e) for e in range(-3, 4)}
    lane1 = iota((1, 128), 1)

    def body(q, c):
        p = q * 2
        live = sub < jnp.where(sub < 4, counts[p], counts[p + 1] + 4)
        v = jnp.where(live, rows[pl.ds(pl.multiple_of(q * 8, 8), 8), :], 0.0)
        out = v
        for e in (-3, -2, -1, 1, 2, 3):
            moved = pltpu.roll(pltpu.roll(v, e % 8, 0), (-8 * e) % 128, 1)
            out = jnp.where(masks[e], moved, out)
        for h in range(2):
            b = brick[p + h]
            send[b, 0:4, :] = out[4 * h : 4 * h + 4]
            meta = jnp.zeros((1, 128), jnp.int32)
            for k in range(CAP):
                meta = jnp.where(lane1 == k, offsets[(p + h) * CAP + k], meta)
            meta = jnp.where(lane1 == CAP, need[p + h], meta)
            send[b, 4:5, :] = meta.astype(F32)
        return c

    lax.fori_loop(0, PAN_DEV // 2, body, 0, unroll=2)


def corner(meta, p, k):
    offset = meta[p, k].astype(jnp.int32)
    return offset >> 13, (offset >> 7) & 63, offset & 127


def block_rows(v, z, k, i, lane):
    moved = pltpu.roll(v, (z - 32 * i - 8 * k + 128) & 127, 1)
    return jnp.where((lane >= z) & (lane < z + BLZ), moved, 0.0)


def deposit_kernel(got, ion, out, x_low, x_high, y_low, y_high, meta, sem):
    copy = pltpu.make_async_copy(got.at[:, 4, :], meta, sem)
    copy.start()
    out[0:BX, 0:BY, :] = ion[...]
    out[0:BX, BY:DEPY, :] = jnp.zeros((BX, DEPY - BY, NZ), F32)
    out[BX:DEPX] = jnp.zeros((DEPX - BX, DEPY, NZ), F32)
    lane = iota((BLY, 128), 1)
    copy.wait()

    def body(p, c):
        v = got[p, 0:4, :]
        for k in range(CAP):
            x, y, z = corner(meta, p, k)
            add = [block_rows(v, z, k, i, lane) for i in range(BLX)]
            old = [out[x + i, pl.ds(y, BLY), :] for i in range(BLX)]
            for i in range(BLX):
                out[x + i, pl.ds(y, BLY), :] = old[i] + add[i]
        return c

    lax.fori_loop(0, PAN_DEV, body, 0, unroll=8)
    x_low[...] = out[0:HIGH]
    x_high[...] = out[BX - LOW : DEPX]
    y_low[...] = out[:, 0:16]
    y_high[...] = out[:, BY - LOW : DEPY]


def inside_y(tiles):
    gy = lax.axis_index("gy")
    lo = jnp.where(gy == 0, LOW, 0)
    hi = jnp.where(gy == N_GY - 1, LOW + BY, WY)
    sub = iota((8, 128), 0)
    ys = [sub * tiles + t for t in range(tiles)]
    return [(y >= lo) & (y < hi) for y in ys]


def lay(nat, at, count, own, below, above):
    nat[at : at + count, 0:LOW] = below
    nat[at : at + count, LOW : LOW + BY] = own
    nat[at : at + count, LOW + BY : LOW + BY + above.shape[1]] = above


def lay_charge(nat, at, count, own, below, above):
    spread = jnp.where(lax.axis_index("gy") > 0, 1.0, 0.0)
    nat[at : at + count, 0:LOW] = below[:, 0:LOW]
    nat[at : at + count, LOW : LOW + DEPY] = own
    nat[at : at + count, LOW : LOW + 8] += below[:, LOW : LOW + 8] * spread
    nat[at : at + count, LOW + BY : LOW + DEPY] += above[:, 0:8]
    nat[at : at + count, LOW + DEPY : WY] = above[:, 8:16]


def strided(nat, x, t, tiles):
    return nat[x, pl.ds(t, 8, stride=tiles), :]


def relax(layers, write):
    tiles = len(layers[0])
    lane = iota((8, 128), 1)
    first, last = lane == 0, lane == NZ - 1
    for u in range(len(layers) - 2):
        prev, cur, nxt = layers[u : u + 3]
        before = [pltpu.roll(cur[-1], 1, 0)] + cur[:-1]
        after = cur[1:] + [pltpu.roll(cur[0], 7, 0)]
        for t in range(tiles):
            left = jnp.where(first, 0.0, pltpu.roll(cur[t], 1, 1))
            right = jnp.where(last, 0.0, pltpu.roll(cur[t], NZ - 1, 1))
            total = (prev[t] + nxt[t]) + (before[t] + after[t]) + (left + right)
            write(u, t, total)


def layer(buf, x):
    return [buf[x, t] for t in range(buf.shape[1])]


def sweep(src, dst, rhs, inv, lo, hi):
    def rows(x0, count):
        def write(u, t, total):
            dst[x0 + u, t] = (rhs[x0 + u, t] + total) * inv[x0 + u, t]

        relax([layer(src, x0 - 1 + u) for u in range(count + 2)], write)

    count = (hi - lo + 1) // 2

    def body(i, c):
        rows(lo + i * count, count)
        return c

    lax.fori_loop(0, (hi - lo) // count, body, 0)
    if (hi - lo) % count:
        rows(lo + count, (hi - lo) % count)


def inner(b0, b1, rhs, inv, k0, a, h):
    bufs = (b0, b1)
    for k in range(k0, SWEEPS + 1):
        sweep(bufs[(k - 1) % 2], bufs[k % 2], rhs, inv, a + k, h - k)


def inner_first(charge, y_below, y_above, density, d_below, d_above, *refs):
    b0, b1, rhs, inv, source, dens = refs
    tiles = b0.shape[1]
    inside = inside_y(tiles)
    lay(dens, 0, BX, density[...], d_below[...], d_above[...])
    lay_charge(source, 0, DEPX, charge[...], y_below, y_above)

    def prep(x, c):
        for t in range(tiles):
            s = strided(source, x, t, tiles)
            d = strided(dens, x, t, tiles)
            scale = jnp.where(inside[t], 1.0 / (6.0 + d), 0.0)
            inv[x, t] = scale
            rhs[x, t] = s - d
            b1[x, t] = (s - d) * scale
        return c

    lax.fori_loop(0, BX, prep, 0, unroll=2)
    inner(b0, b1, rhs, inv, 2, BLX - 2, BX + 1)


def start(p_nat, s, s_at, d, inside, f, outs, to, x):
    p_out, rhs, inv = outs
    tiles = p_out.shape[1]
    for t in range(tiles):
        p = jnp.where(inside[t], strided(p_nat, x, t, tiles) * f, 0.0)
        coef = strided(d, x, t, tiles) * jnp.exp(p)
        p_out[x + to, t] = p
        rhs[x + to, t] = strided(s, x + s_at, t, tiles) + coef * (p - 1.0)
        inv[x + to, t] = jnp.where(inside[t], f / (6.0 + coef), 0.0)


def inner_next(own, y_below, y_above, source, s_low, dens, b0, b1, rhs, inv, nat):
    inside = inside_y(b0.shape[1])
    lay(nat, 0, BX, own[...], y_below[...], y_above[...])
    outs = (b0, rhs, inv)

    def prep_from(src, at):
        def prep(x, c):
            start(nat, src, at, dens, inside, 1.0, outs, 0, x)
            return c

        return prep

    lax.fori_loop(0, BLX - 1, prep_from(s_low, LOW), 0)
    lax.fori_loop(BLX - 1, BX, prep_from(source, 0), 0)
    inner(b0, b1, rhs, inv, 1, 0, BX)


def flanks(b0, b1, lows, highs, rhs, inv, k0, a, h, over):
    (l0, l1, l_rhs, l_inv), (h0, h1, h_rhs, h_inv) = lows, highs
    n_low, n_high = LOW + a, BX + over - h
    for i in range(LOW + a):
        if i + LOW >= len_low_halo(a):
            l_rhs[i + LOW], l_inv[i + LOW] = rhs[i], inv[i]
    for i in range(h - LOW, BX):
        h_rhs[i - (h - LOW)], h_inv[i - (h - LOW)] = rhs[i], inv[i]

    def one(k, near, l_src, l_dst, h_src, h_dst):
        def low_write(u, t, total):
            l_dst[k + u, t] = (l_rhs[k + u, t] + total) * l_inv[k + u, t]

        def high_write(u, t, total):
            r = LOW - k + u
            h_dst[r, t] = (h_rhs[r, t] + total) * h_inv[r, t]

        low = [layer(l_src, k - 1 + j) for j in range(n_low)]
        relax(low + [layer(near, a + k - 1), layer(near, a + k)], low_write)
        high = [layer(h_src, LOW + 1 - k + j) for j in range(n_high)]
        relax([layer(near, h - k - 1), layer(near, h - k)] + high, high_write)

    if k0 == 2:
        one(2, b1, l1, l0, h1, h0)

    def body(j, c):
        one(2 * j + 1, b0, l0, l1, h0, h1)
        one(2 * j + 2, b1, l1, l0, h1, h0)
        return c

    lax.fori_loop(k0 - 1, SWEEPS // 2, body, 0)


def len_low_halo(a):
    return LOW + (BLX - 1 if a else 0)


def finish(b0, l0, h0, nat, a, h, stop):
    tiles = b0.shape[1]

    def take(src, shift):
        def body(x, c):
            for t in range(tiles):
                nat[x, pl.ds(t, 8, stride=tiles), :] = src[x + shift, t]
            return c

        return body

    lax.fori_loop(0, a + LOW, take(l0, LOW), 0, unroll=2)
    lax.fori_loop(a + LOW, h - LOW, take(b0, 0), 0, unroll=2)
    lax.fori_loop(h - LOW, stop, take(h0, LOW - h), 0, unroll=2)


def hand_on(nat, out, x_low, x_high, y_low, y_high):
    out[...] = nat[0:BX, LOW : LOW + BY]
    x_low[...] = nat[0 : x_low.shape[0], LOW : LOW + BY]
    x_high[...] = nat[BX - LOW : BX, LOW : LOW + BY]
    y_low[...] = nat[0:BX, LOW : LOW + y_low.shape[1]]
    y_high[...] = nat[0:BX, BY : LOW + BY]


def edges():
    gx = lax.axis_index("gx")
    return jnp.where(gx > 0, 1.0, 0.0), jnp.where(gx < N_GX - 1, 1.0, 0.0)


def flank_first(*refs):
    b0, b1, rhs, inv, source, dens, x_below, x_above, d_below, d_above = refs[:10]
    outs, (s_low, s_high), nat, spare = refs[10:15], refs[15:17], refs[17], refs[18:]
    l0, l1, l_rhs, l_inv, h0, h1, h_rhs, h_inv = spare
    a, h = BLX - 2, BX + 1
    tiles, over = NEAR
    inside, (f_low, f_high) = inside_y(tiles), edges()
    s_low[...] = x_below[...]
    s_low[LOW:HIGH] = source[0 : HIGH - LOW] + x_below[LOW:HIGH] * f_low
    s_high[...] = x_above[...]
    s_high[0 : DEPX - BX] += source[BX:DEPX]

    def fill(count, s, s_at, d, d_at, f, at, p_out, rhs_out, inv_out):
        def body(r, c):
            for t in range(tiles):
                den = strided(d, r + d_at, t, tiles)
                scale = jnp.where(inside[t], f / (6.0 + den), 0.0)
                value = strided(s, r + s_at, t, tiles) - den
                rhs_out[r + at, t], inv_out[r + at, t] = value, scale
                p_out[r + at, t] = value * scale
            return c

        lax.fori_loop(0, count, body, 0)

    fill(LOW, s_low, 0, d_below, 0, f_low, 0, l1, l_rhs, l_inv)
    fill(BLX - 1, s_low, LOW, dens, 0, 1.0, LOW, l1, l_rhs, l_inv)
    fill(over, s_high, 0, d_above, 0, f_high, LOW - 1, h1, h_rhs, h_inv)
    lows, highs = (l0, l1, l_rhs, l_inv), (h0, h1, h_rhs, h_inv)
    flanks(b0, b1, lows, highs, rhs, inv, 2, a, h, over)
    finish(b0, l0, h0, nat, a, h, BX)
    hand_on(nat, *outs)


def next_flanks(refs, nat, spare, over):
    b0, b1, rhs, inv, x_below, x_above, s_low, s_high, d_low, d_high = refs
    l0, l1, l_rhs, l_inv, h0, h1, h_rhs, h_inv = spare
    inside, (f_low, f_high) = inside_y(b0.shape[1]), edges()

    def low_body(r, c):
        start(x_below, s_low, 0, d_low, inside, f_low, (l0, l_rhs, l_inv), 0, r)
        return c

    def high_body(r, c):
        start(x_above, s_high, 0, d_high, inside, f_high, (h0, h_rhs, h_inv), LOW, r)
        return c

    lax.fori_loop(0, LOW, low_body, 0)
    lax.fori_loop(0, over, high_body, 0)
    lows, highs = (l0, l1, l_rhs, l_inv), (h0, h1, h_rhs, h_inv)
    flanks(b0, b1, lows, highs, rhs, inv, 1, 0, BX, over)
    finish(b0, l0, h0, nat, 0, BX, BX + over - LOW)


def flank_next(*refs):
    outs, (nat, *spare) = refs[10:15], refs[15:]
    next_flanks(refs[:10], nat, spare, NEAR[1])
    hand_on(nat, *outs)


def flank_last(*refs):
    got, out, sums, nat, spare, (meta, sem, named) = refs[10], refs[11], refs[12], refs[13], refs[14:22], refs[22:]
    copy = pltpu.make_async_copy(got.at[:, 4, :], meta, sem)
    copy.start()
    next_flanks(refs[:10], nat, spare, HIGH)
    out[...] = nat[0:BX, LOW : LOW + BY]
    copy.wait()
    read(got, nat, sums, meta, named)


def slab_kernel(x_low, x_high, below, above, low, high):
    for own, at, slab in ((x_low, 0, low), (x_high, BX - LOW, high)):
        n, width = slab.shape[0], slab.shape[1]
        slab[:, 0:LOW] = below[at : at + n]
        slab[:, LOW : LOW + BY] = own[...]
        slab[:, LOW + BY : width] = above[at : at + n]


def charge_slab_kernel(x_low, x_high, below, above, low, high):
    for own, at, slab in ((x_low, 0, low), (x_high, BX - LOW, high)):
        lay_charge(slab, 0, HIGH, own[...], below[at : at + HIGH], above[at : at + HIGH])


def beside(body, width, x_low, x_high, y_low, y_high):
    y_below, y_above = ring(y_high, "gy", 1), ring(y_low, "gy", -1)
    low, high = call(
        body, [(x_low.shape[0], width, NZ), (x_high.shape[0], width, NZ)], [VMEM] * 4
    )(x_low, x_high, y_below, y_above)
    x_below, x_above = ring(high, "gx", 1), ring(low, "gx", -1)
    return (y_below, y_above), (x_below, x_above)


def read(got, field, out, meta, named):
    lane = iota((BLY, 128), 1)

    def note(p, n):
        named[n] = p
        return n + meta[p, CAP].astype(jnp.int32)

    count = lax.fori_loop(0, PAN_DEV, note, 0, unroll=8)
    named[count] = 0

    def body(j, c):
        for u in range(2):
            p = named[2 * j + u]
            v = got[p, 0:4, :]
            total = jnp.zeros((BLY, 128), F32)
            for k in range(CAP):
                x, y, z = corner(meta, p, k)
                for i in range(BLX):
                    piece = field[x + i, pl.ds(y + LOW, BLY), :]
                    total += block_rows(v, z, k, i, lane) * piece
            out[p] = jnp.sum(total, axis=0, keepdims=True)
        return c

    lax.fori_loop(0, (count + 1) // 2, body, 0)


def pick_kernel(brick, counts, aper, got, out, rows):
    sub = iota((1, APER_DEV), 1)
    live = jnp.ones((1, APER_DEV), F32)
    for a in range(APER_DEV):
        p = aper[a]
        rows[a : a + 1, :] = got[brick[p]]
        live = jnp.where(sub == a, counts[p].astype(F32), live)
    out[...] = jnp.sum(rows[...], axis=1) / live[0]


def ring(array, axis, by):
    size = lax.axis_size(axis)
    return lax.ppermute(array, axis, [(i, (i + by) % size) for i in range(size)])


def on_device(
    ion_charge, density, charge_blocks, panel_brick, row_counts, block_offset, aperture_panel
):
    everyone = ("gx", "gy")
    ints = [pltpu.SMEM((n,), jnp.int32) for n in (PAN_DEV, PAN_DEV, PAN_DEV * CAP, APER_DEV)]
    (send,) = call(
        pack_kernel,
        [(PAN_DEV, 8, 128)],
        [pl.BlockSpec(memory_space=pl.ANY)] * 5,
        ints
        + [
            pltpu.VMEM((PAN_DEV * CAP, 128), F32),
            pltpu.SMEM((PAN_DEV,), jnp.int32),
            pltpu.SemaphoreType.DMA((5,)),
        ],
    )(panel_brick, row_counts, block_offset, aperture_panel, charge_blocks)
    got = lax.all_to_all(send, everyone, split_axis=0, concat_axis=0, tiled=True)
    dy, dx = beside(
        slab_kernel, WY, density[:HIGH], density[BX - LOW :], density[:, :16], density[:, BY - LOW :]
    )

    meta = [pltpu.SMEM((PAN_DEV, 128), F32), pltpu.SemaphoreType.DMA]
    charge, *slabs = call(
        deposit_kernel,
        [(DEPX, DEPY, NZ)] + [(HIGH, DEPY, NZ)] * 2 + [(DEPX, 16, NZ)] * 2,
        [VMEM] * 2,
        meta,
    )(got, ion_charge)

    def tiles(n, width):
        return (n, width, 8, NZ)

    def layers(n):
        return pltpu.VMEM((n, WY, NZ), F32)

    def brick(over, width):
        return [(BX, BY, NZ), (over, BY, NZ), (LOW, BY, NZ), (BX, width, NZ), (BX, LOW, NZ)]

    def spare(width):
        return [pltpu.VMEM(tiles(LOW + LOW + BLX, width), F32)] * 8

    near, far = NEAR[0], FAR[0]
    work = 20_000_000_000
    cy, cx = beside(charge_slab_kernel, WY, *slabs)
    *state, source, dens = call(
        inner_first,
        [tiles(BX, near)] * 4 + [(DEPX, WY, NZ), (BX, WY, NZ)],
        [VMEM] * 6,
        (),
        32,
        work,
    )(charge, *cy, density, *dy)
    next_brick = brick(NEAR[1], 8)
    pot, *slabs, s_low, s_high = call(
        flank_first,
        next_brick + [(HIGH, WY, NZ)] * 2,
        [VMEM] * 10,
        [layers(DEPX)] + spare(near),
        32,
    )(*state, source, dens, *cx, *dx)
    for width, over in (NEAR, FAR):
        py, px = beside(slab_kernel, 8 * width, *slabs)
        state = call(inner_next, [tiles(BX, width)] * 4, [VMEM] * 6, [layers(BX)], 32, work)(
            pot, *py, source, s_low, dens
        )
        operands = (*state, *px, s_low, s_high, *dx)
        if over < HIGH:
            pot, *slabs = call(
                flank_next, brick(HIGH, 16), [VMEM] * 10, [layers(DEPX)] + spare(width), 32
            )(*operands)
    pot, sums = call(
        flank_last,
        [(BX, BY, NZ), (PAN_DEV, 1, 128)],
        [VMEM] * 11,
        [layers(DEPX)] + spare(far) + meta + [pltpu.SMEM((PAN_DEV + 8,), jnp.int32)],
        32,
    )(*operands, got)
    back = lax.all_to_all(sums, everyone, split_axis=0, concat_axis=0, tiled=True)
    (picked,) = call(
        pick_kernel,
        [(APER_DEV,)],
        [SMEM] * 3 + [VMEM],
        [pltpu.VMEM((APER_DEV, 128), F32)],
    )(panel_brick, row_counts, aperture_panel, back)
    return pot, picked


def solution(mesh):
    everyone = P(("gx", "gy"))
    grid = P("gx", "gy", None)
    return jax.shard_map(
        on_device,
        mesh=mesh,
        in_specs=(grid, grid, P(("gx", "gy"), None)) + (everyone,) * 4,
        out_specs=(grid, everyone),
        check_vma=False,
    )
```

time: 145 us -> 148 us (1.021)
  blocking collectives: 16.8 us -> 45.2 us
  starting transfers between devices: 56 us -> 29.1 us
  waiting for transfers between devices: 13 us -> 26.8 us
  Pallas kernels: 51.8 us -> 42.1 us
    all_to_all x0 -> x1, blocking collectives: none -> 24.8 us  [on_device(): lax.all_to_all(send, everyone, split_axis=0, concat_axis=0, tiled=True)]
    ppermute x24 -> x16, waiting for transfers between devices: 7.97 us -> 26.8 us  [ring(): lax.ppermute(array, axis, [(i, (i + by) % size) for i in range(size)])]
    ppermute x24 -> x16, starting transfers between devices: 44.5 us -> 29.1 us  [ring(): lax.ppermute(array, axis, [(i, (i + by) % size) for i in range(size)])]
    all_to_all x1 -> x0, starting transfers between devices: 11.5 us -> none  [on_device(): lax.all_to_all(send, everyone, split_axis=0, concat_axis=0, tiled=True)]
    pallas_call x12 -> x11, Pallas kernels: 40.7 us -> 32.8 us  [the longest x2 12.8 us: on_device(): call(inner_next, [tiles(BX, width)] * 4, [VMEM] * 6, [layers(BX)], 32, work)]
    all_to_all x1 -> x0, waiting for transfers between devices: 5.06 us -> none  [on_device(): lax.all_to_all(send, everyone, split_axis=0, concat_axis=0, tiled=True)]
    all_to_all x1, blocking collectives: 16.8 us -> 20.4 us  [on_device(): lax.all_to_all(sums, everyone, split_axis=0, concat_axis=0, tiled=True)]
  transfers between devices with their start and end apart: 25 -> 16, of which waited for: 5 -> 11; matrix products, arithmetic and copies ran while one was open for 1% -> 0% of each run, Pallas kernels for 18% -> 11%
where the time goes in v3:
time: 148 us
  blocking collectives  45.2 us (31%)
  Pallas kernels  42.1 us (28%)
  starting transfers between devices  29.1 us (20%)
  waiting for transfers between devices  26.8 us (18%)
  local copies, waits for them, and re-layouts  3.78 us (3%)
    ppermute x16, starting transfers between devices, ring(): lax.ppermute(array, axis, [(i, (i + by) % size) for i in range(size)])  29.1 us
    ppermute x16, waiting for transfers between devices, ring(): lax.ppermute(array, axis, [(i, (i + by) % size) for i in range(size)])  26.8 us
    all_to_all x1, blocking collectives, on_device(): lax.all_to_all(send, everyone, split_axis=0, concat_axis=0, tiled=True)  24.8 us
    all_to_all x1, blocking collectives, on_device(): lax.all_to_all(sums, everyone, split_axis=0, concat_axis=0, tiled=True)  20.4 us
    pallas_call x2, Pallas kernels, on_device(): call(inner_next, [tiles(BX, width)] * 4, [VMEM] * 6, [layers(BX)], 32, work)  12.8 us
    pallas_call x1, Pallas kernels, on_device(): call(flank_last, [(BX, BY, NZ), (PAN_DEV, 1, 128)], [VMEM] * 11, [layers(...  7.29 us
    pallas_call x1, Pallas kernels, on_device(): call(deposit_kernel, [(DEPX, DEPY, NZ)] + [(HIGH, DEPY, NZ)] * 2 + [(DEPX...  5.94 us
    pallas_call x1, Pallas kernels, on_device(): call(flank_next, brick(HIGH, 16), [VMEM] * 10, [layers(DEPX)] + spare(wid...  3.92 us
  transfers between devices with their start and end apart: 16, of which 11 were waited for; matrix products, arithmetic and copies ran while one was open for 0% of the time, Pallas kernels for 11%

profile of v3, /device:TPU:1, one launch (start us, length us, event | category | flops | bytes accessed | tf_op | source)
XLA Modules:
  0.0 147.8 jit_solution(8166940369080424076)
XLA Ops:
  0.6 0.0 copy-start
  0.6 0.0 copy-start.2
  0.6 1.0 copy-done.2
  1.7 0.0 copy-start.3
  1.7 0.7 copy-done.3
  2.4 0.0 copy-start.4
  2.4 0.7 copy-done.4
  3.0 0.0 copy-start.6
  3.0 0.7 copy-done.6
  3.7 0.0 copy-start.8
  3.7 0.7 copy-done.8
  4.3 3.4 %shard_map.86 = f32[128,8,128]{2,1,0:T(8,128)S(1)} custom-call(s32[128]{0:T(128)S(1)} %copy-done.4, s32[128]{0:T(128)S(1)} %copy-done.6, s32[512]{0:T(512)S(1)} %copy-done.3, s32[16]{0:T(128)S(1)} %copy-done.8, f32[512,128]{1,0:T(8,128)S(1)} %copy-done.2), custom_call_target="tpu_custom_call" | custom-call | tf_op jit(solution)/shard_map/pallas_call | solution.py:458
  7.7 0.0 copy-start.1
  7.7 24.8 %all_to_all.10.got.refs_10_ = f32[128,8,128]{2,1,0:T(8,128)S(1)} all-to-all(f32[128,8,128]{2,1,0:T(8,128)S(1)} %shard_map.86), channel_id=1, replica_groups=mesh['gx'=16,'gy'=8] {'gx','gy'}, dimensions={0} | all-to-all | bytes 1048576 | tf_op jit(solution)/shard_map/all_to_all | solution.py:469
  32.5 0.0 copy-done
  32.5 5.9 %shard_map.87 = (f32[35,72,128]{2,1,0:T(8,128)S(1)}, f32[11,72,128]{2,1,0:T(8,128)S(1)}, f32[11,72,128]{2,1,0:T(8,128)S(1)}, f32[35,16,128]{2,1,0:T(8,128)S(1)}, f32[35,16,128]{2,1,0:T(8,128)S(1)}) custom-call(f32[128,8,128]{2,1,0:T(8,128)S(1)} %all_to_all.10.got.refs_10_, f32[32,64,128]{2,1,0:T(8,128)S(1)} %copy-done), custom_call_target="tpu_custom_call" | custom-call | tf_op jit(solution)/shard_map/pallas_call | solution.py:475
  38.5 1.1 collective-permute-start
  39.6 0.0 collective-permute-start.1
  39.6 0.0 copy-done.1
  39.6 2.9 %collective-permute-start.3 = (f32[32,16,128]{2,1,0:T(8,128)S(1)}, f32[32,16,128]{2,1,0:T(8,128)S(1)}, u32[]{:S(2)}, u32[]{:S(2)}) collective-permute-start(f32[32,16,128]{2,1,0:T(8,128)S(1)} %slice.13), channel_id=1, source_target_pairs={{0,7},{1,0},{2,1},{3,2},{4,3},{5,4},{6,5},{7,6},{8,15},{9,8},{10,9... | collective-permute-start | bytes 786440 | tf_op jit(solution)/shard_map/ppermute | solution.py:450
  42.6 0.0 collective-permute-start.2
  42.7 1.9 %collective-permute-done.2.d_below.below = f32[32,8,128]{2,1,0:T(8,128)S(1)} collective-permute-done((f32[32,8,128]{2,1,0:T(8,128)S(1)}, f32[32,8,128]{2,1,0:T(8,128)S(1)}, u32[]{:S(2)}, u32[]{:S(2)}) %collective-permute-start.2) | collective-permute-done | bytes 131104 | tf_op jit(solution)/shard_map/ppermute | solution.py:450
  44.6 3.9 %collective-permute-done.3.d_above.above = f32[32,16,128]{2,1,0:T(8,128)S(1)} collective-permute-done((f32[32,16,128]{2,1,0:T(8,128)S(1)}, f32[32,16,128]{2,1,0:T(8,128)S(1)}, u32[]{:S(2)}, u32[]{:S(2)}) %collective-permute-start.3) | collective-permute-done | bytes 262176 | tf_op jit(solution)/shard_map/ppermute | solution.py:450
  48.5 0.1 shard_map.90
  48.5 0.1 collective-permute-start.6
  48.6 4.8 %collective-permute-start.7 = (f32[11,88,128]{2,1,0:T(8,128)S(1)}, f32[11,88,128]{2,1,0:T(8,128)S(1)}, u32[]{:S(2)}, u32[]{:S(2)}) collective-permute-start(f32[11,88,128]{2,1,0:T(8,128)S(1)} %get-tuple-element.57), channel_id=1, source_target_pairs={{0,120},{8,0},{16,8},{24,16},{32,24},{40,32},{48,40},{56,48},{64,5... | collective-permute-start | bytes 1486856 | tf_op jit(solution)/shard_map/ppermute | solution.py:450
  53.4 0.0 collective-permute-done.y_below.below
  53.4 0.0 collective-permute-done.1.y_above.above
  53.4 0.1 shard_map.89
  53.5 0.1 collective-permute-start.4
  53.6 4.8 %collective-permute-start.5 = (f32[11,88,128]{2,1,0:T(8,128)S(1)}, f32[11,88,128]{2,1,0:T(8,128)S(1)}, u32[]{:S(2)}, u32[]{:S(2)}) collective-permute-start(f32[11,88,128]{2,1,0:T(8,128)S(1)} %get-tuple-element.55), channel_id=1, source_target_pairs={{0,120},{8,0},{16,8},{24,16},{32,24},{40,32},{48,40},{56,48},{64,5... | collective-permute-start | bytes 1486856 | tf_op jit(solution)/shard_map/ppermute | solution.py:450
  58.3 3.8 %shard_map.88 = (f32[32,10,8,128]{3,2,1,0:T(8,128)S(1)}, f32[32,10,8,128]{3,2,1,0:T(8,128)S(1)}, f32[32,10,8,128]{3,2,1,0:T(8,128)S(1)}, f32[32,10,8,128]{3,2,1,...) custom-call(f32[35,72,128]{2,1,0:T(8,128)S(1)} %get-tuple-element.43.charge, ...), custom_call_target="tpu_custom_call" | custom-call | flops 20000000000 | bytes 1048576 | tf_op jit(solution)/shard_map/pallas_call | solution.py:497
  62.1 0.0 collective-permute-done.6.refs_8_
  62.1 0.6 collective-permute-done.7.refs_9_
  62.7 8.7 %collective-permute-done.4.refs_6_ = f32[11,88,128]{2,1,0:T(8,128)S(1)} collective-permute-done((f32[11,88,128]{2,1,0:T(8,128)S(1)}, f32[11,88,128]{2,1,0:T(8,128)S(1)}, u32[]{:S(2)}, u32[]{:S(2)}) %collective-permute-start.4) | collective-permute-done | bytes 495648 | tf_op jit(solution)/shard_map/ppermute | solution.py:450
  71.4 1.9 %collective-permute-done.5.refs_7_ = f32[11,88,128]{2,1,0:T(8,128)S(1)} collective-permute-done((f32[11,88,128]{2,1,0:T(8,128)S(1)}, f32[11,88,128]{2,1,0:T(8,128)S(1)}, u32[]{:S(2)}, u32[]{:S(2)}) %collective-permute-start.5) | collective-permute-done | bytes 495648 | tf_op jit(solution)/shard_map/ppermute | solution.py:450
  73.3 3.5 %shard_map.91 = (f32[32,64,128]{2,1,0:T(8,128)S(1)}, f32[8,64,128]{2,1,0:T(8,128)S(1)}, f32[8,64,128]{2,1,0:T(8,128)S(1)}, f32[32,8,128]{2,1,0:T(8,128)S(1)}, f3...) custom-call(f32[32,10,8,128]{3,2,1,0:T(8,128)S(1)} %get-tuple-element.46.refs_0_, ...), custom_call_target="tpu_custom_call" | custom-call | tf_op jit(solution)/shard_map/pallas_call | solution.py:506
  76.8 2.0 %collective-permute-start.8 = (f32[32,8,128]{2,1,0:T(8,128)S(1)}, f32[32,8,128]{2,1,0:T(8,128)S(1)}, u32[]{:S(2)}, u32[]{:S(2)}) collective-permute-start(f32[32,8,128]{2,1,0:T(8,128)S(1)} %get-tuple-element.59), channel_id=1, source_target_pairs={{0,1},{1,2},{2,3},{3,4},{4,5},{5,6},{6,7},{7,0},{8,9},{9,10},{10,1... | collective-permute-start | bytes 393224 | tf_op jit(solution)/shard_map/ppermute | solution.py:450
  78.8 0.3 collective-permute-start.9
  79.1 1.7 %collective-permute-done.8.y_below.below = f32[32,8,128]{2,1,0:T(8,128)S(1)} collective-permute-done((f32[32,8,128]{2,1,0:T(8,128)S(1)}, f32[32,8,128]{2,1,0:T(8,128)S(1)}, u32[]{:S(2)}, u32[]{:S(2)}) %collective-permute-start.8) | collective-permute-done | bytes 131104 | tf_op jit(solution)/shard_map/ppermute | solution.py:450
  80.8 2.7 %collective-permute-done.9.y_above.above = f32[32,8,128]{2,1,0:T(8,128)S(1)} collective-permute-done((f32[32,8,128]{2,1,0:T(8,128)S(1)}, f32[32,8,128]{2,1,0:T(8,128)S(1)}, u32[]{:S(2)}, u32[]{:S(2)}) %collective-permute-start.9) | collective-permute-done | bytes 131104 | tf_op jit(solution)/shard_map/ppermute | solution.py:450
  83.6 0.1 collective-permute-start.10
  83.7 5.8 %collective-permute-start.11 = (f32[8,80,128]{2,1,0:T(8,128)S(1)}, f32[8,80,128]{2,1,0:T(8,128)S(1)}, u32[]{:S(2)}, u32[]{:S(2)}) collective-permute-start(f32[8,80,128]{2,1,0:T(8,128)S(1)} %get-tuple-element.69), channel_id=1, source_target_pairs={{0,120},{8,0},{16,8},{24,16},{32,24},{40,32},{48,40},{56,48},{64,5... | collective-permute-start | bytes 983048 | tf_op jit(solution)/shard_map/ppermute | solution.py:450
  89.4 6.1 %shard_map.92 = (f32[32,10,8,128]{3,2,1,0:T(8,128)S(1)}, f32[32,10,8,128]{3,2,1,0:T(8,128)S(1)}, f32[32,10,8,128]{3,2,1,0:T(8,128)S(1)}, f32[32,10,8,128]{3,2,1,0:T(8,128)S(1)}) custom-call(f32[32,64,128]{2,1,0:T(8,128)S(1)} %get-tuple-element.58.own, f32[32,8,128]{2,1,0:T(8,128)S(1)} %collective-permute-done.8.y_below.below, ...), custom_call_target="tpu_custom_call" | custom-call | flops 20000000000 | bytes 1048576 | tf_op jit(solution)/shard_map/pallas_call | solution.py:515
  95.6 0.5 collective-permute-done.10.refs_4_
  96.1 0.0 collective-permute-done.11.refs_5_
  96.1 3.9 %shard_map.94 = (f32[32,64,128]{2,1,0:T(8,128)S(1)}, f32[11,64,128]{2,1,0:T(8,128)S(1)}, f32[8,64,128]{2,1,0:T(8,128)S(1)}, f32[32,16,128]{2,1,0:T(8,128)S(1)}, f32[32,8,128]{2,1,0:T(8,128)S(1)}) custom-call(f32[32,10,8,128]{3,2,1,0:T(8,128)S(1)} %get-tuple-element.62.refs_0_, f32[32,10,8,128]{3,2,1,0:T(8,128)S(1)} %get-tuple-element.63.refs_1_, ...), custom_call_target="tpu_custom_call" | custom-call | tf_op jit(solution)/shard_map/pallas_call | solution.py:520
  100.0 1.8 %collective-permute-start.13 = (f32[32,16,128]{2,1,0:T(8,128)S(1)}, f32[32,16,128]{2,1,0:T(8,128)S(1)}, u32[]{:S(2)}, u32[]{:S(2)}) collective-permute-start(f32[32,16,128]{2,1,0:T(8,128)S(1)} %get-tuple-element.73), channel_id=1, source_target_pairs={{0,7},{1,0},{2,1},{3,2},{4,3},{5,4},{6,5},{7,6},{8,15},{9,8},{10,9... | collective-permute-start | bytes 786440 | tf_op jit(solution)/shard_map/ppermute | solution.py:450
  101.8 0.0 collective-permute-start.12
  101.8 2.7 %collective-permute-done.12.y_below.below = f32[32,8,128]{2,1,0:T(8,128)S(1)} collective-permute-done((f32[32,8,128]{2,1,0:T(8,128)S(1)}, f32[32,8,128]{2,1,0:T(8,128)S(1)}, u32[]{:S(2)}, u32[]{:S(2)}) %collective-permute-start.12) | collective-permute-done | bytes 131104 | tf_op jit(solution)/shard_map/ppermute | solution.py:450
  104.5 1.3 collective-permute-done.13.y_above.above
  105.8 0.1 shard_map.96
  105.9 0.1 collective-permute-start.14
  105.9 5.4 %collective-permute-start.15 = (f32[11,88,128]{2,1,0:T(8,128)S(1)}, f32[11,88,128]{2,1,0:T(8,128)S(1)}, u32[]{:S(2)}, u32[]{:S(2)}) collective-permute-start(f32[11,88,128]{2,1,0:T(8,128)S(1)} %get-tuple-element.81), channel_id=1, source_target_pairs={{0,120},{8,0},{16,8},{24,16},{32,24},{40,32},{48,40},{56,48},{64,5... | collective-permute-start | bytes 1486856 | tf_op jit(solution)/shard_map/ppermute | solution.py:450
  111.4 6.7 %shard_map.95 = (f32[32,11,8,128]{3,2,1,0:T(8,128)S(1)}, f32[32,11,8,128]{3,2,1,0:T(8,128)S(1)}, f32[32,11,8,128]{3,2,1,0:T(8,128)S(1)}, f32[32,11,8,128]{3,2,1,0:T(8,128)S(1)}) custom-call(f32[32,64,128]{2,1,0:T(8,128)S(1)} %get-tuple-element.71.own, f32[32,8,128]{2,1,0:T(8,128)S(1)} %collective-permute-done.12.y_below.below, ...), custom_call_target="tpu_custom_call" | custom-call | flops 20000000000 | bytes 1048576 | tf_op jit(solution)/shard_map/pallas_call | solution.py:515
  118.1 0.0 collective-permute-done.14.refs_4_
  118.1 0.8 collective-permute-done.15.refs_5_
  118.9 0.0 copy-start.5
  118.9 7.3 %shard_map.97 = (f32[32,64,128]{2,1,0:T(8,128)}, f32[128,1,128]{2,1,0:T(1,128)S(1)}) custom-call(f32[32,11,8,128]{3,2,1,0:T(8,128)S(1)} %get-tuple-element.74.refs_0_, f32[32,11,8,128]{3,2,1,0:T(8,128)S(1)} %get-tuple-element.75.refs_1_, f32[32,11,8,128]{3,2,1,0:T(8,128)S(1)} %get-tuple-element.76.refs_2_, f32[32,11,8,128]{3,2,1,0:T(8,128)S(1)} %get-tuple-element.77.refs_3_, ...), custom_call_target="tpu_custom_call" | custom-call | tf_op jit(solution)/shard_map/pallas_call | solution.py:523
  126.2 20.4 %all_to_all.11.got = f32[128,1,128]{2,1,0:T(1,128)S(1)} all-to-all(f32[128,1,128]{2,1,0:T(1,128)S(1)} %get-tuple-element.83), channel_id=1, replica_groups=mesh['gx'=16,'gy'=8] {'gx','gy'}, dimensions={0} | all-to-all | bytes 131072 | tf_op jit(solution)/shard_map/all_to_all | solution.py:530
  146.5 0.0 copy-done.5
  146.5 0.0 copy-done.7
  146.6 0.0 copy-done.9
  146.6 1.2 shard_map.98
  (7 shorter events, 0.1 us)
Async XLA Ops:
  0.6 31.9 %copy-start = (f32[32,64,128]{2,1,0:T(8,128)S(1)}, f32[32,64,128]{2,1,0:T(8,128)}, u32[]{:S(2)}) copy-start(f32[32,64,128]{2,1,0:T(8,128)} %ion.1) | copy-start | bytes 3145732
  0.6 1.0 copy-start.2
  1.7 0.7 copy-start.3
  2.4 0.7 copy-start.4
  3.0 0.7 copy-start.6
  3.7 0.7 copy-start.8
  7.7 31.9 %copy-start.1 = (f32[32,64,128]{2,1,0:T(8,128)S(1)}, f32[32,64,128]{2,1,0:T(8,128)}, u32[]{:S(2)}) copy-start(f32[32,64,128]{2,1,0:T(8,128)} %density.1) | copy-start | bytes 3145732
  38.5 14.9 %collective-permute-start = (f32[35,16,128]{2,1,0:T(8,128)S(1)}, f32[35,16,128]{2,1,0:T(8,128)S(1)}, u32[]{:S(2)}, u32[]{:S(2)}) collective-permute-start(f32[35,16,128]{2,1,0:T(8,128)S(1)} %get-tuple-element.44), channel_id=1, source_target_pairs={{0,1},{1,2},{2,3},{3,4},{4,5},{5,6},{6,7},{7,0},{8,9},{9,10},{10,1... | collective-permute-start | bytes 860168 | tf_op jit(solution)/shard_map/ppermute | solution.py:450
  39.6 13.8 %collective-permute-start.1 = (f32[35,16,128]{2,1,0:T(8,128)S(1)}, f32[35,16,128]{2,1,0:T(8,128)S(1)}, u32[]{:S(2)}, u32[]{:S(2)}) collective-permute-start(f32[35,16,128]{2,1,0:T(8,128)S(1)} %get-tuple-element.45), channel_id=1, source_target_pairs={{0,7},{1,0},{2,1},{3,2},{4,3},{5,4},{6,5},{7,6},{8,15},{9,8},{10,9... | collective-permute-start | bytes 860168 | tf_op jit(solution)/shard_map/ppermute | solution.py:450
  39.6 8.8 %collective-permute-start.3 = (f32[32,16,128]{2,1,0:T(8,128)S(1)}, f32[32,16,128]{2,1,0:T(8,128)S(1)}, u32[]{:S(2)}, u32[]{:S(2)}) collective-permute-start(f32[32,16,128]{2,1,0:T(8,128)S(1)} %slice.13), channel_id=1, source_target_pairs={{0,7},{1,0},{2,1},{3,2},{4,3},{5,4},{6,5},{7,6},{8,15},{9,8},{10,9... | collective-permute-start | bytes 786440 | tf_op jit(solution)/shard_map/ppermute | solution.py:450
  42.6 2.0 %collective-permute-start.2 = (f32[32,8,128]{2,1,0:T(8,128)S(1)}, f32[32,8,128]{2,1,0:T(8,128)S(1)}, u32[]{:S(2)}, u32[]{:S(2)}) collective-permute-start(f32[32,8,128]{2,1,0:T(8,128)S(1)} %slice.12), channel_id=1, source_target_pairs={{0,1},{1,2},{2,3},{3,4},{4,5},{5,6},{6,7},{7,0},{8,9},{9,10},{10,1... | collective-permute-start | bytes 393224 | tf_op jit(solution)/shard_map/ppermute | solution.py:450
  48.5 13.6 %collective-permute-start.6 = (f32[8,88,128]{2,1,0:T(8,128)S(1)}, f32[8,88,128]{2,1,0:T(8,128)S(1)}, u32[]{:S(2)}, u32[]{:S(2)}) collective-permute-start(f32[8,88,128]{2,1,0:T(8,128)S(1)} %get-tuple-element.56), channel_id=1, source_target_pairs={{0,8},{8,16},{16,24},{24,32},{32,40},{40,48},{48,56},{56,64},{64,7... | collective-permute-start | bytes 1081352 | tf_op jit(solution)/shard_map/ppermute | solution.py:450
  48.6 14.1 %collective-permute-start.7 = (f32[11,88,128]{2,1,0:T(8,128)S(1)}, f32[11,88,128]{2,1,0:T(8,128)S(1)}, u32[]{:S(2)}, u32[]{:S(2)}) collective-permute-start(f32[11,88,128]{2,1,0:T(8,128)S(1)} %get-tuple-element.57), channel_id=1, source_target_pairs={{0,120},{8,0},{16,8},{24,16},{32,24},{40,32},{48,40},{56,48},{64,5... | collective-permute-start | bytes 1486856 | tf_op jit(solution)/shard_map/ppermute | solution.py:450
  53.5 18.0 %collective-permute-start.4 = (f32[11,88,128]{2,1,0:T(8,128)S(1)}, f32[11,88,128]{2,1,0:T(8,128)S(1)}, u32[]{:S(2)}, u32[]{:S(2)}) collective-permute-start(f32[11,88,128]{2,1,0:T(8,128)S(1)} %get-tuple-element.54), channel_id=1, source_target_pairs={{0,8},{8,16},{16,24},{24,32},{32,40},{40,48},{48,56},{56,64},{64,7... | collective-permute-start | bytes 1486856 | tf_op jit(solution)/shard_map/ppermute | solution.py:450
  53.6 19.8 %collective-permute-start.5 = (f32[11,88,128]{2,1,0:T(8,128)S(1)}, f32[11,88,128]{2,1,0:T(8,128)S(1)}, u32[]{:S(2)}, u32[]{:S(2)}) collective-permute-start(f32[11,88,128]{2,1,0:T(8,128)S(1)} %get-tuple-element.55), channel_id=1, source_target_pairs={{0,120},{8,0},{16,8},{24,16},{32,24},{40,32},{48,40},{56,48},{64,5... | collective-permute-start | bytes 1486856 | tf_op jit(solution)/shard_map/ppermute | solution.py:450
  76.8 3.9 %collective-permute-start.8 = (f32[32,8,128]{2,1,0:T(8,128)S(1)}, f32[32,8,128]{2,1,0:T(8,128)S(1)}, u32[]{:S(2)}, u32[]{:S(2)}) collective-permute-start(f32[32,8,128]{2,1,0:T(8,128)S(1)} %get-tuple-element.59), channel_id=1, source_target_pairs={{0,1},{1,2},{2,3},{3,4},{4,5},{5,6},{6,7},{7,0},{8,9},{9,10},{10,1... | collective-permute-start | bytes 393224 | tf_op jit(solution)/shard_map/ppermute | solution.py:450
  78.8 4.7 %collective-permute-start.9 = (f32[32,8,128]{2,1,0:T(8,128)S(1)}, f32[32,8,128]{2,1,0:T(8,128)S(1)}, u32[]{:S(2)}, u32[]{:S(2)}) collective-permute-start(f32[32,8,128]{2,1,0:T(8,128)S(1)} %get-tuple-element.60), channel_id=1, source_target_pairs={{0,7},{1,0},{2,1},{3,2},{4,3},{5,4},{6,5},{7,6},{8,15},{9,8},{10,9... | collective-permute-start | bytes 393224 | tf_op jit(solution)/shard_map/ppermute | solution.py:450
  83.6 12.5 %collective-permute-start.10 = (f32[8,80,128]{2,1,0:T(8,128)S(1)}, f32[8,80,128]{2,1,0:T(8,128)S(1)}, u32[]{:S(2)}, u32[]{:S(2)}) collective-permute-start(f32[8,80,128]{2,1,0:T(8,128)S(1)} %get-tuple-element.68), channel_id=1, source_target_pairs={{0,8},{8,16},{16,24},{24,32},{32,40},{40,48},{48,56},{56,64},{64,7... | collective-permute-start | bytes 983048 | tf_op jit(solution)/shard_map/ppermute | solution.py:450
  83.7 12.4 %collective-permute-start.11 = (f32[8,80,128]{2,1,0:T(8,128)S(1)}, f32[8,80,128]{2,1,0:T(8,128)S(1)}, u32[]{:S(2)}, u32[]{:S(2)}) collective-permute-start(f32[8,80,128]{2,1,0:T(8,128)S(1)} %get-tuple-element.69), channel_id=1, source_target_pairs={{0,120},{8,0},{16,8},{24,16},{32,24},{40,32},{48,40},{56,48},{64,5... | collective-permute-start | bytes 983048 | tf_op jit(solution)/shard_map/ppermute | solution.py:450
  100.0 5.8 %collective-permute-start.13 = (f32[32,16,128]{2,1,0:T(8,128)S(1)}, f32[32,16,128]{2,1,0:T(8,128)S(1)}, u32[]{:S(2)}, u32[]{:S(2)}) collective-permute-start(f32[32,16,128]{2,1,0:T(8,128)S(1)} %get-tuple-element.73), channel_id=1, source_target_pairs={{0,7},{1,0},{2,1},{3,2},{4,3},{5,4},{6,5},{7,6},{8,15},{9,8},{10,9... | collective-permute-start | bytes 786440 | tf_op jit(solution)/shard_map/ppermute | solution.py:450
  101.8 2.7 %collective-permute-start.12 = (f32[32,8,128]{2,1,0:T(8,128)S(1)}, f32[32,8,128]{2,1,0:T(8,128)S(1)}, u32[]{:S(2)}, u32[]{:S(2)}) collective-permute-start(f32[32,8,128]{2,1,0:T(8,128)S(1)} %get-tuple-element.72), channel_id=1, source_target_pairs={{0,1},{1,2},{2,3},{3,4},{4,5},{5,6},{6,7},{7,0},{8,9},{9,10},{10,1... | collective-permute-start | bytes 393224 | tf_op jit(solution)/shard_map/ppermute | solution.py:450
  105.9 12.2 %collective-permute-start.14 = (f32[8,88,128]{2,1,0:T(8,128)S(1)}, f32[8,88,128]{2,1,0:T(8,128)S(1)}, u32[]{:S(2)}, u32[]{:S(2)}) collective-permute-start(f32[8,88,128]{2,1,0:T(8,128)S(1)} %get-tuple-element.80), channel_id=1, source_target_pairs={{0,8},{8,16},{16,24},{24,32},{32,40},{40,48},{48,56},{56,64},{64,7... | collective-permute-start | bytes 1081352 | tf_op jit(solution)/shard_map/ppermute | solution.py:450
  105.9 12.9 %collective-permute-start.15 = (f32[11,88,128]{2,1,0:T(8,128)S(1)}, f32[11,88,128]{2,1,0:T(8,128)S(1)}, u32[]{:S(2)}, u32[]{:S(2)}) collective-permute-start(f32[11,88,128]{2,1,0:T(8,128)S(1)} %get-tuple-element.81), channel_id=1, source_target_pairs={{0,120},{8,0},{16,8},{24,16},{32,24},{40,32},{48,40},{56,48},{64,5... | collective-permute-start | bytes 1486856 | tf_op jit(solution)/shard_map/ppermute | solution.py:450
  118.9 27.7 %copy-start.5 = (s32[128]{0:T(128)S(1)}, s32[128]{0:T(128)}, u32[]{:S(2)}) copy-start(s32[128]{0:T(128)} %brick.1) | copy-start | bytes 1540
  118.9 27.7 %copy-start.7 = (s32[128]{0:T(128)S(1)}, s32[128]{0:T(128)}, u32[]{:S(2)}) copy-start(s32[128]{0:T(128)} %counts.1) | copy-start | bytes 1540
  118.9 27.7 %copy-start.9 = (s32[16]{0:T(128)S(1)}, s32[16]{0:T(128)}, u32[]{:S(2)}) copy-start(s32[16]{0:T(128)} %aper.1) | copy-start | bytes 196

commit v4 on v3

--- a/solution.py
+++ b/solution.py
@@ -31,6 +31,7 @@
 
 VMEM = pl.BlockSpec(memory_space=pltpu.VMEM)
 SMEM = pl.BlockSpec(memory_space=pltpu.SMEM)
+ANY = pl.BlockSpec(memory_space=pl.ANY)
 F32 = jnp.float32
 
 
@@ -93,7 +94,7 @@
             send[b, 4:5, :] = meta.astype(F32)
         return c
 
-    lax.fori_loop(0, PAN_DEV // 2, body, 0, unroll=2)
+    lax.fori_loop(0, PAN_DEV // 2, body, 0, unroll=4)
 
 
 def corner(meta, p, k):
@@ -106,7 +107,7 @@
     return jnp.where((lane >= z) & (lane < z + BLZ), moved, 0.0)
 
 
-def deposit_kernel(got, ion, out, x_low, x_high, y_low, y_high, meta, sem):
+def deposit_kernel(got, ion, unused_low, unused_high, out, x_low, x_high, y_low, y_high, meta, sem):
     copy = pltpu.make_async_copy(got.at[:, 4, :], meta, sem)
     copy.start()
     out[0:BX, 0:BY, :] = ion[...]
@@ -395,18 +396,18 @@
         slab[:, LOW + BY : width] = above[at : at + n]
 
 
-def charge_slab_kernel(x_low, x_high, below, above, low, high):
+def charge_slab_kernel(x_low, x_high, below, above, unused_low, unused_high, low, high):
     for own, at, slab in ((x_low, 0, low), (x_high, BX - LOW, high)):
         lay_charge(slab, 0, HIGH, own[...], below[at : at + HIGH], above[at : at + HIGH])
 
 
-def beside(body, width, x_low, x_high, y_low, y_high):
+def beside(body, width, x_low, x_high, y_low, y_high, first=()):
     y_below, y_above = ring(y_high, "gy", 1), ring(y_low, "gy", -1)
     low, high = call(
-        body, [(x_low.shape[0], width, NZ), (x_high.shape[0], width, NZ)], [VMEM] * 4
-    )(x_low, x_high, y_below, y_above)
+        body, [(x_low.shape[0], width, NZ), (x_high.shape[0], width, NZ)], [VMEM] * 4 + [ANY] * len(first)
+    )(x_low, x_high, y_below, y_above, *first)
     x_below, x_above = ring(high, "gx", 1), ring(low, "gx", -1)
-    return (y_below, y_above), (x_below, x_above)
+    return (y_below, y_above), (x_below, x_above), (low, high)
 
 
 def read(got, field, out, meta, named):
@@ -458,16 +459,17 @@
     (send,) = call(
         pack_kernel,
         [(PAN_DEV, 8, 128)],
-        [pl.BlockSpec(memory_space=pl.ANY)] * 5,
+        [ANY] * 5,
         ints
         + [
             pltpu.VMEM((PAN_DEV * CAP, 128), F32),
             pltpu.SMEM((PAN_DEV,), jnp.int32),
             pltpu.SemaphoreType.DMA((5,)),
         ],
+        60,
     )(panel_brick, row_counts, block_offset, aperture_panel, charge_blocks)
     got = lax.all_to_all(send, everyone, split_axis=0, concat_axis=0, tiled=True)
-    dy, dx = beside(
+    dy, dx, d_slabs = beside(
         slab_kernel, WY, density[:HIGH], density[BX - LOW :], density[:, :16], density[:, BY - LOW :]
     )
 
@@ -475,9 +477,9 @@
     charge, *slabs = call(
         deposit_kernel,
         [(DEPX, DEPY, NZ)] + [(HIGH, DEPY, NZ)] * 2 + [(DEPX, 16, NZ)] * 2,
-        [VMEM] * 2,
+        [VMEM] * 2 + [ANY] * 2,
         meta,
-    )(got, ion_charge)
+    )(got, ion_charge, *d_slabs)
 
     def tiles(n, width):
         return (n, width, 8, NZ)
@@ -493,7 +495,7 @@
 
     near, far = NEAR[0], FAR[0]
     work = 20_000_000_000
-    cy, cx = beside(charge_slab_kernel, WY, *slabs)
+    cy, cx, _ = beside(charge_slab_kernel, WY, *slabs, first=dx)
     *state, source, dens = call(
         inner_first,
         [tiles(BX, near)] * 4 + [(DEPX, WY, NZ), (BX, WY, NZ)],
@@ -511,7 +513,7 @@
         32,
     )(*state, source, dens, *cx, *dx)
     for width, over in (NEAR, FAR):
-        py, px = beside(slab_kernel, 8 * width, *slabs)
+        py, px, _ = beside(slab_kernel, 8 * width, *slabs)
         state = call(inner_next, [tiles(BX, width)] * 4, [VMEM] * 6, [layers(BX)], 32, work)(
             pot, *py, source, s_low, dens
         )

time: 148 us -> 137 us (0.926)
  blocking collectives: 45.2 us -> 22.2 us
  starting transfers between devices: 29.1 us -> 39.7 us
  waiting for transfers between devices: 26.8 us -> 31.4 us
  local copies, waits for them, and re-layouts: 3.78 us -> 0.12 us
    all_to_all x1 -> x0, blocking collectives: 24.8 us -> none  [on_device(): lax.all_to_all(send, everyone, split_axis=0, concat_axis=0, tiled=True)]
    all_to_all x0 -> x1, starting transfers between devices: none -> 11.5 us  [on_device(): lax.all_to_all(send, everyone, split_axis=0, concat_axis=0, tiled=True)]
    ppermute x16, waiting for transfers between devices: 26.8 us -> 31.4 us  [ring(): lax.ppermute(array, axis, [(i, (i + by) % size) for i in range(size)])]
    unnamed x20 -> x18, local copies, waits for them, and re-layouts: 3.7 us -> 0.04 us
    all_to_all x1, blocking collectives: 20.4 us -> 22.2 us  [on_device(): lax.all_to_all(sums, everyone, split_axis=0, concat_axis=0, tiled=True)]
  transfers between devices with their start and end apart: 16 -> 17, of which waited for: 11 -> 10; matrix products, arithmetic and copies ran while one was open for 0% -> 0% of each run, Pallas kernels for 11% -> 17%
where the time goes in v4:
time: 137 us
  Pallas kernels  42.7 us (31%)
  starting transfers between devices  39.7 us (29%)
  waiting for transfers between devices  31.4 us (23%)
  blocking collectives  22.2 us (16%)
    ppermute x16, waiting for transfers between devices, ring(): lax.ppermute(array, axis, [(i, (i + by) % size) for i in range(size)])  31.4 us
    ppermute x16, starting transfers between devices, ring(): lax.ppermute(array, axis, [(i, (i + by) % size) for i in range(size)])  28.2 us
    all_to_all x1, blocking collectives, on_device(): lax.all_to_all(sums, everyone, split_axis=0, concat_axis=0, tiled=True)  22.2 us
    pallas_call x2, Pallas kernels, on_device(): call(inner_next, [tiles(BX, width)] * 4, [VMEM] * 6, [layers(BX)], 32, work)  12.5 us
    all_to_all x1, starting transfers between devices, on_device(): lax.all_to_all(send, everyone, split_axis=0, concat_axis=0, tiled=True)  11.5 us
    pallas_call x1, Pallas kernels, on_device(): call(flank_last, [(BX, BY, NZ), (PAN_DEV, 1, 128)], [VMEM] * 11, [layers(...  7.29 us
    pallas_call x1, Pallas kernels, on_device(): call(deposit_kernel, [(DEPX, DEPY, NZ)] + [(HIGH, DEPY, NZ)] * 2 + [(DEPX...  5.94 us
    pallas_call x1, Pallas kernels, on_device(): call(flank_next, brick(HIGH, 16), [VMEM] * 10, [layers(DEPX)] + spare(wid...  3.89 us
  transfers between devices with their start and end apart: 17, of which 10 were waited for; matrix products, arithmetic and copies ran while one was open for 0% of the time, Pallas kernels for 17%

profile of v4, /device:TPU:1, one launch (start us, length us, event | category | flops | bytes accessed | tf_op | source)
XLA Modules:
  0.0 137.0 jit_solution(4554657824632344850)
XLA Ops:
  0.6 0.0 copy-start.1
  0.6 3.5 %shard_map.86 = f32[128,8,128]{2,1,0:T(8,128)} custom-call(s32[128]{0:T(128)} %brick.1, s32[128]{0:T(128)} %counts.1, s32[512]{0:T(512)} %refs_2_.1, s32[16]{0:T(128)} %aper.1, f32[512,128]{1,0:T(8,128)} %refs_4_.1), custom_call_target="tpu_custom_call" | custom-call | tf_op jit(solution)/shard_map/pallas_call | solution.py:459
  4.1 11.5 %all-to-all-start = ((f32[128,8,128]{2,1,0:T(8,128)}), f32[128,8,128]{2,1,0:T(8,128)S(1)}, u32[]{:S(2)}, u32[]{:S(2)}) async-start(f32[128,8,128]{2,1,0:T(8,128)} %shard_map.86), calls=%async_computation | async-start | bytes 1048576 | tf_op jit(solution)/shard_map/all_to_all | solution.py:471
  15.6 0.0 copy-done.1
  15.7 0.0 copy-start
  15.7 1.1 collective-permute-start.1
  16.8 0.7 collective-permute-start
  17.5 5.5 %collective-permute-done.below.d_below = f32[32,8,128]{2,1,0:T(8,128)S(1)} collective-permute-done((f32[32,8,128]{2,1,0:T(8,128)S(1)}, f32[32,8,128]{2,1,0:T(8,128)S(1)}, u32[]{:S(2)}, u32[]{:S(2)}) %collective-permute-start) | collective-permute-done | bytes 131104 | tf_op jit(solution)/shard_map/ppermute | solution.py:451
  23.0 0.0 copy-start.4
  23.0 3.1 %collective-permute-done.1.above.d_above = f32[32,16,128]{2,1,0:T(8,128)S(1)} collective-permute-done((f32[32,16,128]{2,1,0:T(8,128)S(1)}, f32[32,16,128]{2,1,0:T(8,128)S(1)}, u32[]{:S(2)}, u32[]{:S(2)}) %collective-permute-start.1) | collective-permute-done | bytes 262176 | tf_op jit(solution)/shard_map/ppermute | solution.py:451
  26.1 0.0 copy-start.2
  26.1 1.0 shard_map.87
  27.2 5.2 %collective-permute-start.5 = (f32[11,88,128]{2,1,0:T(8,128)}, f32[11,88,128]{2,1,0:T(8,128)S(1)}, u32[]{:S(2)}, u32[]{:S(2)}) collective-permute-start(f32[11,88,128]{2,1,0:T(8,128)} %get-tuple-element.43.unused_low), channel_id=1, source_target_pairs={{0,120},{8,0},{16,8},{24,16},{32,24},{40,32},{48,40},{56,48},{64,5... | collective-permute-start | bytes 1486856 | tf_op jit(solution)/shard_map/ppermute | solution.py:451
  32.3 0.0 copy-done.4
  32.4 0.0 copy-done.2
  32.4 0.0 collective-permute-start.4
  32.4 0.0 all-to-all-done.got.refs_10_
  32.4 0.0 copy-done
  32.4 5.9 %shard_map.88 = (f32[35,72,128]{2,1,0:T(8,128)S(1)}, f32[11,72,128]{2,1,0:T(8,128)S(1)}, f32[11,72,128]{2,1,0:T(8,128)S(1)}, f32[35,16,128]{2,1,0:T(8,128)S(1)}, f32[35,16,128]{2,1,0:T(8,128)S(1)}) custom-call(f32[128,8,128]{2,1,0:T(8,128)S(1)} %all-to-all-done.got.refs_10_, f32[32,64,128]{2,1,0:T(8,128)S(1)} %copy-done, ...), custom_call_target="tpu_custom_call" | custom-call | tf_op jit(solution)/shard_map/pallas_call | solution.py:477
  38.3 0.0 copy-start.3
  38.3 0.0 copy-start.5
  38.3 0.0 collective-permute-start.2
  38.4 0.7 collective-permute-start.3
  39.1 6.0 %collective-permute-done.4.unused_low.refs_8_ = f32[8,88,128]{2,1,0:T(8,128)S(1)} collective-permute-done((f32[8,88,128]{2,1,0:T(8,128)}, f32[8,88,128]{2,1,0:T(8,128)S(1)}, u32[]{:S(2)}, u32[]{:S(2)}) %collective-permute-start.4) | collective-permute-done | bytes 360480 | tf_op jit(solution)/shard_map/ppermute | solution.py:451
  45.1 0.0 collective-permute-done.5.unused_high.refs_9_
  45.1 0.0 collective-permute-done.2.y_below.below
  45.1 0.0 collective-permute-done.3.y_above.above
  45.1 0.1 shard_map.90
  45.2 0.1 collective-permute-start.6
  45.3 4.8 %collective-permute-start.7 = (f32[11,88,128]{2,1,0:T(8,128)S(1)}, f32[11,88,128]{2,1,0:T(8,128)S(1)}, u32[]{:S(2)}, u32[]{:S(2)}) collective-permute-start(f32[11,88,128]{2,1,0:T(8,128)S(1)} %get-tuple-element.57), channel_id=1, source_target_pairs={{0,120},{8,0},{16,8},{24,16},{32,24},{40,32},{48,40},{56,48},{64,5... | collective-permute-start | bytes 1486856 | tf_op jit(solution)/shard_map/ppermute | solution.py:451
  50.1 0.0 copy-done.3
  50.1 0.0 copy-done.5
  50.1 3.8 %shard_map.89 = (f32[32,10,8,128]{3,2,1,0:T(8,128)S(1)}, f32[32,10,8,128]{3,2,1,0:T(8,128)S(1)}, f32[32,10,8,128]{3,2,1,0:T(8,128)S(1)}, f32[32,10,8,128]{3,2,1,...) custom-call(f32[35,72,128]{2,1,0:T(8,128)S(1)} %get-tuple-element.45.charge, ...), custom_call_target="tpu_custom_call" | custom-call | flops 20000000000 | bytes 1048576 | tf_op jit(solution)/shard_map/pallas_call | solution.py:499
  53.8 6.0 %collective-permute-done.6.refs_6_ = f32[11,88,128]{2,1,0:T(8,128)S(1)} collective-permute-done((f32[11,88,128]{2,1,0:T(8,128)S(1)}, f32[11,88,128]{2,1,0:T(8,128)S(1)}, u32[]{:S(2)}, u32[]{:S(2)}) %collective-permute-start.6) | collective-permute-done | bytes 495648 | tf_op jit(solution)/shard_map/ppermute | solution.py:451
  59.8 0.0 collective-permute-done.7.refs_7_
  59.8 3.5 %shard_map.91 = (f32[32,64,128]{2,1,0:T(8,128)S(1)}, f32[8,64,128]{2,1,0:T(8,128)S(1)}, f32[8,64,128]{2,1,0:T(8,128)S(1)}, f32[32,8,128]{2,1,0:T(8,128)S(1)}, f3...) custom-call(f32[32,10,8,128]{3,2,1,0:T(8,128)S(1)} %get-tuple-element.48.refs_0_, ...), custom_call_target="tpu_custom_call" | custom-call | tf_op jit(solution)/shard_map/pallas_call | solution.py:508
  63.3 3.8 %collective-permute-start.8 = (f32[32,8,128]{2,1,0:T(8,128)S(1)}, f32[32,8,128]{2,1,0:T(8,128)S(1)}, u32[]{:S(2)}, u32[]{:S(2)}) collective-permute-start(f32[32,8,128]{2,1,0:T(8,128)S(1)} %get-tuple-element.59), channel_id=1, source_target_pairs={{0,1},{1,2},{2,3},{3,4},{4,5},{5,6},{6,7},{7,0},{8,9},{9,10},{10,1... | collective-permute-start | bytes 393224 | tf_op jit(solution)/shard_map/ppermute | solution.py:451
  67.1 0.0 collective-permute-start.9
  67.1 1.9 %collective-permute-done.8.y_below.below = f32[32,8,128]{2,1,0:T(8,128)S(1)} collective-permute-done((f32[32,8,128]{2,1,0:T(8,128)S(1)}, f32[32,8,128]{2,1,0:T(8,128)S(1)}, u32[]{:S(2)}, u32[]{:S(2)}) %collective-permute-start.8) | collective-permute-done | bytes 131104 | tf_op jit(solution)/shard_map/ppermute | solution.py:451
  69.1 2.4 %collective-permute-done.9.y_above.above = f32[32,8,128]{2,1,0:T(8,128)S(1)} collective-permute-done((f32[32,8,128]{2,1,0:T(8,128)S(1)}, f32[32,8,128]{2,1,0:T(8,128)S(1)}, u32[]{:S(2)}, u32[]{:S(2)}) %collective-permute-start.9) | collective-permute-done | bytes 131104 | tf_op jit(solution)/shard_map/ppermute | solution.py:451
  71.6 0.1 collective-permute-start.10
  71.7 5.1 %collective-permute-start.11 = (f32[8,80,128]{2,1,0:T(8,128)S(1)}, f32[8,80,128]{2,1,0:T(8,128)S(1)}, u32[]{:S(2)}, u32[]{:S(2)}) collective-permute-start(f32[8,80,128]{2,1,0:T(8,128)S(1)} %get-tuple-element.69), channel_id=1, source_target_pairs={{0,120},{8,0},{16,8},{24,16},{32,24},{40,32},{48,40},{56,48},{64,5... | collective-permute-start | bytes 983048 | tf_op jit(solution)/shard_map/ppermute | solution.py:451
  76.8 6.0 %shard_map.92 = (f32[32,10,8,128]{3,2,1,0:T(8,128)S(1)}, f32[32,10,8,128]{3,2,1,0:T(8,128)S(1)}, f32[32,10,8,128]{3,2,1,0:T(8,128)S(1)}, f32[32,10,8,128]{3,2,1,0:T(8,128)S(1)}) custom-call(f32[32,64,128]{2,1,0:T(8,128)S(1)} %get-tuple-element.58.own, f32[32,8,128]{2,1,0:T(8,128)S(1)} %collective-permute-done.8.y_below.below, ...), custom_call_target="tpu_custom_call" | custom-call | flops 20000000000 | bytes 1048576 | tf_op jit(solution)/shard_map/pallas_call | solution.py:517
  82.8 1.5 %collective-permute-done.10.refs_4_ = f32[8,80,128]{2,1,0:T(8,128)S(1)} collective-permute-done((f32[8,80,128]{2,1,0:T(8,128)S(1)}, f32[8,80,128]{2,1,0:T(8,128)S(1)}, u32[]{:S(2)}, u32[]{:S(2)}) %collective-permute-start.10) | collective-permute-done | bytes 327712 | tf_op jit(solution)/shard_map/ppermute | solution.py:451
  84.2 0.0 collective-permute-done.11.refs_5_
  84.3 3.9 %shard_map.94 = (f32[32,64,128]{2,1,0:T(8,128)S(1)}, f32[11,64,128]{2,1,0:T(8,128)S(1)}, f32[8,64,128]{2,1,0:T(8,128)S(1)}, f32[32,16,128]{2,1,0:T(8,128)S(1)}, f32[32,8,128]{2,1,0:T(8,128)S(1)}) custom-call(f32[32,10,8,128]{3,2,1,0:T(8,128)S(1)} %get-tuple-element.62.refs_0_, f32[32,10,8,128]{3,2,1,0:T(8,128)S(1)} %get-tuple-element.63.refs_1_, ...), custom_call_target="tpu_custom_call" | custom-call | tf_op jit(solution)/shard_map/pallas_call | solution.py:522
  88.1 0.9 collective-permute-start.13
  89.1 0.8 collective-permute-start.12
  89.9 2.1 %collective-permute-done.12.y_below.below = f32[32,8,128]{2,1,0:T(8,128)S(1)} collective-permute-done((f32[32,8,128]{2,1,0:T(8,128)S(1)}, f32[32,8,128]{2,1,0:T(8,128)S(1)}, u32[]{:S(2)}, u32[]{:S(2)}) %collective-permute-start.12) | collective-permute-done | bytes 131104 | tf_op jit(solution)/shard_map/ppermute | solution.py:451
  92.0 2.0 %collective-permute-done.13.y_above.above = f32[32,16,128]{2,1,0:T(8,128)S(1)} collective-permute-done((f32[32,16,128]{2,1,0:T(8,128)S(1)}, f32[32,16,128]{2,1,0:T(8,128)S(1)}, u32[]{:S(2)}, u32[]{:S(2)}) %collective-permute-start.13) | collective-permute-done | bytes 262176 | tf_op jit(solution)/shard_map/ppermute | solution.py:451
  94.0 0.1 shard_map.96
  94.0 0.1 collective-permute-start.14
  94.1 4.8 %collective-permute-start.15 = (f32[11,88,128]{2,1,0:T(8,128)S(1)}, f32[11,88,128]{2,1,0:T(8,128)S(1)}, u32[]{:S(2)}, u32[]{:S(2)}) collective-permute-start(f32[11,88,128]{2,1,0:T(8,128)S(1)} %get-tuple-element.81), channel_id=1, source_target_pairs={{0,120},{8,0},{16,8},{24,16},{32,24},{40,32},{48,40},{56,48},{64,5... | collective-permute-start | bytes 1486856 | tf_op jit(solution)/shard_map/ppermute | solution.py:451
  98.9 6.5 %shard_map.95 = (f32[32,11,8,128]{3,2,1,0:T(8,128)S(1)}, f32[32,11,8,128]{3,2,1,0:T(8,128)S(1)}, f32[32,11,8,128]{3,2,1,0:T(8,128)S(1)}, f32[32,11,8,128]{3,2,1,0:T(8,128)S(1)}) custom-call(f32[32,64,128]{2,1,0:T(8,128)S(1)} %get-tuple-element.71.own, f32[32,8,128]{2,1,0:T(8,128)S(1)} %collective-permute-done.12.y_below.below, ...), custom_call_target="tpu_custom_call" | custom-call | flops 20000000000 | bytes 1048576 | tf_op jit(solution)/shard_map/pallas_call | solution.py:517
  105.4 0.0 collective-permute-done.14.refs_4_
  105.4 0.8 collective-permute-done.15.refs_5_
  106.2 0.0 copy-start.6
  106.2 0.0 copy-start.7
  106.2 7.3 %shard_map.97 = (f32[32,64,128]{2,1,0:T(8,128)}, f32[128,1,128]{2,1,0:T(1,128)S(1)}) custom-call(f32[32,11,8,128]{3,2,1,0:T(8,128)S(1)} %get-tuple-element.74.refs_0_, f32[32,11,8,128]{3,2,1,0:T(8,128)S(1)} %get-tuple-element.75.refs_1_, f32[32,11,8,128]{3,2,1,0:T(8,128)S(1)} %get-tuple-element.76.refs_2_, f32[32,11,8,128]{3,2,1,0:T(8,128)S(1)} %get-tuple-element.77.refs_3_, ...), custom_call_target="tpu_custom_call" | custom-call | tf_op jit(solution)/shard_map/pallas_call | solution.py:525
  113.5 22.2 %all_to_all.10.got = f32[128,1,128]{2,1,0:T(1,128)S(1)} all-to-all(f32[128,1,128]{2,1,0:T(1,128)S(1)} %get-tuple-element.83), channel_id=1, replica_groups=mesh['gx'=16,'gy'=8] {'gx','gy'}, dimensions={0} | all-to-all | bytes 131072 | tf_op jit(solution)/shard_map/all_to_all | solution.py:532
  135.7 0.0 copy-done.6
  135.7 0.0 copy-done.7
  135.7 0.0 copy-done.8
  135.7 1.2 shard_map.98
  (6 shorter events, 0.1 us)
Async XLA Ops:
  0.6 15.0 %copy-start.1 = (f32[32,64,128]{2,1,0:T(8,128)S(1)}, f32[32,64,128]{2,1,0:T(8,128)}, u32[]{:S(2)}) copy-start(f32[32,64,128]{2,1,0:T(8,128)} %density.1) | copy-start | bytes 3145732
  4.1 28.3 %all-to-all-start = ((f32[128,8,128]{2,1,0:T(8,128)}), f32[128,8,128]{2,1,0:T(8,128)S(1)}, u32[]{:S(2)}, u32[]{:S(2)}) async-start(f32[128,8,128]{2,1,0:T(8,128)} %shard_map.86), calls=%async_computation | async-start | bytes 1048576 | tf_op jit(solution)/shard_map/all_to_all | solution.py:471
  15.7 16.7 %copy-start = (f32[32,64,128]{2,1,0:T(8,128)S(1)}, f32[32,64,128]{2,1,0:T(8,128)}, u32[]{:S(2)}) copy-start(f32[32,64,128]{2,1,0:T(8,128)} %ion.1) | copy-start | bytes 3145732
  15.7 10.5 %collective-permute-start.1 = (f32[32,16,128]{2,1,0:T(8,128)S(1)}, f32[32,16,128]{2,1,0:T(8,128)S(1)}, u32[]{:S(2)}, u32[]{:S(2)}) collective-permute-start(f32[32,16,128]{2,1,0:T(8,128)S(1)} %slice.15), channel_id=1, source_target_pairs={{0,7},{1,0},{2,1},{3,2},{4,3},{5,4},{6,5},{7,6},{8,15},{9,8},{10,9... | collective-permute-start | bytes 786440 | tf_op jit(solution)/shard_map/ppermute | solution.py:451
  16.8 6.2 %collective-permute-start = (f32[32,8,128]{2,1,0:T(8,128)S(1)}, f32[32,8,128]{2,1,0:T(8,128)S(1)}, u32[]{:S(2)}, u32[]{:S(2)}) collective-permute-start(f32[32,8,128]{2,1,0:T(8,128)S(1)} %slice.14), channel_id=1, source_target_pairs={{0,1},{1,2},{2,3},{3,4},{4,5},{5,6},{6,7},{7,0},{8,9},{9,10},{10,1... | collective-permute-start | bytes 393224 | tf_op jit(solution)/shard_map/ppermute | solution.py:451
  23.0 9.4 %copy-start.4 = (f32[32,8,128]{2,1,0:T(8,128)}, f32[32,8,128]{2,1,0:T(8,128)S(1)}, u32[]{:S(2)}) copy-start(f32[32,8,128]{2,1,0:T(8,128)S(1)} %collective-permute-done.below.d_below) | copy-start | bytes 393220
  26.1 6.2 %copy-start.2 = (f32[32,16,128]{2,1,0:T(8,128)}, f32[32,16,128]{2,1,0:T(8,128)S(1)}, u32[]{:S(2)}) copy-start(f32[32,16,128]{2,1,0:T(8,128)S(1)} %collective-permute-done.1.above.d_above) | copy-start | bytes 786436
  27.2 18.0 %collective-permute-start.5 = (f32[11,88,128]{2,1,0:T(8,128)}, f32[11,88,128]{2,1,0:T(8,128)S(1)}, u32[]{:S(2)}, u32[]{:S(2)}) collective-permute-start(f32[11,88,128]{2,1,0:T(8,128)} %get-tuple-element.43.unused_low), channel_id=1, source_target_pairs={{0,120},{8,0},{16,8},{24,16},{32,24},{40,32},{48,40},{56,48},{64,5... | collective-permute-start | bytes 1486856 | tf_op jit(solution)/shard_map/ppermute | solution.py:451
  32.4 12.8 %collective-permute-start.4 = (f32[8,88,128]{2,1,0:T(8,128)}, f32[8,88,128]{2,1,0:T(8,128)S(1)}, u32[]{:S(2)}, u32[]{:S(2)}) collective-permute-start(f32[8,88,128]{2,1,0:T(8,128)} %get-tuple-element.44.unused_high), channel_id=1, source_target_pairs={{0,8},{8,16},{16,24},{24,32},{32,40},{40,48},{48,56},{56,64},{64,7... | collective-permute-start | bytes 1081352 | tf_op jit(solution)/shard_map/ppermute | solution.py:451
  38.3 11.7 %copy-start.3 = (f32[32,16,128]{2,1,0:T(8,128)S(1)}, f32[32,16,128]{2,1,0:T(8,128)}, u32[]{:S(2)}) copy-start(f32[32,16,128]{2,1,0:T(8,128)} %copy-done.2) | copy-start | bytes 786436
  38.3 11.7 %copy-start.5 = (f32[32,8,128]{2,1,0:T(8,128)S(1)}, f32[32,8,128]{2,1,0:T(8,128)}, u32[]{:S(2)}) copy-start(f32[32,8,128]{2,1,0:T(8,128)} %copy-done.4) | copy-start | bytes 393220
  38.3 6.8 %collective-permute-start.2 = (f32[35,16,128]{2,1,0:T(8,128)S(1)}, f32[35,16,128]{2,1,0:T(8,128)S(1)}, u32[]{:S(2)}, u32[]{:S(2)}) collective-permute-start(f32[35,16,128]{2,1,0:T(8,128)S(1)} %get-tuple-element.46), channel_id=1, source_target_pairs={{0,1},{1,2},{2,3},{3,4},{4,5},{5,6},{6,7},{7,0},{8,9},{9,10},{10,1... | collective-permute-start | bytes 860168 | tf_op jit(solution)/shard_map/ppermute | solution.py:451
  38.4 6.8 %collective-permute-start.3 = (f32[35,16,128]{2,1,0:T(8,128)S(1)}, f32[35,16,128]{2,1,0:T(8,128)S(1)}, u32[]{:S(2)}, u32[]{:S(2)}) collective-permute-start(f32[35,16,128]{2,1,0:T(8,128)S(1)} %get-tuple-element.47), channel_id=1, source_target_pairs={{0,7},{1,0},{2,1},{3,2},{4,3},{5,4},{6,5},{7,6},{8,15},{9,8},{10,9... | collective-permute-start | bytes 860168 | tf_op jit(solution)/shard_map/ppermute | solution.py:451
  45.2 14.6 %collective-permute-start.6 = (f32[11,88,128]{2,1,0:T(8,128)S(1)}, f32[11,88,128]{2,1,0:T(8,128)S(1)}, u32[]{:S(2)}, u32[]{:S(2)}) collective-permute-start(f32[11,88,128]{2,1,0:T(8,128)S(1)} %get-tuple-element.56), channel_id=1, source_target_pairs={{0,8},{8,16},{16,24},{24,32},{32,40},{40,48},{48,56},{56,64},{64,7... | collective-permute-start | bytes 1486856 | tf_op jit(solution)/shard_map/ppermute | solution.py:451
  45.3 14.5 %collective-permute-start.7 = (f32[11,88,128]{2,1,0:T(8,128)S(1)}, f32[11,88,128]{2,1,0:T(8,128)S(1)}, u32[]{:S(2)}, u32[]{:S(2)}) collective-permute-start(f32[11,88,128]{2,1,0:T(8,128)S(1)} %get-tuple-element.57), channel_id=1, source_target_pairs={{0,120},{8,0},{16,8},{24,16},{32,24},{40,32},{48,40},{56,48},{64,5... | collective-permute-start | bytes 1486856 | tf_op jit(solution)/shard_map/ppermute | solution.py:451
  63.3 5.8 %collective-permute-start.8 = (f32[32,8,128]{2,1,0:T(8,128)S(1)}, f32[32,8,128]{2,1,0:T(8,128)S(1)}, u32[]{:S(2)}, u32[]{:S(2)}) collective-permute-start(f32[32,8,128]{2,1,0:T(8,128)S(1)} %get-tuple-element.59), channel_id=1, source_target_pairs={{0,1},{1,2},{2,3},{3,4},{4,5},{5,6},{6,7},{7,0},{8,9},{9,10},{10,1... | collective-permute-start | bytes 393224 | tf_op jit(solution)/shard_map/ppermute | solution.py:451
  67.1 4.4 %collective-permute-start.9 = (f32[32,8,128]{2,1,0:T(8,128)S(1)}, f32[32,8,128]{2,1,0:T(8,128)S(1)}, u32[]{:S(2)}, u32[]{:S(2)}) collective-permute-start(f32[32,8,128]{2,1,0:T(8,128)S(1)} %get-tuple-element.60), channel_id=1, source_target_pairs={{0,7},{1,0},{2,1},{3,2},{4,3},{5,4},{6,5},{7,6},{8,15},{9,8},{10,9... | collective-permute-start | bytes 393224 | tf_op jit(solution)/shard_map/ppermute | solution.py:451
  71.6 12.7 %collective-permute-start.10 = (f32[8,80,128]{2,1,0:T(8,128)S(1)}, f32[8,80,128]{2,1,0:T(8,128)S(1)}, u32[]{:S(2)}, u32[]{:S(2)}) collective-permute-start(f32[8,80,128]{2,1,0:T(8,128)S(1)} %get-tuple-element.68), channel_id=1, source_target_pairs={{0,8},{8,16},{16,24},{24,32},{32,40},{40,48},{48,56},{56,64},{64,7... | collective-permute-start | bytes 983048 | tf_op jit(solution)/shard_map/ppermute | solution.py:451
  71.7 12.6 %collective-permute-start.11 = (f32[8,80,128]{2,1,0:T(8,128)S(1)}, f32[8,80,128]{2,1,0:T(8,128)S(1)}, u32[]{:S(2)}, u32[]{:S(2)}) collective-permute-start(f32[8,80,128]{2,1,0:T(8,128)S(1)} %get-tuple-element.69), channel_id=1, source_target_pairs={{0,120},{8,0},{16,8},{24,16},{32,24},{40,32},{48,40},{56,48},{64,5... | collective-permute-start | bytes 983048 | tf_op jit(solution)/shard_map/ppermute | solution.py:451
  88.1 5.8 %collective-permute-start.13 = (f32[32,16,128]{2,1,0:T(8,128)S(1)}, f32[32,16,128]{2,1,0:T(8,128)S(1)}, u32[]{:S(2)}, u32[]{:S(2)}) collective-permute-start(f32[32,16,128]{2,1,0:T(8,128)S(1)} %get-tuple-element.73), channel_id=1, source_target_pairs={{0,7},{1,0},{2,1},{3,2},{4,3},{5,4},{6,5},{7,6},{8,15},{9,8},{10,9... | collective-permute-start | bytes 786440 | tf_op jit(solution)/shard_map/ppermute | solution.py:451
  89.1 2.9 %collective-permute-start.12 = (f32[32,8,128]{2,1,0:T(8,128)S(1)}, f32[32,8,128]{2,1,0:T(8,128)S(1)}, u32[]{:S(2)}, u32[]{:S(2)}) collective-permute-start(f32[32,8,128]{2,1,0:T(8,128)S(1)} %get-tuple-element.72), channel_id=1, source_target_pairs={{0,1},{1,2},{2,3},{3,4},{4,5},{5,6},{6,7},{7,0},{8,9},{9,10},{10,1... | collective-permute-start | bytes 393224 | tf_op jit(solution)/shard_map/ppermute | solution.py:451
  94.0 11.4 %collective-permute-start.14 = (f32[8,88,128]{2,1,0:T(8,128)S(1)}, f32[8,88,128]{2,1,0:T(8,128)S(1)}, u32[]{:S(2)}, u32[]{:S(2)}) collective-permute-start(f32[8,88,128]{2,1,0:T(8,128)S(1)} %get-tuple-element.80), channel_id=1, source_target_pairs={{0,8},{8,16},{16,24},{24,32},{32,40},{40,48},{48,56},{56,64},{64,7... | collective-permute-start | bytes 1081352 | tf_op jit(solution)/shard_map/ppermute | solution.py:451
  94.1 12.1 %collective-permute-start.15 = (f32[11,88,128]{2,1,0:T(8,128)S(1)}, f32[11,88,128]{2,1,0:T(8,128)S(1)}, u32[]{:S(2)}, u32[]{:S(2)}) collective-permute-start(f32[11,88,128]{2,1,0:T(8,128)S(1)} %get-tuple-element.81), channel_id=1, source_target_pairs={{0,120},{8,0},{16,8},{24,16},{32,24},{40,32},{48,40},{56,48},{64,5... | collective-permute-start | bytes 1486856 | tf_op jit(solution)/shard_map/ppermute | solution.py:451
  106.2 29.5 %copy-start.6 = (s32[128]{0:T(128)S(1)}, s32[128]{0:T(128)}, u32[]{:S(2)}) copy-start(s32[128]{0:T(128)} %brick.1) | copy-start | bytes 1540
  106.2 29.5 %copy-start.7 = (s32[128]{0:T(128)S(1)}, s32[128]{0:T(128)}, u32[]{:S(2)}) copy-start(s32[128]{0:T(128)} %counts.1) | copy-start | bytes 1540
  106.2 29.5 %copy-start.8 = (s32[16]{0:T(128)S(1)}, s32[16]{0:T(128)}, u32[]{:S(2)}) copy-start(s32[16]{0:T(128)} %aper.1) | copy-start | bytes 196

commit v5 on v4

--- a/solution.py
+++ b/solution.py
@@ -20,12 +20,12 @@
 N_GY = 8
 PAN_DEV = 128
 APER_DEV = 16
+READ = 4
 LOW = 8
 HIGH = 11
 TILES = 11
 WY = 8 * TILES
-NEAR = (10, 8)
-FAR = (TILES, HIGH)
+NEAR = 10
 DEPX = BX + BLX - 1
 DEPY = 72
 
@@ -126,7 +126,7 @@
                 out[x + i, pl.ds(y, BLY), :] = old[i] + add[i]
         return c
 
-    lax.fori_loop(0, PAN_DEV, body, 0, unroll=8)
+    lax.fori_loop(0, PAN_DEV, body, 0, unroll=16)
     x_low[...] = out[0:HIGH]
     x_high[...] = out[BX - LOW : DEPX]
     y_low[...] = out[:, 0:16]
@@ -238,7 +238,7 @@
 
 def inner_next(own, y_below, y_above, source, s_low, dens, b0, b1, rhs, inv, nat):
     inside = inside_y(b0.shape[1])
-    lay(nat, 0, BX, own[...], y_below[...], y_above[...])
+    lay(nat, 0, BX, own[...], y_below[0:BX], y_above[0:BX])
     outs = (b0, rhs, inv)
 
     def prep_from(src, at):
@@ -253,9 +253,9 @@
     inner(b0, b1, rhs, inv, 1, 0, BX)
 
 
-def flanks(b0, b1, lows, highs, rhs, inv, k0, a, h, over):
+def flanks(b0, b1, lows, highs, rhs, inv, k0, a, h):
     (l0, l1, l_rhs, l_inv), (h0, h1, h_rhs, h_inv) = lows, highs
-    n_low, n_high = LOW + a, BX + over - h
+    n_low, n_high = LOW + a, BX + HIGH - h
     for i in range(LOW + a):
         if i + LOW >= len_low_halo(a):
             l_rhs[i + LOW], l_inv[i + LOW] = rhs[i], inv[i]
@@ -290,7 +290,7 @@
     return LOW + (BLX - 1 if a else 0)
 
 
-def finish(b0, l0, h0, nat, a, h, stop):
+def finish(b0, l0, h0, nat, a, h):
     tiles = b0.shape[1]
 
     def take(src, shift):
@@ -303,15 +303,16 @@
 
     lax.fori_loop(0, a + LOW, take(l0, LOW), 0, unroll=2)
     lax.fori_loop(a + LOW, h - LOW, take(b0, 0), 0, unroll=2)
-    lax.fori_loop(h - LOW, stop, take(h0, LOW - h), 0, unroll=2)
-
-
-def hand_on(nat, out, x_low, x_high, y_low, y_high):
+    lax.fori_loop(h - LOW, DEPX, take(h0, LOW - h), 0, unroll=2)
+
+
+def hand_on(nat, out, ahead, x_low, x_high, y_low, y_high):
     out[...] = nat[0:BX, LOW : LOW + BY]
-    x_low[...] = nat[0 : x_low.shape[0], LOW : LOW + BY]
+    x_low[...] = nat[HIGH - LOW : HIGH, LOW : LOW + BY]
+    ahead[...] = nat[BX:DEPX, LOW : LOW + BY]
     x_high[...] = nat[BX - LOW : BX, LOW : LOW + BY]
-    y_low[...] = nat[0:BX, LOW : LOW + y_low.shape[1]]
-    y_high[...] = nat[0:BX, BY : LOW + BY]
+    y_low[...] = nat[0:DEPX, LOW : LOW + y_low.shape[1]]
+    y_high[...] = nat[0:DEPX, BY : LOW + BY]
 
 
 def edges():
@@ -320,15 +321,15 @@
 
 
 def flank_first(*refs):
-    b0, b1, rhs, inv, source, dens, x_below, x_above, d_below, d_above = refs[:10]
-    outs, (s_low, s_high), nat, spare = refs[10:15], refs[15:17], refs[17], refs[18:]
+    b0, b1, rhs, inv, source, dens, x_below, x_above, c_below, c_above, d_below, d_above = refs[:12]
+    outs, (s_low, s_high), nat, spare = refs[12:18], refs[18:20], refs[20], refs[21:]
     l0, l1, l_rhs, l_inv, h0, h1, h_rhs, h_inv = spare
     a, h = BLX - 2, BX + 1
-    tiles, over = NEAR
+    tiles = NEAR
     inside, (f_low, f_high) = inside_y(tiles), edges()
-    s_low[...] = x_below[...]
-    s_low[LOW:HIGH] = source[0 : HIGH - LOW] + x_below[LOW:HIGH] * f_low
-    s_high[...] = x_above[...]
+    lay_charge(s_low, 0, HIGH, x_below[...], c_below[:, 0:16], c_below[:, 16:32])
+    lay_charge(s_high, 0, HIGH, x_above[...], c_above[:, 0:16], c_above[:, 16:32])
+    s_low[LOW:HIGH] = source[0 : HIGH - LOW] + s_low[LOW:HIGH] * f_low
     s_high[0 : DEPX - BX] += source[BX:DEPX]
 
     def fill(count, s, s_at, d, d_at, f, at, p_out, rhs_out, inv_out):
@@ -345,15 +346,15 @@
 
     fill(LOW, s_low, 0, d_below, 0, f_low, 0, l1, l_rhs, l_inv)
     fill(BLX - 1, s_low, LOW, dens, 0, 1.0, LOW, l1, l_rhs, l_inv)
-    fill(over, s_high, 0, d_above, 0, f_high, LOW - 1, h1, h_rhs, h_inv)
+    fill(HIGH, s_high, 0, d_above, 0, f_high, LOW - 1, h1, h_rhs, h_inv)
     lows, highs = (l0, l1, l_rhs, l_inv), (h0, h1, h_rhs, h_inv)
-    flanks(b0, b1, lows, highs, rhs, inv, 2, a, h, over)
-    finish(b0, l0, h0, nat, a, h, BX)
+    flanks(b0, b1, lows, highs, rhs, inv, 2, a, h)
+    finish(b0, l0, h0, nat, a, h)
     hand_on(nat, *outs)
 
 
-def next_flanks(refs, nat, spare, over):
-    b0, b1, rhs, inv, x_below, x_above, s_low, s_high, d_low, d_high = refs
+def next_flanks(refs, nat, spare):
+    b0, b1, rhs, inv, ahead, y_below, y_above, x_below, x_above, s_low, s_high, d_low, d_high = refs
     l0, l1, l_rhs, l_inv, h0, h1, h_rhs, h_inv = spare
     inside, (f_low, f_high) = inside_y(b0.shape[1]), edges()
 
@@ -361,53 +362,70 @@
         start(x_below, s_low, 0, d_low, inside, f_low, (l0, l_rhs, l_inv), 0, r)
         return c
 
+    more = HIGH - LOW
+    lay(nat, 0, more, ahead[...], y_below[BX:DEPX], y_above[BX:DEPX])
+    nat[more:HIGH, 0 : x_above.shape[1]] = x_above[...]
+
     def high_body(r, c):
-        start(x_above, s_high, 0, d_high, inside, f_high, (h0, h_rhs, h_inv), LOW, r)
+        start(nat, s_high, 0, d_high, inside, f_high, (h0, h_rhs, h_inv), LOW, r)
         return c
 
     lax.fori_loop(0, LOW, low_body, 0)
-    lax.fori_loop(0, over, high_body, 0)
+    lax.fori_loop(0, HIGH, high_body, 0)
     lows, highs = (l0, l1, l_rhs, l_inv), (h0, h1, h_rhs, h_inv)
-    flanks(b0, b1, lows, highs, rhs, inv, 1, 0, BX, over)
-    finish(b0, l0, h0, nat, 0, BX, BX + over - LOW)
+    flanks(b0, b1, lows, highs, rhs, inv, 1, 0, BX)
+    finish(b0, l0, h0, nat, 0, BX)
 
 
 def flank_next(*refs):
-    outs, (nat, *spare) = refs[10:15], refs[15:]
-    next_flanks(refs[:10], nat, spare, NEAR[1])
+    outs, (nat, *spare) = refs[13:19], refs[19:]
+    next_flanks(refs[:13], nat, spare)
     hand_on(nat, *outs)
 
 
 def flank_last(*refs):
-    got, out, sums, nat, spare, (meta, sem, named) = refs[10], refs[11], refs[12], refs[13], refs[14:22], refs[22:]
+    (got, out, sums, nat), spare, (meta, sem, named) = refs[13:17], refs[17:25], refs[25:]
     copy = pltpu.make_async_copy(got.at[:, 4, :], meta, sem)
     copy.start()
-    next_flanks(refs[:10], nat, spare, HIGH)
+    next_flanks(refs[:13], nat, spare)
     out[...] = nat[0:BX, LOW : LOW + BY]
     copy.wait()
     read(got, nat, sums, meta, named)
 
 
-def slab_kernel(x_low, x_high, below, above, low, high):
-    for own, at, slab in ((x_low, 0, low), (x_high, BX - LOW, high)):
+def slab_kernel(at_low, x_low, x_high, below, above, low, high):
+    for own, at, slab in ((x_low, at_low, low), (x_high, BX - LOW, high)):
         n, width = slab.shape[0], slab.shape[1]
         slab[:, 0:LOW] = below[at : at + n]
         slab[:, LOW : LOW + BY] = own[...]
         slab[:, LOW + BY : width] = above[at : at + n]
 
 
-def charge_slab_kernel(x_low, x_high, below, above, unused_low, unused_high, low, high):
-    for own, at, slab in ((x_low, 0, low), (x_high, BX - LOW, high)):
-        lay_charge(slab, 0, HIGH, own[...], below[at : at + HIGH], above[at : at + HIGH])
-
-
-def beside(body, width, x_low, x_high, y_low, y_high, first=()):
+def beside(at_low, width, x_low, x_high, y_low, y_high):
     y_below, y_above = ring(y_high, "gy", 1), ring(y_low, "gy", -1)
     low, high = call(
-        body, [(x_low.shape[0], width, NZ), (x_high.shape[0], width, NZ)], [VMEM] * 4 + [ANY] * len(first)
-    )(x_low, x_high, y_below, y_above, *first)
+        functools.partial(slab_kernel, at_low),
+        [(x_low.shape[0], width, NZ), (x_high.shape[0], width, NZ)],
+        [VMEM] * 4,
+    )(x_low, x_high, y_below, y_above)
     x_below, x_above = ring(high, "gx", 1), ring(low, "gx", -1)
     return (y_below, y_above), (x_below, x_above), (low, high)
+
+
+def corner_kernel(below, above, unused_low, unused_high, low, high):
+    for at, strip in ((0, low), (BX - LOW, high)):
+        strip[:, 0:16] = below[at : at + HIGH]
+        strip[:, 16:32] = above[at : at + HIGH]
+
+
+def charge_beside(x_low, x_high, y_low, y_high, first):
+    x_below, x_above = ring(x_high, "gx", 1), ring(x_low, "gx", -1)
+    y_below, y_above = ring(y_high, "gy", 1), ring(y_low, "gy", -1)
+    low, high = call(corner_kernel, [(HIGH, 32, NZ)] * 2, [VMEM] * 2 + [ANY] * 2)(
+        y_below, y_above, *first
+    )
+    c_below, c_above = ring(high, "gx", 1), ring(low, "gx", -1)
+    return (y_below, y_above), (x_below, x_above, c_below, c_above)
 
 
 def read(got, field, out, meta, named):
@@ -418,11 +436,12 @@
         return n + meta[p, CAP].astype(jnp.int32)
 
     count = lax.fori_loop(0, PAN_DEV, note, 0, unroll=8)
-    named[count] = 0
+    for u in range(READ):
+        named[count + u] = 0
 
     def body(j, c):
-        for u in range(2):
-            p = named[2 * j + u]
+        for u in range(READ):
+            p = named[READ * j + u]
             v = got[p, 0:4, :]
             total = jnp.zeros((BLY, 128), F32)
             for k in range(CAP):
@@ -433,7 +452,7 @@
             out[p] = jnp.sum(total, axis=0, keepdims=True)
         return c
 
-    lax.fori_loop(0, (count + 1) // 2, body, 0)
+    lax.fori_loop(0, (count + READ - 1) // READ, body, 0)
 
 
 def pick_kernel(brick, counts, aper, got, out, rows):
@@ -470,7 +489,7 @@
     )(panel_brick, row_counts, block_offset, aperture_panel, charge_blocks)
     got = lax.all_to_all(send, everyone, split_axis=0, concat_axis=0, tiled=True)
     dy, dx, d_slabs = beside(
-        slab_kernel, WY, density[:HIGH], density[BX - LOW :], density[:, :16], density[:, BY - LOW :]
+        0, WY, density[:HIGH], density[BX - LOW :], density[:, :16], density[:, BY - LOW :]
     )
 
     meta = [pltpu.SMEM((PAN_DEV, 128), F32), pltpu.SemaphoreType.DMA]
@@ -487,46 +506,46 @@
     def layers(n):
         return pltpu.VMEM((n, WY, NZ), F32)
 
-    def brick(over, width):
-        return [(BX, BY, NZ), (over, BY, NZ), (LOW, BY, NZ), (BX, width, NZ), (BX, LOW, NZ)]
+    def brick(width):
+        slabs = [(HIGH - LOW, BY, NZ), (LOW, BY, NZ), (LOW, BY, NZ), (DEPX, width, NZ), (DEPX, LOW, NZ)]
+        return [(BX, BY, NZ)] + slabs
 
     def spare(width):
         return [pltpu.VMEM(tiles(LOW + LOW + BLX, width), F32)] * 8
 
-    near, far = NEAR[0], FAR[0]
     work = 20_000_000_000
-    cy, cx, _ = beside(charge_slab_kernel, WY, *slabs, first=dx)
+    cy, cx = charge_beside(*slabs, first=dx)
     *state, source, dens = call(
         inner_first,
-        [tiles(BX, near)] * 4 + [(DEPX, WY, NZ), (BX, WY, NZ)],
+        [tiles(BX, NEAR)] * 4 + [(DEPX, WY, NZ), (BX, WY, NZ)],
         [VMEM] * 6,
         (),
         32,
         work,
     )(charge, *cy, density, *dy)
-    next_brick = brick(NEAR[1], 8)
-    pot, *slabs, s_low, s_high = call(
+    pot, ahead, *slabs, s_low, s_high = call(
         flank_first,
-        next_brick + [(HIGH, WY, NZ)] * 2,
-        [VMEM] * 10,
-        [layers(DEPX)] + spare(near),
+        brick(8) + [(HIGH, WY, NZ)] * 2,
+        [VMEM] * 12,
+        [layers(DEPX)] + spare(NEAR),
         32,
     )(*state, source, dens, *cx, *dx)
-    for width, over in (NEAR, FAR):
-        py, px, _ = beside(slab_kernel, 8 * width, *slabs)
+    for step in range(1, NEWTON):
+        width = NEAR if step < NEWTON - 1 else TILES
+        py, px, _ = beside(HIGH - LOW, 8 * width, *slabs)
         state = call(inner_next, [tiles(BX, width)] * 4, [VMEM] * 6, [layers(BX)], 32, work)(
             pot, *py, source, s_low, dens
         )
-        operands = (*state, *px, s_low, s_high, *dx)
-        if over < HIGH:
-            pot, *slabs = call(
-                flank_next, brick(HIGH, 16), [VMEM] * 10, [layers(DEPX)] + spare(width), 32
+        operands = (*state, ahead, *py, *px, s_low, s_high, *dx)
+        if step < NEWTON - 1:
+            pot, ahead, *slabs = call(
+                flank_next, brick(16), [VMEM] * 13, [layers(DEPX)] + spare(width), 32
             )(*operands)
     pot, sums = call(
         flank_last,
         [(BX, BY, NZ), (PAN_DEV, 1, 128)],
-        [VMEM] * 11,
-        [layers(DEPX)] + spare(far) + meta + [pltpu.SMEM((PAN_DEV + 8,), jnp.int32)],
+        [VMEM] * 14,
+        [layers(DEPX)] + spare(TILES) + meta + [pltpu.SMEM((PAN_DEV + 8,), jnp.int32)],
         32,
     )(*operands, got)
     back = lax.all_to_all(sums, everyone, split_axis=0, concat_axis=0, tiled=True)

time: 137 us -> 134 us (0.978)
  blocking collectives: 22.2 us -> 17.9 us
    all_to_all x1, blocking collectives: 22.2 us -> 17.9 us  [on_device(): lax.all_to_all(sums, everyone, split_axis=0, concat_axis=0, tiled=True)]
    ppermute x16 -> x18, starting transfers between devices: 28.2 us -> 29.4 us  [ring(): lax.ppermute(array, axis, [(i, (i + by) % size) for i in range(size)])]
    ppermute x16 -> x18, waiting for transfers between devices: 31.4 us -> 30.9 us  [ring(): lax.ppermute(array, axis, [(i, (i + by) % size) for i in range(size)])]
  transfers between devices with their start and end apart: 17 -> 19, of which waited for: 10 -> 10; matrix products, arithmetic and copies ran while one was open for 0% -> 0% of each run, Pallas kernels for 17% -> 17%
where the time goes in v5:
time: 134 us
  Pallas kernels  43 us (32%)
  starting transfers between devices  40.9 us (31%)
  waiting for transfers between devices  31 us (23%)
  blocking collectives  17.9 us (13%)
    ppermute x18, waiting for transfers between devices, ring(): lax.ppermute(array, axis, [(i, (i + by) % size) for i in range(size)])  30.9 us
    ppermute x18, starting transfers between devices, ring(): lax.ppermute(array, axis, [(i, (i + by) % size) for i in range(size)])  29.4 us
    all_to_all x1, blocking collectives, on_device(): lax.all_to_all(sums, everyone, split_axis=0, concat_axis=0, tiled=True)  17.9 us
    pallas_call x2, Pallas kernels, on_device(): call(inner_next, [tiles(BX, width)] * 4, [VMEM] * 6, [layers(BX)], 32, work)  12.5 us
    all_to_all x1, starting transfers between devices, on_device(): lax.all_to_all(send, everyone, split_axis=0, concat_axis=0, tiled=True)  11.5 us
    pallas_call x1, Pallas kernels, on_device(): call(flank_last, [(BX, BY, NZ), (PAN_DEV, 1, 128)], [VMEM] * 14, [layers(...  6.86 us
    pallas_call x1, Pallas kernels, on_device(): call(deposit_kernel, [(DEPX, DEPY, NZ)] + [(HIGH, DEPY, NZ)] * 2 + [(DEPX...  5.49 us
    pallas_call x1, Pallas kernels, on_device(): call(flank_next, brick(16), [VMEM] * 13, [layers(DEPX)] + spare(width), 32)  4.51 us
  transfers between devices with their start and end apart: 19, of which 10 were waited for; matrix products, arithmetic and copies ran while one was open for 0% of the time, Pallas kernels for 17%

profile of v5, /device:TPU:1, one launch (start us, length us, event | category | flops | bytes accessed | tf_op | source)
XLA Modules:
  0.0 133.7 jit_solution(14387313241722752376)
XLA Ops:
  0.6 0.0 copy-start.1
  0.6 3.5 %shard_map.86 = f32[128,8,128]{2,1,0:T(8,128)} custom-call(s32[128]{0:T(128)} %brick.1, s32[128]{0:T(128)} %counts.1, s32[512]{0:T(512)} %refs_2_.1, s32[16]{0:T(128)} %aper.1, f32[512,128]{1,0:T(8,128)} %refs_4_.1), custom_call_target="tpu_custom_call" | custom-call | tf_op jit(solution)/shard_map/pallas_call | solution.py:478
  4.1 11.5 %all-to-all-start = ((f32[128,8,128]{2,1,0:T(8,128)}), f32[128,8,128]{2,1,0:T(8,128)S(1)}, u32[]{:S(2)}, u32[]{:S(2)}) async-start(f32[128,8,128]{2,1,0:T(8,128)} %shard_map.86), calls=%async_computation | async-start | bytes 1048576 | tf_op jit(solution)/shard_map/all_to_all | solution.py:490
  15.6 0.0 copy-done.1
  15.7 0.0 copy-start
  15.7 1.1 collective-permute-start.1
  16.8 0.7 collective-permute-start
  17.5 5.5 %collective-permute-done.below.d_below = f32[32,8,128]{2,1,0:T(8,128)S(1)} collective-permute-done((f32[32,8,128]{2,1,0:T(8,128)S(1)}, f32[32,8,128]{2,1,0:T(8,128)S(1)}, u32[]{:S(2)}, u32[]{:S(2)}) %collective-permute-start) | collective-permute-done | bytes 131104 | tf_op jit(solution)/shard_map/ppermute | solution.py:470
  23.0 0.0 copy-start.4
  23.0 3.1 %collective-permute-done.1.above.d_above = f32[32,16,128]{2,1,0:T(8,128)S(1)} collective-permute-done((f32[32,16,128]{2,1,0:T(8,128)S(1)}, f32[32,16,128]{2,1,0:T(8,128)S(1)}, u32[]{:S(2)}, u32[]{:S(2)}) %collective-permute-start.1) | collective-permute-done | bytes 262176 | tf_op jit(solution)/shard_map/ppermute | solution.py:470
  26.1 0.0 copy-start.2
  26.1 1.0 shard_map.87
  27.1 5.2 %collective-permute-start.7 = (f32[11,88,128]{2,1,0:T(8,128)}, f32[11,88,128]{2,1,0:T(8,128)S(1)}, u32[]{:S(2)}, u32[]{:S(2)}) collective-permute-start(f32[11,88,128]{2,1,0:T(8,128)} %get-tuple-element.45.unused_low), channel_id=1, source_target_pairs={{0,120},{8,0},{16,8},{24,16},{32,24},{40,32},{48,40},{56,48},{64,5... | collective-permute-start | bytes 1486856 | tf_op jit(solution)/shard_map/ppermute | solution.py:470
  32.3 0.0 copy-done.4
  32.3 0.0 copy-done.2
  32.3 0.0 collective-permute-start.6
  32.4 0.0 all-to-all-done.got.refs_13_
  32.4 0.0 copy-done
  32.4 5.5 %shard_map.88 = (f32[35,72,128]{2,1,0:T(8,128)S(1)}, f32[11,72,128]{2,1,0:T(8,128)S(1)}, f32[11,72,128]{2,1,0:T(8,128)S(1)}, f32[35,16,128]{2,1,0:T(8,128)S(1)}, f32[35,16,128]{2,1,0:T(8,128)S(1)}) custom-call(f32[128,8,128]{2,1,0:T(8,128)S(1)} %all-to-all-done.got.refs_13_, f32[32,64,128]{2,1,0:T(8,128)S(1)} %copy-done, ...), custom_call_target="tpu_custom_call" | custom-call | tf_op jit(solution)/shard_map/pallas_call | solution.py:496
  37.9 0.0 copy-start.3
  37.9 0.0 copy-start.5
  37.9 0.0 collective-permute-start.2
  37.9 0.7 collective-permute-start.3
  38.7 0.0 collective-permute-start.4
  38.7 6.4 %collective-permute-done.6.unused_low.refs_10_.refs_11_ = f32[8,88,128]{2,1,0:T(8,128)S(1)} collective-permute-done((f32[8,88,128]{2,1,0:T(8,128)}, f32[8,88,128]{2,1,0:T(8,128)S(1)}, u32[]{:S(2)}, u32[]{:S(2)}) %collective-permute-start.6) | collective-permute-done | bytes 360480 | tf_op jit(solution)/shard_map/ppermute | solution.py:470
  45.1 0.0 collective-permute-start.5
  45.1 0.0 collective-permute-done.7.unused_high.refs_11_.refs_12_
  45.1 0.0 collective-permute-done.2.y_below.below
  45.1 0.0 collective-permute-done.3.y_above.above
  45.2 1.5 %collective-permute-start.8 = (f32[11,32,128]{2,1,0:T(8,128)S(1)}, f32[11,32,128]{2,1,0:T(8,128)S(1)}, u32[]{:S(2)}, u32[]{:S(2)}) collective-permute-start(f32[11,32,128]{2,1,0:T(8,128)S(1)} %get-tuple-element.58), channel_id=1, source_target_pairs={{0,8},{8,16},{16,24},{24,32},{32,40},{40,48},{48,56},{56,64},{64,7... | collective-permute-start | bytes 540680 | tf_op jit(solution)/shard_map/ppermute | solution.py:470
  46.7 3.3 %collective-permute-start.9 = (f32[11,32,128]{2,1,0:T(8,128)S(1)}, f32[11,32,128]{2,1,0:T(8,128)S(1)}, u32[]{:S(2)}, u32[]{:S(2)}) collective-permute-start(f32[11,32,128]{2,1,0:T(8,128)S(1)} %get-tuple-element.59), channel_id=1, source_target_pairs={{0,120},{8,0},{16,8},{24,16},{32,24},{40,32},{48,40},{56,48},{64,5... | collective-permute-start | bytes 540680 | tf_op jit(solution)/shard_map/ppermute | solution.py:470
  50.0 0.0 copy-done.3
  50.0 0.0 copy-done.5
  50.0 3.8 %shard_map.89 = (f32[32,10,8,128]{3,2,1,0:T(8,128)S(1)}, f32[32,10,8,128]{3,2,1,0:T(8,128)S(1)}, f32[32,10,8,128]{3,2,1,0:T(8,128)S(1)}, f32[32,10,8,128]{3,2,1,...) custom-call(f32[35,72,128]{2,1,0:T(8,128)S(1)} %get-tuple-element.47.charge, ...), custom_call_target="tpu_custom_call" | custom-call | flops 20000000000 | bytes 1048576 | tf_op jit(solution)/shard_map/pallas_call | solution.py:518
  53.8 0.0 collective-permute-done.4.refs_6_
  53.8 0.0 collective-permute-done.5.refs_7_
  53.8 3.2 %collective-permute-done.8.refs_8_ = f32[11,32,128]{2,1,0:T(8,128)S(1)} collective-permute-done((f32[11,32,128]{2,1,0:T(8,128)S(1)}, f32[11,32,128]{2,1,0:T(8,128)S(1)}, u32[]{:S(2)}, u32[]{:S(2)}) %collective-permute-start.8) | collective-permute-done | bytes 180256 | tf_op jit(solution)/shard_map/ppermute | solution.py:470
  57.0 0.0 collective-permute-done.9.refs_9_
  57.0 4.1 %shard_map.91 = (f32[32,64,128]{2,1,0:T(8,128)S(1)}, f32[3,64,128]{2,1,0:T(8,128)S(1)}, f32[8,64,128]{2,1,0:T(8,128)S(1)}, f32[8,64,128]{2,1,0:T(8,128)S(1)}, f3...) custom-call(f32[32,10,8,128]{3,2,1,0:T(8,128)S(1)} %get-tuple-elemen, ...), custom_call_target="tpu_custom_call" | custom-call | tf_op jit(solution)/shard_map/pallas_call | solution.py:526
  61.1 5.4 %collective-permute-start.10 = (f32[35,8,128]{2,1,0:T(8,128)S(1)}, f32[35,8,128]{2,1,0:T(8,128)S(1)}, u32[]{:S(2)}, u32[]{:S(2)}) collective-permute-start(f32[35,8,128]{2,1,0:T(8,128)S(1)} %get-tuple-element.61), channel_id=1, source_target_pairs={{0,1},{1,2},{2,3},{3,4},{4,5},{5,6},{6,7},{7,0},{8,9},{9,10},{10,1... | collective-permute-start | bytes 430088 | tf_op jit(solution)/shard_map/ppermute | solution.py:470
  66.5 0.0 collective-permute-start.11
  66.5 2.1 %collective-permute-done.10.y_below.below.refs_5_ = f32[35,8,128]{2,1,0:T(8,128)S(1)} collective-permute-done((f32[35,8,128]{2,1,0:T(8,128)S(1)}, f32[35,8,128]{2,1,0:T(8,128)S(1)}, u32[]{:S(2)}, u32[]{:S(2)}) %collective-permute-start.10) | collective-permute-done | bytes 143392 | tf_op jit(solution)/shard_map/ppermute | solution.py:470
  68.6 2.5 %collective-permute-done.11.y_above.above.refs_6_ = f32[35,8,128]{2,1,0:T(8,128)S(1)} collective-permute-done((f32[35,8,128]{2,1,0:T(8,128)S(1)}, f32[35,8,128]{2,1,0:T(8,128)S(1)}, u32[]{:S(2)}, u32[]{:S(2)}) %collective-permute-start.11) | collective-permute-done | bytes 143392 | tf_op jit(solution)/shard_map/ppermute | solution.py:470
  71.1 0.1 collective-permute-start.12
  71.1 4.8 %collective-permute-start.13 = (f32[8,80,128]{2,1,0:T(8,128)S(1)}, f32[8,80,128]{2,1,0:T(8,128)S(1)}, u32[]{:S(2)}, u32[]{:S(2)}) collective-permute-start(f32[8,80,128]{2,1,0:T(8,128)S(1)} %get-tuple-element.72), channel_id=1, source_target_pairs={{0,120},{8,0},{16,8},{24,16},{32,24},{40,32},{48,40},{56,48},{64,5... | collective-permute-start | bytes 983048 | tf_op jit(solution)/shard_map/ppermute | solution.py:470
  75.9 6.0 %shard_map.92 = (f32[32,10,8,128]{3,2,1,0:T(8,128)S(1)}, f32[32,10,8,128]{3,2,1,0:T(8,128)S(1)}, f32[32,10,8,128]{3,2,1,0:T(8,128)S(1)}, f32[32,10,8,128]{3,2,1,0:T(8,128)S(1)}) custom-call(f32[32,64,128]{2,1,0:T(8,128)S(1)} %get-tuple-element.60.own, f32[35,8,128]{2,1,0:T(8,128)S(1)} %collective-permute-done.10.y_below.below.refs_5_, ...), custom_call_target="tpu_custom_call" | custom-call | flops 20000000000 | bytes 1048576 | tf_op jit(solution)/shard_map/pallas_call | solution.py:536
  81.9 2.2 %collective-permute-done.12.refs_7_ = f32[8,80,128]{2,1,0:T(8,128)S(1)} collective-permute-done((f32[8,80,128]{2,1,0:T(8,128)S(1)}, f32[8,80,128]{2,1,0:T(8,128)S(1)}, u32[]{:S(2)}, u32[]{:S(2)}) %collective-permute-start.12) | collective-permute-done | bytes 327712 | tf_op jit(solution)/shard_map/ppermute | solution.py:470
  84.1 0.0 collective-permute-done.13.refs_8_
  84.1 4.5 %shard_map.94 = (f32[32,64,128]{2,1,0:T(8,128)S(1)}, f32[3,64,128]{2,1,0:T(8,128)S(1)}, f32[8,64,128]{2,1,0:T(8,128)S(1)}, f32[8,64,128]{2,1,0:T(8,128)S(1)}, f3...) custom-call(f32[32,10,8,128]{3,2,1,0:T(8,128)S(1)} %get-tuple-element.64.refs_0_, ...), custom_call_target="tpu_custom_call" | custom-call | tf_op jit(solution)/shard_map/pallas_call | solution.py:541
  88.7 0.5 collective-permute-start.15
  89.1 1.3 collective-permute-start.14
  90.4 2.1 %collective-permute-done.14.y_below.below.refs_5_ = f32[35,8,128]{2,1,0:T(8,128)S(1)} collective-permute-done((f32[35,8,128]{2,1,0:T(8,128)S(1)}, f32[35,8,128]{2,1,0:T(8,128)S(1)}, u32[]{:S(2)}, u32[]{:S(2)}) %collective-permute-start.14) | collective-permute-done | bytes 143392 | tf_op jit(solution)/shard_map/ppermute | solution.py:470
  92.5 2.5 %collective-permute-done.15.y_above.above.refs_6_ = f32[35,16,128]{2,1,0:T(8,128)S(1)} collective-permute-done((f32[35,16,128]{2,1,0:T(8,128)S(1)}, f32[35,16,128]{2,1,0:T(8,128)S(1)}, u32[]{:S(2)}, u32[]{:S(2)}) %collective-permute-start.15) | collective-permute-done | bytes 286752 | tf_op jit(solution)/shard_map/ppermute | solution.py:470
  95.1 0.1 collective-permute-start.16
  95.2 4.8 %collective-permute-start.17 = (f32[8,88,128]{2,1,0:T(8,128)S(1)}, f32[8,88,128]{2,1,0:T(8,128)S(1)}, u32[]{:S(2)}, u32[]{:S(2)}) collective-permute-start(f32[8,88,128]{2,1,0:T(8,128)S(1)} %get-tuple-element.85), channel_id=1, source_target_pairs={{0,120},{8,0},{16,8},{24,16},{32,24},{40,32},{48,40},{56,48},{64,5... | collective-permute-start | bytes 1081352 | tf_op jit(solution)/shard_map/ppermute | solution.py:470
  99.9 6.5 %shard_map.95 = (f32[32,11,8,128]{3,2,1,0:T(8,128)S(1)}, f32[32,11,8,128]{3,2,1,0:T(8,128)S(1)}, f32[32,11,8,128]{3,2,1,0:T(8,128)S(1)}, f32[32,11,8,128]{3,2,1,0:T(8,128)S(1)}) custom-call(f32[32,64,128]{2,1,0:T(8,128)S(1)} %get-tuple-element.74.own, f32[35,8,128]{2,1,0:T(8,128)S(1)} %collective-permute-done.14.y_below.below.refs_5_, ...), custom_call_target="tpu_custom_call" | custom-call | flops 20000000000 | bytes 1048576 | tf_op jit(solution)/shard_map/pallas_call | solution.py:536
  106.4 1.3 collective-permute-done.16.refs_7_
  107.7 0.0 collective-permute-done.17.refs_8_
  107.7 6.9 %shard_map.97 = (f32[32,64,128]{2,1,0:T(8,128)}, f32[128,1,128]{2,1,0:T(1,128)S(1)}) custom-call(f32[32,11,8,128]{3,2,1,0:T(8,128)S(1)} %get-tuple-element.77.refs_0_, f32[32,11,8,128]{3,2,1,0:T(8,128)S(1)} %get-tuple-element.78.refs_1_, f32[32,11,8,128]{3,2,1,0:T(8,128)S(1)} %get-tuple-element.79.refs_2_, f32[32,11,8,128]{3,2,1,0:T(8,128)S(1)} %get-tuple-element.80.refs_3_, ...), custom_call_target="tpu_custom_call" | custom-call | tf_op jit(solution)/shard_map/pallas_call | solution.py:544
  114.6 17.9 %all_to_all.10.got = f32[128,1,128]{2,1,0:T(1,128)S(1)} all-to-all(f32[128,1,128]{2,1,0:T(1,128)S(1)} %get-tuple-element.87), channel_id=1, replica_groups=mesh['gx'=16,'gy'=8] {'gx','gy'}, dimensions={0} | all-to-all | bytes 131072 | tf_op jit(solution)/shard_map/all_to_all | solution.py:551
  132.5 0.0 copy-done.6
  132.5 0.0 copy-done.7
  132.5 0.0 copy-done.8
  132.5 1.2 shard_map.98
  (10 shorter events, 0.2 us)
Async XLA Ops:
  0.6 15.0 %copy-start.1 = (f32[32,64,128]{2,1,0:T(8,128)S(1)}, f32[32,64,128]{2,1,0:T(8,128)}, u32[]{:S(2)}) copy-start(f32[32,64,128]{2,1,0:T(8,128)} %density.1) | copy-start | bytes 3145732
  4.1 28.2 %all-to-all-start = ((f32[128,8,128]{2,1,0:T(8,128)}), f32[128,8,128]{2,1,0:T(8,128)S(1)}, u32[]{:S(2)}, u32[]{:S(2)}) async-start(f32[128,8,128]{2,1,0:T(8,128)} %shard_map.86), calls=%async_computation | async-start | bytes 1048576 | tf_op jit(solution)/shard_map/all_to_all | solution.py:490
  15.7 16.7 %copy-start = (f32[32,64,128]{2,1,0:T(8,128)S(1)}, f32[32,64,128]{2,1,0:T(8,128)}, u32[]{:S(2)}) copy-start(f32[32,64,128]{2,1,0:T(8,128)} %ion.1) | copy-start | bytes 3145732
  15.7 10.5 %collective-permute-start.1 = (f32[32,16,128]{2,1,0:T(8,128)S(1)}, f32[32,16,128]{2,1,0:T(8,128)S(1)}, u32[]{:S(2)}, u32[]{:S(2)}) collective-permute-start(f32[32,16,128]{2,1,0:T(8,128)S(1)} %slice.15), channel_id=1, source_target_pairs={{0,7},{1,0},{2,1},{3,2},{4,3},{5,4},{6,5},{7,6},{8,15},{9,8},{10,9... | collective-permute-start | bytes 786440 | tf_op jit(solution)/shard_map/ppermute | solution.py:470
  16.8 6.2 %collective-permute-start = (f32[32,8,128]{2,1,0:T(8,128)S(1)}, f32[32,8,128]{2,1,0:T(8,128)S(1)}, u32[]{:S(2)}, u32[]{:S(2)}) collective-permute-start(f32[32,8,128]{2,1,0:T(8,128)S(1)} %slice.14), channel_id=1, source_target_pairs={{0,1},{1,2},{2,3},{3,4},{4,5},{5,6},{6,7},{7,0},{8,9},{9,10},{10,1... | collective-permute-start | bytes 393224 | tf_op jit(solution)/shard_map/ppermute | solution.py:470
  23.0 9.4 %copy-start.4 = (f32[32,8,128]{2,1,0:T(8,128)}, f32[32,8,128]{2,1,0:T(8,128)S(1)}, u32[]{:S(2)}) copy-start(f32[32,8,128]{2,1,0:T(8,128)S(1)} %collective-permute-done.below.d_below) | copy-start | bytes 393220
  26.1 6.2 %copy-start.2 = (f32[32,16,128]{2,1,0:T(8,128)}, f32[32,16,128]{2,1,0:T(8,128)S(1)}, u32[]{:S(2)}) copy-start(f32[32,16,128]{2,1,0:T(8,128)S(1)} %collective-permute-done.1.above.d_above) | copy-start | bytes 786436
  27.1 18.0 %collective-permute-start.7 = (f32[11,88,128]{2,1,0:T(8,128)}, f32[11,88,128]{2,1,0:T(8,128)S(1)}, u32[]{:S(2)}, u32[]{:S(2)}) collective-permute-start(f32[11,88,128]{2,1,0:T(8,128)} %get-tuple-element.45.unused_low), channel_id=1, source_target_pairs={{0,120},{8,0},{16,8},{24,16},{32,24},{40,32},{48,40},{56,48},{64,5... | collective-permute-start | bytes 1486856 | tf_op jit(solution)/shard_map/ppermute | solution.py:470
  32.3 12.8 %collective-permute-start.6 = (f32[8,88,128]{2,1,0:T(8,128)}, f32[8,88,128]{2,1,0:T(8,128)S(1)}, u32[]{:S(2)}, u32[]{:S(2)}) collective-permute-start(f32[8,88,128]{2,1,0:T(8,128)} %get-tuple-element.46.unused_high), channel_id=1, source_target_pairs={{0,8},{8,16},{16,24},{24,32},{32,40},{40,48},{48,56},{56,64},{64,7... | collective-permute-start | bytes 1081352 | tf_op jit(solution)/shard_map/ppermute | solution.py:470
  37.9 12.1 %copy-start.3 = (f32[32,16,128]{2,1,0:T(8,128)S(1)}, f32[32,16,128]{2,1,0:T(8,128)}, u32[]{:S(2)}) copy-start(f32[32,16,128]{2,1,0:T(8,128)} %copy-done.2) | copy-start | bytes 786436
  37.9 12.1 %copy-start.5 = (f32[32,8,128]{2,1,0:T(8,128)S(1)}, f32[32,8,128]{2,1,0:T(8,128)}, u32[]{:S(2)}) copy-start(f32[32,8,128]{2,1,0:T(8,128)} %copy-done.4) | copy-start | bytes 393220
  37.9 7.2 %collective-permute-start.2 = (f32[35,16,128]{2,1,0:T(8,128)S(1)}, f32[35,16,128]{2,1,0:T(8,128)S(1)}, u32[]{:S(2)}, u32[]{:S(2)}) collective-permute-start(f32[35,16,128]{2,1,0:T(8,128)S(1)} %get-tuple-element.48), channel_id=1, source_target_pairs={{0,1},{1,2},{2,3},{3,4},{4,5},{5,6},{6,7},{7,0},{8,9},{9,10},{10,1... | collective-permute-start | bytes 860168 | tf_op jit(solution)/shard_map/ppermute | solution.py:470
  37.9 7.2 %collective-permute-start.3 = (f32[35,16,128]{2,1,0:T(8,128)S(1)}, f32[35,16,128]{2,1,0:T(8,128)S(1)}, u32[]{:S(2)}, u32[]{:S(2)}) collective-permute-start(f32[35,16,128]{2,1,0:T(8,128)S(1)} %get-tuple-element.49), channel_id=1, source_target_pairs={{0,7},{1,0},{2,1},{3,2},{4,3},{5,4},{6,5},{7,6},{8,15},{9,8},{10,9... | collective-permute-start | bytes 860168 | tf_op jit(solution)/shard_map/ppermute | solution.py:470
  38.7 15.1 %collective-permute-start.4 = (f32[11,72,128]{2,1,0:T(8,128)S(1)}, f32[11,72,128]{2,1,0:T(8,128)S(1)}, u32[]{:S(2)}, u32[]{:S(2)}) collective-permute-start(f32[11,72,128]{2,1,0:T(8,128)S(1)} %get-tuple-element.56), channel_id=1, source_target_pairs={{0,8},{8,16},{16,24},{24,32},{32,40},{40,48},{48,56},{56,64},{64,7... | collective-permute-start | bytes 1216520 | tf_op jit(solution)/shard_map/ppermute | solution.py:470
  45.1 8.7 %collective-permute-start.5 = (f32[11,72,128]{2,1,0:T(8,128)S(1)}, f32[11,72,128]{2,1,0:T(8,128)S(1)}, u32[]{:S(2)}, u32[]{:S(2)}) collective-permute-start(f32[11,72,128]{2,1,0:T(8,128)S(1)} %get-tuple-element.57), channel_id=1, source_target_pairs={{0,120},{8,0},{16,8},{24,16},{32,24},{40,32},{48,40},{56,48},{64,5... | collective-permute-start | bytes 1216520 | tf_op jit(solution)/shard_map/ppermute | solution.py:470
  45.2 11.9 %collective-permute-start.8 = (f32[11,32,128]{2,1,0:T(8,128)S(1)}, f32[11,32,128]{2,1,0:T(8,128)S(1)}, u32[]{:S(2)}, u32[]{:S(2)}) collective-permute-start(f32[11,32,128]{2,1,0:T(8,128)S(1)} %get-tuple-element.58), channel_id=1, source_target_pairs={{0,8},{8,16},{16,24},{24,32},{32,40},{40,48},{48,56},{56,64},{64,7... | collective-permute-start | bytes 540680 | tf_op jit(solution)/shard_map/ppermute | solution.py:470
  46.7 10.3 %collective-permute-start.9 = (f32[11,32,128]{2,1,0:T(8,128)S(1)}, f32[11,32,128]{2,1,0:T(8,128)S(1)}, u32[]{:S(2)}, u32[]{:S(2)}) collective-permute-start(f32[11,32,128]{2,1,0:T(8,128)S(1)} %get-tuple-element.59), channel_id=1, source_target_pairs={{0,120},{8,0},{16,8},{24,16},{32,24},{40,32},{48,40},{56,48},{64,5... | collective-permute-start | bytes 540680 | tf_op jit(solution)/shard_map/ppermute | solution.py:470
  61.1 7.4 %collective-permute-start.10 = (f32[35,8,128]{2,1,0:T(8,128)S(1)}, f32[35,8,128]{2,1,0:T(8,128)S(1)}, u32[]{:S(2)}, u32[]{:S(2)}) collective-permute-start(f32[35,8,128]{2,1,0:T(8,128)S(1)} %get-tuple-element.61), channel_id=1, source_target_pairs={{0,1},{1,2},{2,3},{3,4},{4,5},{5,6},{6,7},{7,0},{8,9},{9,10},{10,1... | collective-permute-start | bytes 430088 | tf_op jit(solution)/shard_map/ppermute | solution.py:470
  66.5 4.5 %collective-permute-start.11 = (f32[35,8,128]{2,1,0:T(8,128)S(1)}, f32[35,8,128]{2,1,0:T(8,128)S(1)}, u32[]{:S(2)}, u32[]{:S(2)}) collective-permute-start(f32[35,8,128]{2,1,0:T(8,128)S(1)} %get-tuple-element.62), channel_id=1, source_target_pairs={{0,7},{1,0},{2,1},{3,2},{4,3},{5,4},{6,5},{7,6},{8,15},{9,8},{10,9... | collective-permute-start | bytes 430088 | tf_op jit(solution)/shard_map/ppermute | solution.py:470
  71.1 13.1 %collective-permute-start.12 = (f32[8,80,128]{2,1,0:T(8,128)S(1)}, f32[8,80,128]{2,1,0:T(8,128)S(1)}, u32[]{:S(2)}, u32[]{:S(2)}) collective-permute-start(f32[8,80,128]{2,1,0:T(8,128)S(1)} %get-tuple-element.71), channel_id=1, source_target_pairs={{0,8},{8,16},{16,24},{24,32},{32,40},{40,48},{48,56},{56,64},{64,7... | collective-permute-start | bytes 983048 | tf_op jit(solution)/shard_map/ppermute | solution.py:470
  71.1 13.0 %collective-permute-start.13 = (f32[8,80,128]{2,1,0:T(8,128)S(1)}, f32[8,80,128]{2,1,0:T(8,128)S(1)}, u32[]{:S(2)}, u32[]{:S(2)}) collective-permute-start(f32[8,80,128]{2,1,0:T(8,128)S(1)} %get-tuple-element.72), channel_id=1, source_target_pairs={{0,120},{8,0},{16,8},{24,16},{32,24},{40,32},{48,40},{56,48},{64,5... | collective-permute-start | bytes 983048 | tf_op jit(solution)/shard_map/ppermute | solution.py:470
  88.7 6.4 %collective-permute-start.15 = (f32[35,16,128]{2,1,0:T(8,128)S(1)}, f32[35,16,128]{2,1,0:T(8,128)S(1)}, u32[]{:S(2)}, u32[]{:S(2)}) collective-permute-start(f32[35,16,128]{2,1,0:T(8,128)S(1)} %get-tuple-element.76), channel_id=1, source_target_pairs={{0,7},{1,0},{2,1},{3,2},{4,3},{5,4},{6,5},{7,6},{8,15},{9,8},{10,9... | collective-permute-start | bytes 860168 | tf_op jit(solution)/shard_map/ppermute | solution.py:470
  89.1 3.4 %collective-permute-start.14 = (f32[35,8,128]{2,1,0:T(8,128)S(1)}, f32[35,8,128]{2,1,0:T(8,128)S(1)}, u32[]{:S(2)}, u32[]{:S(2)}) collective-permute-start(f32[35,8,128]{2,1,0:T(8,128)S(1)} %get-tuple-element.75), channel_id=1, source_target_pairs={{0,1},{1,2},{2,3},{3,4},{4,5},{5,6},{6,7},{7,0},{8,9},{9,10},{10,1... | collective-permute-start | bytes 430088 | tf_op jit(solution)/shard_map/ppermute | solution.py:470
  95.1 12.6 %collective-permute-start.16 = (f32[8,88,128]{2,1,0:T(8,128)S(1)}, f32[8,88,128]{2,1,0:T(8,128)S(1)}, u32[]{:S(2)}, u32[]{:S(2)}) collective-permute-start(f32[8,88,128]{2,1,0:T(8,128)S(1)} %get-tuple-element.84), channel_id=1, source_target_pairs={{0,8},{8,16},{16,24},{24,32},{32,40},{40,48},{48,56},{56,64},{64,7... | collective-permute-start | bytes 1081352 | tf_op jit(solution)/shard_map/ppermute | solution.py:470
  95.2 12.6 %collective-permute-start.17 = (f32[8,88,128]{2,1,0:T(8,128)S(1)}, f32[8,88,128]{2,1,0:T(8,128)S(1)}, u32[]{:S(2)}, u32[]{:S(2)}) collective-permute-start(f32[8,88,128]{2,1,0:T(8,128)S(1)} %get-tuple-element.85), channel_id=1, source_target_pairs={{0,120},{8,0},{16,8},{24,16},{32,24},{40,32},{48,40},{56,48},{64,5... | collective-permute-start | bytes 1081352 | tf_op jit(solution)/shard_map/ppermute | solution.py:470
  107.7 24.7 %copy-start.6 = (s32[128]{0:T(128)S(1)}, s32[128]{0:T(128)}, u32[]{:S(2)}) copy-start(s32[128]{0:T(128)} %brick.1) | copy-start | bytes 1540
  107.7 24.7 %copy-start.7 = (s32[128]{0:T(128)S(1)}, s32[128]{0:T(128)}, u32[]{:S(2)}) copy-start(s32[128]{0:T(128)} %counts.1) | copy-start | bytes 1540
  107.7 24.7 %copy-start.8 = (s32[16]{0:T(128)S(1)}, s32[16]{0:T(128)}, u32[]{:S(2)}) copy-start(s32[16]{0:T(128)} %aper.1) | copy-start | bytes 196

commit v6 on v5

--- a/solution.py
+++ b/solution.py
@@ -20,11 +20,13 @@
 N_GY = 8
 PAN_DEV = 128
 APER_DEV = 16
+MSG = CAP + 1
 READ = 4
 LOW = 8
 HIGH = 11
 TILES = 11
 WY = 8 * TILES
+BY_PRODUCT = 4
 NEAR = 10
 DEPX = BX + BLX - 1
 DEPY = 72
@@ -86,19 +88,27 @@
             out = jnp.where(masks[e], moved, out)
         for h in range(2):
             b = brick[p + h]
-            send[b, 0:4, :] = out[4 * h : 4 * h + 4]
+            send[pl.ds(b * MSG, 4), :] = out[4 * h : 4 * h + 4]
             meta = jnp.zeros((1, 128), jnp.int32)
             for k in range(CAP):
                 meta = jnp.where(lane1 == k, offsets[(p + h) * CAP + k], meta)
             meta = jnp.where(lane1 == CAP, need[p + h], meta)
-            send[b, 4:5, :] = meta.astype(F32)
+            send[pl.ds(b * MSG + 4, 1), :] = meta.astype(F32)
         return c
 
     lax.fori_loop(0, PAN_DEV // 2, body, 0, unroll=4)
 
 
+def numbers(got, turned, meta, sem):
+    rows = got[pl.ds(CAP, PAN_DEV, stride=MSG), :]
+    turned[...] = jnp.transpose(rows)[0:8].astype(jnp.int32)
+    copy = pltpu.make_async_copy(turned, meta, sem)
+    copy.start()
+    return copy
+
+
 def corner(meta, p, k):
-    offset = meta[p, k].astype(jnp.int32)
+    offset = meta[k, p]
     return offset >> 13, (offset >> 7) & 63, offset & 127
 
 
@@ -107,9 +117,8 @@
     return jnp.where((lane >= z) & (lane < z + BLZ), moved, 0.0)
 
 
-def deposit_kernel(got, ion, unused_low, unused_high, out, x_low, x_high, y_low, y_high, meta, sem):
-    copy = pltpu.make_async_copy(got.at[:, 4, :], meta, sem)
-    copy.start()
+def deposit_kernel(got, ion, unused_low, unused_high, out, x_low, x_high, y_low, y_high, turned, meta, sem):
+    copy = numbers(got, turned, meta, sem)
     out[0:BX, 0:BY, :] = ion[...]
     out[0:BX, BY:DEPY, :] = jnp.zeros((BX, DEPY - BY, NZ), F32)
     out[BX:DEPX] = jnp.zeros((DEPX - BX, DEPY, NZ), F32)
@@ -117,7 +126,7 @@
     copy.wait()
 
     def body(p, c):
-        v = got[p, 0:4, :]
+        v = got[pl.ds(p * MSG, CAP), :]
         for k in range(CAP):
             x, y, z = corner(meta, p, k)
             add = [block_rows(v, z, k, i, lane) for i in range(BLX)]
@@ -148,13 +157,14 @@
     nat[at : at + count, LOW + BY : LOW + BY + above.shape[1]] = above
 
 
-def lay_charge(nat, at, count, own, below, above):
+def lay_charge(nat, at, count, own, below, spilled, above):
     spread = jnp.where(lax.axis_index("gy") > 0, 1.0, 0.0)
-    nat[at : at + count, 0:LOW] = below[:, 0:LOW]
+    nat[at : at + count, 0:LOW] = below
     nat[at : at + count, LOW : LOW + DEPY] = own
-    nat[at : at + count, LOW : LOW + 8] += below[:, LOW : LOW + 8] * spread
+    nat[at : at + count, LOW : LOW + BLY - 1] += spilled * spread
     nat[at : at + count, LOW + BY : LOW + DEPY] += above[:, 0:8]
-    nat[at : at + count, LOW + DEPY : WY] = above[:, 8:16]
+    nat[at : at + count, LOW + DEPY : LOW + DEPY + 3] = above[:, 8:HIGH]
+    nat[at : at + count, LOW + DEPY + 3 : WY] = jnp.zeros((count, WY - LOW - DEPY - 3, NZ), F32)
 
 
 def strided(nat, x, t, tiles):
@@ -163,16 +173,32 @@
 
 def relax(layers, write):
     tiles = len(layers[0])
+    rolled = tiles - BY_PRODUCT
     lane = iota((8, 128), 1)
     first, last = lane == 0, lane == NZ - 1
-    for u in range(len(layers) - 2):
+    inner_layers = layers[1:-1]
+    flat = jnp.concatenate(sum([cur[rolled:] for cur in inner_layers], []), axis=0)
+    high = flat.astype(jnp.bfloat16)
+    low = (flat - high.astype(F32)).astype(jnp.bfloat16)
+    from_z, to_z = iota((2 * NZ, NZ), 0) & (NZ - 1), iota((2 * NZ, NZ), 1)
+    beside_z = jnp.where((from_z - to_z == 1) | (to_z - from_z == 1), 1.0, 0.0)
+    product = jnp.dot(
+        jnp.concatenate([high, low], axis=1),
+        beside_z.astype(jnp.bfloat16),
+        preferred_element_type=F32,
+    )
+    for u in range(len(inner_layers)):
         prev, cur, nxt = layers[u : u + 3]
         before = [pltpu.roll(cur[-1], 1, 0)] + cur[:-1]
         after = cur[1:] + [pltpu.roll(cur[0], 7, 0)]
         for t in range(tiles):
-            left = jnp.where(first, 0.0, pltpu.roll(cur[t], 1, 1))
-            right = jnp.where(last, 0.0, pltpu.roll(cur[t], NZ - 1, 1))
-            total = (prev[t] + nxt[t]) + (before[t] + after[t]) + (left + right)
+            if t < rolled:
+                left = jnp.where(first, 0.0, pltpu.roll(cur[t], 1, 1))
+                along_z = left + jnp.where(last, 0.0, pltpu.roll(cur[t], NZ - 1, 1))
+            else:
+                at = (u * BY_PRODUCT + t - rolled) * 8
+                along_z = product[at : at + 8]
+            total = (prev[t] + nxt[t]) + (before[t] + after[t]) + along_z
             write(u, t, total)
 
 
@@ -209,7 +235,7 @@
     tiles = b0.shape[1]
     inside = inside_y(tiles)
     lay(dens, 0, BX, density[...], d_below[...], d_above[...])
-    lay_charge(source, 0, DEPX, charge[...], y_below, y_above)
+    lay_charge(source, 0, DEPX, charge[...], y_below[:, 0:8], y_below[:, 8:HIGH], y_above)
 
     def prep(x, c):
         for t in range(tiles):
@@ -327,8 +353,8 @@
     a, h = BLX - 2, BX + 1
     tiles = NEAR
     inside, (f_low, f_high) = inside_y(tiles), edges()
-    lay_charge(s_low, 0, HIGH, x_below[...], c_below[:, 0:16], c_below[:, 16:32])
-    lay_charge(s_high, 0, HIGH, x_above[...], c_above[:, 0:16], c_above[:, 16:32])
+    for c, s, x in ((c_below, s_low, x_below), (c_above, s_high, x_above)):
+        lay_charge(s, 0, HIGH, x[...], c[:, 0:8], c[:, 19:22], c[:, 8:19])
     s_low[LOW:HIGH] = source[0 : HIGH - LOW] + s_low[LOW:HIGH] * f_low
     s_high[0 : DEPX - BX] += source[BX:DEPX]
 
@@ -384,9 +410,8 @@
 
 
 def flank_last(*refs):
-    (got, out, sums, nat), spare, (meta, sem, named) = refs[13:17], refs[17:25], refs[25:]
-    copy = pltpu.make_async_copy(got.at[:, 4, :], meta, sem)
-    copy.start()
+    (got, out, sums, nat), spare, (turned, meta, sem, named) = refs[13:17], refs[17:25], refs[25:]
+    copy = numbers(got, turned, meta, sem)
     next_flanks(refs[:13], nat, spare)
     out[...] = nat[0:BX, LOW : LOW + BY]
     copy.wait()
@@ -414,14 +439,17 @@
 
 def corner_kernel(below, above, unused_low, unused_high, low, high):
     for at, strip in ((0, low), (BX - LOW, high)):
-        strip[:, 0:16] = below[at : at + HIGH]
-        strip[:, 16:32] = above[at : at + HIGH]
+        strip[:, 0:8] = below[at : at + HIGH, 0:8]
+        strip[:, 8:16] = above[at : at + HIGH, 0:8]
+        strip[:, 16:19] = above[at : at + HIGH, 8:HIGH]
+        strip[:, 19:22] = below[at : at + HIGH, 8:HIGH]
+        strip[:, 22:24] = jnp.zeros((HIGH, 2, NZ), F32)
 
 
 def charge_beside(x_low, x_high, y_low, y_high, first):
     x_below, x_above = ring(x_high, "gx", 1), ring(x_low, "gx", -1)
     y_below, y_above = ring(y_high, "gy", 1), ring(y_low, "gy", -1)
-    low, high = call(corner_kernel, [(HIGH, 32, NZ)] * 2, [VMEM] * 2 + [ANY] * 2)(
+    low, high = call(corner_kernel, [(HIGH, 24, NZ)] * 2, [VMEM] * 2 + [ANY] * 2)(
         y_below, y_above, *first
     )
     c_below, c_above = ring(high, "gx", 1), ring(low, "gx", -1)
@@ -433,7 +461,7 @@
 
     def note(p, n):
         named[n] = p
-        return n + meta[p, CAP].astype(jnp.int32)
+        return n + meta[CAP, p]
 
     count = lax.fori_loop(0, PAN_DEV, note, 0, unroll=8)
     for u in range(READ):
@@ -442,7 +470,7 @@
     def body(j, c):
         for u in range(READ):
             p = named[READ * j + u]
-            v = got[p, 0:4, :]
+            v = got[pl.ds(p * MSG, CAP), :]
             total = jnp.zeros((BLY, 128), F32)
             for k in range(CAP):
                 x, y, z = corner(meta, p, k)
@@ -477,7 +505,7 @@
     ints = [pltpu.SMEM((n,), jnp.int32) for n in (PAN_DEV, PAN_DEV, PAN_DEV * CAP, APER_DEV)]
     (send,) = call(
         pack_kernel,
-        [(PAN_DEV, 8, 128)],
+        [(PAN_DEV * MSG, 128)],
         [ANY] * 5,
         ints
         + [
@@ -487,12 +515,18 @@
         ],
         60,
     )(panel_brick, row_counts, block_offset, aperture_panel, charge_blocks)
+    send = send.reshape(PAN_DEV, 1, MSG * 128)
     got = lax.all_to_all(send, everyone, split_axis=0, concat_axis=0, tiled=True)
+    got = got.reshape(PAN_DEV * MSG, 128)
     dy, dx, d_slabs = beside(
         0, WY, density[:HIGH], density[BX - LOW :], density[:, :16], density[:, BY - LOW :]
     )
 
-    meta = [pltpu.SMEM((PAN_DEV, 128), F32), pltpu.SemaphoreType.DMA]
+    meta = [
+        pltpu.VMEM((8, 128), jnp.int32),
+        pltpu.SMEM((8, 128), jnp.int32),
+        pltpu.SemaphoreType.DMA,
+    ]
     charge, *slabs = call(
         deposit_kernel,
         [(DEPX, DEPY, NZ)] + [(HIGH, DEPY, NZ)] * 2 + [(DEPX, 16, NZ)] * 2,

time: 134 us -> 125 us (0.933)
  waiting for transfers between devices: 31 us -> 21.8 us
  Pallas kernels: 43 us -> 36.6 us
  blocking collectives: 17.9 us -> 21.2 us
  local copies, waits for them, and re-layouts: 0.12 us -> 2.76 us
    ppermute x18, waiting for transfers between devices: 30.9 us -> 16.7 us  [ring(): lax.ppermute(array, axis, [(i, (i + by) % size) for i in range(size)])]
    all_to_all x1, waiting for transfers between devices: 0.01 us -> 5.07 us  [on_device(): lax.all_to_all(send, everyone, split_axis=0, concat_axis=0, tiled=True)]
    all_to_all x1, blocking collectives: 17.9 us -> 21.2 us  [on_device(): lax.all_to_all(sums, everyone, split_axis=0, concat_axis=0, tiled=True)]
    pallas_call x2, Pallas kernels: 12.5 us -> 10.4 us  [on_device(): call(inner_next, [tiles(BX, width)] * 4, [VMEM] * 6, [layers(BX)], 32, work)]
    slice x1, local copies, waits for them, and re-layouts: 0.02 us -> 1.76 us  [on_device(): density[:, :16]]
    ppermute x18, starting transfers between devices: 29.4 us -> 31.1 us  [ring(): lax.ppermute(array, axis, [(i, (i + by) % size) for i in range(size)])]
  transfers between devices with their start and end apart: 19 -> 19, of which waited for: 10 -> 9; matrix products, arithmetic and copies ran while one was open for 0% -> 1% of each run, Pallas kernels for 17% -> 18%
where the time goes in v6:
time: 125 us
  starting transfers between devices  42.1 us (34%)
  Pallas kernels  36.6 us (29%)
  waiting for transfers between devices  21.8 us (17%)
  blocking collectives  21.2 us (17%)
  local copies, waits for them, and re-layouts  2.76 us (2%)
    ppermute x18, starting transfers between devices, ring(): lax.ppermute(array, axis, [(i, (i + by) % size) for i in range(size)])  31.1 us
    all_to_all x1, blocking collectives, on_device(): lax.all_to_all(sums, everyone, split_axis=0, concat_axis=0, tiled=True)  21.2 us
    ppermute x18, waiting for transfers between devices, ring(): lax.ppermute(array, axis, [(i, (i + by) % size) for i in range(size)])  16.7 us
    all_to_all x1, starting transfers between devices, on_device(): lax.all_to_all(send, everyone, split_axis=0, concat_axis=0, tiled=True)  11 us
    pallas_call x2, Pallas kernels, on_device(): call(inner_next, [tiles(BX, width)] * 4, [VMEM] * 6, [layers(BX)], 32, work)  10.4 us
    pallas_call x1, Pallas kernels, on_device(): call(flank_last, [(BX, BY, NZ), (PAN_DEV, 1, 128)], [VMEM] * 14, [layers(...  6.15 us
    all_to_all x1, waiting for transfers between devices, on_device(): lax.all_to_all(send, everyone, split_axis=0, concat_axis=0, tiled=True)  5.07 us
    pallas_call x1, Pallas kernels, on_device(): call(deposit_kernel, [(DEPX, DEPY, NZ)] + [(HIGH, DEPY, NZ)] * 2 + [(DEPX...  4.22 us
  transfers between devices with their start and end apart: 19, of which 9 were waited for; matrix products, arithmetic and copies ran while one was open for 1% of the time, Pallas kernels for 18%

profile of v6, /device:TPU:1, one launch (start us, length us, event | category | flops | bytes accessed | tf_op | source)
XLA Modules:
  0.0 125.3 jit_solution(17175218720874409153)
XLA Ops:
  0.6 0.0 copy-start.1
  0.6 1.8 %slice.15 = f32[32,16,128]{2,1,0:T(8,128)} slice(f32[32,64,128]{2,1,0:T(8,128)} %density.1), slice={[0:32], [0:16], [0:128]} | slice | bytes 524288 | tf_op jit(solution)/shard_map/slice | solution.py:522
  2.4 1.4 %collective-permute-start.1 = (f32[32,16,128]{2,1,0:T(8,128)}, f32[32,16,128]{2,1,0:T(8,128)S(1)}, u32[]{:S(2)}, u32[]{:S(2)}) collective-permute-start(f32[32,16,128]{2,1,0:T(8,128)} %slice.15), channel_id=1, source_target_pairs={{0,7},{1,0},{2,1},{3,2},{4,3},{5,4},{6,5},{7,6},{8,15},{9,8},{10,9... | collective-permute-start | bytes 786440 | tf_op jit(solution)/shard_map/ppermute | solution.py:498
  3.8 0.9 slice.14
  4.7 1.3 %collective-permute-start = (f32[32,8,128]{2,1,0:T(8,128)S(1)}, f32[32,8,128]{2,1,0:T(8,128)S(1)}, u32[]{:S(2)}, u32[]{:S(2)}) collective-permute-start(f32[32,8,128]{2,1,0:T(8,128)S(1)} %slice.14), channel_id=1, source_target_pairs={{0,1},{1,2},{2,3},{3,4},{4,5},{5,6},{6,7},{7,0},{8,9},{9,10},{10,1... | collective-permute-start | bytes 393224 | tf_op jit(solution)/shard_map/ppermute | solution.py:498
  6.0 3.3 %shard_map.86 = f32[640,128]{1,0:T(8,128)} custom-call(s32[128]{0:T(128)} %brick.1, s32[128]{0:T(128)} %counts.1, s32[512]{0:T(512)} %refs_2_.1, s32[16]{0:T(128)} %aper.1, f32[512,128]{1,0:T(8,128)} %refs_4_.1), custom_call_target="tpu_custom_call" | custom-call | tf_op jit(solution)/shard_map/pallas_call | solution.py:506
  9.3 0.0 copy-start
  9.4 11.0 %all-to-all-start = ((f32[128,1,640]{2,1,0:T(1,128)}), f32[128,1,640]{2,1,0:T(1,128)S(1)}, u32[]{:S(2)}, u32[]{:S(2)}) async-start(f32[128,1,640]{2,1,0:T(1,128)} %bitcast.4), calls=%async_computation | async-start | bytes 655360 | tf_op jit(solution)/shard_map/all_to_all | solution.py:519
  20.4 0.0 copy-done.1
  20.5 0.0 collective-permute-done.below.d_below
  20.5 0.0 copy-start.2
  20.5 0.0 collective-permute-done.1.above.d_above
  20.5 1.0 shard_map.87
  21.5 0.0 copy-done.2
  21.5 5.4 %collective-permute-start.7 = (f32[11,88,128]{2,1,0:T(8,128)}, f32[11,88,128]{2,1,0:T(8,128)S(1)}, u32[]{:S(2)}, u32[]{:S(2)}) collective-permute-start(f32[11,88,128]{2,1,0:T(8,128)} %get-tuple-element.45.unused_low), channel_id=1, source_target_pairs={{0,120},{8,0},{16,8},{24,16},{32,24},{40,32},{48,40},{56,48},{64,5... | collective-permute-start | bytes 1486856 | tf_op jit(solution)/shard_map/ppermute | solution.py:498
  26.9 0.0 collective-permute-start.6
  26.9 5.1 %all-to-all-done = f32[128,1,640]{2,1,0:T(1,128)S(1)} async-done(((f32[128,1,640]{2,1,0:T(1,128)}), f32[128,1,640]{2,1,0:T(1,128)S(1)}, u32[]{:S(2)}, u32[]{:S(2)}) %all-to-all-start) | async-done | bytes 327712 | tf_op jit(solution)/shard_map/all_to_all | solution.py:519
  32.0 0.0 copy-done
  32.0 4.2 %shard_map.88 = (f32[35,72,128]{2,1,0:T(8,128)S(1)}, f32[11,72,128]{2,1,0:T(8,128)S(1)}, f32[11,72,128]{2,1,0:T(8,128)S(1)}, f32[35,16,128]{2,1,0:T(8,128)S(1)}, f32[35,16,128]{2,1,0:T(8,128)S(1)}) custom-call(f32[640,128]{1,0:T(8,128)S(1)} %bitcast.2, f32[32,64,128]{2,1,0:T(8,128)S(1)} %copy-done, f32[11,88,128]{2,1,0:T(8,128)} %get-tuple-element.45.unused_low, ...), custom_call_target="tpu_custom_call" | custom-call | tf_op jit(solution)/shard_map/pallas_call | solution.py:530
  36.2 0.9 collective-permute-start.2
  37.1 0.2 collective-permute-start.3
  37.3 0.7 collective-permute-start.4
  38.0 2.7 %collective-permute-done.2.y_below.below = f32[35,16,128]{2,1,0:T(8,128)S(1)} collective-permute-done((f32[35,16,128]{2,1,0:T(8,128)S(1)}, f32[35,16,128]{2,1,0:T(8,128)S(1)}, u32[]{:S(2)}, u32[]{:S(2)}) %collective-permute-start.2) | collective-permute-done | bytes 286752 | tf_op jit(solution)/shard_map/ppermute | solution.py:498
  40.7 1.4 %collective-permute-start.5 = (f32[11,72,128]{2,1,0:T(8,128)S(1)}, f32[11,72,128]{2,1,0:T(8,128)S(1)}, u32[]{:S(2)}, u32[]{:S(2)}) collective-permute-start(f32[11,72,128]{2,1,0:T(8,128)S(1)} %get-tuple-element.57), channel_id=1, source_target_pairs={{0,120},{8,0},{16,8},{24,16},{32,24},{40,32},{48,40},{56,48},{64,5... | collective-permute-start | bytes 1216520 | tf_op jit(solution)/shard_map/ppermute | solution.py:498
  42.1 1.4 %collective-permute-done.3.y_above.above = f32[35,16,128]{2,1,0:T(8,128)S(1)} collective-permute-done((f32[35,16,128]{2,1,0:T(8,128)S(1)}, f32[35,16,128]{2,1,0:T(8,128)S(1)}, u32[]{:S(2)}, u32[]{:S(2)}) %collective-permute-start.3) | collective-permute-done | bytes 286752 | tf_op jit(solution)/shard_map/ppermute | solution.py:498
  43.5 0.0 collective-permute-done.6.unused_low.refs_10_.refs_11_
  43.5 0.0 collective-permute-done.7.unused_high.refs_11_.refs_12_
  43.5 0.2 collective-permute-start.8
  43.7 4.7 %collective-permute-start.9 = (f32[11,24,128]{2,1,0:T(8,128)S(1)}, f32[11,24,128]{2,1,0:T(8,128)S(1)}, u32[]{:S(2)}, u32[]{:S(2)}) collective-permute-start(f32[11,24,128]{2,1,0:T(8,128)S(1)} %get-tuple-element.59), channel_id=1, source_target_pairs={{0,120},{8,0},{16,8},{24,16},{32,24},{40,32},{48,40},{56,48},{64,5... | collective-permute-start | bytes 405512 | tf_op jit(solution)/shard_map/ppermute | solution.py:498
  48.4 0.0 copy-done.3
  48.4 3.1 %shard_map.89 = (f32[32,10,8,128]{3,2,1,0:T(8,128)S(1)}, f32[32,10,8,128]{3,2,1,0:T(8,128)S(1)}, f32[32,10,8,128]{3,2,1,0:T(8,128)S(1)}, f32[32,10,8,128]{3,2,1,...) custom-call(f32[35,72,128]{2,1,0:T(8,128)S(1)} %get-tuple-element.47.charge, ...), custom_call_target="tpu_custom_call" | custom-call | flops 20000000000 | bytes 1048576 | tf_op jit(solution)/shard_map/pallas_call | solution.py:552
  51.5 0.0 collective-permute-done.4.refs_6_
  51.5 0.0 collective-permute-done.5.refs_7_
  51.5 1.1 collective-permute-done.8.refs_8_
  52.6 0.0 collective-permute-done.9.refs_9_
  52.6 3.4 %shard_map.91 = (f32[32,64,128]{2,1,0:T(8,128)S(1)}, f32[3,64,128]{2,1,0:T(8,128)S(1)}, f32[8,64,128]{2,1,0:T(8,128)S(1)}, f32[8,64,128]{2,1,0:T(8,128)S(1)}, f3...) custom-call(f32[32,10,8,128]{3,2,1,0:T(8,128)S(1)} %get-tuple-elemen, ...), custom_call_target="tpu_custom_call" | custom-call | tf_op jit(solution)/shard_map/pallas_call | solution.py:560
  56.0 3.0 %collective-permute-start.10 = (f32[35,8,128]{2,1,0:T(8,128)S(1)}, f32[35,8,128]{2,1,0:T(8,128)S(1)}, u32[]{:S(2)}, u32[]{:S(2)}) collective-permute-start(f32[35,8,128]{2,1,0:T(8,128)S(1)} %get-tuple-element.61), channel_id=1, source_target_pairs={{0,1},{1,2},{2,3},{3,4},{4,5},{5,6},{6,7},{7,0},{8,9},{9,10},{10,1... | collective-permute-start | bytes 430088 | tf_op jit(solution)/shard_map/ppermute | solution.py:498
  59.0 0.0 collective-permute-start.11
  59.0 2.1 %collective-permute-done.10.y_below.below.refs_5_ = f32[35,8,128]{2,1,0:T(8,128)S(1)} collective-permute-done((f32[35,8,128]{2,1,0:T(8,128)S(1)}, f32[35,8,128]{2,1,0:T(8,128)S(1)}, u32[]{:S(2)}, u32[]{:S(2)}) %collective-permute-start.10) | collective-permute-done | bytes 143392 | tf_op jit(solution)/shard_map/ppermute | solution.py:498
  61.0 2.8 %collective-permute-done.11.y_above.above.refs_6_ = f32[35,8,128]{2,1,0:T(8,128)S(1)} collective-permute-done((f32[35,8,128]{2,1,0:T(8,128)S(1)}, f32[35,8,128]{2,1,0:T(8,128)S(1)}, u32[]{:S(2)}, u32[]{:S(2)}) %collective-permute-start.11) | collective-permute-done | bytes 143392 | tf_op jit(solution)/shard_map/ppermute | solution.py:498
  63.8 0.5 collective-permute-start.12
  64.3 4.7 %collective-permute-start.13 = (f32[8,80,128]{2,1,0:T(8,128)S(1)}, f32[8,80,128]{2,1,0:T(8,128)S(1)}, u32[]{:S(2)}, u32[]{:S(2)}) collective-permute-start(f32[8,80,128]{2,1,0:T(8,128)S(1)} %get-tuple-element.72), channel_id=1, source_target_pairs={{0,120},{8,0},{16,8},{24,16},{32,24},{40,32},{48,40},{56,48},{64,5... | collective-permute-start | bytes 983048 | tf_op jit(solution)/shard_map/ppermute | solution.py:498
  69.0 5.0 %shard_map.92 = (f32[32,10,8,128]{3,2,1,0:T(8,128)S(1)}, f32[32,10,8,128]{3,2,1,0:T(8,128)S(1)}, f32[32,10,8,128]{3,2,1,0:T(8,128)S(1)}, f32[32,10,8,128]{3,2,1,0:T(8,128)S(1)}) custom-call(f32[32,64,128]{2,1,0:T(8,128)S(1)} %get-tuple-element.60.own, f32[35,8,128]{2,1,0:T(8,128)S(1)} %collective-permute-done.10.y_below.below.refs_5_, ...), custom_call_target="tpu_custom_call" | custom-call | flops 20000000000 | bytes 1048576 | tf_op jit(solution)/shard_map/pallas_call | solution.py:570
  74.0 2.3 %collective-permute-done.12.refs_7_ = f32[8,80,128]{2,1,0:T(8,128)S(1)} collective-permute-done((f32[8,80,128]{2,1,0:T(8,128)S(1)}, f32[8,80,128]{2,1,0:T(8,128)S(1)}, u32[]{:S(2)}, u32[]{:S(2)}) %collective-permute-start.12) | collective-permute-done | bytes 327712 | tf_op jit(solution)/shard_map/ppermute | solution.py:498
  76.3 0.0 collective-permute-done.13.refs_8_
  76.3 3.7 %shard_map.94 = (f32[32,64,128]{2,1,0:T(8,128)S(1)}, f32[3,64,128]{2,1,0:T(8,128)S(1)}, f32[8,64,128]{2,1,0:T(8,128)S(1)}, f32[8,64,128]{2,1,0:T(8,128)S(1)}, f3...) custom-call(f32[32,10,8,128]{3,2,1,0:T(8,128)S(1)} %get-tuple-element.64.refs_0_, ...), custom_call_target="tpu_custom_call" | custom-call | tf_op jit(solution)/shard_map/pallas_call | solution.py:575
  80.0 1.3 %collective-permute-start.15 = (f32[35,16,128]{2,1,0:T(8,128)S(1)}, f32[35,16,128]{2,1,0:T(8,128)S(1)}, u32[]{:S(2)}, u32[]{:S(2)}) collective-permute-start(f32[35,16,128]{2,1,0:T(8,128)S(1)} %get-tuple-element.76), channel_id=1, source_target_pairs={{0,7},{1,0},{2,1},{3,2},{4,3},{5,4},{6,5},{7,6},{8,15},{9,8},{10,9... | collective-permute-start | bytes 860168 | tf_op jit(solution)/shard_map/ppermute | solution.py:498
  81.3 0.4 collective-permute-start.14
  81.7 2.5 %collective-permute-done.14.y_below.below.refs_5_ = f32[35,8,128]{2,1,0:T(8,128)S(1)} collective-permute-done((f32[35,8,128]{2,1,0:T(8,128)S(1)}, f32[35,8,128]{2,1,0:T(8,128)S(1)}, u32[]{:S(2)}, u32[]{:S(2)}) %collective-permute-start.14) | collective-permute-done | bytes 143392 | tf_op jit(solution)/shard_map/ppermute | solution.py:498
  84.3 1.8 %collective-permute-done.15.y_above.above.refs_6_ = f32[35,16,128]{2,1,0:T(8,128)S(1)} collective-permute-done((f32[35,16,128]{2,1,0:T(8,128)S(1)}, f32[35,16,128]{2,1,0:T(8,128)S(1)}, u32[]{:S(2)}, u32[]{:S(2)}) %collective-permute-start.15) | collective-permute-done | bytes 286752 | tf_op jit(solution)/shard_map/ppermute | solution.py:498
  86.1 0.3 collective-permute-start.16
  86.4 4.8 %collective-permute-start.17 = (f32[8,88,128]{2,1,0:T(8,128)S(1)}, f32[8,88,128]{2,1,0:T(8,128)S(1)}, u32[]{:S(2)}, u32[]{:S(2)}) collective-permute-start(f32[8,88,128]{2,1,0:T(8,128)S(1)} %get-tuple-element.85), channel_id=1, source_target_pairs={{0,120},{8,0},{16,8},{24,16},{32,24},{40,32},{48,40},{56,48},{64,5... | collective-permute-start | bytes 1081352 | tf_op jit(solution)/shard_map/ppermute | solution.py:498
  91.1 5.5 %shard_map.95 = (f32[32,11,8,128]{3,2,1,0:T(8,128)S(1)}, f32[32,11,8,128]{3,2,1,0:T(8,128)S(1)}, f32[32,11,8,128]{3,2,1,0:T(8,128)S(1)}, f32[32,11,8,128]{3,2,1,0:T(8,128)S(1)}) custom-call(f32[32,64,128]{2,1,0:T(8,128)S(1)} %get-tuple-element.74.own, f32[35,8,128]{2,1,0:T(8,128)S(1)} %collective-permute-done.14.y_below.below.refs_5_, ...), custom_call_target="tpu_custom_call" | custom-call | flops 20000000000 | bytes 1048576 | tf_op jit(solution)/shard_map/pallas_call | solution.py:570
  96.6 0.0 collective-permute-done.16.refs_7_
  96.6 0.0 collective-permute-done.17.refs_8_
  96.7 0.0 copy-start.4
  96.7 0.0 copy-start.5
  96.7 0.0 copy-start.6
  96.7 6.2 %shard_map.97 = (f32[32,64,128]{2,1,0:T(8,128)}, f32[128,1,128]{2,1,0:T(1,128)S(1)}) custom-call(f32[32,11,8,128]{3,2,1,0:T(8,128)S(1)} %get-tuple-element.77.refs_0_, f32[32,11,8,128]{3,2,1,0:T(8,128)S(1)} %get-tuple-element.78.refs_1_, f32[32,11,8,128]{3,2,1,0:T(8,128)S(1)} %get-tuple-element.79.refs_2_, f32[32,11,8,128]{3,2,1,0:T(8,128)S(1)} %get-tuple-element.80.refs_3_, ...), custom_call_target="tpu_custom_call" | custom-call | tf_op jit(solution)/shard_map/pallas_call | solution.py:578
  102.8 21.2 %all_to_all.10.got = f32[128,1,128]{2,1,0:T(1,128)S(1)} all-to-all(f32[128,1,128]{2,1,0:T(1,128)S(1)} %get-tuple-element.87), channel_id=1, replica_groups=mesh['gx'=16,'gy'=8] {'gx','gy'}, dimensions={0} | all-to-all | bytes 131072 | tf_op jit(solution)/shard_map/all_to_all | solution.py:585
  124.0 0.0 copy-done.4
  124.0 0.0 copy-done.5
  124.0 0.0 copy-done.6
  124.1 1.2 shard_map.98
  (6 shorter events, 0.2 us)
Async XLA Ops:
  0.6 19.8 %copy-start.1 = (f32[32,64,128]{2,1,0:T(8,128)S(1)}, f32[32,64,128]{2,1,0:T(8,128)}, u32[]{:S(2)}) copy-start(f32[32,64,128]{2,1,0:T(8,128)} %density.1) | copy-start | bytes 3145732
  2.4 18.1 %collective-permute-start.1 = (f32[32,16,128]{2,1,0:T(8,128)}, f32[32,16,128]{2,1,0:T(8,128)S(1)}, u32[]{:S(2)}, u32[]{:S(2)}) collective-permute-start(f32[32,16,128]{2,1,0:T(8,128)} %slice.15), channel_id=1, source_target_pairs={{0,7},{1,0},{2,1},{3,2},{4,3},{5,4},{6,5},{7,6},{8,15},{9,8},{10,9... | collective-permute-start | bytes 786440 | tf_op jit(solution)/shard_map/ppermute | solution.py:498
  4.7 15.7 %collective-permute-start = (f32[32,8,128]{2,1,0:T(8,128)S(1)}, f32[32,8,128]{2,1,0:T(8,128)S(1)}, u32[]{:S(2)}, u32[]{:S(2)}) collective-permute-start(f32[32,8,128]{2,1,0:T(8,128)S(1)} %slice.14), channel_id=1, source_target_pairs={{0,1},{1,2},{2,3},{3,4},{4,5},{5,6},{6,7},{7,0},{8,9},{9,10},{10,1... | collective-permute-start | bytes 393224 | tf_op jit(solution)/shard_map/ppermute | solution.py:498
  9.3 22.6 %copy-start = (f32[32,64,128]{2,1,0:T(8,128)S(1)}, f32[32,64,128]{2,1,0:T(8,128)}, u32[]{:S(2)}) copy-start(f32[32,64,128]{2,1,0:T(8,128)} %ion.1) | copy-start | bytes 3145732
  9.4 22.6 %all-to-all-start = ((f32[128,1,640]{2,1,0:T(1,128)}), f32[128,1,640]{2,1,0:T(1,128)S(1)}, u32[]{:S(2)}, u32[]{:S(2)}) async-start(f32[128,1,640]{2,1,0:T(1,128)} %bitcast.4), calls=%async_computation | async-start | bytes 655360 | tf_op jit(solution)/shard_map/all_to_all | solution.py:519
  20.5 1.0 copy-start.2
  21.5 22.0 %collective-permute-start.7 = (f32[11,88,128]{2,1,0:T(8,128)}, f32[11,88,128]{2,1,0:T(8,128)S(1)}, u32[]{:S(2)}, u32[]{:S(2)}) collective-permute-start(f32[11,88,128]{2,1,0:T(8,128)} %get-tuple-element.45.unused_low), channel_id=1, source_target_pairs={{0,120},{8,0},{16,8},{24,16},{32,24},{40,32},{48,40},{56,48},{64,5... | collective-permute-start | bytes 1486856 | tf_op jit(solution)/shard_map/ppermute | solution.py:498
  26.9 16.6 %collective-permute-start.6 = (f32[8,88,128]{2,1,0:T(8,128)}, f32[8,88,128]{2,1,0:T(8,128)S(1)}, u32[]{:S(2)}, u32[]{:S(2)}) collective-permute-start(f32[8,88,128]{2,1,0:T(8,128)} %get-tuple-element.46.unused_high), channel_id=1, source_target_pairs={{0,8},{8,16},{16,24},{24,32},{32,40},{40,48},{48,56},{56,64},{64,7... | collective-permute-start | bytes 1081352 | tf_op jit(solution)/shard_map/ppermute | solution.py:498
  32.0 16.4 %copy-start.3 = (f32[32,8,128]{2,1,0:T(8,128)S(1)}, f32[32,8,128]{2,1,0:T(8,128)}, u32[]{:S(2)}) copy-start(f32[32,8,128]{2,1,0:T(8,128)} %copy-done.2) | copy-start | bytes 393220
  36.2 4.5 %collective-permute-start.2 = (f32[35,16,128]{2,1,0:T(8,128)S(1)}, f32[35,16,128]{2,1,0:T(8,128)S(1)}, u32[]{:S(2)}, u32[]{:S(2)}) collective-permute-start(f32[35,16,128]{2,1,0:T(8,128)S(1)} %get-tuple-element.48), channel_id=1, source_target_pairs={{0,1},{1,2},{2,3},{3,4},{4,5},{5,6},{6,7},{7,0},{8,9},{9,10},{10,1... | collective-permute-start | bytes 860168 | tf_op jit(solution)/shard_map/ppermute | solution.py:498
  37.1 6.4 %collective-permute-start.3 = (f32[35,16,128]{2,1,0:T(8,128)S(1)}, f32[35,16,128]{2,1,0:T(8,128)S(1)}, u32[]{:S(2)}, u32[]{:S(2)}) collective-permute-start(f32[35,16,128]{2,1,0:T(8,128)S(1)} %get-tuple-element.49), channel_id=1, source_target_pairs={{0,7},{1,0},{2,1},{3,2},{4,3},{5,4},{6,5},{7,6},{8,15},{9,8},{10,9... | collective-permute-start | bytes 860168 | tf_op jit(solution)/shard_map/ppermute | solution.py:498
  37.3 14.2 %collective-permute-start.4 = (f32[11,72,128]{2,1,0:T(8,128)S(1)}, f32[11,72,128]{2,1,0:T(8,128)S(1)}, u32[]{:S(2)}, u32[]{:S(2)}) collective-permute-start(f32[11,72,128]{2,1,0:T(8,128)S(1)} %get-tuple-element.56), channel_id=1, source_target_pairs={{0,8},{8,16},{16,24},{24,32},{32,40},{40,48},{48,56},{56,64},{64,7... | collective-permute-start | bytes 1216520 | tf_op jit(solution)/shard_map/ppermute | solution.py:498
  40.7 10.8 %collective-permute-start.5 = (f32[11,72,128]{2,1,0:T(8,128)S(1)}, f32[11,72,128]{2,1,0:T(8,128)S(1)}, u32[]{:S(2)}, u32[]{:S(2)}) collective-permute-start(f32[11,72,128]{2,1,0:T(8,128)S(1)} %get-tuple-element.57), channel_id=1, source_target_pairs={{0,120},{8,0},{16,8},{24,16},{32,24},{40,32},{48,40},{56,48},{64,5... | collective-permute-start | bytes 1216520 | tf_op jit(solution)/shard_map/ppermute | solution.py:498
  43.5 9.1 %collective-permute-start.8 = (f32[11,24,128]{2,1,0:T(8,128)S(1)}, f32[11,24,128]{2,1,0:T(8,128)S(1)}, u32[]{:S(2)}, u32[]{:S(2)}) collective-permute-start(f32[11,24,128]{2,1,0:T(8,128)S(1)} %get-tuple-element.58), channel_id=1, source_target_pairs={{0,8},{8,16},{16,24},{24,32},{32,40},{40,48},{48,56},{56,64},{64,7... | collective-permute-start | bytes 405512 | tf_op jit(solution)/shard_map/ppermute | solution.py:498
  43.7 8.9 %collective-permute-start.9 = (f32[11,24,128]{2,1,0:T(8,128)S(1)}, f32[11,24,128]{2,1,0:T(8,128)S(1)}, u32[]{:S(2)}, u32[]{:S(2)}) collective-permute-start(f32[11,24,128]{2,1,0:T(8,128)S(1)} %get-tuple-element.59), channel_id=1, source_target_pairs={{0,120},{8,0},{16,8},{24,16},{32,24},{40,32},{48,40},{56,48},{64,5... | collective-permute-start | bytes 405512 | tf_op jit(solution)/shard_map/ppermute | solution.py:498
  56.0 5.1 %collective-permute-start.10 = (f32[35,8,128]{2,1,0:T(8,128)S(1)}, f32[35,8,128]{2,1,0:T(8,128)S(1)}, u32[]{:S(2)}, u32[]{:S(2)}) collective-permute-start(f32[35,8,128]{2,1,0:T(8,128)S(1)} %get-tuple-element.61), channel_id=1, source_target_pairs={{0,1},{1,2},{2,3},{3,4},{4,5},{5,6},{6,7},{7,0},{8,9},{9,10},{10,1... | collective-permute-start | bytes 430088 | tf_op jit(solution)/shard_map/ppermute | solution.py:498
  59.0 4.8 %collective-permute-start.11 = (f32[35,8,128]{2,1,0:T(8,128)S(1)}, f32[35,8,128]{2,1,0:T(8,128)S(1)}, u32[]{:S(2)}, u32[]{:S(2)}) collective-permute-start(f32[35,8,128]{2,1,0:T(8,128)S(1)} %get-tuple-element.62), channel_id=1, source_target_pairs={{0,7},{1,0},{2,1},{3,2},{4,3},{5,4},{6,5},{7,6},{8,15},{9,8},{10,9... | collective-permute-start | bytes 430088 | tf_op jit(solution)/shard_map/ppermute | solution.py:498
  63.8 12.5 %collective-permute-start.12 = (f32[8,80,128]{2,1,0:T(8,128)S(1)}, f32[8,80,128]{2,1,0:T(8,128)S(1)}, u32[]{:S(2)}, u32[]{:S(2)}) collective-permute-start(f32[8,80,128]{2,1,0:T(8,128)S(1)} %get-tuple-element.71), channel_id=1, source_target_pairs={{0,8},{8,16},{16,24},{24,32},{32,40},{40,48},{48,56},{56,64},{64,7... | collective-permute-start | bytes 983048 | tf_op jit(solution)/shard_map/ppermute | solution.py:498
  64.3 12.0 %collective-permute-start.13 = (f32[8,80,128]{2,1,0:T(8,128)S(1)}, f32[8,80,128]{2,1,0:T(8,128)S(1)}, u32[]{:S(2)}, u32[]{:S(2)}) collective-permute-start(f32[8,80,128]{2,1,0:T(8,128)S(1)} %get-tuple-element.72), channel_id=1, source_target_pairs={{0,120},{8,0},{16,8},{24,16},{32,24},{40,32},{48,40},{56,48},{64,5... | collective-permute-start | bytes 983048 | tf_op jit(solution)/shard_map/ppermute | solution.py:498
  80.0 6.1 %collective-permute-start.15 = (f32[35,16,128]{2,1,0:T(8,128)S(1)}, f32[35,16,128]{2,1,0:T(8,128)S(1)}, u32[]{:S(2)}, u32[]{:S(2)}) collective-permute-start(f32[35,16,128]{2,1,0:T(8,128)S(1)} %get-tuple-element.76), channel_id=1, source_target_pairs={{0,7},{1,0},{2,1},{3,2},{4,3},{5,4},{6,5},{7,6},{8,15},{9,8},{10,9... | collective-permute-start | bytes 860168 | tf_op jit(solution)/shard_map/ppermute | solution.py:498
  81.3 3.0 %collective-permute-start.14 = (f32[35,8,128]{2,1,0:T(8,128)S(1)}, f32[35,8,128]{2,1,0:T(8,128)S(1)}, u32[]{:S(2)}, u32[]{:S(2)}) collective-permute-start(f32[35,8,128]{2,1,0:T(8,128)S(1)} %get-tuple-element.75), channel_id=1, source_target_pairs={{0,1},{1,2},{2,3},{3,4},{4,5},{5,6},{6,7},{7,0},{8,9},{9,10},{10,1... | collective-permute-start | bytes 430088 | tf_op jit(solution)/shard_map/ppermute | solution.py:498
  86.1 10.5 %collective-permute-start.16 = (f32[8,88,128]{2,1,0:T(8,128)S(1)}, f32[8,88,128]{2,1,0:T(8,128)S(1)}, u32[]{:S(2)}, u32[]{:S(2)}) collective-permute-start(f32[8,88,128]{2,1,0:T(8,128)S(1)} %get-tuple-element.84), channel_id=1, source_target_pairs={{0,8},{8,16},{16,24},{24,32},{32,40},{40,48},{48,56},{56,64},{64,7... | collective-permute-start | bytes 1081352 | tf_op jit(solution)/shard_map/ppermute | solution.py:498
  86.4 10.3 %collective-permute-start.17 = (f32[8,88,128]{2,1,0:T(8,128)S(1)}, f32[8,88,128]{2,1,0:T(8,128)S(1)}, u32[]{:S(2)}, u32[]{:S(2)}) collective-permute-start(f32[8,88,128]{2,1,0:T(8,128)S(1)} %get-tuple-element.85), channel_id=1, source_target_pairs={{0,120},{8,0},{16,8},{24,16},{32,24},{40,32},{48,40},{56,48},{64,5... | collective-permute-start | bytes 1081352 | tf_op jit(solution)/shard_map/ppermute | solution.py:498
  96.7 27.4 %copy-start.4 = (s32[128]{0:T(128)S(1)}, s32[128]{0:T(128)}, u32[]{:S(2)}) copy-start(s32[128]{0:T(128)} %brick.1) | copy-start | bytes 1540
  96.7 27.4 %copy-start.5 = (s32[128]{0:T(128)S(1)}, s32[128]{0:T(128)}, u32[]{:S(2)}) copy-start(s32[128]{0:T(128)} %counts.1) | copy-start | bytes 1540
  96.7 27.4 %copy-start.6 = (s32[16]{0:T(128)S(1)}, s32[16]{0:T(128)}, u32[]{:S(2)}) copy-start(s32[16]{0:T(128)} %aper.1) | copy-start | bytes 196

commit v7 on v6

--- a/solution.py
+++ b/solution.py
@@ -57,9 +57,14 @@
 
 
 def pack_kernel(*refs):
-    arrays, send, local, need, sems = refs[:5], refs[5], refs[6:11], refs[11], refs[12]
+    arrays, density, (send, y_low, y_high) = refs[:5], refs[5], refs[6:9]
+    local, need, sems = refs[9:14], refs[14], refs[15]
     copies = [pltpu.make_async_copy(a, b, sems.at[i]) for i, (a, b) in enumerate(zip(arrays, local))]
-    for copy in copies:
+    cuts = [
+        pltpu.make_async_copy(density.at[:, 0:16, :], y_low, sems.at[5]),
+        pltpu.make_async_copy(density.at[:, BY - LOW : BY, :], y_high, sems.at[6]),
+    ]
+    for copy in copies + cuts:
         copy.start()
     brick, counts, offsets, aper, rows = local
 
@@ -97,6 +102,8 @@
         return c
 
     lax.fori_loop(0, PAN_DEV // 2, body, 0, unroll=4)
+    for copy in cuts:
+        copy.wait()
 
 
 def numbers(got, turned, meta, sem):
@@ -251,11 +258,11 @@
     inner(b0, b1, rhs, inv, 2, BLX - 2, BX + 1)
 
 
-def start(p_nat, s, s_at, d, inside, f, outs, to, x):
+def start(p_nat, p_at, s, s_at, d, inside, f, outs, to, x):
     p_out, rhs, inv = outs
     tiles = p_out.shape[1]
     for t in range(tiles):
-        p = jnp.where(inside[t], strided(p_nat, x, t, tiles) * f, 0.0)
+        p = jnp.where(inside[t], strided(p_nat, x + p_at, t, tiles) * f, 0.0)
         coef = strided(d, x, t, tiles) * jnp.exp(p)
         p_out[x + to, t] = p
         rhs[x + to, t] = strided(s, x + s_at, t, tiles) + coef * (p - 1.0)
@@ -269,7 +276,7 @@
 
     def prep_from(src, at):
         def prep(x, c):
-            start(nat, src, at, dens, inside, 1.0, outs, 0, x)
+            start(nat, 0, src, at, dens, inside, 1.0, outs, 0, x)
             return c
 
         return prep
@@ -380,20 +387,22 @@
 
 
 def next_flanks(refs, nat, spare):
-    b0, b1, rhs, inv, ahead, y_below, y_above, x_below, x_above, s_low, s_high, d_low, d_high = refs
+    b0, b1, rhs, inv, ahead, y_below, y_above, x_below, x_above, c_below, c_above = refs[:11]
+    s_low, s_high, d_low, d_high = refs[11:]
     l0, l1, l_rhs, l_inv, h0, h1, h_rhs, h_inv = spare
     inside, (f_low, f_high) = inside_y(b0.shape[1]), edges()
 
     def low_body(r, c):
-        start(x_below, s_low, 0, d_low, inside, f_low, (l0, l_rhs, l_inv), 0, r)
+        start(nat, HIGH, s_low, 0, d_low, inside, f_low, (l0, l_rhs, l_inv), 0, r)
         return c
 
     more = HIGH - LOW
     lay(nat, 0, more, ahead[...], y_below[BX:DEPX], y_above[BX:DEPX])
-    nat[more:HIGH, 0 : x_above.shape[1]] = x_above[...]
+    lay(nat, more, LOW, x_above[...], c_above[:, 0:LOW], c_above[:, LOW:])
+    lay(nat, HIGH, LOW, x_below[...], c_below[:, 0:LOW], c_below[:, LOW:])
 
     def high_body(r, c):
-        start(nat, s_high, 0, d_high, inside, f_high, (h0, h_rhs, h_inv), LOW, r)
+        start(nat, 0, s_high, 0, d_high, inside, f_high, (h0, h_rhs, h_inv), LOW, r)
         return c
 
     lax.fori_loop(0, LOW, low_body, 0)
@@ -404,37 +413,38 @@
 
 
 def flank_next(*refs):
-    outs, (nat, *spare) = refs[13:19], refs[19:]
-    next_flanks(refs[:13], nat, spare)
+    outs, (nat, *spare) = refs[15:21], refs[21:]
+    next_flanks(refs[:15], nat, spare)
     hand_on(nat, *outs)
 
 
 def flank_last(*refs):
-    (got, out, sums, nat), spare, (turned, meta, sem, named) = refs[13:17], refs[17:25], refs[25:]
+    (got, out, sums, nat), spare, (turned, meta, sem, named) = refs[15:19], refs[19:27], refs[27:]
     copy = numbers(got, turned, meta, sem)
-    next_flanks(refs[:13], nat, spare)
+    next_flanks(refs[:15], nat, spare)
     out[...] = nat[0:BX, LOW : LOW + BY]
     copy.wait()
     read(got, nat, sums, meta, named)
 
 
-def slab_kernel(at_low, x_low, x_high, below, above, low, high):
-    for own, at, slab in ((x_low, at_low, low), (x_high, BX - LOW, high)):
-        n, width = slab.shape[0], slab.shape[1]
-        slab[:, 0:LOW] = below[at : at + n]
-        slab[:, LOW : LOW + BY] = own[...]
-        slab[:, LOW + BY : width] = above[at : at + n]
-
-
-def beside(at_low, width, x_low, x_high, y_low, y_high):
+def slab_kernel(x_low, x_high, below, above, low, high):
+    lay(low, 0, HIGH, x_low[...], below[0:HIGH], above[0:HIGH])
+    lay(high, 0, LOW, x_high[...], below[BX - LOW :], above[BX - LOW :])
+
+
+def beside(x_low, x_high, y_low, y_high):
     y_below, y_above = ring(y_high, "gy", 1), ring(y_low, "gy", -1)
-    low, high = call(
-        functools.partial(slab_kernel, at_low),
-        [(x_low.shape[0], width, NZ), (x_high.shape[0], width, NZ)],
-        [VMEM] * 4,
-    )(x_low, x_high, y_below, y_above)
+    low, high = call(slab_kernel, [(HIGH, WY, NZ), (LOW, WY, NZ)], [VMEM] * 4)(
+        x_low, x_high, y_below, y_above
+    )
     x_below, x_above = ring(high, "gx", 1), ring(low, "gx", -1)
     return (y_below, y_above), (x_below, x_above), (low, high)
+
+
+def strip_kernel(below, above, low, high):
+    for at, strip in ((HIGH - LOW, low), (BX - LOW, high)):
+        strip[:, 0:LOW] = below[at : at + LOW]
+        strip[:, LOW:] = above[at : at + LOW]
 
 
 def corner_kernel(below, above, unused_low, unused_high, low, high):
@@ -446,12 +456,10 @@
         strip[:, 22:24] = jnp.zeros((HIGH, 2, NZ), F32)
 
 
-def charge_beside(x_low, x_high, y_low, y_high, first):
+def around(x_low, x_high, y_low, y_high, body, strip, first=()):
     x_below, x_above = ring(x_high, "gx", 1), ring(x_low, "gx", -1)
     y_below, y_above = ring(y_high, "gy", 1), ring(y_low, "gy", -1)
-    low, high = call(corner_kernel, [(HIGH, 24, NZ)] * 2, [VMEM] * 2 + [ANY] * 2)(
-        y_below, y_above, *first
-    )
+    low, high = call(body, [strip] * 2, [VMEM] * 2 + [ANY] * len(first))(y_below, y_above, *first)
     c_below, c_above = ring(high, "gx", 1), ring(low, "gx", -1)
     return (y_below, y_above), (x_below, x_above, c_below, c_above)
 
@@ -503,24 +511,22 @@
 ):
     everyone = ("gx", "gy")
     ints = [pltpu.SMEM((n,), jnp.int32) for n in (PAN_DEV, PAN_DEV, PAN_DEV * CAP, APER_DEV)]
-    (send,) = call(
+    send, *d_slabs = call(
         pack_kernel,
-        [(PAN_DEV * MSG, 128)],
-        [ANY] * 5,
+        [(PAN_DEV * MSG, 128), (BX, 16, NZ), (BX, LOW, NZ)],
+        [ANY] * 6,
         ints
         + [
             pltpu.VMEM((PAN_DEV * CAP, 128), F32),
             pltpu.SMEM((PAN_DEV,), jnp.int32),
-            pltpu.SemaphoreType.DMA((5,)),
+            pltpu.SemaphoreType.DMA((7,)),
         ],
         60,
-    )(panel_brick, row_counts, block_offset, aperture_panel, charge_blocks)
+    )(panel_brick, row_counts, block_offset, aperture_panel, charge_blocks, density)
     send = send.reshape(PAN_DEV, 1, MSG * 128)
     got = lax.all_to_all(send, everyone, split_axis=0, concat_axis=0, tiled=True)
     got = got.reshape(PAN_DEV * MSG, 128)
-    dy, dx, d_slabs = beside(
-        0, WY, density[:HIGH], density[BX - LOW :], density[:, :16], density[:, BY - LOW :]
-    )
+    dy, dx, d_slabs = beside(density[:HIGH], density[BX - LOW :], *d_slabs)
 
     meta = [
         pltpu.VMEM((8, 128), jnp.int32),
@@ -548,7 +554,7 @@
         return [pltpu.VMEM(tiles(LOW + LOW + BLX, width), F32)] * 8
 
     work = 20_000_000_000
-    cy, cx = charge_beside(*slabs, first=dx)
+    cy, cx = around(*slabs, corner_kernel, (HIGH, 24, NZ), dx)
     *state, source, dens = call(
         inner_first,
         [tiles(BX, NEAR)] * 4 + [(DEPX, WY, NZ), (BX, WY, NZ)],
@@ -566,19 +572,19 @@
     )(*state, source, dens, *cx, *dx)
     for step in range(1, NEWTON):
         width = NEAR if step < NEWTON - 1 else TILES
-        py, px, _ = beside(HIGH - LOW, 8 * width, *slabs)
+        py, px = around(*slabs, strip_kernel, (LOW, 8 * width - BY, NZ))
         state = call(inner_next, [tiles(BX, width)] * 4, [VMEM] * 6, [layers(BX)], 32, work)(
             pot, *py, source, s_low, dens
         )
         operands = (*state, ahead, *py, *px, s_low, s_high, *dx)
         if step < NEWTON - 1:
             pot, ahead, *slabs = call(
-                flank_next, brick(16), [VMEM] * 13, [layers(DEPX)] + spare(width), 32
+                flank_next, brick(16), [VMEM] * 15, [layers(DEPX)] + spare(width), 32
             )(*operands)
     pot, sums = call(
         flank_last,
         [(BX, BY, NZ), (PAN_DEV, 1, 128)],
-        [VMEM] * 14,
+        [VMEM] * 16,
         [layers(DEPX)] + spare(TILES) + meta + [pltpu.SMEM((PAN_DEV + 8,), jnp.int32)],
         32,
     )(*operands, got)

time: 125 us -> 118 us (0.944)
  starting transfers between devices: 42.1 us -> 53.3 us
  waiting for transfers between devices: 21.8 us -> 10.7 us
  blocking collectives: 21.2 us -> 16.9 us
  local copies, waits for them, and re-layouts: 2.76 us -> 0.08 us
    ppermute x18 -> x22, starting transfers between devices: 31.1 us -> 42.3 us  [ring(): lax.ppermute(array, axis, [(i, (i + by) % size) for i in range(size)])]
    ppermute x18 -> x22, waiting for transfers between devices: 16.7 us -> 5.62 us  [ring(): lax.ppermute(array, axis, [(i, (i + by) % size) for i in range(size)])]
    all_to_all x1, blocking collectives: 21.2 us -> 16.9 us  [on_device(): lax.all_to_all(sums, everyone, split_axis=0, concat_axis=0, tiled=True)]
    slice x4 -> x2, local copies, waits for them, and re-layouts: 2.72 us -> 0.04 us  [on_device(): dy, dx, d_slabs = beside(density[:HIGH], density[BX - LOW:], *d_slabs)]
  transfers between devices with their start and end apart: 19 -> 23, of which waited for: 9 -> 4; matrix products, arithmetic and copies ran while one was open for 1% -> 0% of each run, Pallas kernels for 18% -> 16%
where the time goes in v7:
time: 118 us
  starting transfers between devices  53.3 us (45%)
  Pallas kernels  36.2 us (31%)
  blocking collectives  16.9 us (14%)
  waiting for transfers between devices  10.7 us (9%)
    ppermute x22, starting transfers between devices, ring(): lax.ppermute(array, axis, [(i, (i + by) % size) for i in range(size)])  42.3 us
    all_to_all x1, blocking collectives, on_device(): lax.all_to_all(sums, everyone, split_axis=0, concat_axis=0, tiled=True)  16.9 us
    all_to_all x1, starting transfers between devices, on_device(): lax.all_to_all(send, everyone, split_axis=0, concat_axis=0, tiled=True)  11 us
    pallas_call x2, Pallas kernels, on_device(): call(inner_next, [tiles(BX, width)] * 4, [VMEM] * 6, [layers(BX)], 32, work)  10.4 us
    pallas_call x1, Pallas kernels, on_device(): call(flank_last, [(BX, BY, NZ), (PAN_DEV, 1, 128)], [VMEM] * 16, [layers(...  5.98 us
    ppermute x22, waiting for transfers between devices, ring(): lax.ppermute(array, axis, [(i, (i + by) % size) for i in range(size)])  5.62 us
    all_to_all x1, waiting for transfers between devices, on_device(): lax.all_to_all(send, everyone, split_axis=0, concat_axis=0, tiled=True)  5.07 us
    pallas_call x1, Pallas kernels, on_device(): call(deposit_kernel, [(DEPX, DEPY, NZ)] + [(HIGH, DEPY, NZ)] * 2 + [(DEPX...  4.22 us
  transfers between devices with their start and end apart: 23, of which 4 were waited for; matrix products, arithmetic and copies ran while one was open for 0% of the time, Pallas kernels for 16%

profile of v7, /device:TPU:1, one launch (start us, length us, event | category | flops | bytes accessed | tf_op | source)
XLA Modules:
  0.0 118.1 jit_solution(633281837601760867)
XLA Ops:
  0.6 0.0 copy-start
  0.6 3.5 %shard_map.86 = (f32[640,128]{1,0:T(8,128)}, f32[32,16,128]{2,1,0:T(8,128)}, f32[32,8,128]{2,1,0:T(8,128)}) custom-call(s32[128]{0:T(128)} %brick.1, s32[128]{0:T(128)} %counts.1, s32[512]{0:T(512)} %refs_2_.1, s32[16]{0:T(128)} %aper.1, f32[512,128]{1,0:T(8,128)} %refs_4_.1, f32[32,64,128]{2,1,0:T(8,128)} %density.1), custom_call_target="tpu_custom_call" | custom-call | tf_op jit(solution)/shard_map/pallas_call | solution.py:514
  4.2 1.4 %collective-permute-start.1 = (f32[32,16,128]{2,1,0:T(8,128)}, f32[32,16,128]{2,1,0:T(8,128)S(1)}, u32[]{:S(2)}, u32[]{:S(2)}) collective-permute-start(f32[32,16,128]{2,1,0:T(8,128)} %get-tuple-element.50), channel_id=1, source_target_pairs={{0,7},{1,0},{2,1},{3,2},{4,3},{5,4},{6,5},{7,6},{8,15},{9,8},{10,9... | collective-permute-start | bytes 786440 | tf_op jit(solution)/shard_map/ppermute | solution.py:506
  5.6 1.3 %collective-permute-start = (f32[32,8,128]{2,1,0:T(8,128)}, f32[32,8,128]{2,1,0:T(8,128)S(1)}, u32[]{:S(2)}, u32[]{:S(2)}) collective-permute-start(f32[32,8,128]{2,1,0:T(8,128)} %get-tuple-element.49), channel_id=1, source_target_pairs={{0,1},{1,2},{2,3},{3,4},{4,5},{5,6},{6,7},{7,0},{8,9},{9,10},{10,1... | collective-permute-start | bytes 393224 | tf_op jit(solution)/shard_map/ppermute | solution.py:506
  6.9 11.0 %all-to-all-start = ((f32[128,1,640]{2,1,0:T(1,128)}), f32[128,1,640]{2,1,0:T(1,128)S(1)}, u32[]{:S(2)}, u32[]{:S(2)}) async-start(f32[128,1,640]{2,1,0:T(1,128)} %bitcast.4), calls=%async_computation | async-start | bytes 655360 | tf_op jit(solution)/shard_map/all_to_all | solution.py:527
  17.9 0.0 copy-done
  18.0 0.0 collective-permute-done.below.d_below
  18.0 0.0 collective-permute-done.1.above.d_above
  18.0 1.0 shard_map.87
  19.0 5.4 %collective-permute-start.7 = (f32[11,88,128]{2,1,0:T(8,128)}, f32[11,88,128]{2,1,0:T(8,128)S(1)}, u32[]{:S(2)}, u32[]{:S(2)}) collective-permute-start(f32[11,88,128]{2,1,0:T(8,128)} %get-tuple-element.51.unused_low), channel_id=1, source_target_pairs={{0,120},{8,0},{16,8},{24,16},{32,24},{40,32},{48,40},{56,48},{64,5... | collective-permute-start | bytes 1486856 | tf_op jit(solution)/shard_map/ppermute | solution.py:506
  24.4 0.0 collective-permute-start.6
  24.4 5.1 %all-to-all-done = f32[128,1,640]{2,1,0:T(1,128)S(1)} async-done(((f32[128,1,640]{2,1,0:T(1,128)}), f32[128,1,640]{2,1,0:T(1,128)S(1)}, u32[]{:S(2)}, u32[]{:S(2)}) %all-to-all-start) | async-done | bytes 327712 | tf_op jit(solution)/shard_map/all_to_all | solution.py:527
  29.5 0.0 copy-done.1
  29.5 4.2 %shard_map.88 = (f32[35,72,128]{2,1,0:T(8,128)S(1)}, f32[11,72,128]{2,1,0:T(8,128)S(1)}, f32[11,72,128]{2,1,0:T(8,128)S(1)}, f32[35,16,128]{2,1,0:T(8,128)S(1)}, f32[35,16,128]{2,1,0:T(8,128)S(1)}) custom-call(f32[640,128]{1,0:T(8,128)S(1)} %bitcast.2, f32[32,64,128]{2,1,0:T(8,128)S(1)} %copy-done.1, f32[11,88,128]{2,1,0:T(8,128)} %get-tuple-element.51.unused_low, ...), custom_call_target="tpu_custom_call" | custom-call | tf_op jit(solution)/shard_map/pallas_call | solution.py:536
  33.7 0.9 collective-permute-start.2
  34.6 0.1 collective-permute-start.3
  34.8 0.7 collective-permute-start.4
  35.5 2.8 %collective-permute-done.2.y_below.below = f32[35,16,128]{2,1,0:T(8,128)S(1)} collective-permute-done((f32[35,16,128]{2,1,0:T(8,128)S(1)}, f32[35,16,128]{2,1,0:T(8,128)S(1)}, u32[]{:S(2)}, u32[]{:S(2)}) %collective-permute-start.2) | collective-permute-done | bytes 286752 | tf_op jit(solution)/shard_map/ppermute | solution.py:506
  38.2 1.4 %collective-permute-start.5 = (f32[11,72,128]{2,1,0:T(8,128)S(1)}, f32[11,72,128]{2,1,0:T(8,128)S(1)}, u32[]{:S(2)}, u32[]{:S(2)}) collective-permute-start(f32[11,72,128]{2,1,0:T(8,128)S(1)} %get-tuple-element.63), channel_id=1, source_target_pairs={{0,120},{8,0},{16,8},{24,16},{32,24},{40,32},{48,40},{56,48},{64,5... | collective-permute-start | bytes 1216520 | tf_op jit(solution)/shard_map/ppermute | solution.py:506
  39.6 1.4 %collective-permute-done.3.y_above.above = f32[35,16,128]{2,1,0:T(8,128)S(1)} collective-permute-done((f32[35,16,128]{2,1,0:T(8,128)S(1)}, f32[35,16,128]{2,1,0:T(8,128)S(1)}, u32[]{:S(2)}, u32[]{:S(2)}) %collective-permute-start.3) | collective-permute-done | bytes 286752 | tf_op jit(solution)/shard_map/ppermute | solution.py:506
  41.0 0.0 collective-permute-done.6.unused_low.refs_10_.refs_13_
  41.0 0.0 collective-permute-done.7.unused_high.refs_11_.refs_14_
  41.0 0.2 collective-permute-start.8
  41.2 4.7 %collective-permute-start.9 = (f32[11,24,128]{2,1,0:T(8,128)S(1)}, f32[11,24,128]{2,1,0:T(8,128)S(1)}, u32[]{:S(2)}, u32[]{:S(2)}) collective-permute-start(f32[11,24,128]{2,1,0:T(8,128)S(1)} %get-tuple-element.65), channel_id=1, source_target_pairs={{0,120},{8,0},{16,8},{24,16},{32,24},{40,32},{48,40},{56,48},{64,5... | collective-permute-start | bytes 405512 | tf_op jit(solution)/shard_map/ppermute | solution.py:506
  45.9 0.0 copy-done.3
  45.9 2.8 %shard_map.89 = (f32[32,10,8,128]{3,2,1,0:T(8,128)S(1)}, f32[32,10,8,128]{3,2,1,0:T(8,128)S(1)}, f32[32,10,8,128]{3,2,1,0:T(8,128)S(1)}, f32[32,10,8,128]{3,2,1,...) custom-call(f32[35,72,128]{2,1,0:T(8,128)S(1)} %get-tuple-element.53.charge, ...), custom_call_target="tpu_custom_call" | custom-call | flops 20000000000 | bytes 1048576 | tf_op jit(solution)/shard_map/pallas_call | solution.py:558
  48.7 0.0 collective-permute-done.4.refs_6_
  48.7 0.0 collective-permute-done.5.refs_7_
  48.7 1.4 %collective-permute-done.8.refs_8_ = f32[11,24,128]{2,1,0:T(8,128)S(1)} collective-permute-done((f32[11,24,128]{2,1,0:T(8,128)S(1)}, f32[11,24,128]{2,1,0:T(8,128)S(1)}, u32[]{:S(2)}, u32[]{:S(2)}) %collective-permute-start.8) | collective-permute-done | bytes 135200 | tf_op jit(solution)/shard_map/ppermute | solution.py:506
  50.1 0.0 collective-permute-done.9.refs_9_
  50.1 3.3 %shard_map.91 = (f32[32,64,128]{2,1,0:T(8,128)S(1)}, f32[3,64,128]{2,1,0:T(8,128)S(1)}, f32[8,64,128]{2,1,0:T(8,128)S(1)}, f32[8,64,128]{2,1,0:T(8,128)S(1)}, f3...) custom-call(f32[32,10,8,128]{3,2,1,0:T(8,128)S(1)} %get-tuple-elemen, ...), custom_call_target="tpu_custom_call" | custom-call | tf_op jit(solution)/shard_map/pallas_call | solution.py:566
  53.4 3.0 %collective-permute-start.10 = (f32[35,8,128]{2,1,0:T(8,128)S(1)}, f32[35,8,128]{2,1,0:T(8,128)S(1)}, u32[]{:S(2)}, u32[]{:S(2)}) collective-permute-start(f32[35,8,128]{2,1,0:T(8,128)S(1)} %get-tuple-element.67), channel_id=1, source_target_pairs={{0,1},{1,2},{2,3},{3,4},{4,5},{5,6},{6,7},{7,0},{8,9},{9,10},{10,1... | collective-permute-start | bytes 430088 | tf_op jit(solution)/shard_map/ppermute | solution.py:506
  56.4 0.0 collective-permute-start.11
  56.4 0.6 collective-permute-start.12
  57.1 4.5 %collective-permute-start.13 = (f32[8,64,128]{2,1,0:T(8,128)S(1)}, f32[8,64,128]{2,1,0:T(8,128)S(1)}, u32[]{:S(2)}, u32[]{:S(2)}) collective-permute-start(f32[8,64,128]{2,1,0:T(8,128)S(1)} %get-tuple-element.76), channel_id=1, source_target_pairs={{0,120},{8,0},{16,8},{24,16},{32,24},{40,32},{48,40},{56,48},{64,5... | collective-permute-start | bytes 786440 | tf_op jit(solution)/shard_map/ppermute | solution.py:506
  61.6 0.0 collective-permute-done.10.y_below.below.refs_5_
  61.6 0.0 collective-permute-done.11.y_above.above.refs_6_
  61.6 0.2 collective-permute-start.14
  61.8 4.9 %collective-permute-start.15 = (f32[8,16,128]{2,1,0:T(8,128)S(1)}, f32[8,16,128]{2,1,0:T(8,128)S(1)}, u32[]{:S(2)}, u32[]{:S(2)}) collective-permute-start(f32[8,16,128]{2,1,0:T(8,128)S(1)} %get-tuple-element.78), channel_id=1, source_target_pairs={{0,120},{8,0},{16,8},{24,16},{32,24},{40,32},{48,40},{56,48},{64,5... | collective-permute-start | bytes 196616 | tf_op jit(solution)/shard_map/ppermute | solution.py:506
  66.7 5.0 %shard_map.92 = (f32[32,10,8,128]{3,2,1,0:T(8,128)S(1)}, f32[32,10,8,128]{3,2,1,0:T(8,128)S(1)}, f32[32,10,8,128]{3,2,1,0:T(8,128)S(1)}, f32[32,10,8,128]{3,2,1,0:T(8,128)S(1)}) custom-call(f32[32,64,128]{2,1,0:T(8,128)S(1)} %get-tuple-element.66.own, f32[35,8,128]{2,1,0:T(8,128)S(1)} %collective-permute-done.10.y_below.below.refs_5_, ...), custom_call_target="tpu_custom_call" | custom-call | flops 20000000000 | bytes 1048576 | tf_op jit(solution)/shard_map/pallas_call | solution.py:576
  71.6 0.0 collective-permute-done.14.refs_9_
  71.6 0.0 collective-permute-done.15.refs_10_
  71.6 0.0 collective-permute-done.12.refs_7_
  71.7 0.0 collective-permute-done.13.refs_8_
  71.7 3.7 %shard_map.94 = (f32[32,64,128]{2,1,0:T(8,128)S(1)}, f32[3,64,128]{2,1,0:T(8,128)S(1)}, f32[8,64,128]{2,1,0:T(8,128)S(1)}, f32[8,64,128]{2,1,0:T(8,128)S(1)}, f3...) custom-call(f32[32,10,8,128]{3,2,1,0:T(8,128)S(1)} %get-tuple-element.70.refs_0_, ...), custom_call_target="tpu_custom_call" | custom-call | tf_op jit(solution)/shard_map/pallas_call | solution.py:581
  75.4 3.4 %collective-permute-start.17 = (f32[35,16,128]{2,1,0:T(8,128)S(1)}, f32[35,16,128]{2,1,0:T(8,128)S(1)}, u32[]{:S(2)}, u32[]{:S(2)}) collective-permute-start(f32[35,16,128]{2,1,0:T(8,128)S(1)} %get-tuple-element.82), channel_id=1, source_target_pairs={{0,7},{1,0},{2,1},{3,2},{4,3},{5,4},{6,5},{7,6},{8,15},{9,8},{10,9... | collective-permute-start | bytes 860168 | tf_op jit(solution)/shard_map/ppermute | solution.py:506
  78.7 0.0 collective-permute-start.16
  78.7 0.0 collective-permute-start.18
  78.7 4.8 %collective-permute-start.19 = (f32[8,64,128]{2,1,0:T(8,128)S(1)}, f32[8,64,128]{2,1,0:T(8,128)S(1)}, u32[]{:S(2)}, u32[]{:S(2)}) collective-permute-start(f32[8,64,128]{2,1,0:T(8,128)S(1)} %get-tuple-element.89), channel_id=1, source_target_pairs={{0,120},{8,0},{16,8},{24,16},{32,24},{40,32},{48,40},{56,48},{64,5... | collective-permute-start | bytes 786440 | tf_op jit(solution)/shard_map/ppermute | solution.py:506
  83.5 0.0 collective-permute-done.16.y_below.below.refs_5_
  83.5 0.0 collective-permute-done.17.y_above.above.refs_6_
  83.5 0.1 collective-permute-start.20
  83.6 4.8 %collective-permute-start.21 = (f32[8,24,128]{2,1,0:T(8,128)S(1)}, f32[8,24,128]{2,1,0:T(8,128)S(1)}, u32[]{:S(2)}, u32[]{:S(2)}) collective-permute-start(f32[8,24,128]{2,1,0:T(8,128)S(1)} %get-tuple-element.91), channel_id=1, source_target_pairs={{0,120},{8,0},{16,8},{24,16},{32,24},{40,32},{48,40},{56,48},{64,5... | collective-permute-start | bytes 294920 | tf_op jit(solution)/shard_map/ppermute | solution.py:506
  88.4 5.5 %shard_map.95 = (f32[32,11,8,128]{3,2,1,0:T(8,128)S(1)}, f32[32,11,8,128]{3,2,1,0:T(8,128)S(1)}, f32[32,11,8,128]{3,2,1,0:T(8,128)S(1)}, f32[32,11,8,128]{3,2,1,0:T(8,128)S(1)}) custom-call(f32[32,64,128]{2,1,0:T(8,128)S(1)} %get-tuple-element.80.own, f32[35,8,128]{2,1,0:T(8,128)S(1)} %collective-permute-done.16.y_below.below.refs_5_, ...), custom_call_target="tpu_custom_call" | custom-call | flops 20000000000 | bytes 1048576 | tf_op jit(solution)/shard_map/pallas_call | solution.py:576
  93.9 0.0 collective-permute-done.18.refs_7_
  93.9 0.0 collective-permute-done.19.refs_8_
  93.9 0.0 collective-permute-done.20.refs_9_
  93.9 0.0 collective-permute-done.21.refs_10_
  93.9 0.0 copy-start.4
  93.9 0.0 copy-start.5
  93.9 0.0 copy-start.6
  94.0 6.0 %shard_map.97 = (f32[32,64,128]{2,1,0:T(8,128)}, f32[128,1,128]{2,1,0:T(1,128)S(1)}) custom-call(f32[32,11,8,128]{3,2,1,0:T(8,128)S(1)} %get-tuple-element.83.refs_0_, f32[32,11,8,128]{3,2,1,0:T(8,128)S(1)} %get-tuple-element.84.refs_1_, f32[32,11,8,128]{3,2,1,0:T(8,128)S(1)} %get-tuple-element.85.refs_2_, f32[32,11,8,128]{3,2,1,0:T(8,128)S(1)} %get-tuple-element.86.refs_3_, ...), custom_call_target="tpu_custom_call" | custom-call | tf_op jit(solution)/shard_map/pallas_call | solution.py:584
  99.9 16.9 %all_to_all.10.got = f32[128,1,128]{2,1,0:T(1,128)S(1)} all-to-all(f32[128,1,128]{2,1,0:T(1,128)S(1)} %get-tuple-element.93), channel_id=1, replica_groups=mesh['gx'=16,'gy'=8] {'gx','gy'}, dimensions={0} | all-to-all | bytes 131072 | tf_op jit(solution)/shard_map/all_to_all | solution.py:591
  116.8 1.2 %shard_map.98 = f32[16]{0:T(128)} custom-call(s32[128]{0:T(128)S(1)} %copy-done.4, s32[128]{0:T(128)S(1)} %copy-done.5, s32[16]{0:T(128)S(1)} %copy-done.6, f32[128,1,128]{2,1,0:T(1,128)S(1)} %all_to_all.10.got), custom_call_target="tpu_custom_call" | custom-call | tf_op jit(solution)/shard_map/pallas_call | solution.py:592
  (12 shorter events, 0.1 us)
Async XLA Ops:
  0.6 17.3 %copy-start = (f32[32,64,128]{2,1,0:T(8,128)S(1)}, f32[32,64,128]{2,1,0:T(8,128)}, u32[]{:S(2)}) copy-start(f32[32,64,128]{2,1,0:T(8,128)} %density.1) | copy-start | bytes 3145732
  4.2 13.8 %collective-permute-start.1 = (f32[32,16,128]{2,1,0:T(8,128)}, f32[32,16,128]{2,1,0:T(8,128)S(1)}, u32[]{:S(2)}, u32[]{:S(2)}) collective-permute-start(f32[32,16,128]{2,1,0:T(8,128)} %get-tuple-element.50), channel_id=1, source_target_pairs={{0,7},{1,0},{2,1},{3,2},{4,3},{5,4},{6,5},{7,6},{8,15},{9,8},{10,9... | collective-permute-start | bytes 786440 | tf_op jit(solution)/shard_map/ppermute | solution.py:506
  5.6 12.4 %collective-permute-start = (f32[32,8,128]{2,1,0:T(8,128)}, f32[32,8,128]{2,1,0:T(8,128)S(1)}, u32[]{:S(2)}, u32[]{:S(2)}) collective-permute-start(f32[32,8,128]{2,1,0:T(8,128)} %get-tuple-element.49), channel_id=1, source_target_pairs={{0,1},{1,2},{2,3},{3,4},{4,5},{5,6},{6,7},{7,0},{8,9},{9,10},{10,1... | collective-permute-start | bytes 393224 | tf_op jit(solution)/shard_map/ppermute | solution.py:506
  6.9 22.6 %copy-start.1 = (f32[32,64,128]{2,1,0:T(8,128)S(1)}, f32[32,64,128]{2,1,0:T(8,128)}, u32[]{:S(2)}) copy-start(f32[32,64,128]{2,1,0:T(8,128)} %ion.1) | copy-start | bytes 3145732
  6.9 22.6 %all-to-all-start = ((f32[128,1,640]{2,1,0:T(1,128)}), f32[128,1,640]{2,1,0:T(1,128)S(1)}, u32[]{:S(2)}, u32[]{:S(2)}) async-start(f32[128,1,640]{2,1,0:T(1,128)} %bitcast.4), calls=%async_computation | async-start | bytes 655360 | tf_op jit(solution)/shard_map/all_to_all | solution.py:527
  18.0 1.0 copy-start.2
  19.0 22.0 %collective-permute-start.7 = (f32[11,88,128]{2,1,0:T(8,128)}, f32[11,88,128]{2,1,0:T(8,128)S(1)}, u32[]{:S(2)}, u32[]{:S(2)}) collective-permute-start(f32[11,88,128]{2,1,0:T(8,128)} %get-tuple-element.51.unused_low), channel_id=1, source_target_pairs={{0,120},{8,0},{16,8},{24,16},{32,24},{40,32},{48,40},{56,48},{64,5... | collective-permute-start | bytes 1486856 | tf_op jit(solution)/shard_map/ppermute | solution.py:506
  24.4 16.6 %collective-permute-start.6 = (f32[8,88,128]{2,1,0:T(8,128)}, f32[8,88,128]{2,1,0:T(8,128)S(1)}, u32[]{:S(2)}, u32[]{:S(2)}) collective-permute-start(f32[8,88,128]{2,1,0:T(8,128)} %get-tuple-element.52.unused_high), channel_id=1, source_target_pairs={{0,8},{8,16},{16,24},{24,32},{32,40},{40,48},{48,56},{56,64},{64,7... | collective-permute-start | bytes 1081352 | tf_op jit(solution)/shard_map/ppermute | solution.py:506
  29.5 16.4 %copy-start.3 = (f32[32,8,128]{2,1,0:T(8,128)S(1)}, f32[32,8,128]{2,1,0:T(8,128)}, u32[]{:S(2)}) copy-start(f32[32,8,128]{2,1,0:T(8,128)} %copy-done.2) | copy-start | bytes 393220
  33.7 4.5 %collective-permute-start.2 = (f32[35,16,128]{2,1,0:T(8,128)S(1)}, f32[35,16,128]{2,1,0:T(8,128)S(1)}, u32[]{:S(2)}, u32[]{:S(2)}) collective-permute-start(f32[35,16,128]{2,1,0:T(8,128)S(1)} %get-tuple-element.54), channel_id=1, source_target_pairs={{0,1},{1,2},{2,3},{3,4},{4,5},{5,6},{6,7},{7,0},{8,9},{9,10},{10,1... | collective-permute-start | bytes 860168 | tf_op jit(solution)/shard_map/ppermute | solution.py:506
  34.6 6.4 %collective-permute-start.3 = (f32[35,16,128]{2,1,0:T(8,128)S(1)}, f32[35,16,128]{2,1,0:T(8,128)S(1)}, u32[]{:S(2)}, u32[]{:S(2)}) collective-permute-start(f32[35,16,128]{2,1,0:T(8,128)S(1)} %get-tuple-element.55), channel_id=1, source_target_pairs={{0,7},{1,0},{2,1},{3,2},{4,3},{5,4},{6,5},{7,6},{8,15},{9,8},{10,9... | collective-permute-start | bytes 860168 | tf_op jit(solution)/shard_map/ppermute | solution.py:506
  34.8 13.9 %collective-permute-start.4 = (f32[11,72,128]{2,1,0:T(8,128)S(1)}, f32[11,72,128]{2,1,0:T(8,128)S(1)}, u32[]{:S(2)}, u32[]{:S(2)}) collective-permute-start(f32[11,72,128]{2,1,0:T(8,128)S(1)} %get-tuple-element.62), channel_id=1, source_target_pairs={{0,8},{8,16},{16,24},{24,32},{32,40},{40,48},{48,56},{56,64},{64,7... | collective-permute-start | bytes 1216520 | tf_op jit(solution)/shard_map/ppermute | solution.py:506
  38.2 10.5 %collective-permute-start.5 = (f32[11,72,128]{2,1,0:T(8,128)S(1)}, f32[11,72,128]{2,1,0:T(8,128)S(1)}, u32[]{:S(2)}, u32[]{:S(2)}) collective-permute-start(f32[11,72,128]{2,1,0:T(8,128)S(1)} %get-tuple-element.63), channel_id=1, source_target_pairs={{0,120},{8,0},{16,8},{24,16},{32,24},{40,32},{48,40},{56,48},{64,5... | collective-permute-start | bytes 1216520 | tf_op jit(solution)/shard_map/ppermute | solution.py:506
  41.0 9.1 %collective-permute-start.8 = (f32[11,24,128]{2,1,0:T(8,128)S(1)}, f32[11,24,128]{2,1,0:T(8,128)S(1)}, u32[]{:S(2)}, u32[]{:S(2)}) collective-permute-start(f32[11,24,128]{2,1,0:T(8,128)S(1)} %get-tuple-element.64), channel_id=1, source_target_pairs={{0,8},{8,16},{16,24},{24,32},{32,40},{40,48},{48,56},{56,64},{64,7... | collective-permute-start | bytes 405512 | tf_op jit(solution)/shard_map/ppermute | solution.py:506
  41.2 8.9 %collective-permute-start.9 = (f32[11,24,128]{2,1,0:T(8,128)S(1)}, f32[11,24,128]{2,1,0:T(8,128)S(1)}, u32[]{:S(2)}, u32[]{:S(2)}) collective-permute-start(f32[11,24,128]{2,1,0:T(8,128)S(1)} %get-tuple-element.65), channel_id=1, source_target_pairs={{0,120},{8,0},{16,8},{24,16},{32,24},{40,32},{48,40},{56,48},{64,5... | collective-permute-start | bytes 405512 | tf_op jit(solution)/shard_map/ppermute | solution.py:506
  53.4 8.1 %collective-permute-start.10 = (f32[35,8,128]{2,1,0:T(8,128)S(1)}, f32[35,8,128]{2,1,0:T(8,128)S(1)}, u32[]{:S(2)}, u32[]{:S(2)}) collective-permute-start(f32[35,8,128]{2,1,0:T(8,128)S(1)} %get-tuple-element.67), channel_id=1, source_target_pairs={{0,1},{1,2},{2,3},{3,4},{4,5},{5,6},{6,7},{7,0},{8,9},{9,10},{10,1... | collective-permute-start | bytes 430088 | tf_op jit(solution)/shard_map/ppermute | solution.py:506
  56.4 5.1 %collective-permute-start.11 = (f32[35,8,128]{2,1,0:T(8,128)S(1)}, f32[35,8,128]{2,1,0:T(8,128)S(1)}, u32[]{:S(2)}, u32[]{:S(2)}) collective-permute-start(f32[35,8,128]{2,1,0:T(8,128)S(1)} %get-tuple-element.68), channel_id=1, source_target_pairs={{0,7},{1,0},{2,1},{3,2},{4,3},{5,4},{6,5},{7,6},{8,15},{9,8},{10,9... | collective-permute-start | bytes 430088 | tf_op jit(solution)/shard_map/ppermute | solution.py:506
  56.4 15.2 %collective-permute-start.12 = (f32[8,64,128]{2,1,0:T(8,128)S(1)}, f32[8,64,128]{2,1,0:T(8,128)S(1)}, u32[]{:S(2)}, u32[]{:S(2)}) collective-permute-start(f32[8,64,128]{2,1,0:T(8,128)S(1)} %get-tuple-element.75), channel_id=1, source_target_pairs={{0,8},{8,16},{16,24},{24,32},{32,40},{40,48},{48,56},{56,64},{64,7... | collective-permute-start | bytes 786440 | tf_op jit(solution)/shard_map/ppermute | solution.py:506
  57.1 14.6 %collective-permute-start.13 = (f32[8,64,128]{2,1,0:T(8,128)S(1)}, f32[8,64,128]{2,1,0:T(8,128)S(1)}, u32[]{:S(2)}, u32[]{:S(2)}) collective-permute-start(f32[8,64,128]{2,1,0:T(8,128)S(1)} %get-tuple-element.76), channel_id=1, source_target_pairs={{0,120},{8,0},{16,8},{24,16},{32,24},{40,32},{48,40},{56,48},{64,5... | collective-permute-start | bytes 786440 | tf_op jit(solution)/shard_map/ppermute | solution.py:506
  61.6 10.0 %collective-permute-start.14 = (f32[8,16,128]{2,1,0:T(8,128)S(1)}, f32[8,16,128]{2,1,0:T(8,128)S(1)}, u32[]{:S(2)}, u32[]{:S(2)}) collective-permute-start(f32[8,16,128]{2,1,0:T(8,128)S(1)} %get-tuple-element.77), channel_id=1, source_target_pairs={{0,8},{8,16},{16,24},{24,32},{32,40},{40,48},{48,56},{56,64},{64,7... | collective-permute-start | bytes 196616 | tf_op jit(solution)/shard_map/ppermute | solution.py:506
  61.8 9.9 %collective-permute-start.15 = (f32[8,16,128]{2,1,0:T(8,128)S(1)}, f32[8,16,128]{2,1,0:T(8,128)S(1)}, u32[]{:S(2)}, u32[]{:S(2)}) collective-permute-start(f32[8,16,128]{2,1,0:T(8,128)S(1)} %get-tuple-element.78), channel_id=1, source_target_pairs={{0,120},{8,0},{16,8},{24,16},{32,24},{40,32},{48,40},{56,48},{64,5... | collective-permute-start | bytes 196616 | tf_op jit(solution)/shard_map/ppermute | solution.py:506
  75.4 8.2 %collective-permute-start.17 = (f32[35,16,128]{2,1,0:T(8,128)S(1)}, f32[35,16,128]{2,1,0:T(8,128)S(1)}, u32[]{:S(2)}, u32[]{:S(2)}) collective-permute-start(f32[35,16,128]{2,1,0:T(8,128)S(1)} %get-tuple-element.82), channel_id=1, source_target_pairs={{0,7},{1,0},{2,1},{3,2},{4,3},{5,4},{6,5},{7,6},{8,15},{9,8},{10,9... | collective-permute-start | bytes 860168 | tf_op jit(solution)/shard_map/ppermute | solution.py:506
  78.7 4.8 %collective-permute-start.16 = (f32[35,8,128]{2,1,0:T(8,128)S(1)}, f32[35,8,128]{2,1,0:T(8,128)S(1)}, u32[]{:S(2)}, u32[]{:S(2)}) collective-permute-start(f32[35,8,128]{2,1,0:T(8,128)S(1)} %get-tuple-element.81), channel_id=1, source_target_pairs={{0,1},{1,2},{2,3},{3,4},{4,5},{5,6},{6,7},{7,0},{8,9},{9,10},{10,1... | collective-permute-start | bytes 430088 | tf_op jit(solution)/shard_map/ppermute | solution.py:506
  78.7 15.1 %collective-permute-start.18 = (f32[8,64,128]{2,1,0:T(8,128)S(1)}, f32[8,64,128]{2,1,0:T(8,128)S(1)}, u32[]{:S(2)}, u32[]{:S(2)}) collective-permute-start(f32[8,64,128]{2,1,0:T(8,128)S(1)} %get-tuple-element.88), channel_id=1, source_target_pairs={{0,8},{8,16},{16,24},{24,32},{32,40},{40,48},{48,56},{56,64},{64,7... | collective-permute-start | bytes 786440 | tf_op jit(solution)/shard_map/ppermute | solution.py:506
  78.7 15.2 %collective-permute-start.19 = (f32[8,64,128]{2,1,0:T(8,128)S(1)}, f32[8,64,128]{2,1,0:T(8,128)S(1)}, u32[]{:S(2)}, u32[]{:S(2)}) collective-permute-start(f32[8,64,128]{2,1,0:T(8,128)S(1)} %get-tuple-element.89), channel_id=1, source_target_pairs={{0,120},{8,0},{16,8},{24,16},{32,24},{40,32},{48,40},{56,48},{64,5... | collective-permute-start | bytes 786440 | tf_op jit(solution)/shard_map/ppermute | solution.py:506
  83.5 10.4 %collective-permute-start.20 = (f32[8,24,128]{2,1,0:T(8,128)S(1)}, f32[8,24,128]{2,1,0:T(8,128)S(1)}, u32[]{:S(2)}, u32[]{:S(2)}) collective-permute-start(f32[8,24,128]{2,1,0:T(8,128)S(1)} %get-tuple-element.90), channel_id=1, source_target_pairs={{0,8},{8,16},{16,24},{24,32},{32,40},{40,48},{48,56},{56,64},{64,7... | collective-permute-start | bytes 294920 | tf_op jit(solution)/shard_map/ppermute | solution.py:506
  83.6 10.3 %collective-permute-start.21 = (f32[8,24,128]{2,1,0:T(8,128)S(1)}, f32[8,24,128]{2,1,0:T(8,128)S(1)}, u32[]{:S(2)}, u32[]{:S(2)}) collective-permute-start(f32[8,24,128]{2,1,0:T(8,128)S(1)} %get-tuple-element.91), channel_id=1, source_target_pairs={{0,120},{8,0},{16,8},{24,16},{32,24},{40,32},{48,40},{56,48},{64,5... | collective-permute-start | bytes 294920 | tf_op jit(solution)/shard_map/ppermute | solution.py:506
  93.9 22.9 %copy-start.4 = (s32[128]{0:T(128)S(1)}, s32[128]{0:T(128)}, u32[]{:S(2)}) copy-start(s32[128]{0:T(128)} %brick.1) | copy-start | bytes 1540
  93.9 22.9 %copy-start.5 = (s32[128]{0:T(128)S(1)}, s32[128]{0:T(128)}, u32[]{:S(2)}) copy-start(s32[128]{0:T(128)} %counts.1) | copy-start | bytes 1540
  93.9 22.9 %copy-start.6 = (s32[16]{0:T(128)S(1)}, s32[16]{0:T(128)}, u32[]{:S(2)}) copy-start(s32[16]{0:T(128)} %aper.1) | copy-start | bytes 196

commit v8 on v7

--- a/solution.py
+++ b/solution.py
@@ -25,6 +25,7 @@
 LOW = 8
 HIGH = 11
 TILES = 11
+SRC = HIGH - 1
 WY = 8 * TILES
 BY_PRODUCT = 4
 NEAR = 10
@@ -143,8 +144,8 @@
         return c
 
     lax.fori_loop(0, PAN_DEV, body, 0, unroll=16)
-    x_low[...] = out[0:HIGH]
-    x_high[...] = out[BX - LOW : DEPX]
+    x_low[...] = out[0:SRC]
+    x_high[...] = out[DEPX - SRC : DEPX]
     y_low[...] = out[:, 0:16]
     y_high[...] = out[:, BY - LOW : DEPY]
 
@@ -214,21 +215,10 @@
 
 
 def sweep(src, dst, rhs, inv, lo, hi):
-    def rows(x0, count):
-        def write(u, t, total):
-            dst[x0 + u, t] = (rhs[x0 + u, t] + total) * inv[x0 + u, t]
-
-        relax([layer(src, x0 - 1 + u) for u in range(count + 2)], write)
-
-    count = (hi - lo + 1) // 2
-
-    def body(i, c):
-        rows(lo + i * count, count)
-        return c
-
-    lax.fori_loop(0, (hi - lo) // count, body, 0)
-    if (hi - lo) % count:
-        rows(lo + count, (hi - lo) % count)
+    def write(u, t, total):
+        dst[lo + u, t] = (rhs[lo + u, t] + total) * inv[lo + u, t]
+
+    relax([layer(src, x) for x in range(lo - 1, hi + 1)], write)
 
 
 def inner(b0, b1, rhs, inv, k0, a, h):
@@ -254,7 +244,7 @@
             b1[x, t] = (s - d) * scale
         return c
 
-    lax.fori_loop(0, BX, prep, 0, unroll=2)
+    lax.fori_loop(0, BX, prep, 0, unroll=8)
     inner(b0, b1, rhs, inv, 2, BLX - 2, BX + 1)
 
 
@@ -281,8 +271,8 @@
 
         return prep
 
-    lax.fori_loop(0, BLX - 1, prep_from(s_low, LOW), 0)
-    lax.fori_loop(BLX - 1, BX, prep_from(source, 0), 0)
+    lax.fori_loop(0, BLX - 1, prep_from(s_low, LOW), 0, unroll=BLX - 1)
+    lax.fori_loop(BLX - 1, BX, prep_from(source, 0), 0, unroll=8)
     inner(b0, b1, rhs, inv, 1, 0, BX)
 
 
@@ -334,9 +324,9 @@
 
         return body
 
-    lax.fori_loop(0, a + LOW, take(l0, LOW), 0, unroll=2)
-    lax.fori_loop(a + LOW, h - LOW, take(b0, 0), 0, unroll=2)
-    lax.fori_loop(h - LOW, DEPX, take(h0, LOW - h), 0, unroll=2)
+    lax.fori_loop(0, a + LOW, take(l0, LOW), 0, unroll=8)
+    lax.fori_loop(a + LOW, h - LOW, take(b0, 0), 0, unroll=8)
+    lax.fori_loop(h - LOW, DEPX, take(h0, LOW - h), 0, unroll=11)
 
 
 def hand_on(nat, out, ahead, x_low, x_high, y_low, y_high):
@@ -360,8 +350,10 @@
     a, h = BLX - 2, BX + 1
     tiles = NEAR
     inside, (f_low, f_high) = inside_y(tiles), edges()
-    for c, s, x in ((c_below, s_low, x_below), (c_above, s_high, x_above)):
-        lay_charge(s, 0, HIGH, x[...], c[:, 0:8], c[:, 19:22], c[:, 8:19])
+    s_low[0] = jnp.zeros((WY, NZ), F32)
+    s_high[SRC] = jnp.zeros((WY, NZ), F32)
+    for c, s, x, at in ((c_below, s_low, x_below, 1), (c_above, s_high, x_above, 0)):
+        lay_charge(s, at, SRC, x[...], c[:, 0:8], c[:, 19:22], c[:, 8:19])
     s_low[LOW:HIGH] = source[0 : HIGH - LOW] + s_low[LOW:HIGH] * f_low
     s_high[0 : DEPX - BX] += source[BX:DEPX]
 
@@ -375,7 +367,7 @@
                 p_out[r + at, t] = value * scale
             return c
 
-        lax.fori_loop(0, count, body, 0)
+        lax.fori_loop(0, count, body, 0, unroll=count)
 
     fill(LOW, s_low, 0, d_below, 0, f_low, 0, l1, l_rhs, l_inv)
     fill(BLX - 1, s_low, LOW, dens, 0, 1.0, LOW, l1, l_rhs, l_inv)
@@ -405,8 +397,8 @@
         start(nat, 0, s_high, 0, d_high, inside, f_high, (h0, h_rhs, h_inv), LOW, r)
         return c
 
-    lax.fori_loop(0, LOW, low_body, 0)
-    lax.fori_loop(0, HIGH, high_body, 0)
+    lax.fori_loop(0, LOW, low_body, 0, unroll=LOW)
+    lax.fori_loop(0, HIGH, high_body, 0, unroll=HIGH)
     lows, highs = (l0, l1, l_rhs, l_inv), (h0, h1, h_rhs, h_inv)
     flanks(b0, b1, lows, highs, rhs, inv, 1, 0, BX)
     finish(b0, l0, h0, nat, 0, BX)
@@ -448,12 +440,12 @@
 
 
 def corner_kernel(below, above, unused_low, unused_high, low, high):
-    for at, strip in ((0, low), (BX - LOW, high)):
-        strip[:, 0:8] = below[at : at + HIGH, 0:8]
-        strip[:, 8:16] = above[at : at + HIGH, 0:8]
-        strip[:, 16:19] = above[at : at + HIGH, 8:HIGH]
-        strip[:, 19:22] = below[at : at + HIGH, 8:HIGH]
-        strip[:, 22:24] = jnp.zeros((HIGH, 2, NZ), F32)
+    for at, strip in ((0, low), (DEPX - SRC, high)):
+        strip[:, 0:8] = below[at : at + SRC, 0:8]
+        strip[:, 8:16] = above[at : at + SRC, 0:8]
+        strip[:, 16:19] = above[at : at + SRC, 8:HIGH]
+        strip[:, 19:22] = below[at : at + SRC, 8:HIGH]
+        strip[:, 22:24] = jnp.zeros((SRC, 2, NZ), F32)
 
 
 def around(x_low, x_high, y_low, y_high, body, strip, first=()):
@@ -535,7 +527,7 @@
     ]
     charge, *slabs = call(
         deposit_kernel,
-        [(DEPX, DEPY, NZ)] + [(HIGH, DEPY, NZ)] * 2 + [(DEPX, 16, NZ)] * 2,
+        [(DEPX, DEPY, NZ)] + [(SRC, DEPY, NZ)] * 2 + [(DEPX, 16, NZ)] * 2,
         [VMEM] * 2 + [ANY] * 2,
         meta,
     )(got, ion_charge, *d_slabs)
@@ -554,7 +546,7 @@
         return [pltpu.VMEM(tiles(LOW + LOW + BLX, width), F32)] * 8
 
     work = 20_000_000_000
-    cy, cx = around(*slabs, corner_kernel, (HIGH, 24, NZ), dx)
+    cy, cx = around(*slabs, corner_kernel, (SRC, 24, NZ), dx)
     *state, source, dens = call(
         inner_first,
         [tiles(BX, NEAR)] * 4 + [(DEPX, WY, NZ), (BX, WY, NZ)],

time: 118 us -> 115 us (0.975)
  Pallas kernels: 36.2 us -> 32.5 us
    pallas_call x2, Pallas kernels: 10.4 us -> 7.7 us  [on_device(): call(inner_next, [tiles(BX, width)] * 4, [VMEM] * 6, [layers(BX)], 32, work)]
  transfers between devices with their start and end apart: 23 -> 23, of which waited for: 4 -> 4; matrix products, arithmetic and copies ran while one was open for 0% -> 0% of each run, Pallas kernels for 16% -> 14%
where the time goes in v8:
time: 115 us
  starting transfers between devices  52.8 us (46%)
  Pallas kernels  32.5 us (28%)
  blocking collectives  17.7 us (15%)
  waiting for transfers between devices  10.5 us (9%)
    ppermute x22, starting transfers between devices, ring(): lax.ppermute(array, axis, [(i, (i + by) % size) for i in range(size)])  41.8 us
    all_to_all x1, blocking collectives, on_device(): lax.all_to_all(sums, everyone, split_axis=0, concat_axis=0, tiled=True)  17.7 us
    all_to_all x1, starting transfers between devices, on_device(): lax.all_to_all(send, everyone, split_axis=0, concat_axis=0, tiled=True)  11 us
    pallas_call x2, Pallas kernels, on_device(): call(inner_next, [tiles(BX, width)] * 4, [VMEM] * 6, [layers(BX)], 32, work)  7.7 us
    pallas_call x1, Pallas kernels, on_device(): call(flank_last, [(BX, BY, NZ), (PAN_DEV, 1, 128)], [VMEM] * 16, [layers(...  5.78 us
    ppermute x22, waiting for transfers between devices, ring(): lax.ppermute(array, axis, [(i, (i + by) % size) for i in range(size)])  5.46 us
    all_to_all x1, waiting for transfers between devices, on_device(): lax.all_to_all(send, everyone, split_axis=0, concat_axis=0, tiled=True)  5.07 us
    pallas_call x1, Pallas kernels, on_device(): call(deposit_kernel, [(DEPX, DEPY, NZ)] + [(SRC, DEPY, NZ)] * 2 + [(DEPX,...  4.22 us
  transfers between devices with their start and end apart: 23, of which 4 were waited for; matrix products, arithmetic and copies ran while one was open for 0% of the time, Pallas kernels for 14%

profile of v8, /device:TPU:1, one launch (start us, length us, event | category | flops | bytes accessed | tf_op | source)
XLA Modules:
  0.0 114.5 jit_solution(14412978970527114636)
XLA Ops:
  0.6 0.0 copy-start
  0.6 3.5 %shard_map.86 = (f32[640,128]{1,0:T(8,128)}, f32[32,16,128]{2,1,0:T(8,128)}, f32[32,8,128]{2,1,0:T(8,128)}) custom-call(s32[128]{0:T(128)} %brick.1, s32[128]{0:T(128)} %counts.1, s32[512]{0:T(512)} %refs_2_.1, s32[16]{0:T(128)} %aper.1, f32[512,128]{1,0:T(8,128)} %refs_4_.1, f32[32,64,128]{2,1,0:T(8,128)} %density.1), custom_call_target="tpu_custom_call" | custom-call | tf_op jit(solution)/shard_map/pallas_call | solution.py:506
  4.2 1.4 %collective-permute-start.1 = (f32[32,16,128]{2,1,0:T(8,128)}, f32[32,16,128]{2,1,0:T(8,128)S(1)}, u32[]{:S(2)}, u32[]{:S(2)}) collective-permute-start(f32[32,16,128]{2,1,0:T(8,128)} %get-tuple-element.50), channel_id=1, source_target_pairs={{0,7},{1,0},{2,1},{3,2},{4,3},{5,4},{6,5},{7,6},{8,15},{9,8},{10,9... | collective-permute-start | bytes 786440 | tf_op jit(solution)/shard_map/ppermute | solution.py:498
  5.6 1.3 %collective-permute-start = (f32[32,8,128]{2,1,0:T(8,128)}, f32[32,8,128]{2,1,0:T(8,128)S(1)}, u32[]{:S(2)}, u32[]{:S(2)}) collective-permute-start(f32[32,8,128]{2,1,0:T(8,128)} %get-tuple-element.49), channel_id=1, source_target_pairs={{0,1},{1,2},{2,3},{3,4},{4,5},{5,6},{6,7},{7,0},{8,9},{9,10},{10,1... | collective-permute-start | bytes 393224 | tf_op jit(solution)/shard_map/ppermute | solution.py:498
  6.9 11.0 %all-to-all-start = ((f32[128,1,640]{2,1,0:T(1,128)}), f32[128,1,640]{2,1,0:T(1,128)S(1)}, u32[]{:S(2)}, u32[]{:S(2)}) async-start(f32[128,1,640]{2,1,0:T(1,128)} %bitcast.4), calls=%async_computation | async-start | bytes 655360 | tf_op jit(solution)/shard_map/all_to_all | solution.py:519
  17.9 0.0 copy-done
  18.0 0.0 collective-permute-done.below.d_below
  18.0 0.0 copy-start.2
  18.0 0.0 collective-permute-done.1.above.d_above
  18.0 1.0 shard_map.87
  19.0 5.4 %collective-permute-start.7 = (f32[11,88,128]{2,1,0:T(8,128)}, f32[11,88,128]{2,1,0:T(8,128)S(1)}, u32[]{:S(2)}, u32[]{:S(2)}) collective-permute-start(f32[11,88,128]{2,1,0:T(8,128)} %get-tuple-element.51.unused_low), channel_id=1, source_target_pairs={{0,120},{8,0},{16,8},{24,16},{32,24},{40,32},{48,40},{56,48},{64,5... | collective-permute-start | bytes 1486856 | tf_op jit(solution)/shard_map/ppermute | solution.py:498
  24.4 0.0 collective-permute-start.6
  24.4 5.1 %all-to-all-done = f32[128,1,640]{2,1,0:T(1,128)S(1)} async-done(((f32[128,1,640]{2,1,0:T(1,128)}), f32[128,1,640]{2,1,0:T(1,128)S(1)}, u32[]{:S(2)}, u32[]{:S(2)}) %all-to-all-start) | async-done | bytes 327712 | tf_op jit(solution)/shard_map/all_to_all | solution.py:519
  29.5 0.0 copy-done.1
  29.5 4.2 %shard_map.88 = (f32[35,72,128]{2,1,0:T(8,128)S(1)}, f32[10,72,128]{2,1,0:T(8,128)S(1)}, f32[10,72,128]{2,1,0:T(8,128)S(1)}, f32[35,16,128]{2,1,0:T(8,128)S(1)}, f32[35,16,128]{2,1,0:T(8,128)S(1)}) custom-call(f32[640,128]{1,0:T(8,128)S(1)} %bitcast.2, f32[32,64,128]{2,1,0:T(8,128)S(1)} %copy-done.1, f32[11,88,128]{2,1,0:T(8,128)} %get-tuple-element.51.unused_low, ...), custom_call_target="tpu_custom_call" | custom-call | tf_op jit(solution)/shard_map/pallas_call | solution.py:528
  33.7 0.9 collective-permute-start.2
  34.6 0.2 collective-permute-start.3
  34.8 0.7 collective-permute-start.4
  35.5 2.7 %collective-permute-done.2.y_below.below = f32[35,16,128]{2,1,0:T(8,128)S(1)} collective-permute-done((f32[35,16,128]{2,1,0:T(8,128)S(1)}, f32[35,16,128]{2,1,0:T(8,128)S(1)}, u32[]{:S(2)}, u32[]{:S(2)}) %collective-permute-start.2) | collective-permute-done | bytes 286752 | tf_op jit(solution)/shard_map/ppermute | solution.py:498
  38.2 1.4 %collective-permute-start.5 = (f32[10,72,128]{2,1,0:T(8,128)S(1)}, f32[10,72,128]{2,1,0:T(8,128)S(1)}, u32[]{:S(2)}, u32[]{:S(2)}) collective-permute-start(f32[10,72,128]{2,1,0:T(8,128)S(1)} %get-tuple-element.63), channel_id=1, source_target_pairs={{0,120},{8,0},{16,8},{24,16},{32,24},{40,32},{48,40},{56,48},{64,5... | collective-permute-start | bytes 1105928 | tf_op jit(solution)/shard_map/ppermute | solution.py:498
  39.6 1.4 %collective-permute-done.3.y_above.above = f32[35,16,128]{2,1,0:T(8,128)S(1)} collective-permute-done((f32[35,16,128]{2,1,0:T(8,128)S(1)}, f32[35,16,128]{2,1,0:T(8,128)S(1)}, u32[]{:S(2)}, u32[]{:S(2)}) %collective-permute-start.3) | collective-permute-done | bytes 286752 | tf_op jit(solution)/shard_map/ppermute | solution.py:498
  41.0 0.0 collective-permute-done.6.unused_low.refs_10_.refs_13_
  41.0 0.0 collective-permute-done.7.unused_high.refs_11_.refs_14_
  41.0 0.2 collective-permute-start.8
  41.2 4.7 %collective-permute-start.9 = (f32[10,24,128]{2,1,0:T(8,128)S(1)}, f32[10,24,128]{2,1,0:T(8,128)S(1)}, u32[]{:S(2)}, u32[]{:S(2)}) collective-permute-start(f32[10,24,128]{2,1,0:T(8,128)S(1)} %get-tuple-element.65), channel_id=1, source_target_pairs={{0,120},{8,0},{16,8},{24,16},{32,24},{40,32},{48,40},{56,48},{64,5... | collective-permute-start | bytes 368648 | tf_op jit(solution)/shard_map/ppermute | solution.py:498
  45.9 2.6 %shard_map.89 = (f32[32,10,8,128]{3,2,1,0:T(8,128)S(1)}, f32[32,10,8,128]{3,2,1,0:T(8,128)S(1)}, f32[32,10,8,128]{3,2,1,0:T(8,128)S(1)}, f32[32,10,8,128]{3,2,1,...) custom-call(f32[35,72,128]{2,1,0:T(8,128)S(1)} %get-tuple-element.53.charge, ...), custom_call_target="tpu_custom_call" | custom-call | flops 20000000000 | bytes 1048576 | tf_op jit(solution)/shard_map/pallas_call | solution.py:550
  48.5 0.0 collective-permute-done.4.refs_6_
  48.5 0.0 collective-permute-done.5.refs_7_
  48.5 1.3 %collective-permute-done.8.refs_8_ = f32[10,24,128]{2,1,0:T(8,128)S(1)} collective-permute-done((f32[10,24,128]{2,1,0:T(8,128)S(1)}, f32[10,24,128]{2,1,0:T(8,128)S(1)}, u32[]{:S(2)}, u32[]{:S(2)}) %collective-permute-start.8) | collective-permute-done | bytes 122912 | tf_op jit(solution)/shard_map/ppermute | solution.py:498
  49.8 0.0 collective-permute-done.9.refs_9_
  49.8 3.1 %shard_map.91 = (f32[32,64,128]{2,1,0:T(8,128)S(1)}, f32[3,64,128]{2,1,0:T(8,128)S(1)}, f32[8,64,128]{2,1,0:T(8,128)S(1)}, f32[8,64,128]{2,1,0:T(8,128)S(1)}, f3...) custom-call(f32[32,10,8,128]{3,2,1,0:T(8,128)S(1)} %get-tuple-elemen, ...), custom_call_target="tpu_custom_call" | custom-call | tf_op jit(solution)/shard_map/pallas_call | solution.py:558
  52.9 2.2 %collective-permute-start.10 = (f32[35,8,128]{2,1,0:T(8,128)S(1)}, f32[35,8,128]{2,1,0:T(8,128)S(1)}, u32[]{:S(2)}, u32[]{:S(2)}) collective-permute-start(f32[35,8,128]{2,1,0:T(8,128)S(1)} %get-tuple-element.67), channel_id=1, source_target_pairs={{0,1},{1,2},{2,3},{3,4},{4,5},{5,6},{6,7},{7,0},{8,9},{9,10},{10,1... | collective-permute-start | bytes 430088 | tf_op jit(solution)/shard_map/ppermute | solution.py:498
  55.1 0.1 collective-permute-start.11
  55.2 0.5 collective-permute-start.12
  55.8 4.5 %collective-permute-start.13 = (f32[8,64,128]{2,1,0:T(8,128)S(1)}, f32[8,64,128]{2,1,0:T(8,128)S(1)}, u32[]{:S(2)}, u32[]{:S(2)}) collective-permute-start(f32[8,64,128]{2,1,0:T(8,128)S(1)} %get-tuple-element.76), channel_id=1, source_target_pairs={{0,120},{8,0},{16,8},{24,16},{32,24},{40,32},{48,40},{56,48},{64,5... | collective-permute-start | bytes 786440 | tf_op jit(solution)/shard_map/ppermute | solution.py:498
  60.3 0.0 collective-permute-done.10.y_below.below.refs_5_
  60.3 0.0 collective-permute-done.11.y_above.above.refs_6_
  60.3 0.2 collective-permute-start.14
  60.5 5.0 %collective-permute-start.15 = (f32[8,16,128]{2,1,0:T(8,128)S(1)}, f32[8,16,128]{2,1,0:T(8,128)S(1)}, u32[]{:S(2)}, u32[]{:S(2)}) collective-permute-start(f32[8,16,128]{2,1,0:T(8,128)S(1)} %get-tuple-element.78), channel_id=1, source_target_pairs={{0,120},{8,0},{16,8},{24,16},{32,24},{40,32},{48,40},{56,48},{64,5... | collective-permute-start | bytes 196616 | tf_op jit(solution)/shard_map/ppermute | solution.py:498
  65.4 3.6 %shard_map.92 = (f32[32,10,8,128]{3,2,1,0:T(8,128)S(1)}, f32[32,10,8,128]{3,2,1,0:T(8,128)S(1)}, f32[32,10,8,128]{3,2,1,0:T(8,128)S(1)}, f32[32,10,8,128]{3,2,1,0:T(8,128)S(1)}) custom-call(f32[32,64,128]{2,1,0:T(8,128)S(1)} %get-tuple-element.66.own, f32[35,8,128]{2,1,0:T(8,128)S(1)} %collective-permute-done.10.y_below.below.refs_5_, ...), custom_call_target="tpu_custom_call" | custom-call | flops 20000000000 | bytes 1048576 | tf_op jit(solution)/shard_map/pallas_call | solution.py:568
  69.0 0.0 collective-permute-done.14.refs_9_
  69.0 0.0 collective-permute-done.15.refs_10_
  69.1 0.0 collective-permute-done.12.refs_7_
  69.1 0.0 collective-permute-done.13.refs_8_
  69.1 3.3 %shard_map.94 = (f32[32,64,128]{2,1,0:T(8,128)S(1)}, f32[3,64,128]{2,1,0:T(8,128)S(1)}, f32[8,64,128]{2,1,0:T(8,128)S(1)}, f32[8,64,128]{2,1,0:T(8,128)S(1)}, f3...) custom-call(f32[32,10,8,128]{3,2,1,0:T(8,128)S(1)} %get-tuple-element.70.refs_0_, ...), custom_call_target="tpu_custom_call" | custom-call | tf_op jit(solution)/shard_map/pallas_call | solution.py:573
  72.4 3.5 %collective-permute-start.17 = (f32[35,16,128]{2,1,0:T(8,128)S(1)}, f32[35,16,128]{2,1,0:T(8,128)S(1)}, u32[]{:S(2)}, u32[]{:S(2)}) collective-permute-start(f32[35,16,128]{2,1,0:T(8,128)S(1)} %get-tuple-element.82), channel_id=1, source_target_pairs={{0,7},{1,0},{2,1},{3,2},{4,3},{5,4},{6,5},{7,6},{8,15},{9,8},{10,9... | collective-permute-start | bytes 860168 | tf_op jit(solution)/shard_map/ppermute | solution.py:498
  75.9 0.0 collective-permute-start.16
  75.9 0.0 collective-permute-start.18
  75.9 4.8 %collective-permute-start.19 = (f32[8,64,128]{2,1,0:T(8,128)S(1)}, f32[8,64,128]{2,1,0:T(8,128)S(1)}, u32[]{:S(2)}, u32[]{:S(2)}) collective-permute-start(f32[8,64,128]{2,1,0:T(8,128)S(1)} %get-tuple-element.89), channel_id=1, source_target_pairs={{0,120},{8,0},{16,8},{24,16},{32,24},{40,32},{48,40},{56,48},{64,5... | collective-permute-start | bytes 786440 | tf_op jit(solution)/shard_map/ppermute | solution.py:498
  80.7 0.0 collective-permute-done.16.y_below.below.refs_5_
  80.7 0.0 collective-permute-done.17.y_above.above.refs_6_
  80.7 0.1 collective-permute-start.20
  80.8 4.8 %collective-permute-start.21 = (f32[8,24,128]{2,1,0:T(8,128)S(1)}, f32[8,24,128]{2,1,0:T(8,128)S(1)}, u32[]{:S(2)}, u32[]{:S(2)}) collective-permute-start(f32[8,24,128]{2,1,0:T(8,128)S(1)} %get-tuple-element.91), channel_id=1, source_target_pairs={{0,120},{8,0},{16,8},{24,16},{32,24},{40,32},{48,40},{56,48},{64,5... | collective-permute-start | bytes 294920 | tf_op jit(solution)/shard_map/ppermute | solution.py:498
  85.6 4.1 %shard_map.95 = (f32[32,11,8,128]{3,2,1,0:T(8,128)S(1)}, f32[32,11,8,128]{3,2,1,0:T(8,128)S(1)}, f32[32,11,8,128]{3,2,1,0:T(8,128)S(1)}, f32[32,11,8,128]{3,2,1,0:T(8,128)S(1)}) custom-call(f32[32,64,128]{2,1,0:T(8,128)S(1)} %get-tuple-element.80.own, f32[35,8,128]{2,1,0:T(8,128)S(1)} %collective-permute-done.16.y_below.below.refs_5_, ...), custom_call_target="tpu_custom_call" | custom-call | flops 20000000000 | bytes 1048576 | tf_op jit(solution)/shard_map/pallas_call | solution.py:568
  89.7 0.0 collective-permute-done.18.refs_7_
  89.7 0.0 collective-permute-done.19.refs_8_
  89.7 0.0 collective-permute-done.20.refs_9_
  89.7 0.0 collective-permute-done.21.refs_10_
  89.7 0.0 copy-start.4
  89.8 0.0 copy-start.5
  89.8 0.0 copy-start.6
  89.8 5.8 %shard_map.97 = (f32[32,64,128]{2,1,0:T(8,128)}, f32[128,1,128]{2,1,0:T(1,128)S(1)}) custom-call(f32[32,11,8,128]{3,2,1,0:T(8,128)S(1)} %get-tuple-element.83.refs_0_, f32[32,11,8,128]{3,2,1,0:T(8,128)S(1)} %get-tuple-element.84.refs_1_, f32[32,11,8,128]{3,2,1,0:T(8,128)S(1)} %get-tuple-element.85.refs_2_, f32[32,11,8,128]{3,2,1,0:T(8,128)S(1)} %get-tuple-element.86.refs_3_, ...), custom_call_target="tpu_custom_call" | custom-call | tf_op jit(solution)/shard_map/pallas_call | solution.py:576
  95.6 17.7 %all_to_all.10.got = f32[128,1,128]{2,1,0:T(1,128)S(1)} all-to-all(f32[128,1,128]{2,1,0:T(1,128)S(1)} %get-tuple-element.93), channel_id=1, replica_groups=mesh['gx'=16,'gy'=8] {'gx','gy'}, dimensions={0} | all-to-all | bytes 131072 | tf_op jit(solution)/shard_map/all_to_all | solution.py:583
  113.3 1.2 %shard_map.98 = f32[16]{0:T(128)} custom-call(s32[128]{0:T(128)S(1)} %copy-done.4, s32[128]{0:T(128)S(1)} %copy-done.5, s32[16]{0:T(128)S(1)} %copy-done.6, f32[128,1,128]{2,1,0:T(1,128)S(1)} %all_to_all.10.got), custom_call_target="tpu_custom_call" | custom-call | tf_op jit(solution)/shard_map/pallas_call | solution.py:584
  (12 shorter events, 0.1 us)
Async XLA Ops:
  0.6 17.3 %copy-start = (f32[32,64,128]{2,1,0:T(8,128)S(1)}, f32[32,64,128]{2,1,0:T(8,128)}, u32[]{:S(2)}) copy-start(f32[32,64,128]{2,1,0:T(8,128)} %density.1) | copy-start | bytes 3145732
  4.2 13.8 %collective-permute-start.1 = (f32[32,16,128]{2,1,0:T(8,128)}, f32[32,16,128]{2,1,0:T(8,128)S(1)}, u32[]{:S(2)}, u32[]{:S(2)}) collective-permute-start(f32[32,16,128]{2,1,0:T(8,128)} %get-tuple-element.50), channel_id=1, source_target_pairs={{0,7},{1,0},{2,1},{3,2},{4,3},{5,4},{6,5},{7,6},{8,15},{9,8},{10,9... | collective-permute-start | bytes 786440 | tf_op jit(solution)/shard_map/ppermute | solution.py:498
  5.6 12.4 %collective-permute-start = (f32[32,8,128]{2,1,0:T(8,128)}, f32[32,8,128]{2,1,0:T(8,128)S(1)}, u32[]{:S(2)}, u32[]{:S(2)}) collective-permute-start(f32[32,8,128]{2,1,0:T(8,128)} %get-tuple-element.49), channel_id=1, source_target_pairs={{0,1},{1,2},{2,3},{3,4},{4,5},{5,6},{6,7},{7,0},{8,9},{9,10},{10,1... | collective-permute-start | bytes 393224 | tf_op jit(solution)/shard_map/ppermute | solution.py:498
  6.9 22.6 %copy-start.1 = (f32[32,64,128]{2,1,0:T(8,128)S(1)}, f32[32,64,128]{2,1,0:T(8,128)}, u32[]{:S(2)}) copy-start(f32[32,64,128]{2,1,0:T(8,128)} %ion.1) | copy-start | bytes 3145732
  6.9 22.6 %all-to-all-start = ((f32[128,1,640]{2,1,0:T(1,128)}), f32[128,1,640]{2,1,0:T(1,128)S(1)}, u32[]{:S(2)}, u32[]{:S(2)}) async-start(f32[128,1,640]{2,1,0:T(1,128)} %bitcast.4), calls=%async_computation | async-start | bytes 655360 | tf_op jit(solution)/shard_map/all_to_all | solution.py:519
  18.0 1.0 copy-start.2
  19.0 22.0 %collective-permute-start.7 = (f32[11,88,128]{2,1,0:T(8,128)}, f32[11,88,128]{2,1,0:T(8,128)S(1)}, u32[]{:S(2)}, u32[]{:S(2)}) collective-permute-start(f32[11,88,128]{2,1,0:T(8,128)} %get-tuple-element.51.unused_low), channel_id=1, source_target_pairs={{0,120},{8,0},{16,8},{24,16},{32,24},{40,32},{48,40},{56,48},{64,5... | collective-permute-start | bytes 1486856 | tf_op jit(solution)/shard_map/ppermute | solution.py:498
  24.4 16.6 %collective-permute-start.6 = (f32[8,88,128]{2,1,0:T(8,128)}, f32[8,88,128]{2,1,0:T(8,128)S(1)}, u32[]{:S(2)}, u32[]{:S(2)}) collective-permute-start(f32[8,88,128]{2,1,0:T(8,128)} %get-tuple-element.52.unused_high), channel_id=1, source_target_pairs={{0,8},{8,16},{16,24},{24,32},{32,40},{40,48},{48,56},{56,64},{64,7... | collective-permute-start | bytes 1081352 | tf_op jit(solution)/shard_map/ppermute | solution.py:498
  29.5 16.4 %copy-start.3 = (f32[32,8,128]{2,1,0:T(8,128)S(1)}, f32[32,8,128]{2,1,0:T(8,128)}, u32[]{:S(2)}) copy-start(f32[32,8,128]{2,1,0:T(8,128)} %copy-done.2) | copy-start | bytes 393220
  33.7 4.5 %collective-permute-start.2 = (f32[35,16,128]{2,1,0:T(8,128)S(1)}, f32[35,16,128]{2,1,0:T(8,128)S(1)}, u32[]{:S(2)}, u32[]{:S(2)}) collective-permute-start(f32[35,16,128]{2,1,0:T(8,128)S(1)} %get-tuple-element.54), channel_id=1, source_target_pairs={{0,1},{1,2},{2,3},{3,4},{4,5},{5,6},{6,7},{7,0},{8,9},{9,10},{10,1... | collective-permute-start | bytes 860168 | tf_op jit(solution)/shard_map/ppermute | solution.py:498
  34.6 6.4 %collective-permute-start.3 = (f32[35,16,128]{2,1,0:T(8,128)S(1)}, f32[35,16,128]{2,1,0:T(8,128)S(1)}, u32[]{:S(2)}, u32[]{:S(2)}) collective-permute-start(f32[35,16,128]{2,1,0:T(8,128)S(1)} %get-tuple-element.55), channel_id=1, source_target_pairs={{0,7},{1,0},{2,1},{3,2},{4,3},{5,4},{6,5},{7,6},{8,15},{9,8},{10,9... | collective-permute-start | bytes 860168 | tf_op jit(solution)/shard_map/ppermute | solution.py:498
  34.8 13.7 %collective-permute-start.4 = (f32[10,72,128]{2,1,0:T(8,128)S(1)}, f32[10,72,128]{2,1,0:T(8,128)S(1)}, u32[]{:S(2)}, u32[]{:S(2)}) collective-permute-start(f32[10,72,128]{2,1,0:T(8,128)S(1)} %get-tuple-element.62), channel_id=1, source_target_pairs={{0,8},{8,16},{16,24},{24,32},{32,40},{40,48},{48,56},{56,64},{64,7... | collective-permute-start | bytes 1105928 | tf_op jit(solution)/shard_map/ppermute | solution.py:498
  38.2 10.3 %collective-permute-start.5 = (f32[10,72,128]{2,1,0:T(8,128)S(1)}, f32[10,72,128]{2,1,0:T(8,128)S(1)}, u32[]{:S(2)}, u32[]{:S(2)}) collective-permute-start(f32[10,72,128]{2,1,0:T(8,128)S(1)} %get-tuple-element.63), channel_id=1, source_target_pairs={{0,120},{8,0},{16,8},{24,16},{32,24},{40,32},{48,40},{56,48},{64,5... | collective-permute-start | bytes 1105928 | tf_op jit(solution)/shard_map/ppermute | solution.py:498
  41.0 8.8 %collective-permute-start.8 = (f32[10,24,128]{2,1,0:T(8,128)S(1)}, f32[10,24,128]{2,1,0:T(8,128)S(1)}, u32[]{:S(2)}, u32[]{:S(2)}) collective-permute-start(f32[10,24,128]{2,1,0:T(8,128)S(1)} %get-tuple-element.64), channel_id=1, source_target_pairs={{0,8},{8,16},{16,24},{24,32},{32,40},{40,48},{48,56},{56,64},{64,7... | collective-permute-start | bytes 368648 | tf_op jit(solution)/shard_map/ppermute | solution.py:498
  41.2 8.6 %collective-permute-start.9 = (f32[10,24,128]{2,1,0:T(8,128)S(1)}, f32[10,24,128]{2,1,0:T(8,128)S(1)}, u32[]{:S(2)}, u32[]{:S(2)}) collective-permute-start(f32[10,24,128]{2,1,0:T(8,128)S(1)} %get-tuple-element.65), channel_id=1, source_target_pairs={{0,120},{8,0},{16,8},{24,16},{32,24},{40,32},{48,40},{56,48},{64,5... | collective-permute-start | bytes 368648 | tf_op jit(solution)/shard_map/ppermute | solution.py:498
  52.9 7.4 %collective-permute-start.10 = (f32[35,8,128]{2,1,0:T(8,128)S(1)}, f32[35,8,128]{2,1,0:T(8,128)S(1)}, u32[]{:S(2)}, u32[]{:S(2)}) collective-permute-start(f32[35,8,128]{2,1,0:T(8,128)S(1)} %get-tuple-element.67), channel_id=1, source_target_pairs={{0,1},{1,2},{2,3},{3,4},{4,5},{5,6},{6,7},{7,0},{8,9},{9,10},{10,1... | collective-permute-start | bytes 430088 | tf_op jit(solution)/shard_map/ppermute | solution.py:498
  55.1 5.2 %collective-permute-start.11 = (f32[35,8,128]{2,1,0:T(8,128)S(1)}, f32[35,8,128]{2,1,0:T(8,128)S(1)}, u32[]{:S(2)}, u32[]{:S(2)}) collective-permute-start(f32[35,8,128]{2,1,0:T(8,128)S(1)} %get-tuple-element.68), channel_id=1, source_target_pairs={{0,7},{1,0},{2,1},{3,2},{4,3},{5,4},{6,5},{7,6},{8,15},{9,8},{10,9... | collective-permute-start | bytes 430088 | tf_op jit(solution)/shard_map/ppermute | solution.py:498
  55.2 13.8 %collective-permute-start.12 = (f32[8,64,128]{2,1,0:T(8,128)S(1)}, f32[8,64,128]{2,1,0:T(8,128)S(1)}, u32[]{:S(2)}, u32[]{:S(2)}) collective-permute-start(f32[8,64,128]{2,1,0:T(8,128)S(1)} %get-tuple-element.75), channel_id=1, source_target_pairs={{0,8},{8,16},{16,24},{24,32},{32,40},{40,48},{48,56},{56,64},{64,7... | collective-permute-start | bytes 786440 | tf_op jit(solution)/shard_map/ppermute | solution.py:498
  55.8 13.3 %collective-permute-start.13 = (f32[8,64,128]{2,1,0:T(8,128)S(1)}, f32[8,64,128]{2,1,0:T(8,128)S(1)}, u32[]{:S(2)}, u32[]{:S(2)}) collective-permute-start(f32[8,64,128]{2,1,0:T(8,128)S(1)} %get-tuple-element.76), channel_id=1, source_target_pairs={{0,120},{8,0},{16,8},{24,16},{32,24},{40,32},{48,40},{56,48},{64,5... | collective-permute-start | bytes 786440 | tf_op jit(solution)/shard_map/ppermute | solution.py:498
  60.3 8.7 %collective-permute-start.14 = (f32[8,16,128]{2,1,0:T(8,128)S(1)}, f32[8,16,128]{2,1,0:T(8,128)S(1)}, u32[]{:S(2)}, u32[]{:S(2)}) collective-permute-start(f32[8,16,128]{2,1,0:T(8,128)S(1)} %get-tuple-element.77), channel_id=1, source_target_pairs={{0,8},{8,16},{16,24},{24,32},{32,40},{40,48},{48,56},{56,64},{64,7... | collective-permute-start | bytes 196616 | tf_op jit(solution)/shard_map/ppermute | solution.py:498
  60.5 8.6 %collective-permute-start.15 = (f32[8,16,128]{2,1,0:T(8,128)S(1)}, f32[8,16,128]{2,1,0:T(8,128)S(1)}, u32[]{:S(2)}, u32[]{:S(2)}) collective-permute-start(f32[8,16,128]{2,1,0:T(8,128)S(1)} %get-tuple-element.78), channel_id=1, source_target_pairs={{0,120},{8,0},{16,8},{24,16},{32,24},{40,32},{48,40},{56,48},{64,5... | collective-permute-start | bytes 196616 | tf_op jit(solution)/shard_map/ppermute | solution.py:498
  72.4 8.3 %collective-permute-start.17 = (f32[35,16,128]{2,1,0:T(8,128)S(1)}, f32[35,16,128]{2,1,0:T(8,128)S(1)}, u32[]{:S(2)}, u32[]{:S(2)}) collective-permute-start(f32[35,16,128]{2,1,0:T(8,128)S(1)} %get-tuple-element.82), channel_id=1, source_target_pairs={{0,7},{1,0},{2,1},{3,2},{4,3},{5,4},{6,5},{7,6},{8,15},{9,8},{10,9... | collective-permute-start | bytes 860168 | tf_op jit(solution)/shard_map/ppermute | solution.py:498
  75.9 4.8 %collective-permute-start.16 = (f32[35,8,128]{2,1,0:T(8,128)S(1)}, f32[35,8,128]{2,1,0:T(8,128)S(1)}, u32[]{:S(2)}, u32[]{:S(2)}) collective-permute-start(f32[35,8,128]{2,1,0:T(8,128)S(1)} %get-tuple-element.81), channel_id=1, source_target_pairs={{0,1},{1,2},{2,3},{3,4},{4,5},{5,6},{6,7},{7,0},{8,9},{9,10},{10,1... | collective-permute-start | bytes 430088 | tf_op jit(solution)/shard_map/ppermute | solution.py:498
  75.9 13.8 %collective-permute-start.18 = (f32[8,64,128]{2,1,0:T(8,128)S(1)}, f32[8,64,128]{2,1,0:T(8,128)S(1)}, u32[]{:S(2)}, u32[]{:S(2)}) collective-permute-start(f32[8,64,128]{2,1,0:T(8,128)S(1)} %get-tuple-element.88), channel_id=1, source_target_pairs={{0,8},{8,16},{16,24},{24,32},{32,40},{40,48},{48,56},{56,64},{64,7... | collective-permute-start | bytes 786440 | tf_op jit(solution)/shard_map/ppermute | solution.py:498
  75.9 13.8 %collective-permute-start.19 = (f32[8,64,128]{2,1,0:T(8,128)S(1)}, f32[8,64,128]{2,1,0:T(8,128)S(1)}, u32[]{:S(2)}, u32[]{:S(2)}) collective-permute-start(f32[8,64,128]{2,1,0:T(8,128)S(1)} %get-tuple-element.89), channel_id=1, source_target_pairs={{0,120},{8,0},{16,8},{24,16},{32,24},{40,32},{48,40},{56,48},{64,5... | collective-permute-start | bytes 786440 | tf_op jit(solution)/shard_map/ppermute | solution.py:498
  80.7 9.0 %collective-permute-start.20 = (f32[8,24,128]{2,1,0:T(8,128)S(1)}, f32[8,24,128]{2,1,0:T(8,128)S(1)}, u32[]{:S(2)}, u32[]{:S(2)}) collective-permute-start(f32[8,24,128]{2,1,0:T(8,128)S(1)} %get-tuple-element.90), channel_id=1, source_target_pairs={{0,8},{8,16},{16,24},{24,32},{32,40},{40,48},{48,56},{56,64},{64,7... | collective-permute-start | bytes 294920 | tf_op jit(solution)/shard_map/ppermute | solution.py:498
  80.8 8.9 %collective-permute-start.21 = (f32[8,24,128]{2,1,0:T(8,128)S(1)}, f32[8,24,128]{2,1,0:T(8,128)S(1)}, u32[]{:S(2)}, u32[]{:S(2)}) collective-permute-start(f32[8,24,128]{2,1,0:T(8,128)S(1)} %get-tuple-element.91), channel_id=1, source_target_pairs={{0,120},{8,0},{16,8},{24,16},{32,24},{40,32},{48,40},{56,48},{64,5... | collective-permute-start | bytes 294920 | tf_op jit(solution)/shard_map/ppermute | solution.py:498
  89.7 23.5 %copy-start.4 = (s32[128]{0:T(128)S(1)}, s32[128]{0:T(128)}, u32[]{:S(2)}) copy-start(s32[128]{0:T(128)} %brick.1) | copy-start | bytes 1540
  89.8 23.5 %copy-start.5 = (s32[128]{0:T(128)S(1)}, s32[128]{0:T(128)}, u32[]{:S(2)}) copy-start(s32[128]{0:T(128)} %counts.1) | copy-start | bytes 1540
  89.8 23.5 %copy-start.6 = (s32[16]{0:T(128)S(1)}, s32[16]{0:T(128)}, u32[]{:S(2)}) copy-start(s32[16]{0:T(128)} %aper.1) | copy-start | bytes 196

commit v9 on v8

--- a/solution.py
+++ b/solution.py
@@ -21,7 +21,7 @@
 PAN_DEV = 128
 APER_DEV = 16
 MSG = CAP + 1
-READ = 4
+READ = 8
 LOW = 8
 HIGH = 11
 TILES = 11
@@ -38,7 +38,7 @@
 F32 = jnp.float32
 
 
-def call(body, outs, ins, scratch=(), mib=24, flops=None):
+def call(body, outs, ins, scratch=(), mib=24, flops=None, out_specs=None):
     cost = None
     if flops is not None:
         cost = pl.CostEstimate(flops=flops, bytes_accessed=1 << 20, transcendentals=0)
@@ -46,7 +46,7 @@
         body,
         out_shape=[jax.ShapeDtypeStruct(s, F32) for s in outs],
         in_specs=list(ins),
-        out_specs=[VMEM] * len(outs),
+        out_specs=out_specs or [VMEM] * len(outs),
         scratch_shapes=list(scratch),
         cost_estimate=cost,
         compiler_params=pltpu.CompilerParams(vmem_limit_bytes=mib << 20),
@@ -58,8 +58,8 @@
 
 
 def pack_kernel(*refs):
-    arrays, density, (send, y_low, y_high) = refs[:5], refs[5], refs[6:9]
-    local, need, sems = refs[9:14], refs[14], refs[15]
+    arrays, density, (send, y_low, y_high, table) = refs[:5], refs[5], refs[6:10]
+    local, need, sems = refs[10:15], refs[15], refs[16]
     copies = [pltpu.make_async_copy(a, b, sems.at[i]) for i, (a, b) in enumerate(zip(arrays, local))]
     cuts = [
         pltpu.make_async_copy(density.at[:, 0:16, :], y_low, sems.at[5]),
@@ -76,13 +76,18 @@
     lax.fori_loop(0, PAN_DEV, clear, 0, unroll=8)
     for copy in copies:
         copy.wait()
+    lane1 = iota((1, 128), 1)
+    picks = jnp.zeros((1, 128), jnp.int32)
     for a in range(APER_DEV):
-        need[aper[a]] = 1
+        p = aper[a]
+        need[p] = 1
+        picks = jnp.where(lane1 == a, brick[p], picks)
+        picks = jnp.where(lane1 == APER_DEV + a, counts[p], picks)
+    table[...] = picks.astype(F32)
     sub = iota((8, 128), 0)
     group = (iota((8, 128), 1) >> 3) & 3
     j = sub & 3
     masks = {e: (group == j - e) for e in range(-3, 4)}
-    lane1 = iota((1, 128), 1)
 
     def body(q, c):
         p = q * 2
@@ -102,7 +107,7 @@
             send[pl.ds(b * MSG + 4, 1), :] = meta.astype(F32)
         return c
 
-    lax.fori_loop(0, PAN_DEV // 2, body, 0, unroll=4)
+    lax.fori_loop(0, PAN_DEV // 2, body, 0, unroll=8)
     for copy in cuts:
         copy.wait()
 
@@ -411,12 +416,14 @@
 
 
 def flank_last(*refs):
-    (got, out, sums, nat), spare, (turned, meta, sem, named) = refs[15:19], refs[19:27], refs[27:]
+    (got, out, sums, nat), spare, (turned, meta, sem, named, out_sem) = refs[15:19], refs[19:27], refs[27:]
     copy = numbers(got, turned, meta, sem)
     next_flanks(refs[:15], nat, spare)
-    out[...] = nat[0:BX, LOW : LOW + BY]
+    result = pltpu.make_async_copy(nat.at[0:BX, LOW : LOW + BY, :], out, out_sem)
+    result.start()
     copy.wait()
     read(got, nat, sums, meta, named)
+    result.wait()
 
 
 def slab_kernel(x_low, x_high, below, above, low, high):
@@ -483,13 +490,12 @@
     lax.fori_loop(0, (count + READ - 1) // READ, body, 0)
 
 
-def pick_kernel(brick, counts, aper, got, out, rows):
-    sub = iota((1, APER_DEV), 1)
+def pick_kernel(table, got, out, rows):
+    lane = iota((1, APER_DEV), 1)
     live = jnp.ones((1, APER_DEV), F32)
     for a in range(APER_DEV):
-        p = aper[a]
-        rows[a : a + 1, :] = got[brick[p]]
-        live = jnp.where(sub == a, counts[p].astype(F32), live)
+        rows[a : a + 1, :] = got[table[0, a].astype(jnp.int32)]
+        live = jnp.where(lane == a, table[0, APER_DEV + a], live)
     out[...] = jnp.sum(rows[...], axis=1) / live[0]
 
 
@@ -503,9 +509,9 @@
 ):
     everyone = ("gx", "gy")
     ints = [pltpu.SMEM((n,), jnp.int32) for n in (PAN_DEV, PAN_DEV, PAN_DEV * CAP, APER_DEV)]
-    send, *d_slabs = call(
+    send, d_low, d_high, table = call(
         pack_kernel,
-        [(PAN_DEV * MSG, 128), (BX, 16, NZ), (BX, LOW, NZ)],
+        [(PAN_DEV * MSG, 128), (BX, 16, NZ), (BX, LOW, NZ), (1, 128)],
         [ANY] * 6,
         ints
         + [
@@ -518,7 +524,7 @@
     send = send.reshape(PAN_DEV, 1, MSG * 128)
     got = lax.all_to_all(send, everyone, split_axis=0, concat_axis=0, tiled=True)
     got = got.reshape(PAN_DEV * MSG, 128)
-    dy, dx, d_slabs = beside(density[:HIGH], density[BX - LOW :], *d_slabs)
+    dy, dx, d_slabs = beside(density[:HIGH], density[BX - LOW :], d_low, d_high)
 
     meta = [
         pltpu.VMEM((8, 128), jnp.int32),
@@ -577,16 +583,17 @@
         flank_last,
         [(BX, BY, NZ), (PAN_DEV, 1, 128)],
         [VMEM] * 16,
-        [layers(DEPX)] + spare(TILES) + meta + [pltpu.SMEM((PAN_DEV + 8,), jnp.int32)],
+        [layers(DEPX)] + spare(TILES) + meta + [pltpu.SMEM((PAN_DEV + READ,), jnp.int32), pltpu.SemaphoreType.DMA],
         32,
+        out_specs=[ANY, VMEM],
     )(*operands, got)
     back = lax.all_to_all(sums, everyone, split_axis=0, concat_axis=0, tiled=True)
     (picked,) = call(
         pick_kernel,
         [(APER_DEV,)],
-        [SMEM] * 3 + [VMEM],
+        [SMEM, VMEM],
         [pltpu.VMEM((APER_DEV, 128), F32)],
-    )(panel_brick, row_counts, aperture_panel, back)
+    )(table, back)
     return pot, picked
 
 

time: 115 us -> 113 us (0.983)
  Pallas kernels: 32.5 us -> 30.9 us
where the time goes in v9:
time: 113 us
  starting transfers between devices  52.8 us (47%)
  Pallas kernels  30.9 us (27%)
  blocking collectives  17.7 us (16%)
  waiting for transfers between devices  10.5 us (9%)
    ppermute x22, starting transfers between devices, ring(): lax.ppermute(array, axis, [(i, (i + by) % size) for i in range(size)])  41.8 us
    all_to_all x1, blocking collectives, on_device(): lax.all_to_all(sums, everyone, split_axis=0, concat_axis=0, tiled=True)  17.7 us
    all_to_all x1, starting transfers between devices, on_device(): lax.all_to_all(send, everyone, split_axis=0, concat_axis=0, tiled=True)  11 us
    pallas_call x2, Pallas kernels, on_device(): call(inner_next, [tiles(BX, width)] * 4, [VMEM] * 6, [layers(BX)], 32, work)  7.7 us
    ppermute x22, waiting for transfers between devices, ring(): lax.ppermute(array, axis, [(i, (i + by) % size) for i in range(size)])  5.47 us
    all_to_all x1, waiting for transfers between devices, on_device(): lax.all_to_all(send, everyone, split_axis=0, concat_axis=0, tiled=True)  5.06 us
    pallas_call x1, Pallas kernels, on_device(): call(flank_last, [(BX, BY, NZ), (PAN_DEV, 1, 128)], [VMEM] * 16, [layers(...  4.69 us
    pallas_call x1, Pallas kernels, on_device(): call(deposit_kernel, [(DEPX, DEPY, NZ)] + [(SRC, DEPY, NZ)] * 2 + [(DEPX,...  4.22 us
  transfers between devices with their start and end apart: 23, of which 4 were waited for; matrix products, arithmetic and copies ran while one was open for 0% of the time, Pallas kernels for 14%

profile of v9, /device:TPU:1, one launch (start us, length us, event | category | flops | bytes accessed | tf_op | source)
XLA Modules:
  0.0 112.9 jit_solution(7225147422051750897)
XLA Ops:
  0.6 0.0 copy-start
  0.6 3.0 %shard_map.86 = (f32[640,128]{1,0:T(8,128)}, f32[32,16,128]{2,1,0:T(8,128)}, f32[32,8,128]{2,1,0:T(8,128)}, f32[1,128]{1,0:T(1,128)}) custom-call(s32[128]{0:T(128)} %refs_0_.1, s32[128]{0:T(128)} %refs_1_.1, s32[512]{0:T(512)} %refs_2_.1, s32[16]{0:T(128)} %refs_3_.1, f32[512,128]{1,0:T(8,128)} %refs_4_.1, f32[32,64,128]{2,1,0:T(8,128)} %density.1), custom_call_target="tpu_custom_call" | custom-call | tf_op jit(solution)/shard_map/pallas_call | solution.py:512
  3.6 1.4 %collective-permute-start.1 = (f32[32,16,128]{2,1,0:T(8,128)}, f32[32,16,128]{2,1,0:T(8,128)S(1)}, u32[]{:S(2)}, u32[]{:S(2)}) collective-permute-start(f32[32,16,128]{2,1,0:T(8,128)} %get-tuple-element.51), channel_id=1, source_target_pairs={{0,7},{1,0},{2,1},{3,2},{4,3},{5,4},{6,5},{7,6},{8,15},{9,8},{10,9... | collective-permute-start | bytes 786440 | tf_op jit(solution)/shard_map/ppermute | solution.py:504
  5.1 1.3 %collective-permute-start = (f32[32,8,128]{2,1,0:T(8,128)}, f32[32,8,128]{2,1,0:T(8,128)S(1)}, u32[]{:S(2)}, u32[]{:S(2)}) collective-permute-start(f32[32,8,128]{2,1,0:T(8,128)} %get-tuple-element.50), channel_id=1, source_target_pairs={{0,1},{1,2},{2,3},{3,4},{4,5},{5,6},{6,7},{7,0},{8,9},{9,10},{10,1... | collective-permute-start | bytes 393224 | tf_op jit(solution)/shard_map/ppermute | solution.py:504
  6.4 11.0 %all-to-all-start = ((f32[128,1,640]{2,1,0:T(1,128)}), f32[128,1,640]{2,1,0:T(1,128)S(1)}, u32[]{:S(2)}, u32[]{:S(2)}) async-start(f32[128,1,640]{2,1,0:T(1,128)} %bitcast.4), calls=%async_computation | async-start | bytes 655360 | tf_op jit(solution)/shard_map/all_to_all | solution.py:525
  17.4 0.0 copy-done
  17.4 0.0 collective-permute-done.below.d_below
  17.4 0.0 copy-start.2
  17.5 0.0 collective-permute-done.1.above.d_above
  17.5 1.0 shard_map.87
  18.4 0.0 copy-done.2
  18.4 5.4 %collective-permute-start.7 = (f32[11,88,128]{2,1,0:T(8,128)}, f32[11,88,128]{2,1,0:T(8,128)S(1)}, u32[]{:S(2)}, u32[]{:S(2)}) collective-permute-start(f32[11,88,128]{2,1,0:T(8,128)} %get-tuple-element.52.unused_low), channel_id=1, source_target_pairs={{0,120},{8,0},{16,8},{24,16},{32,24},{40,32},{48,40},{56,48},{64,5... | collective-permute-start | bytes 1486856 | tf_op jit(solution)/shard_map/ppermute | solution.py:504
  23.9 0.0 collective-permute-start.6
  23.9 5.1 %all-to-all-done = f32[128,1,640]{2,1,0:T(1,128)S(1)} async-done(((f32[128,1,640]{2,1,0:T(1,128)}), f32[128,1,640]{2,1,0:T(1,128)S(1)}, u32[]{:S(2)}, u32[]{:S(2)}) %all-to-all-start) | async-done | bytes 327712 | tf_op jit(solution)/shard_map/all_to_all | solution.py:525
  28.9 0.0 copy-done.1
  28.9 4.2 %shard_map.88 = (f32[35,72,128]{2,1,0:T(8,128)S(1)}, f32[10,72,128]{2,1,0:T(8,128)S(1)}, f32[10,72,128]{2,1,0:T(8,128)S(1)}, f32[35,16,128]{2,1,0:T(8,128)S(1)}, f32[35,16,128]{2,1,0:T(8,128)S(1)}) custom-call(f32[640,128]{1,0:T(8,128)S(1)} %bitcast.2, f32[32,64,128]{2,1,0:T(8,128)S(1)} %copy-done.1, f32[11,88,128]{2,1,0:T(8,128)} %get-tuple-element.52.unused_low, ...), custom_call_target="tpu_custom_call" | custom-call | tf_op jit(solution)/shard_map/pallas_call | solution.py:534
  33.2 0.9 collective-permute-start.2
  34.1 0.1 collective-permute-start.3
  34.2 0.7 collective-permute-start.4
  34.9 2.7 %collective-permute-done.2.y_below.below = f32[35,16,128]{2,1,0:T(8,128)S(1)} collective-permute-done((f32[35,16,128]{2,1,0:T(8,128)S(1)}, f32[35,16,128]{2,1,0:T(8,128)S(1)}, u32[]{:S(2)}, u32[]{:S(2)}) %collective-permute-start.2) | collective-permute-done | bytes 286752 | tf_op jit(solution)/shard_map/ppermute | solution.py:504
  37.7 1.4 %collective-permute-start.5 = (f32[10,72,128]{2,1,0:T(8,128)S(1)}, f32[10,72,128]{2,1,0:T(8,128)S(1)}, u32[]{:S(2)}, u32[]{:S(2)}) collective-permute-start(f32[10,72,128]{2,1,0:T(8,128)S(1)} %get-tuple-element.64), channel_id=1, source_target_pairs={{0,120},{8,0},{16,8},{24,16},{32,24},{40,32},{48,40},{56,48},{64,5... | collective-permute-start | bytes 1105928 | tf_op jit(solution)/shard_map/ppermute | solution.py:504
  39.1 1.4 %collective-permute-done.3.y_above.above = f32[35,16,128]{2,1,0:T(8,128)S(1)} collective-permute-done((f32[35,16,128]{2,1,0:T(8,128)S(1)}, f32[35,16,128]{2,1,0:T(8,128)S(1)}, u32[]{:S(2)}, u32[]{:S(2)}) %collective-permute-start.3) | collective-permute-done | bytes 286752 | tf_op jit(solution)/shard_map/ppermute | solution.py:504
  40.5 0.0 collective-permute-done.6.unused_low.refs_10_.refs_13_
  40.5 0.0 collective-permute-done.7.unused_high.refs_11_.refs_14_
  40.5 0.2 collective-permute-start.8
  40.7 4.7 %collective-permute-start.9 = (f32[10,24,128]{2,1,0:T(8,128)S(1)}, f32[10,24,128]{2,1,0:T(8,128)S(1)}, u32[]{:S(2)}, u32[]{:S(2)}) collective-permute-start(f32[10,24,128]{2,1,0:T(8,128)S(1)} %get-tuple-element.66), channel_id=1, source_target_pairs={{0,120},{8,0},{16,8},{24,16},{32,24},{40,32},{48,40},{56,48},{64,5... | collective-permute-start | bytes 368648 | tf_op jit(solution)/shard_map/ppermute | solution.py:504
  45.3 0.0 copy-done.3
  45.3 2.6 %shard_map.89 = (f32[32,10,8,128]{3,2,1,0:T(8,128)S(1)}, f32[32,10,8,128]{3,2,1,0:T(8,128)S(1)}, f32[32,10,8,128]{3,2,1,0:T(8,128)S(1)}, f32[32,10,8,128]{3,2,1,...) custom-call(f32[35,72,128]{2,1,0:T(8,128)S(1)} %get-tuple-element.54.charge, ...), custom_call_target="tpu_custom_call" | custom-call | flops 20000000000 | bytes 1048576 | tf_op jit(solution)/shard_map/pallas_call | solution.py:556
  48.0 0.0 collective-permute-done.4.refs_6_
  48.0 0.0 collective-permute-done.5.refs_7_
  48.0 1.3 %collective-permute-done.8.refs_8_ = f32[10,24,128]{2,1,0:T(8,128)S(1)} collective-permute-done((f32[10,24,128]{2,1,0:T(8,128)S(1)}, f32[10,24,128]{2,1,0:T(8,128)S(1)}, u32[]{:S(2)}, u32[]{:S(2)}) %collective-permute-start.8) | collective-permute-done | bytes 122912 | tf_op jit(solution)/shard_map/ppermute | solution.py:504
  49.3 0.0 collective-permute-done.9.refs_9_
  49.3 3.1 %shard_map.91 = (f32[32,64,128]{2,1,0:T(8,128)S(1)}, f32[3,64,128]{2,1,0:T(8,128)S(1)}, f32[8,64,128]{2,1,0:T(8,128)S(1)}, f32[8,64,128]{2,1,0:T(8,128)S(1)}, f3...) custom-call(f32[32,10,8,128]{3,2,1,0:T(8,128)S(1)} %get-tuple-elemen, ...), custom_call_target="tpu_custom_call" | custom-call | tf_op jit(solution)/shard_map/pallas_call | solution.py:564
  52.4 2.2 %collective-permute-start.10 = (f32[35,8,128]{2,1,0:T(8,128)S(1)}, f32[35,8,128]{2,1,0:T(8,128)S(1)}, u32[]{:S(2)}, u32[]{:S(2)}) collective-permute-start(f32[35,8,128]{2,1,0:T(8,128)S(1)} %get-tuple-element.68), channel_id=1, source_target_pairs={{0,1},{1,2},{2,3},{3,4},{4,5},{5,6},{6,7},{7,0},{8,9},{9,10},{10,1... | collective-permute-start | bytes 430088 | tf_op jit(solution)/shard_map/ppermute | solution.py:504
  54.6 0.1 collective-permute-start.11
  54.7 0.6 collective-permute-start.12
  55.2 4.5 %collective-permute-start.13 = (f32[8,64,128]{2,1,0:T(8,128)S(1)}, f32[8,64,128]{2,1,0:T(8,128)S(1)}, u32[]{:S(2)}, u32[]{:S(2)}) collective-permute-start(f32[8,64,128]{2,1,0:T(8,128)S(1)} %get-tuple-element.77), channel_id=1, source_target_pairs={{0,120},{8,0},{16,8},{24,16},{32,24},{40,32},{48,40},{56,48},{64,5... | collective-permute-start | bytes 786440 | tf_op jit(solution)/shard_map/ppermute | solution.py:504
  59.7 0.0 collective-permute-done.10.y_below.below.refs_5_
  59.7 0.0 collective-permute-done.11.y_above.above.refs_6_
  59.8 0.2 collective-permute-start.14
  59.9 5.0 %collective-permute-start.15 = (f32[8,16,128]{2,1,0:T(8,128)S(1)}, f32[8,16,128]{2,1,0:T(8,128)S(1)}, u32[]{:S(2)}, u32[]{:S(2)}) collective-permute-start(f32[8,16,128]{2,1,0:T(8,128)S(1)} %get-tuple-element.79), channel_id=1, source_target_pairs={{0,120},{8,0},{16,8},{24,16},{32,24},{40,32},{48,40},{56,48},{64,5... | collective-permute-start | bytes 196616 | tf_op jit(solution)/shard_map/ppermute | solution.py:504
  64.9 3.6 %shard_map.92 = (f32[32,10,8,128]{3,2,1,0:T(8,128)S(1)}, f32[32,10,8,128]{3,2,1,0:T(8,128)S(1)}, f32[32,10,8,128]{3,2,1,0:T(8,128)S(1)}, f32[32,10,8,128]{3,2,1,0:T(8,128)S(1)}) custom-call(f32[32,64,128]{2,1,0:T(8,128)S(1)} %get-tuple-element.67.own, f32[35,8,128]{2,1,0:T(8,128)S(1)} %collective-permute-done.10.y_below.below.refs_5_, ...), custom_call_target="tpu_custom_call" | custom-call | flops 20000000000 | bytes 1048576 | tf_op jit(solution)/shard_map/pallas_call | solution.py:574
  68.5 0.0 collective-permute-done.14.refs_9_
  68.5 0.0 collective-permute-done.15.refs_10_
  68.5 0.0 collective-permute-done.12.refs_7_
  68.5 0.0 collective-permute-done.13.refs_8_
  68.5 3.3 %shard_map.94 = (f32[32,64,128]{2,1,0:T(8,128)S(1)}, f32[3,64,128]{2,1,0:T(8,128)S(1)}, f32[8,64,128]{2,1,0:T(8,128)S(1)}, f32[8,64,128]{2,1,0:T(8,128)S(1)}, f3...) custom-call(f32[32,10,8,128]{3,2,1,0:T(8,128)S(1)} %get-tuple-element.71.refs_0_, ...), custom_call_target="tpu_custom_call" | custom-call | tf_op jit(solution)/shard_map/pallas_call | solution.py:579
  71.9 3.5 %collective-permute-start.17 = (f32[35,16,128]{2,1,0:T(8,128)S(1)}, f32[35,16,128]{2,1,0:T(8,128)S(1)}, u32[]{:S(2)}, u32[]{:S(2)}) collective-permute-start(f32[35,16,128]{2,1,0:T(8,128)S(1)} %get-tuple-element.83), channel_id=1, source_target_pairs={{0,7},{1,0},{2,1},{3,2},{4,3},{5,4},{6,5},{7,6},{8,15},{9,8},{10,9... | collective-permute-start | bytes 860168 | tf_op jit(solution)/shard_map/ppermute | solution.py:504
  75.4 0.0 collective-permute-start.16
  75.4 0.0 collective-permute-start.18
  75.4 4.8 %collective-permute-start.19 = (f32[8,64,128]{2,1,0:T(8,128)S(1)}, f32[8,64,128]{2,1,0:T(8,128)S(1)}, u32[]{:S(2)}, u32[]{:S(2)}) collective-permute-start(f32[8,64,128]{2,1,0:T(8,128)S(1)} %get-tuple-element.90), channel_id=1, source_target_pairs={{0,120},{8,0},{16,8},{24,16},{32,24},{40,32},{48,40},{56,48},{64,5... | collective-permute-start | bytes 786440 | tf_op jit(solution)/shard_map/ppermute | solution.py:504
  80.2 0.0 collective-permute-done.16.y_below.below.refs_5_
  80.2 0.0 collective-permute-done.17.y_above.above.refs_6_
  80.2 0.1 collective-permute-start.20
  80.3 4.8 %collective-permute-start.21 = (f32[8,24,128]{2,1,0:T(8,128)S(1)}, f32[8,24,128]{2,1,0:T(8,128)S(1)}, u32[]{:S(2)}, u32[]{:S(2)}) collective-permute-start(f32[8,24,128]{2,1,0:T(8,128)S(1)} %get-tuple-element.92), channel_id=1, source_target_pairs={{0,120},{8,0},{16,8},{24,16},{32,24},{40,32},{48,40},{56,48},{64,5... | collective-permute-start | bytes 294920 | tf_op jit(solution)/shard_map/ppermute | solution.py:504
  85.0 4.1 %shard_map.95 = (f32[32,11,8,128]{3,2,1,0:T(8,128)S(1)}, f32[32,11,8,128]{3,2,1,0:T(8,128)S(1)}, f32[32,11,8,128]{3,2,1,0:T(8,128)S(1)}, f32[32,11,8,128]{3,2,1,0:T(8,128)S(1)}) custom-call(f32[32,64,128]{2,1,0:T(8,128)S(1)} %get-tuple-element.81.own, f32[35,8,128]{2,1,0:T(8,128)S(1)} %collective-permute-done.16.y_below.below.refs_5_, ...), custom_call_target="tpu_custom_call" | custom-call | flops 20000000000 | bytes 1048576 | tf_op jit(solution)/shard_map/pallas_call | solution.py:574
  89.1 0.0 collective-permute-done.18.refs_7_
  89.2 0.0 collective-permute-done.19.refs_8_
  89.2 0.0 collective-permute-done.20.refs_9_
  89.2 0.0 collective-permute-done.21.refs_10_
  89.2 0.0 copy-start.4
  89.2 4.7 %shard_map.97 = (f32[32,64,128]{2,1,0:T(8,128)}, f32[128,1,128]{2,1,0:T(1,128)S(1)}) custom-call(f32[32,11,8,128]{3,2,1,0:T(8,128)S(1)} %get-tuple-element.84.refs_0_, f32[32,11,8,128]{3,2,1,0:T(8,128)S(1)} %get-tuple-element.85.refs_1_, f32[32,11,8,128]{3,2,1,0:T(8,128)S(1)} %get-tuple-element.86.refs_2_, f32[32,11,8,128]{3,2,1,0:T(8,128)S(1)} %get-tuple-element.87.refs_3_, ...), custom_call_target="tpu_custom_call" | custom-call | tf_op jit(solution)/shard_map/pallas_call | solution.py:582
  93.9 17.7 %all_to_all.10.got = f32[128,1,128]{2,1,0:T(1,128)S(1)} all-to-all(f32[128,1,128]{2,1,0:T(1,128)S(1)} %get-tuple-element.95), channel_id=1, replica_groups=mesh['gx'=16,'gy'=8] {'gx','gy'}, dimensions={0} | all-to-all | bytes 131072 | tf_op jit(solution)/shard_map/all_to_all | solution.py:590
  111.6 1.2 %shard_map.98 = f32[16]{0:T(128)} custom-call(f32[1,128]{1,0:T(1,128)S(1)} %copy-done.4, f32[128,1,128]{2,1,0:T(1,128)S(1)} %all_to_all.10.got), custom_call_target="tpu_custom_call" | custom-call | tf_op jit(solution)/shard_map/pallas_call | solution.py:591
  (8 shorter events, 0.1 us)
Async XLA Ops:
  0.6 16.7 %copy-start = (f32[32,64,128]{2,1,0:T(8,128)S(1)}, f32[32,64,128]{2,1,0:T(8,128)}, u32[]{:S(2)}) copy-start(f32[32,64,128]{2,1,0:T(8,128)} %density.1) | copy-start | bytes 3145732
  3.6 13.8 %collective-permute-start.1 = (f32[32,16,128]{2,1,0:T(8,128)}, f32[32,16,128]{2,1,0:T(8,128)S(1)}, u32[]{:S(2)}, u32[]{:S(2)}) collective-permute-start(f32[32,16,128]{2,1,0:T(8,128)} %get-tuple-element.51), channel_id=1, source_target_pairs={{0,7},{1,0},{2,1},{3,2},{4,3},{5,4},{6,5},{7,6},{8,15},{9,8},{10,9... | collective-permute-start | bytes 786440 | tf_op jit(solution)/shard_map/ppermute | solution.py:504
  5.1 12.4 %collective-permute-start = (f32[32,8,128]{2,1,0:T(8,128)}, f32[32,8,128]{2,1,0:T(8,128)S(1)}, u32[]{:S(2)}, u32[]{:S(2)}) collective-permute-start(f32[32,8,128]{2,1,0:T(8,128)} %get-tuple-element.50), channel_id=1, source_target_pairs={{0,1},{1,2},{2,3},{3,4},{4,5},{5,6},{6,7},{7,0},{8,9},{9,10},{10,1... | collective-permute-start | bytes 393224 | tf_op jit(solution)/shard_map/ppermute | solution.py:504
  6.4 22.6 %copy-start.1 = (f32[32,64,128]{2,1,0:T(8,128)S(1)}, f32[32,64,128]{2,1,0:T(8,128)}, u32[]{:S(2)}) copy-start(f32[32,64,128]{2,1,0:T(8,128)} %ion.1) | copy-start | bytes 3145732
  6.4 22.6 %all-to-all-start = ((f32[128,1,640]{2,1,0:T(1,128)}), f32[128,1,640]{2,1,0:T(1,128)S(1)}, u32[]{:S(2)}, u32[]{:S(2)}) async-start(f32[128,1,640]{2,1,0:T(1,128)} %bitcast.4), calls=%async_computation | async-start | bytes 655360 | tf_op jit(solution)/shard_map/all_to_all | solution.py:525
  17.4 1.0 copy-start.2
  18.4 22.0 %collective-permute-start.7 = (f32[11,88,128]{2,1,0:T(8,128)}, f32[11,88,128]{2,1,0:T(8,128)S(1)}, u32[]{:S(2)}, u32[]{:S(2)}) collective-permute-start(f32[11,88,128]{2,1,0:T(8,128)} %get-tuple-element.52.unused_low), channel_id=1, source_target_pairs={{0,120},{8,0},{16,8},{24,16},{32,24},{40,32},{48,40},{56,48},{64,5... | collective-permute-start | bytes 1486856 | tf_op jit(solution)/shard_map/ppermute | solution.py:504
  23.9 16.6 %collective-permute-start.6 = (f32[8,88,128]{2,1,0:T(8,128)}, f32[8,88,128]{2,1,0:T(8,128)S(1)}, u32[]{:S(2)}, u32[]{:S(2)}) collective-permute-start(f32[8,88,128]{2,1,0:T(8,128)} %get-tuple-element.53.unused_high), channel_id=1, source_target_pairs={{0,8},{8,16},{16,24},{24,32},{32,40},{40,48},{48,56},{56,64},{64,7... | collective-permute-start | bytes 1081352 | tf_op jit(solution)/shard_map/ppermute | solution.py:504
  28.9 16.4 %copy-start.3 = (f32[32,8,128]{2,1,0:T(8,128)S(1)}, f32[32,8,128]{2,1,0:T(8,128)}, u32[]{:S(2)}) copy-start(f32[32,8,128]{2,1,0:T(8,128)} %copy-done.2) | copy-start | bytes 393220
  33.2 4.5 %collective-permute-start.2 = (f32[35,16,128]{2,1,0:T(8,128)S(1)}, f32[35,16,128]{2,1,0:T(8,128)S(1)}, u32[]{:S(2)}, u32[]{:S(2)}) collective-permute-start(f32[35,16,128]{2,1,0:T(8,128)S(1)} %get-tuple-element.55), channel_id=1, source_target_pairs={{0,1},{1,2},{2,3},{3,4},{4,5},{5,6},{6,7},{7,0},{8,9},{9,10},{10,1... | collective-permute-start | bytes 860168 | tf_op jit(solution)/shard_map/ppermute | solution.py:504
  34.1 6.4 %collective-permute-start.3 = (f32[35,16,128]{2,1,0:T(8,128)S(1)}, f32[35,16,128]{2,1,0:T(8,128)S(1)}, u32[]{:S(2)}, u32[]{:S(2)}) collective-permute-start(f32[35,16,128]{2,1,0:T(8,128)S(1)} %get-tuple-element.56), channel_id=1, source_target_pairs={{0,7},{1,0},{2,1},{3,2},{4,3},{5,4},{6,5},{7,6},{8,15},{9,8},{10,9... | collective-permute-start | bytes 860168 | tf_op jit(solution)/shard_map/ppermute | solution.py:504
  34.2 13.8 %collective-permute-start.4 = (f32[10,72,128]{2,1,0:T(8,128)S(1)}, f32[10,72,128]{2,1,0:T(8,128)S(1)}, u32[]{:S(2)}, u32[]{:S(2)}) collective-permute-start(f32[10,72,128]{2,1,0:T(8,128)S(1)} %get-tuple-element.63), channel_id=1, source_target_pairs={{0,8},{8,16},{16,24},{24,32},{32,40},{40,48},{48,56},{56,64},{64,7... | collective-permute-start | bytes 1105928 | tf_op jit(solution)/shard_map/ppermute | solution.py:504
  37.7 10.3 %collective-permute-start.5 = (f32[10,72,128]{2,1,0:T(8,128)S(1)}, f32[10,72,128]{2,1,0:T(8,128)S(1)}, u32[]{:S(2)}, u32[]{:S(2)}) collective-permute-start(f32[10,72,128]{2,1,0:T(8,128)S(1)} %get-tuple-element.64), channel_id=1, source_target_pairs={{0,120},{8,0},{16,8},{24,16},{32,24},{40,32},{48,40},{56,48},{64,5... | collective-permute-start | bytes 1105928 | tf_op jit(solution)/shard_map/ppermute | solution.py:504
  40.5 8.8 %collective-permute-start.8 = (f32[10,24,128]{2,1,0:T(8,128)S(1)}, f32[10,24,128]{2,1,0:T(8,128)S(1)}, u32[]{:S(2)}, u32[]{:S(2)}) collective-permute-start(f32[10,24,128]{2,1,0:T(8,128)S(1)} %get-tuple-element.65), channel_id=1, source_target_pairs={{0,8},{8,16},{16,24},{24,32},{32,40},{40,48},{48,56},{56,64},{64,7... | collective-permute-start | bytes 368648 | tf_op jit(solution)/shard_map/ppermute | solution.py:504
  40.7 8.6 %collective-permute-start.9 = (f32[10,24,128]{2,1,0:T(8,128)S(1)}, f32[10,24,128]{2,1,0:T(8,128)S(1)}, u32[]{:S(2)}, u32[]{:S(2)}) collective-permute-start(f32[10,24,128]{2,1,0:T(8,128)S(1)} %get-tuple-element.66), channel_id=1, source_target_pairs={{0,120},{8,0},{16,8},{24,16},{32,24},{40,32},{48,40},{56,48},{64,5... | collective-permute-start | bytes 368648 | tf_op jit(solution)/shard_map/ppermute | solution.py:504
  52.4 7.4 %collective-permute-start.10 = (f32[35,8,128]{2,1,0:T(8,128)S(1)}, f32[35,8,128]{2,1,0:T(8,128)S(1)}, u32[]{:S(2)}, u32[]{:S(2)}) collective-permute-start(f32[35,8,128]{2,1,0:T(8,128)S(1)} %get-tuple-element.68), channel_id=1, source_target_pairs={{0,1},{1,2},{2,3},{3,4},{4,5},{5,6},{6,7},{7,0},{8,9},{9,10},{10,1... | collective-permute-start | bytes 430088 | tf_op jit(solution)/shard_map/ppermute | solution.py:504
  54.6 5.1 %collective-permute-start.11 = (f32[35,8,128]{2,1,0:T(8,128)S(1)}, f32[35,8,128]{2,1,0:T(8,128)S(1)}, u32[]{:S(2)}, u32[]{:S(2)}) collective-permute-start(f32[35,8,128]{2,1,0:T(8,128)S(1)} %get-tuple-element.69), channel_id=1, source_target_pairs={{0,7},{1,0},{2,1},{3,2},{4,3},{5,4},{6,5},{7,6},{8,15},{9,8},{10,9... | collective-permute-start | bytes 430088 | tf_op jit(solution)/shard_map/ppermute | solution.py:504
  54.7 13.8 %collective-permute-start.12 = (f32[8,64,128]{2,1,0:T(8,128)S(1)}, f32[8,64,128]{2,1,0:T(8,128)S(1)}, u32[]{:S(2)}, u32[]{:S(2)}) collective-permute-start(f32[8,64,128]{2,1,0:T(8,128)S(1)} %get-tuple-element.76), channel_id=1, source_target_pairs={{0,8},{8,16},{16,24},{24,32},{32,40},{40,48},{48,56},{56,64},{64,7... | collective-permute-start | bytes 786440 | tf_op jit(solution)/shard_map/ppermute | solution.py:504
  55.2 13.3 %collective-permute-start.13 = (f32[8,64,128]{2,1,0:T(8,128)S(1)}, f32[8,64,128]{2,1,0:T(8,128)S(1)}, u32[]{:S(2)}, u32[]{:S(2)}) collective-permute-start(f32[8,64,128]{2,1,0:T(8,128)S(1)} %get-tuple-element.77), channel_id=1, source_target_pairs={{0,120},{8,0},{16,8},{24,16},{32,24},{40,32},{48,40},{56,48},{64,5... | collective-permute-start | bytes 786440 | tf_op jit(solution)/shard_map/ppermute | solution.py:504
  59.8 8.7 %collective-permute-start.14 = (f32[8,16,128]{2,1,0:T(8,128)S(1)}, f32[8,16,128]{2,1,0:T(8,128)S(1)}, u32[]{:S(2)}, u32[]{:S(2)}) collective-permute-start(f32[8,16,128]{2,1,0:T(8,128)S(1)} %get-tuple-element.78), channel_id=1, source_target_pairs={{0,8},{8,16},{16,24},{24,32},{32,40},{40,48},{48,56},{56,64},{64,7... | collective-permute-start | bytes 196616 | tf_op jit(solution)/shard_map/ppermute | solution.py:504
  59.9 8.6 %collective-permute-start.15 = (f32[8,16,128]{2,1,0:T(8,128)S(1)}, f32[8,16,128]{2,1,0:T(8,128)S(1)}, u32[]{:S(2)}, u32[]{:S(2)}) collective-permute-start(f32[8,16,128]{2,1,0:T(8,128)S(1)} %get-tuple-element.79), channel_id=1, source_target_pairs={{0,120},{8,0},{16,8},{24,16},{32,24},{40,32},{48,40},{56,48},{64,5... | collective-permute-start | bytes 196616 | tf_op jit(solution)/shard_map/ppermute | solution.py:504
  71.9 8.3 %collective-permute-start.17 = (f32[35,16,128]{2,1,0:T(8,128)S(1)}, f32[35,16,128]{2,1,0:T(8,128)S(1)}, u32[]{:S(2)}, u32[]{:S(2)}) collective-permute-start(f32[35,16,128]{2,1,0:T(8,128)S(1)} %get-tuple-element.83), channel_id=1, source_target_pairs={{0,7},{1,0},{2,1},{3,2},{4,3},{5,4},{6,5},{7,6},{8,15},{9,8},{10,9... | collective-permute-start | bytes 860168 | tf_op jit(solution)/shard_map/ppermute | solution.py:504
  75.4 4.8 %collective-permute-start.16 = (f32[35,8,128]{2,1,0:T(8,128)S(1)}, f32[35,8,128]{2,1,0:T(8,128)S(1)}, u32[]{:S(2)}, u32[]{:S(2)}) collective-permute-start(f32[35,8,128]{2,1,0:T(8,128)S(1)} %get-tuple-element.82), channel_id=1, source_target_pairs={{0,1},{1,2},{2,3},{3,4},{4,5},{5,6},{6,7},{7,0},{8,9},{9,10},{10,1... | collective-permute-start | bytes 430088 | tf_op jit(solution)/shard_map/ppermute | solution.py:504
  75.4 13.8 %collective-permute-start.18 = (f32[8,64,128]{2,1,0:T(8,128)S(1)}, f32[8,64,128]{2,1,0:T(8,128)S(1)}, u32[]{:S(2)}, u32[]{:S(2)}) collective-permute-start(f32[8,64,128]{2,1,0:T(8,128)S(1)} %get-tuple-element.89), channel_id=1, source_target_pairs={{0,8},{8,16},{16,24},{24,32},{32,40},{40,48},{48,56},{56,64},{64,7... | collective-permute-start | bytes 786440 | tf_op jit(solution)/shard_map/ppermute | solution.py:504
  75.4 13.8 %collective-permute-start.19 = (f32[8,64,128]{2,1,0:T(8,128)S(1)}, f32[8,64,128]{2,1,0:T(8,128)S(1)}, u32[]{:S(2)}, u32[]{:S(2)}) collective-permute-start(f32[8,64,128]{2,1,0:T(8,128)S(1)} %get-tuple-element.90), channel_id=1, source_target_pairs={{0,120},{8,0},{16,8},{24,16},{32,24},{40,32},{48,40},{56,48},{64,5... | collective-permute-start | bytes 786440 | tf_op jit(solution)/shard_map/ppermute | solution.py:504
  80.2 9.0 %collective-permute-start.20 = (f32[8,24,128]{2,1,0:T(8,128)S(1)}, f32[8,24,128]{2,1,0:T(8,128)S(1)}, u32[]{:S(2)}, u32[]{:S(2)}) collective-permute-start(f32[8,24,128]{2,1,0:T(8,128)S(1)} %get-tuple-element.91), channel_id=1, source_target_pairs={{0,8},{8,16},{16,24},{24,32},{32,40},{40,48},{48,56},{56,64},{64,7... | collective-permute-start | bytes 294920 | tf_op jit(solution)/shard_map/ppermute | solution.py:504
  80.3 8.9 %collective-permute-start.21 = (f32[8,24,128]{2,1,0:T(8,128)S(1)}, f32[8,24,128]{2,1,0:T(8,128)S(1)}, u32[]{:S(2)}, u32[]{:S(2)}) collective-permute-start(f32[8,24,128]{2,1,0:T(8,128)S(1)} %get-tuple-element.92), channel_id=1, source_target_pairs={{0,120},{8,0},{16,8},{24,16},{32,24},{40,32},{48,40},{56,48},{64,5... | collective-permute-start | bytes 294920 | tf_op jit(solution)/shard_map/ppermute | solution.py:504
  89.2 22.5 %copy-start.4 = (f32[1,128]{1,0:T(1,128)S(1)}, f32[1,128]{1,0:T(1,128)}, u32[]{:S(2)}) copy-start(f32[1,128]{1,0:T(1,128)} %get-tuple-element.94.table) | copy-start | bytes 1540

commit v10 on v9

--- a/solution.py
+++ b/solution.py
@@ -311,7 +311,8 @@
         one(2 * j + 2, b1, l1, l0, h1, h0)
         return c
 
-    lax.fori_loop(k0 - 1, SWEEPS // 2, body, 0)
+    for j in range(k0 - 1, SWEEPS // 2):
+        body(j, 0)
 
 
 def len_low_halo(a):

time: 113 us -> 113 us (level)
  no operation moved by 1% of the time
where the time goes in v10:
time: 113 us; the launch traced here: 112 us
  starting transfers between devices  52.8 us (47%)
  Pallas kernels  30.4 us (27%)
  blocking collectives  17.7 us (16%)
  waiting for transfers between devices  10.5 us (9%)
    ppermute x22, starting transfers between devices, ring(): lax.ppermute(array, axis, [(i, (i + by) % size) for i in range(size)])  41.8 us
    all_to_all x1, blocking collectives, on_device(): lax.all_to_all(sums, everyone, split_axis=0, concat_axis=0, tiled=True)  17.7 us
    all_to_all x1, starting transfers between devices, on_device(): lax.all_to_all(send, everyone, split_axis=0, concat_axis=0, tiled=True)  11 us
    pallas_call x2, Pallas kernels, on_device(): call(inner_next, [tiles(BX, width)] * 4, [VMEM] * 6, [layers(BX)], 32, work)  7.7 us
    ppermute x22, waiting for transfers between devices, ring(): lax.ppermute(array, axis, [(i, (i + by) % size) for i in range(size)])  5.47 us
    all_to_all x1, waiting for transfers between devices, on_device(): lax.all_to_all(send, everyone, split_axis=0, concat_axis=0, tiled=True)  5.05 us
    pallas_call x1, Pallas kernels, on_device(): call(flank_last, [(BX, BY, NZ), (PAN_DEV, 1, 128)], [VMEM] * 16, [layers(...  4.92 us
    pallas_call x1, Pallas kernels, on_device(): call(deposit_kernel, [(DEPX, DEPY, NZ)] + [(SRC, DEPY, NZ)] * 2 + [(DEPX,...  4.22 us
  transfers between devices with their start and end apart: 23, of which 4 were waited for; matrix products, arithmetic and copies ran while one was open for 0% of the time, Pallas kernels for 14%

profile of v10, /device:TPU:1, one launch (start us, length us, event | category | flops | bytes accessed | tf_op | source)
XLA Modules:
  0.0 112.4 jit_solution(5371331417112692680)
XLA Ops:
  0.6 0.0 copy-start
  0.6 3.0 %shard_map.86 = (f32[640,128]{1,0:T(8,128)}, f32[32,16,128]{2,1,0:T(8,128)}, f32[32,8,128]{2,1,0:T(8,128)}, f32[1,128]{1,0:T(1,128)}) custom-call(s32[128]{0:T(128)} %refs_0_.1, s32[128]{0:T(128)} %refs_1_.1, s32[512]{0:T(512)} %refs_2_.1, s32[16]{0:T(128)} %refs_3_.1, f32[512,128]{1,0:T(8,128)} %refs_4_.1, f32[32,64,128]{2,1,0:T(8,128)} %density.1), custom_call_target="tpu_custom_call" | custom-call | tf_op jit(solution)/shard_map/pallas_call | solution.py:513
  3.6 1.4 %collective-permute-start.1 = (f32[32,16,128]{2,1,0:T(8,128)}, f32[32,16,128]{2,1,0:T(8,128)S(1)}, u32[]{:S(2)}, u32[]{:S(2)}) collective-permute-start(f32[32,16,128]{2,1,0:T(8,128)} %get-tuple-element.51), channel_id=1, source_target_pairs={{0,7},{1,0},{2,1},{3,2},{4,3},{5,4},{6,5},{7,6},{8,15},{9,8},{10,9... | collective-permute-start | bytes 786440 | tf_op jit(solution)/shard_map/ppermute | solution.py:505
  5.1 1.3 %collective-permute-start = (f32[32,8,128]{2,1,0:T(8,128)}, f32[32,8,128]{2,1,0:T(8,128)S(1)}, u32[]{:S(2)}, u32[]{:S(2)}) collective-permute-start(f32[32,8,128]{2,1,0:T(8,128)} %get-tuple-element.50), channel_id=1, source_target_pairs={{0,1},{1,2},{2,3},{3,4},{4,5},{5,6},{6,7},{7,0},{8,9},{9,10},{10,1... | collective-permute-start | bytes 393224 | tf_op jit(solution)/shard_map/ppermute | solution.py:505
  6.4 11.0 %all-to-all-start = ((f32[128,1,640]{2,1,0:T(1,128)}), f32[128,1,640]{2,1,0:T(1,128)S(1)}, u32[]{:S(2)}, u32[]{:S(2)}) async-start(f32[128,1,640]{2,1,0:T(1,128)} %bitcast.4), calls=%async_computation | async-start | bytes 655360 | tf_op jit(solution)/shard_map/all_to_all | solution.py:526
  17.4 0.0 copy-done
  17.4 0.0 collective-permute-done.below.d_below
  17.4 0.0 copy-start.2
  17.5 0.0 collective-permute-done.1.above.d_above
  17.5 1.0 shard_map.87
  18.5 0.0 copy-done.2
  18.5 5.4 %collective-permute-start.7 = (f32[11,88,128]{2,1,0:T(8,128)}, f32[11,88,128]{2,1,0:T(8,128)S(1)}, u32[]{:S(2)}, u32[]{:S(2)}) collective-permute-start(f32[11,88,128]{2,1,0:T(8,128)} %get-tuple-element.52.unused_low), channel_id=1, source_target_pairs={{0,120},{8,0},{16,8},{24,16},{32,24},{40,32},{48,40},{56,48},{64,5... | collective-permute-start | bytes 1486856 | tf_op jit(solution)/shard_map/ppermute | solution.py:505
  23.9 0.0 collective-permute-start.6
  23.9 5.1 %all-to-all-done = f32[128,1,640]{2,1,0:T(1,128)S(1)} async-done(((f32[128,1,640]{2,1,0:T(1,128)}), f32[128,1,640]{2,1,0:T(1,128)S(1)}, u32[]{:S(2)}, u32[]{:S(2)}) %all-to-all-start) | async-done | bytes 327712 | tf_op jit(solution)/shard_map/all_to_all | solution.py:526
  28.9 0.0 copy-done.1
  28.9 4.2 %shard_map.88 = (f32[35,72,128]{2,1,0:T(8,128)S(1)}, f32[10,72,128]{2,1,0:T(8,128)S(1)}, f32[10,72,128]{2,1,0:T(8,128)S(1)}, f32[35,16,128]{2,1,0:T(8,128)S(1)}, f32[35,16,128]{2,1,0:T(8,128)S(1)}) custom-call(f32[640,128]{1,0:T(8,128)S(1)} %bitcast.2, f32[32,64,128]{2,1,0:T(8,128)S(1)} %copy-done.1, f32[11,88,128]{2,1,0:T(8,128)} %get-tuple-element.52.unused_low, ...), custom_call_target="tpu_custom_call" | custom-call | tf_op jit(solution)/shard_map/pallas_call | solution.py:535
  33.2 0.9 collective-permute-start.2
  34.1 0.1 collective-permute-start.3
  34.2 0.7 collective-permute-start.4
  34.9 2.7 %collective-permute-done.2.y_below.below = f32[35,16,128]{2,1,0:T(8,128)S(1)} collective-permute-done((f32[35,16,128]{2,1,0:T(8,128)S(1)}, f32[35,16,128]{2,1,0:T(8,128)S(1)}, u32[]{:S(2)}, u32[]{:S(2)}) %collective-permute-start.2) | collective-permute-done | bytes 286752 | tf_op jit(solution)/shard_map/ppermute | solution.py:505
  37.7 1.4 %collective-permute-start.5 = (f32[10,72,128]{2,1,0:T(8,128)S(1)}, f32[10,72,128]{2,1,0:T(8,128)S(1)}, u32[]{:S(2)}, u32[]{:S(2)}) collective-permute-start(f32[10,72,128]{2,1,0:T(8,128)S(1)} %get-tuple-element.64), channel_id=1, source_target_pairs={{0,120},{8,0},{16,8},{24,16},{32,24},{40,32},{48,40},{56,48},{64,5... | collective-permute-start | bytes 1105928 | tf_op jit(solution)/shard_map/ppermute | solution.py:505
  39.1 1.4 %collective-permute-done.3.y_above.above = f32[35,16,128]{2,1,0:T(8,128)S(1)} collective-permute-done((f32[35,16,128]{2,1,0:T(8,128)S(1)}, f32[35,16,128]{2,1,0:T(8,128)S(1)}, u32[]{:S(2)}, u32[]{:S(2)}) %collective-permute-start.3) | collective-permute-done | bytes 286752 | tf_op jit(solution)/shard_map/ppermute | solution.py:505
  40.5 0.0 collective-permute-done.6.unused_low.refs_10_.refs_13_
  40.5 0.0 collective-permute-done.7.unused_high.refs_11_.refs_14_
  40.5 0.2 collective-permute-start.8
  40.7 4.7 %collective-permute-start.9 = (f32[10,24,128]{2,1,0:T(8,128)S(1)}, f32[10,24,128]{2,1,0:T(8,128)S(1)}, u32[]{:S(2)}, u32[]{:S(2)}) collective-permute-start(f32[10,24,128]{2,1,0:T(8,128)S(1)} %get-tuple-element.66), channel_id=1, source_target_pairs={{0,120},{8,0},{16,8},{24,16},{32,24},{40,32},{48,40},{56,48},{64,5... | collective-permute-start | bytes 368648 | tf_op jit(solution)/shard_map/ppermute | solution.py:505
  45.3 0.0 copy-done.3
  45.3 2.6 %shard_map.89 = (f32[32,10,8,128]{3,2,1,0:T(8,128)S(1)}, f32[32,10,8,128]{3,2,1,0:T(8,128)S(1)}, f32[32,10,8,128]{3,2,1,0:T(8,128)S(1)}, f32[32,10,8,128]{3,2,1,...) custom-call(f32[35,72,128]{2,1,0:T(8,128)S(1)} %get-tuple-element.54.charge, ...), custom_call_target="tpu_custom_call" | custom-call | flops 20000000000 | bytes 1048576 | tf_op jit(solution)/shard_map/pallas_call | solution.py:557
  48.0 0.0 collective-permute-done.4.refs_6_
  48.0 0.0 collective-permute-done.5.refs_7_
  48.0 1.3 %collective-permute-done.8.refs_8_ = f32[10,24,128]{2,1,0:T(8,128)S(1)} collective-permute-done((f32[10,24,128]{2,1,0:T(8,128)S(1)}, f32[10,24,128]{2,1,0:T(8,128)S(1)}, u32[]{:S(2)}, u32[]{:S(2)}) %collective-permute-start.8) | collective-permute-done | bytes 122912 | tf_op jit(solution)/shard_map/ppermute | solution.py:505
  49.3 0.0 collective-permute-done.9.refs_9_
  49.3 2.6 %shard_map.91 = (f32[32,64,128]{2,1,0:T(8,128)S(1)}, f32[3,64,128]{2,1,0:T(8,128)S(1)}, f32[8,64,128]{2,1,0:T(8,128)S(1)}, f32[8,64,128]{2,1,0:T(8,128)S(1)}, f3...) custom-call(f32[32,10,8,128]{3,2,1,0:T(8,128)S(1)} %get-tuple-elemen, ...), custom_call_target="tpu_custom_call" | custom-call | tf_op jit(solution)/shard_map/pallas_call | solution.py:565
  51.9 2.2 %collective-permute-start.10 = (f32[35,8,128]{2,1,0:T(8,128)S(1)}, f32[35,8,128]{2,1,0:T(8,128)S(1)}, u32[]{:S(2)}, u32[]{:S(2)}) collective-permute-start(f32[35,8,128]{2,1,0:T(8,128)S(1)} %get-tuple-element.68), channel_id=1, source_target_pairs={{0,1},{1,2},{2,3},{3,4},{4,5},{5,6},{6,7},{7,0},{8,9},{9,10},{10,1... | collective-permute-start | bytes 430088 | tf_op jit(solution)/shard_map/ppermute | solution.py:505
  54.1 0.1 collective-permute-start.11
  54.2 0.5 collective-permute-start.12
  54.7 4.5 %collective-permute-start.13 = (f32[8,64,128]{2,1,0:T(8,128)S(1)}, f32[8,64,128]{2,1,0:T(8,128)S(1)}, u32[]{:S(2)}, u32[]{:S(2)}) collective-permute-start(f32[8,64,128]{2,1,0:T(8,128)S(1)} %get-tuple-element.77), channel_id=1, source_target_pairs={{0,120},{8,0},{16,8},{24,16},{32,24},{40,32},{48,40},{56,48},{64,5... | collective-permute-start | bytes 786440 | tf_op jit(solution)/shard_map/ppermute | solution.py:505
  59.2 0.0 collective-permute-done.10.y_below.below.refs_5_
  59.3 0.0 collective-permute-done.11.y_above.above.refs_6_
  59.3 0.2 collective-permute-start.14
  59.4 5.0 %collective-permute-start.15 = (f32[8,16,128]{2,1,0:T(8,128)S(1)}, f32[8,16,128]{2,1,0:T(8,128)S(1)}, u32[]{:S(2)}, u32[]{:S(2)}) collective-permute-start(f32[8,16,128]{2,1,0:T(8,128)S(1)} %get-tuple-element.79), channel_id=1, source_target_pairs={{0,120},{8,0},{16,8},{24,16},{32,24},{40,32},{48,40},{56,48},{64,5... | collective-permute-start | bytes 196616 | tf_op jit(solution)/shard_map/ppermute | solution.py:505
  64.4 3.6 %shard_map.92 = (f32[32,10,8,128]{3,2,1,0:T(8,128)S(1)}, f32[32,10,8,128]{3,2,1,0:T(8,128)S(1)}, f32[32,10,8,128]{3,2,1,0:T(8,128)S(1)}, f32[32,10,8,128]{3,2,1,0:T(8,128)S(1)}) custom-call(f32[32,64,128]{2,1,0:T(8,128)S(1)} %get-tuple-element.67.own, f32[35,8,128]{2,1,0:T(8,128)S(1)} %collective-permute-done.10.y_below.below.refs_5_, ...), custom_call_target="tpu_custom_call" | custom-call | flops 20000000000 | bytes 1048576 | tf_op jit(solution)/shard_map/pallas_call | solution.py:575
  68.0 0.0 collective-permute-done.14.refs_9_
  68.0 0.0 collective-permute-done.15.refs_10_
  68.0 0.0 collective-permute-done.12.refs_7_
  68.0 0.0 collective-permute-done.13.refs_8_
  68.1 3.1 %shard_map.94 = (f32[32,64,128]{2,1,0:T(8,128)S(1)}, f32[3,64,128]{2,1,0:T(8,128)S(1)}, f32[8,64,128]{2,1,0:T(8,128)S(1)}, f32[8,64,128]{2,1,0:T(8,128)S(1)}, f3...) custom-call(f32[32,10,8,128]{3,2,1,0:T(8,128)S(1)} %get-tuple-element.71.refs_0_, ...), custom_call_target="tpu_custom_call" | custom-call | tf_op jit(solution)/shard_map/pallas_call | solution.py:580
  71.1 3.5 %collective-permute-start.17 = (f32[35,16,128]{2,1,0:T(8,128)S(1)}, f32[35,16,128]{2,1,0:T(8,128)S(1)}, u32[]{:S(2)}, u32[]{:S(2)}) collective-permute-start(f32[35,16,128]{2,1,0:T(8,128)S(1)} %get-tuple-element.83), channel_id=1, source_target_pairs={{0,7},{1,0},{2,1},{3,2},{4,3},{5,4},{6,5},{7,6},{8,15},{9,8},{10,9... | collective-permute-start | bytes 860168 | tf_op jit(solution)/shard_map/ppermute | solution.py:505
  74.6 0.0 collective-permute-start.16
  74.6 0.0 collective-permute-start.18
  74.6 4.8 %collective-permute-start.19 = (f32[8,64,128]{2,1,0:T(8,128)S(1)}, f32[8,64,128]{2,1,0:T(8,128)S(1)}, u32[]{:S(2)}, u32[]{:S(2)}) collective-permute-start(f32[8,64,128]{2,1,0:T(8,128)S(1)} %get-tuple-element.90), channel_id=1, source_target_pairs={{0,120},{8,0},{16,8},{24,16},{32,24},{40,32},{48,40},{56,48},{64,5... | collective-permute-start | bytes 786440 | tf_op jit(solution)/shard_map/ppermute | solution.py:505
  79.4 0.0 collective-permute-done.16.y_below.below.refs_5_
  79.4 0.0 collective-permute-done.17.y_above.above.refs_6_
  79.4 0.1 collective-permute-start.20
  79.5 4.8 %collective-permute-start.21 = (f32[8,24,128]{2,1,0:T(8,128)S(1)}, f32[8,24,128]{2,1,0:T(8,128)S(1)}, u32[]{:S(2)}, u32[]{:S(2)}) collective-permute-start(f32[8,24,128]{2,1,0:T(8,128)S(1)} %get-tuple-element.92), channel_id=1, source_target_pairs={{0,120},{8,0},{16,8},{24,16},{32,24},{40,32},{48,40},{56,48},{64,5... | collective-permute-start | bytes 294920 | tf_op jit(solution)/shard_map/ppermute | solution.py:505
  84.3 4.1 %shard_map.95 = (f32[32,11,8,128]{3,2,1,0:T(8,128)S(1)}, f32[32,11,8,128]{3,2,1,0:T(8,128)S(1)}, f32[32,11,8,128]{3,2,1,0:T(8,128)S(1)}, f32[32,11,8,128]{3,2,1,0:T(8,128)S(1)}) custom-call(f32[32,64,128]{2,1,0:T(8,128)S(1)} %get-tuple-element.81.own, f32[35,8,128]{2,1,0:T(8,128)S(1)} %collective-permute-done.16.y_below.below.refs_5_, ...), custom_call_target="tpu_custom_call" | custom-call | flops 20000000000 | bytes 1048576 | tf_op jit(solution)/shard_map/pallas_call | solution.py:575
  88.4 0.0 collective-permute-done.18.refs_7_
  88.4 0.0 collective-permute-done.19.refs_8_
  88.4 0.0 collective-permute-done.20.refs_9_
  88.4 0.0 collective-permute-done.21.refs_10_
  88.4 0.0 copy-start.4
  88.5 4.9 %shard_map.97 = (f32[32,64,128]{2,1,0:T(8,128)}, f32[128,1,128]{2,1,0:T(1,128)S(1)}) custom-call(f32[32,11,8,128]{3,2,1,0:T(8,128)S(1)} %get-tuple-element.84.refs_0_, f32[32,11,8,128]{3,2,1,0:T(8,128)S(1)} %get-tuple-element.85.refs_1_, f32[32,11,8,128]{3,2,1,0:T(8,128)S(1)} %get-tuple-element.86.refs_2_, f32[32,11,8,128]{3,2,1,0:T(8,128)S(1)} %get-tuple-element.87.refs_3_, ...), custom_call_target="tpu_custom_call" | custom-call | tf_op jit(solution)/shard_map/pallas_call | solution.py:583
  93.4 17.7 %all_to_all.10.got = f32[128,1,128]{2,1,0:T(1,128)S(1)} all-to-all(f32[128,1,128]{2,1,0:T(1,128)S(1)} %get-tuple-element.95), channel_id=1, replica_groups=mesh['gx'=16,'gy'=8] {'gx','gy'}, dimensions={0} | all-to-all | bytes 131072 | tf_op jit(solution)/shard_map/all_to_all | solution.py:591
  111.1 1.2 %shard_map.98 = f32[16]{0:T(128)} custom-call(f32[1,128]{1,0:T(1,128)S(1)} %copy-done.4, f32[128,1,128]{2,1,0:T(1,128)S(1)} %all_to_all.10.got), custom_call_target="tpu_custom_call" | custom-call | tf_op jit(solution)/shard_map/pallas_call | solution.py:592
  (8 shorter events, 0.1 us)
Async XLA Ops:
  0.6 16.7 %copy-start = (f32[32,64,128]{2,1,0:T(8,128)S(1)}, f32[32,64,128]{2,1,0:T(8,128)}, u32[]{:S(2)}) copy-start(f32[32,64,128]{2,1,0:T(8,128)} %density.1) | copy-start | bytes 3145732
  3.6 13.8 %collective-permute-start.1 = (f32[32,16,128]{2,1,0:T(8,128)}, f32[32,16,128]{2,1,0:T(8,128)S(1)}, u32[]{:S(2)}, u32[]{:S(2)}) collective-permute-start(f32[32,16,128]{2,1,0:T(8,128)} %get-tuple-element.51), channel_id=1, source_target_pairs={{0,7},{1,0},{2,1},{3,2},{4,3},{5,4},{6,5},{7,6},{8,15},{9,8},{10,9... | collective-permute-start | bytes 786440 | tf_op jit(solution)/shard_map/ppermute | solution.py:505
  5.1 12.4 %collective-permute-start = (f32[32,8,128]{2,1,0:T(8,128)}, f32[32,8,128]{2,1,0:T(8,128)S(1)}, u32[]{:S(2)}, u32[]{:S(2)}) collective-permute-start(f32[32,8,128]{2,1,0:T(8,128)} %get-tuple-element.50), channel_id=1, source_target_pairs={{0,1},{1,2},{2,3},{3,4},{4,5},{5,6},{6,7},{7,0},{8,9},{9,10},{10,1... | collective-permute-start | bytes 393224 | tf_op jit(solution)/shard_map/ppermute | solution.py:505
  6.4 22.6 %copy-start.1 = (f32[32,64,128]{2,1,0:T(8,128)S(1)}, f32[32,64,128]{2,1,0:T(8,128)}, u32[]{:S(2)}) copy-start(f32[32,64,128]{2,1,0:T(8,128)} %ion.1) | copy-start | bytes 3145732
  6.4 22.6 %all-to-all-start = ((f32[128,1,640]{2,1,0:T(1,128)}), f32[128,1,640]{2,1,0:T(1,128)S(1)}, u32[]{:S(2)}, u32[]{:S(2)}) async-start(f32[128,1,640]{2,1,0:T(1,128)} %bitcast.4), calls=%async_computation | async-start | bytes 655360 | tf_op jit(solution)/shard_map/all_to_all | solution.py:526
  17.4 1.0 copy-start.2
  18.5 22.0 %collective-permute-start.7 = (f32[11,88,128]{2,1,0:T(8,128)}, f32[11,88,128]{2,1,0:T(8,128)S(1)}, u32[]{:S(2)}, u32[]{:S(2)}) collective-permute-start(f32[11,88,128]{2,1,0:T(8,128)} %get-tuple-element.52.unused_low), channel_id=1, source_target_pairs={{0,120},{8,0},{16,8},{24,16},{32,24},{40,32},{48,40},{56,48},{64,5... | collective-permute-start | bytes 1486856 | tf_op jit(solution)/shard_map/ppermute | solution.py:505
  23.9 16.6 %collective-permute-start.6 = (f32[8,88,128]{2,1,0:T(8,128)}, f32[8,88,128]{2,1,0:T(8,128)S(1)}, u32[]{:S(2)}, u32[]{:S(2)}) collective-permute-start(f32[8,88,128]{2,1,0:T(8,128)} %get-tuple-element.53.unused_high), channel_id=1, source_target_pairs={{0,8},{8,16},{16,24},{24,32},{32,40},{40,48},{48,56},{56,64},{64,7... | collective-permute-start | bytes 1081352 | tf_op jit(solution)/shard_map/ppermute | solution.py:505
  28.9 16.4 %copy-start.3 = (f32[32,8,128]{2,1,0:T(8,128)S(1)}, f32[32,8,128]{2,1,0:T(8,128)}, u32[]{:S(2)}) copy-start(f32[32,8,128]{2,1,0:T(8,128)} %copy-done.2) | copy-start | bytes 393220
  33.2 4.5 %collective-permute-start.2 = (f32[35,16,128]{2,1,0:T(8,128)S(1)}, f32[35,16,128]{2,1,0:T(8,128)S(1)}, u32[]{:S(2)}, u32[]{:S(2)}) collective-permute-start(f32[35,16,128]{2,1,0:T(8,128)S(1)} %get-tuple-element.55), channel_id=1, source_target_pairs={{0,1},{1,2},{2,3},{3,4},{4,5},{5,6},{6,7},{7,0},{8,9},{9,10},{10,1... | collective-permute-start | bytes 860168 | tf_op jit(solution)/shard_map/ppermute | solution.py:505
  34.1 6.4 %collective-permute-start.3 = (f32[35,16,128]{2,1,0:T(8,128)S(1)}, f32[35,16,128]{2,1,0:T(8,128)S(1)}, u32[]{:S(2)}, u32[]{:S(2)}) collective-permute-start(f32[35,16,128]{2,1,0:T(8,128)S(1)} %get-tuple-element.56), channel_id=1, source_target_pairs={{0,7},{1,0},{2,1},{3,2},{4,3},{5,4},{6,5},{7,6},{8,15},{9,8},{10,9... | collective-permute-start | bytes 860168 | tf_op jit(solution)/shard_map/ppermute | solution.py:505
  34.2 13.8 %collective-permute-start.4 = (f32[10,72,128]{2,1,0:T(8,128)S(1)}, f32[10,72,128]{2,1,0:T(8,128)S(1)}, u32[]{:S(2)}, u32[]{:S(2)}) collective-permute-start(f32[10,72,128]{2,1,0:T(8,128)S(1)} %get-tuple-element.63), channel_id=1, source_target_pairs={{0,8},{8,16},{16,24},{24,32},{32,40},{40,48},{48,56},{56,64},{64,7... | collective-permute-start | bytes 1105928 | tf_op jit(solution)/shard_map/ppermute | solution.py:505
  37.7 10.3 %collective-permute-start.5 = (f32[10,72,128]{2,1,0:T(8,128)S(1)}, f32[10,72,128]{2,1,0:T(8,128)S(1)}, u32[]{:S(2)}, u32[]{:S(2)}) collective-permute-start(f32[10,72,128]{2,1,0:T(8,128)S(1)} %get-tuple-element.64), channel_id=1, source_target_pairs={{0,120},{8,0},{16,8},{24,16},{32,24},{40,32},{48,40},{56,48},{64,5... | collective-permute-start | bytes 1105928 | tf_op jit(solution)/shard_map/ppermute | solution.py:505
  40.5 8.8 %collective-permute-start.8 = (f32[10,24,128]{2,1,0:T(8,128)S(1)}, f32[10,24,128]{2,1,0:T(8,128)S(1)}, u32[]{:S(2)}, u32[]{:S(2)}) collective-permute-start(f32[10,24,128]{2,1,0:T(8,128)S(1)} %get-tuple-element.65), channel_id=1, source_target_pairs={{0,8},{8,16},{16,24},{24,32},{32,40},{40,48},{48,56},{56,64},{64,7... | collective-permute-start | bytes 368648 | tf_op jit(solution)/shard_map/ppermute | solution.py:505
  40.7 8.6 %collective-permute-start.9 = (f32[10,24,128]{2,1,0:T(8,128)S(1)}, f32[10,24,128]{2,1,0:T(8,128)S(1)}, u32[]{:S(2)}, u32[]{:S(2)}) collective-permute-start(f32[10,24,128]{2,1,0:T(8,128)S(1)} %get-tuple-element.66), channel_id=1, source_target_pairs={{0,120},{8,0},{16,8},{24,16},{32,24},{40,32},{48,40},{56,48},{64,5... | collective-permute-start | bytes 368648 | tf_op jit(solution)/shard_map/ppermute | solution.py:505
  51.9 7.4 %collective-permute-start.10 = (f32[35,8,128]{2,1,0:T(8,128)S(1)}, f32[35,8,128]{2,1,0:T(8,128)S(1)}, u32[]{:S(2)}, u32[]{:S(2)}) collective-permute-start(f32[35,8,128]{2,1,0:T(8,128)S(1)} %get-tuple-element.68), channel_id=1, source_target_pairs={{0,1},{1,2},{2,3},{3,4},{4,5},{5,6},{6,7},{7,0},{8,9},{9,10},{10,1... | collective-permute-start | bytes 430088 | tf_op jit(solution)/shard_map/ppermute | solution.py:505
  54.1 5.1 %collective-permute-start.11 = (f32[35,8,128]{2,1,0:T(8,128)S(1)}, f32[35,8,128]{2,1,0:T(8,128)S(1)}, u32[]{:S(2)}, u32[]{:S(2)}) collective-permute-start(f32[35,8,128]{2,1,0:T(8,128)S(1)} %get-tuple-element.69), channel_id=1, source_target_pairs={{0,7},{1,0},{2,1},{3,2},{4,3},{5,4},{6,5},{7,6},{8,15},{9,8},{10,9... | collective-permute-start | bytes 430088 | tf_op jit(solution)/shard_map/ppermute | solution.py:505
  54.2 13.9 %collective-permute-start.12 = (f32[8,64,128]{2,1,0:T(8,128)S(1)}, f32[8,64,128]{2,1,0:T(8,128)S(1)}, u32[]{:S(2)}, u32[]{:S(2)}) collective-permute-start(f32[8,64,128]{2,1,0:T(8,128)S(1)} %get-tuple-element.76), channel_id=1, source_target_pairs={{0,8},{8,16},{16,24},{24,32},{32,40},{40,48},{48,56},{56,64},{64,7... | collective-permute-start | bytes 786440 | tf_op jit(solution)/shard_map/ppermute | solution.py:505
  54.7 13.3 %collective-permute-start.13 = (f32[8,64,128]{2,1,0:T(8,128)S(1)}, f32[8,64,128]{2,1,0:T(8,128)S(1)}, u32[]{:S(2)}, u32[]{:S(2)}) collective-permute-start(f32[8,64,128]{2,1,0:T(8,128)S(1)} %get-tuple-element.77), channel_id=1, source_target_pairs={{0,120},{8,0},{16,8},{24,16},{32,24},{40,32},{48,40},{56,48},{64,5... | collective-permute-start | bytes 786440 | tf_op jit(solution)/shard_map/ppermute | solution.py:505
  59.3 8.7 %collective-permute-start.14 = (f32[8,16,128]{2,1,0:T(8,128)S(1)}, f32[8,16,128]{2,1,0:T(8,128)S(1)}, u32[]{:S(2)}, u32[]{:S(2)}) collective-permute-start(f32[8,16,128]{2,1,0:T(8,128)S(1)} %get-tuple-element.78), channel_id=1, source_target_pairs={{0,8},{8,16},{16,24},{24,32},{32,40},{40,48},{48,56},{56,64},{64,7... | collective-permute-start | bytes 196616 | tf_op jit(solution)/shard_map/ppermute | solution.py:505
  59.4 8.6 %collective-permute-start.15 = (f32[8,16,128]{2,1,0:T(8,128)S(1)}, f32[8,16,128]{2,1,0:T(8,128)S(1)}, u32[]{:S(2)}, u32[]{:S(2)}) collective-permute-start(f32[8,16,128]{2,1,0:T(8,128)S(1)} %get-tuple-element.79), channel_id=1, source_target_pairs={{0,120},{8,0},{16,8},{24,16},{32,24},{40,32},{48,40},{56,48},{64,5... | collective-permute-start | bytes 196616 | tf_op jit(solution)/shard_map/ppermute | solution.py:505
  71.1 8.3 %collective-permute-start.17 = (f32[35,16,128]{2,1,0:T(8,128)S(1)}, f32[35,16,128]{2,1,0:T(8,128)S(1)}, u32[]{:S(2)}, u32[]{:S(2)}) collective-permute-start(f32[35,16,128]{2,1,0:T(8,128)S(1)} %get-tuple-element.83), channel_id=1, source_target_pairs={{0,7},{1,0},{2,1},{3,2},{4,3},{5,4},{6,5},{7,6},{8,15},{9,8},{10,9... | collective-permute-start | bytes 860168 | tf_op jit(solution)/shard_map/ppermute | solution.py:505
  74.6 4.8 %collective-permute-start.16 = (f32[35,8,128]{2,1,0:T(8,128)S(1)}, f32[35,8,128]{2,1,0:T(8,128)S(1)}, u32[]{:S(2)}, u32[]{:S(2)}) collective-permute-start(f32[35,8,128]{2,1,0:T(8,128)S(1)} %get-tuple-element.82), channel_id=1, source_target_pairs={{0,1},{1,2},{2,3},{3,4},{4,5},{5,6},{6,7},{7,0},{8,9},{9,10},{10,1... | collective-permute-start | bytes 430088 | tf_op jit(solution)/shard_map/ppermute | solution.py:505
  74.6 13.8 %collective-permute-start.18 = (f32[8,64,128]{2,1,0:T(8,128)S(1)}, f32[8,64,128]{2,1,0:T(8,128)S(1)}, u32[]{:S(2)}, u32[]{:S(2)}) collective-permute-start(f32[8,64,128]{2,1,0:T(8,128)S(1)} %get-tuple-element.89), channel_id=1, source_target_pairs={{0,8},{8,16},{16,24},{24,32},{32,40},{40,48},{48,56},{56,64},{64,7... | collective-permute-start | bytes 786440 | tf_op jit(solution)/shard_map/ppermute | solution.py:505
  74.6 13.8 %collective-permute-start.19 = (f32[8,64,128]{2,1,0:T(8,128)S(1)}, f32[8,64,128]{2,1,0:T(8,128)S(1)}, u32[]{:S(2)}, u32[]{:S(2)}) collective-permute-start(f32[8,64,128]{2,1,0:T(8,128)S(1)} %get-tuple-element.90), channel_id=1, source_target_pairs={{0,120},{8,0},{16,8},{24,16},{32,24},{40,32},{48,40},{56,48},{64,5... | collective-permute-start | bytes 786440 | tf_op jit(solution)/shard_map/ppermute | solution.py:505
  79.4 9.0 %collective-permute-start.20 = (f32[8,24,128]{2,1,0:T(8,128)S(1)}, f32[8,24,128]{2,1,0:T(8,128)S(1)}, u32[]{:S(2)}, u32[]{:S(2)}) collective-permute-start(f32[8,24,128]{2,1,0:T(8,128)S(1)} %get-tuple-element.91), channel_id=1, source_target_pairs={{0,8},{8,16},{16,24},{24,32},{32,40},{40,48},{48,56},{56,64},{64,7... | collective-permute-start | bytes 294920 | tf_op jit(solution)/shard_map/ppermute | solution.py:505
  79.5 8.9 %collective-permute-start.21 = (f32[8,24,128]{2,1,0:T(8,128)S(1)}, f32[8,24,128]{2,1,0:T(8,128)S(1)}, u32[]{:S(2)}, u32[]{:S(2)}) collective-permute-start(f32[8,24,128]{2,1,0:T(8,128)S(1)} %get-tuple-element.92), channel_id=1, source_target_pairs={{0,120},{8,0},{16,8},{24,16},{32,24},{40,32},{48,40},{56,48},{64,5... | collective-permute-start | bytes 294920 | tf_op jit(solution)/shard_map/ppermute | solution.py:505
  88.4 22.7 %copy-start.4 = (f32[1,128]{1,0:T(1,128)S(1)}, f32[1,128]{1,0:T(1,128)}, u32[]{:S(2)}) copy-start(f32[1,128]{1,0:T(1,128)} %get-tuple-element.94.table) | copy-start | bytes 1540
